TPU v7x, 32 devices: a whole 2x2x4 slice. The times are simulated.
32 devices in a mesh: row: 8 (over y, x, core), col: 4 (over z).
Axes of the slice: x: 2, y: 2, z: 4, core: 2. Of those that a mesh axis runs over, the one named last changes fastest.
Arguments:
- block_in: bfloat16 [8192, 1024], P(('row', 'col')), may hold values from -6 to 6
- attn_gain: bfloat16 [1024], P('row'), may hold values from 0.5 to 1.5
- moe_gain: bfloat16 [1024], P('row'), may hold values from 0.5 to 1.5
- w_query: bfloat16 [1024, 1024], P('row', 'col'), may hold values from -0.1875 to 0.1875
- w_key: bfloat16 [1024, 512], P('row', 'col'), may hold values from -0.1875 to 0.1875
- w_value: bfloat16 [1024, 512], P('row', 'col'), may hold values from -0.1875 to 0.1875
- w_out: bfloat16 [1024, 1024], P('row', 'col'), may hold values from -1 to 1
- w_router: bfloat16 [1024, 32], P('row', 'col'), may hold values from -0.09375 to 0.09375
- w_gate: bfloat16 [32, 1024, 512], P('row', None, 'col'), may hold values from -0.1875 to 0.1875
- w_up: bfloat16 [32, 1024, 512], P('row', None, 'col'), may hold values from -0.1875 to 0.1875
- w_down: bfloat16 [32, 1024, 512], P('row', None, 'col'), may hold values from -1 to 1
- expert_ids: int32 [8192, 8], P(('row', 'col')), may hold values from 0 to 31, all different within a row
- fill_order: int32 [32, 256], P(('row', 'col')), may hold values from 0 to 255, each once within a row
- prefix_len: int32 [8], P('row'), may hold values from 102 to 512
- out_grad: bfloat16 [8192, 1024], P(('row', 'col')), may hold values from -6 to 6
Outputs:
- block_out: float32 [8192, 1024], P(('row', 'col'))
- block_in_grad: float32 [8192, 1024], P(('row', 'col'))
- attn_gain_grad: float32 [1024], P('row')
- moe_gain_grad: float32 [1024], P('row')
- w_query_grad: float32 [1024, 1024], P('row', 'col')
- w_key_grad: float32 [1024, 512], P('row', 'col')
- w_value_grad: float32 [1024, 512], P('row', 'col')
- w_out_grad: float32 [1024, 1024], P('row', 'col')
- w_router_grad: float32 [1024, 32], P('row', 'col')
- w_gate_grad: float32 [32, 1024, 512], P('row', None, 'col')
- w_up_grad: float32 [32, 1024, 512], P('row', None, 'col')
- w_down_grad: float32 [32, 1024, 512], P('row', None, 'col')
Inputs may be any that keep to these rules, and one draw needn't show every extreme that they name: `expert_ids`: each token names 8 different experts. `fill_order`: each row lists the 256 tokens of its block, each once.
All inputs are finite; a program needn't handle non-finite values.
Results may differ from a plain program's by a relative error of at most 0.024.
Values may be sent and summed in bfloat16 or wider, within the bound.
No kernel may reach another device: no remote copies, remote signals or barrier semaphores. Data moves between devices by JAX's collectives and lax.ppermute only.
A program may use at most 192 MiB of HBM per device.

v0:
```python
import functools

import jax
import jax.numpy as jnp
from jax import lax
from jax.experimental import pallas as pl
from jax.experimental.pallas import tpu as pltpu
from jax.sharding import PartitionSpec as P

D = 1024
H = 16
KVH = 8
HD = 64
E = 32
TOPK = 8
CAP = 80


EPS = 1e-06
NEGATIVE = -1e30


def cross_rows(left, right):
    return lax.dot_general(
        left, right, (((0,), (0,)), ((), ())), preferred_element_type=jnp.float32
    )


def times_back(left, right):
    return lax.dot_general(
        left, right, (((1,), (1,)), ((), ())), preferred_element_type=jnp.float32
    )


def rope_tables(first_position, count):
    position = (first_position + jnp.arange(count, dtype=jnp.int32)).astype(jnp.float32)
    inverse = 10000.0 ** (-jnp.arange(HD // 2, dtype=jnp.float32) * 2.0 / HD)
    angle = position[:, None] * inverse[None, :]
    return (jnp.cos(angle), jnp.sin(angle))


def rotate(values, cosine, sine):
    half = HD // 2
    first, second = (values[..., :half], values[..., half:])
    cos_rows = cosine[:, None, :]
    sin_rows = sine[:, None, :]
    return jnp.concatenate(
        [first * cos_rows - second * sin_rows, second * cos_rows + first * sin_rows], axis=-1
    )


def rotate_back(grads, cosine, sine):
    half = HD // 2
    first, second = (grads[..., :half], grads[..., half:])
    cos_rows = cosine[:, None, :]
    sin_rows = sine[:, None, :]
    return jnp.concatenate(
        [first * cos_rows + second * sin_rows, second * cos_rows - first * sin_rows], axis=-1
    )


def norm_rows(values, gain):
    scale = lax.rsqrt(jnp.mean(values * values, axis=1, keepdims=True) + EPS)
    normed = values * scale
    return (normed, scale, (normed * gain).astype(jnp.bfloat16))


def norm_back(grad_in, normed, scale, gain):
    gain_grad = jnp.sum(grad_in * normed, axis=0)
    inner = grad_in * gain
    return (scale * (inner - normed * jnp.mean(inner * normed, axis=1, keepdims=True)), gain_grad)


def to_heads(rows, count, group):
    return rows.reshape(count, KVH, group, HD).transpose(1, 2, 0, 3).reshape(KVH, group * count, HD)


def from_heads(heads, count, group):
    return heads.reshape(KVH, group, count, HD).transpose(2, 0, 1, 3).reshape(count, H, HD)


def general(
    block_in,
    attn_gain,
    moe_gain,
    w_query,
    w_key,
    w_value,
    w_out,
    w_router,
    w_gate,
    w_up,
    w_down,
    expert_ids,
    fill_order,
    prefix_len,
    out_grad,
):
    tok_rows = block_in.shape[0]
    n_col = lax.axis_size("col")
    col_index = lax.axis_index("col")
    seq_rows = tok_rows * n_col
    group = H // KVH
    scale_attn = HD ** (-0.5)
    bf16 = jnp.bfloat16
    f32 = jnp.float32
    shared = (
        lax.all_gather(w_query, "row", axis=0, tiled=True),
        lax.all_gather(w_key, "row", axis=0, tiled=True),
        lax.all_gather(w_value, "row", axis=0, tiled=True),
        lax.all_gather(w_out, "row", axis=0, tiled=True),
        lax.all_gather(w_router, "row", axis=0, tiled=True),
        lax.all_gather(attn_gain, "row", axis=0, tiled=True),
        lax.all_gather(moe_gain, "row", axis=0, tiled=True),
    )
    wq_full, wk_full, wv_full, wo_full, wr_full = (
        lax.all_gather(shared[0], "col", axis=1, tiled=True),
        lax.all_gather(shared[1], "col", axis=1, tiled=True),
        lax.all_gather(shared[2], "col", axis=1, tiled=True),
        lax.all_gather(shared[3], "col", axis=1, tiled=True),
        lax.all_gather(shared[4], "col", axis=1, tiled=True),
    )
    gain_one = shared[5].astype(f32)
    gain_two = shared[6].astype(f32)
    x_rows = block_in.astype(f32)
    normed_one, scale_one, attn_in = norm_rows(x_rows, gain_one)
    query = jnp.dot(attn_in, wq_full, preferred_element_type=f32)
    key = jnp.dot(attn_in, wk_full, preferred_element_type=f32)
    value = jnp.dot(attn_in, wv_full, preferred_element_type=f32).astype(bf16)
    cosine, sine = rope_tables(col_index * tok_rows, tok_rows)
    query_rot = rotate(query.reshape(tok_rows, H, HD), cosine, sine).astype(bf16)
    key_rot = (
        rotate(key.reshape(tok_rows, KVH, HD), cosine, sine)
        .astype(bf16)
        .reshape(tok_rows, KVH * HD)
    )
    keys_all, values_all = (
        lax.all_gather(key_rot, "col", axis=0, tiled=True),
        lax.all_gather(value, "col", axis=0, tiled=True),
    )
    prefix = prefix_len[0]
    query_spot = col_index * tok_rows + jnp.arange(tok_rows, dtype=jnp.int32)
    key_spot = jnp.arange(seq_rows, dtype=jnp.int32)
    allowed = (key_spot[None, :] <= query_spot[:, None]) | (key_spot[None, :] < prefix)
    allowed_rows = jnp.tile(allowed, (group, 1))
    query_heads = to_heads(query_rot.reshape(tok_rows, H * HD), tok_rows, group)
    key_heads = keys_all.reshape(seq_rows, KVH, HD).transpose(1, 0, 2)
    value_heads = values_all.reshape(seq_rows, KVH, HD).transpose(1, 0, 2)

    def attend(pieces):
        queries, keys, values = pieces
        scores = times_back(queries, keys) * scale_attn
        scores = jnp.where(allowed_rows, scores, NEGATIVE)
        highest = jnp.max(scores, axis=1, keepdims=True)
        expo = jnp.exp(scores - highest)
        total = jnp.sum(expo, axis=1, keepdims=True)
        weights = (expo / total).astype(bf16)
        mixed_heads = jnp.dot(weights, values, preferred_element_type=f32).astype(bf16)
        return (mixed_heads, (highest + jnp.log(total))[:, 0])

    mixed_heads, lse_heads = lax.map(attend, (query_heads, key_heads, value_heads))
    mixed = from_heads(mixed_heads, tok_rows, group).reshape(tok_rows, H * HD)
    resid = x_rows + jnp.dot(mixed, wo_full, preferred_element_type=f32)
    normed_two, scale_two, moe_in = norm_rows(resid, gain_two)
    logits = jnp.dot(moe_in, wr_full, preferred_element_type=f32)
    choice_hot = (expert_ids[:, :, None] == jnp.arange(E, dtype=jnp.int32)).astype(f32)
    picked = jnp.sum(choice_hot * logits[:, None, :], axis=2)
    highest = jnp.max(picked, axis=1, keepdims=True)
    expo = jnp.exp(picked - highest)
    gates = expo / jnp.sum(expo, axis=1, keepdims=True)
    order = fill_order[0]
    ranked = expert_ids[order]
    onehot = (ranked.reshape(-1, 1) == jnp.arange(E, dtype=jnp.int32)).astype(jnp.int32)
    before = jnp.cumsum(onehot, axis=0) - onehot
    ranked_slot = jnp.sum(before * onehot, axis=1).reshape(tok_rows, TOPK)
    slot = jnp.zeros((tok_rows, TOPK), jnp.int32).at[order].set(ranked_slot)
    kept = slot < CAP
    dest_grid = jnp.where(kept, expert_ids * CAP + slot, E * CAP)
    pair_ids = jnp.arange(tok_rows * TOPK, dtype=jnp.int32)
    slot_pair = (
        jnp.full((E * CAP + 1,), tok_rows * TOPK, jnp.int32)
        .at[dest_grid.reshape(-1)]
        .set(pair_ids)[: E * CAP]
    )
    slot_token = slot_pair // TOPK
    gate_slot = jnp.concatenate([gates.reshape(-1), jnp.zeros((1,), f32)])[slot_pair]
    moe_pad = jnp.concatenate([moe_in, jnp.zeros((1, D), bf16)])
    dispatch = moe_pad[slot_token].reshape(E, CAP, D)
    received = lax.all_to_all(dispatch, "row", split_axis=0, concat_axis=1, tiled=True)
    gate_w, up_w, down_w = (
        lax.all_gather(w_gate, "col", axis=2, tiled=True),
        lax.all_gather(w_up, "col", axis=2, tiled=True),
        lax.all_gather(w_down, "col", axis=2, tiled=True),
    )
    hidden_gate = jnp.einsum("erd,edf->erf", received, gate_w, preferred_element_type=f32)
    hidden_up = jnp.einsum("erd,edf->erf", received, up_w, preferred_element_type=f32)
    active = (jax.nn.silu(hidden_gate) * hidden_up).astype(bf16)
    expert_out = jnp.einsum("erf,edf->erd", active, down_w, preferred_element_type=f32).astype(bf16)
    returned = lax.all_to_all(expert_out, "row", split_axis=1, concat_axis=0, tiled=True)
    out_pad = jnp.concatenate([returned.reshape(E * CAP, D), jnp.zeros((1, D), bf16)])
    pair_out = out_pad[dest_grid]
    weight_pair = gates * kept.astype(f32)
    moe_out = jnp.zeros((tok_rows, D), f32)
    for choice_index in range(TOPK):
        moe_out = moe_out + weight_pair[:, choice_index : choice_index + 1] * pair_out[
            :, choice_index
        ].astype(f32)
    block_out = resid + moe_out
    grad_out = out_grad.astype(f32)
    gate_grad = jnp.stack(
        [
            jnp.sum(pair_out[:, choice_index].astype(f32) * grad_out, axis=1)
            for choice_index in range(TOPK)
        ],
        axis=1,
    )
    grad_pad = jnp.concatenate([grad_out, jnp.zeros((1, D), f32)])
    slot_grad = (gate_slot[:, None] * grad_pad[slot_token]).astype(bf16).reshape(E, CAP, D)
    out_grads = lax.all_to_all(slot_grad, "row", split_axis=0, concat_axis=1, tiled=True)
    act_grad = jnp.einsum("erd,edf->erf", out_grads, down_w, preferred_element_type=f32)
    sigma = jax.nn.sigmoid(hidden_gate)
    gate_h_grad = (act_grad * hidden_up * sigma * (1.0 + hidden_gate * (1.0 - sigma))).astype(bf16)
    up_h_grad = (act_grad * hidden_gate * sigma).astype(bf16)
    down_wgrad = jnp.einsum("erd,erf->edf", out_grads, active, preferred_element_type=f32)
    gate_wgrad = jnp.einsum("erd,erf->edf", received, gate_h_grad, preferred_element_type=f32)
    up_wgrad = jnp.einsum("erd,erf->edf", received, up_h_grad, preferred_element_type=f32)
    in_grad = (
        jnp.einsum("erf,edf->erd", gate_h_grad, gate_w, preferred_element_type=f32)
        + jnp.einsum("erf,edf->erd", up_h_grad, up_w, preferred_element_type=f32)
    ).astype(bf16)
    back_rows = lax.all_to_all(in_grad, "row", split_axis=1, concat_axis=0, tiled=True)
    gate_sum, up_sum, down_sum = (
        lax.psum_scatter(
            gate_wgrad.astype(jnp.bfloat16), "col", scatter_dimension=2, tiled=True
        ).astype(jnp.float32),
        lax.psum_scatter(
            up_wgrad.astype(jnp.bfloat16), "col", scatter_dimension=2, tiled=True
        ).astype(jnp.float32),
        lax.psum_scatter(
            down_wgrad.astype(jnp.bfloat16), "col", scatter_dimension=2, tiled=True
        ).astype(jnp.float32),
    )
    back_pad = jnp.concatenate([back_rows.reshape(E * CAP, D), jnp.zeros((1, D), bf16)])
    pair_back = back_pad[dest_grid]
    moe_in_grad = jnp.zeros((tok_rows, D), f32)
    for choice_index in range(TOPK):
        moe_in_grad = moe_in_grad + pair_back[:, choice_index].astype(f32)
    picked_grad = gates * (gate_grad - jnp.sum(gates * gate_grad, axis=1, keepdims=True))
    logit_grad = jnp.sum(choice_hot * picked_grad[:, :, None], axis=1).astype(bf16)
    router_wgrad = cross_rows(moe_in, logit_grad)
    moe_in_grad = moe_in_grad + times_back(logit_grad, wr_full)
    norm_two_grad, gain_two_grad = norm_back(moe_in_grad, normed_two, scale_two, gain_two)
    resid_grad = grad_out + norm_two_grad
    branch_grad = resid_grad.astype(bf16)
    out_wgrad = cross_rows(mixed, branch_grad)
    mixed_grad = times_back(branch_grad, wo_full).astype(bf16)
    grad_heads = to_heads(mixed_grad, tok_rows, group)

    def query_side(pieces):
        queries, keys, values, lse_rows, grad_rows = pieces
        scores = jnp.where(allowed_rows, times_back(queries, keys) * scale_attn, NEGATIVE)
        probs = jnp.exp(scores - lse_rows[:, None])
        prob_grad = times_back(grad_rows, values)
        delta = jnp.sum(probs * prob_grad, axis=1, keepdims=True)
        score_grad = (probs * (prob_grad - delta)).astype(bf16)
        query_grad = jnp.dot(score_grad, keys, preferred_element_type=f32) * scale_attn
        return (query_grad, delta[:, 0], score_grad, probs)

    def both_sides(pieces):
        queries, keys, values, lse_rows, grad_rows = pieces
        query_grad, delta, score_grad, probs = query_side(pieces)
        key_grad = cross_rows(score_grad, queries) * scale_attn
        value_grad = cross_rows(probs.astype(bf16), grad_rows)
        return (query_grad, key_grad, value_grad)

    query_rot_grad, key_parts, value_parts = lax.map(
        both_sides, (query_heads, key_heads, value_heads, lse_heads, grad_heads)
    )
    key_rot_grad, value_grad = (
        lax.psum_scatter(
            key_parts.transpose(1, 0, 2).reshape(seq_rows, KVH * HD).astype(jnp.bfloat16),
            "col",
            scatter_dimension=0,
            tiled=True,
        ).astype(jnp.float32),
        lax.psum_scatter(
            value_parts.transpose(1, 0, 2).reshape(seq_rows, KVH * HD).astype(jnp.bfloat16),
            "col",
            scatter_dimension=0,
            tiled=True,
        ).astype(jnp.float32),
    )
    query_grad = (
        rotate_back(from_heads(query_rot_grad, tok_rows, group), cosine, sine)
        .reshape(tok_rows, H * HD)
        .astype(bf16)
    )
    key_grad = (
        rotate_back(key_rot_grad.reshape(tok_rows, KVH, HD), cosine, sine)
        .reshape(tok_rows, KVH * HD)
        .astype(bf16)
    )
    value_grad = value_grad.astype(bf16)
    query_wgrad = cross_rows(attn_in, query_grad)
    key_wgrad = cross_rows(attn_in, key_grad)
    value_wgrad = cross_rows(attn_in, value_grad)
    attn_in_grad = (
        times_back(query_grad, wq_full)
        + times_back(key_grad, wk_full)
        + times_back(value_grad, wv_full)
    )
    norm_one_grad, gain_one_grad = norm_back(attn_in_grad, normed_one, scale_one, gain_one)
    block_in_grad = resid_grad + norm_one_grad
    spread_one = jnp.broadcast_to(gain_one_grad[:, None], (D, n_col))
    spread_two = jnp.broadcast_to(gain_two_grad[:, None], (D, n_col))
    col_sums = (
        lax.psum_scatter(
            query_wgrad.astype(jnp.bfloat16), "col", scatter_dimension=1, tiled=True
        ).astype(jnp.float32),
        lax.psum_scatter(
            key_wgrad.astype(jnp.bfloat16), "col", scatter_dimension=1, tiled=True
        ).astype(jnp.float32),
        lax.psum_scatter(
            value_wgrad.astype(jnp.bfloat16), "col", scatter_dimension=1, tiled=True
        ).astype(jnp.float32),
        lax.psum_scatter(
            out_wgrad.astype(jnp.bfloat16), "col", scatter_dimension=1, tiled=True
        ).astype(jnp.float32),
        lax.psum_scatter(
            router_wgrad.astype(jnp.bfloat16), "col", scatter_dimension=1, tiled=True
        ).astype(jnp.float32),
        lax.psum_scatter(
            spread_one.astype(jnp.bfloat16), "col", scatter_dimension=1, tiled=True
        ).astype(jnp.float32),
        lax.psum_scatter(
            spread_two.astype(jnp.bfloat16), "col", scatter_dimension=1, tiled=True
        ).astype(jnp.float32),
    )
    row_sums = (
        lax.psum_scatter(
            col_sums[0].astype(jnp.bfloat16), "row", scatter_dimension=0, tiled=True
        ).astype(jnp.float32),
        lax.psum_scatter(
            col_sums[1].astype(jnp.bfloat16), "row", scatter_dimension=0, tiled=True
        ).astype(jnp.float32),
        lax.psum_scatter(
            col_sums[2].astype(jnp.bfloat16), "row", scatter_dimension=0, tiled=True
        ).astype(jnp.float32),
        lax.psum_scatter(
            col_sums[3].astype(jnp.bfloat16), "row", scatter_dimension=0, tiled=True
        ).astype(jnp.float32),
        lax.psum_scatter(
            col_sums[4].astype(jnp.bfloat16), "row", scatter_dimension=0, tiled=True
        ).astype(jnp.float32),
        lax.psum_scatter(
            col_sums[5].astype(jnp.bfloat16), "row", scatter_dimension=0, tiled=True
        ).astype(jnp.float32),
        lax.psum_scatter(
            col_sums[6].astype(jnp.bfloat16), "row", scatter_dimension=0, tiled=True
        ).astype(jnp.float32),
    )
    return (
        block_out,
        block_in_grad,
        row_sums[5][:, 0],
        row_sums[6][:, 0],
        row_sums[0],
        row_sums[1],
        row_sums[2],
        row_sums[3],
        row_sums[4],
        gate_sum,
        up_sum,
        down_sum,
    )


F32 = jnp.float32
BF16 = jnp.bfloat16
MIB = 1024 * 1024
LANES = 128


def dot_nn(a, b):
    return lax.dot_general(a, b, (((1,), (0,)), ((), ())), preferred_element_type=F32)


def dot_nt(a, b):
    return lax.dot_general(a, b, (((1,), (1,)), ((), ())), preferred_element_type=F32)


def dot_tn(a, b):
    return lax.dot_general(a, b, (((0,), (0,)), ((), ())), preferred_element_type=F32)


def in_vmem():
    return pl.BlockSpec(memory_space=pltpu.VMEM)


def in_smem():
    return pl.BlockSpec(memory_space=pltpu.SMEM)


def partner(values):
    lane = lax.broadcasted_iota(jnp.int32, values.shape, 1)
    half = HD // 2
    return jnp.where(
        lane % HD < half,
        pltpu.roll(values, LANES - half, 1),
        pltpu.roll(values, half, 1),
    )


def attend_kernel(
    spot_ref, x0, x1, x2, x3, pack_ref, cos_ref, sin_ref,
    attn_ref, mixed_ref, q_ref, k_ref, v_ref, lse_ref, w_ref, gain_ref,
):
    rows = x0.shape[0]
    col, prefix = spot_ref[0], spot_ref[1]
    for part in range(8):
        span = pl.ds(part * LANES, LANES)
        w_ref[span, :] = pack_ref[part, :LANES, :]
        gain_ref[0:1, span] = pack_ref[part, LANES : LANES + 1, :LANES].astype(F32)
        gain_ref[1:2, span] = pack_ref[part, LANES : LANES + 1, LANES : 2 * LANES].astype(F32)
    gain = gain_ref[0:1, :]
    for step, chunk in enumerate((x0, x1, x2, x3)):
        source = lax.rem(col - step + 4, 4)
        x = chunk[...].astype(F32)
        scale = lax.rsqrt(jnp.mean(x * x, axis=1, keepdims=True) + EPS)
        attn_ref[pl.ds(pl.multiple_of(source * rows, rows), rows), :] = (x * scale * gain).astype(BF16)
    for tile in range(4):
        span = pl.ds(tile * rows, rows)
        qkv = dot_nn(attn_ref[span, :], w_ref[...])
        cosine, sine = cos_ref[span, :], sin_ref[span, :]
        for block in range(3):
            v = qkv[:, block * LANES : (block + 1) * LANES]
            y = v * cosine + partner(v) * sine
            if block < 2:
                y = (y * HD ** (-0.5)).astype(BF16)
                q_ref[2 * block, span, :] = y[:, :HD]
                q_ref[2 * block + 1, span, :] = y[:, HD:]
            else:
                y = y.astype(BF16)
                k_ref[0, span, :] = y[:, :HD]
                k_ref[1, span, :] = y[:, HD:]
        v = qkv[:, 3 * LANES :].astype(BF16)
        v_ref[0, span, :] = v[:, :HD]
        v_ref[1, span, :] = v[:, HD:]
    total = 4 * rows
    for tile in range(4):
        span = pl.ds(tile * rows, rows)
        keys = max((tile + 1) * rows, total // 2)
        key_spot = lax.broadcasted_iota(jnp.int32, (rows, keys), 1)
        query_spot = lax.broadcasted_iota(jnp.int32, (rows, keys), 0) + tile * rows
        allowed = (key_spot <= query_spot) | (key_spot < prefix)
        for pair in range(2):
            k, v = k_ref[pair, pl.ds(0, keys), :], v_ref[pair, pl.ds(0, keys), :]
            outs = []
            for head in (2 * pair, 2 * pair + 1):
                scores = jnp.where(allowed, dot_nt(q_ref[head, span, :], k), NEGATIVE)
                highest = jnp.max(scores, axis=1, keepdims=True)
                expo = jnp.exp(scores - highest)
                summed = jnp.sum(expo, axis=1, keepdims=True)
                outs.append(dot_nn(expo.astype(BF16), v) * (1.0 / summed))
                lse_ref[span, head : head + 1] = highest + jnp.log(summed)
            mixed_ref[span, pair * LANES : (pair + 1) * LANES] = jnp.concatenate(outs, axis=1).astype(BF16)


def attend(spots, chunks, pack, cosine, sine):
    rows = chunks[0].shape[0]
    seq = 4 * rows
    shapes = (
        jax.ShapeDtypeStruct((seq, D), BF16),
        jax.ShapeDtypeStruct((seq, 256), BF16),
        jax.ShapeDtypeStruct((4, seq, HD), BF16),
        jax.ShapeDtypeStruct((2, seq, HD), BF16),
        jax.ShapeDtypeStruct((2, seq, HD), BF16),
        jax.ShapeDtypeStruct((seq, 4), F32),
        jax.ShapeDtypeStruct((D, 512), BF16),
        jax.ShapeDtypeStruct((2, D), F32),
    )
    return pl.pallas_call(
        attend_kernel,
        out_shape=shapes,
        in_specs=[in_smem()] + [in_vmem()] * 7,
        out_specs=tuple(in_vmem() for _ in shapes),
        compiler_params=pltpu.CompilerParams(vmem_limit_bytes=40 * MIB),
        cost_estimate=pl.CostEstimate(flops=4 * 10**9, bytes_accessed=8 * MIB, transcendentals=3 * 10**6),
    )(spots, *chunks, pack, cosine, sine)


def attend_back_kernel(
    spot_ref, grad_ref, mixed_ref, q_ref, k_ref, v_ref, lse_ref, attn_ref, w_ref, cos_ref, sin_ref, gain_ref,
    wgrad_ref, in0, in1, in2, in3, dqkv_ref, dk_ref, dv_ref, dq_ref, mg_ref,
):
    seq = attn_ref.shape[0]
    rows = seq // 4
    prefix = spot_ref[1]
    for tile in range(4):
        span = pl.ds(tile * rows, rows)
        for pair in range(2):
            g = grad_ref[span, pair * LANES : (pair + 1) * LANES]
            mg_ref[2 * pair, span, :] = g[:, :HD]
            mg_ref[2 * pair + 1, span, :] = g[:, HD:]
    dk_ref[...] = jnp.zeros_like(dk_ref)
    dv_ref[...] = jnp.zeros_like(dv_ref)
    for tile in range(4):
        span = pl.ds(tile * rows, rows)
        keys = max((tile + 1) * rows, seq // 2)
        key_spot = lax.broadcasted_iota(jnp.int32, (rows, keys), 1)
        query_spot = lax.broadcasted_iota(jnp.int32, (rows, keys), 0) + tile * rows
        allowed = (key_spot <= query_spot) | (key_spot < prefix)
        for pair in range(2):
            k, v = k_ref[pair, pl.ds(0, keys), :], v_ref[pair, pl.ds(0, keys), :]
            both = grad_ref[span, pair * LANES : (pair + 1) * LANES].astype(F32) * mixed_ref[
                span, pair * LANES : (pair + 1) * LANES
            ].astype(F32)
            outs = []
            for at, head in enumerate((2 * pair, 2 * pair + 1)):
                q, g = q_ref[head, span, :], mg_ref[head, span, :]
                delta = jnp.sum(both[:, at * HD : (at + 1) * HD], axis=1, keepdims=True)
                scores = jnp.where(allowed, dot_nt(q, k), NEGATIVE)
                probs = jnp.exp(scores - lse_ref[span, head : head + 1])
                score_grad = (probs * (dot_nt(g, v) - delta)).astype(BF16)
                dv_ref[pair, pl.ds(0, keys), :] += dot_tn(probs.astype(BF16), g)
                dk_ref[pair, pl.ds(0, keys), :] += dot_tn(score_grad, q)
                outs.append(dot_nn(score_grad, k) * HD ** (-0.5))
            dq_ref[span, pair * LANES : (pair + 1) * LANES] = jnp.concatenate(outs, axis=1)
    for tile in range(4):
        span = pl.ds(tile * rows, rows)
        cosine, sine = cos_ref[span, :], sin_ref[span, :]
        for block in range(3):
            if block < 2:
                g = dq_ref[span, block * LANES : (block + 1) * LANES]
            else:
                g = jnp.concatenate([dk_ref[0, span, :], dk_ref[1, span, :]], axis=1)
            dqkv_ref[span, block * LANES : (block + 1) * LANES] = (g * cosine - partner(g) * sine).astype(BF16)
        dqkv_ref[span, 3 * LANES :] = jnp.concatenate([dv_ref[0, span, :], dv_ref[1, span, :]], axis=1).astype(BF16)
    gain_total = jnp.zeros((1, D), F32)
    for step, out in enumerate((in0, in1, in2, in3)):
        source = lax.rem(spot_ref[0] - step + 4, 4)
        span = pl.ds(pl.multiple_of(source * rows, rows), rows)
        back = dot_nt(dqkv_ref[span, :], w_ref[...])
        out[...] = back.astype(BF16)
        gain_total = gain_total + jnp.sum(back * attn_ref[span, :].astype(F32), axis=0, keepdims=True)
    gain_total = gain_total / gain_ref[0:1, :]
    for part in range(8):
        span = pl.ds(part * LANES, LANES)
        wgrad_ref[part, LANES:, :LANES] = jnp.broadcast_to(gain_total[:, part * LANES : (part + 1) * LANES], (8, LANES)).astype(BF16)
        wgrad_ref[part, LANES:, LANES:] = jnp.zeros((8, 3 * LANES), BF16)
        wgrad_ref[part, :LANES, :] = dot_tn(attn_ref[:, span], dqkv_ref[...]).astype(BF16)


def attend_back(spots, grads, mixed, q, k, v, lse, attn_in, w_qkv, cosine, sine, gain):
    seq = attn_in.shape[0]
    shapes = (
        jax.ShapeDtypeStruct((8, 136, 512), BF16),
    ) + (jax.ShapeDtypeStruct((seq // 4, D), BF16),) * 4
    return pl.pallas_call(
        attend_back_kernel,
        out_shape=shapes,
        in_specs=[in_smem()] + [in_vmem()] * 11,
        out_specs=tuple(in_vmem() for _ in shapes),
        scratch_shapes=[
            pltpu.VMEM((seq, 512), BF16),
            pltpu.VMEM((2, seq, HD), F32),
            pltpu.VMEM((2, seq, HD), F32),
            pltpu.VMEM((seq, 256), F32),
            pltpu.VMEM((4, seq, HD), BF16),
        ],
        compiler_params=pltpu.CompilerParams(vmem_limit_bytes=48 * MIB),
        cost_estimate=pl.CostEstimate(flops=10 * 10**9, bytes_accessed=14 * MIB, transcendentals=3 * 10**6),
    )(spots, grads, mixed, q, k, v, lse, attn_in, w_qkv, cosine, sine, gain)


def route_kernel(
    spot_ref, mixed_ref, x_ref, pack_ref, gain_ref, wr_ref, ids_ref, order_ref,
    resid_ref, send_ref, gates_ref, kept_ref, wo_ref,
):
    rows = x_ref.shape[0]
    for part in range(32):
        wo_ref[pl.ds(part // 4 * LANES, LANES), pl.ds(part % 4 * 256, 256)] = pack_ref[part, :LANES, :]
    resid = x_ref[...].astype(F32)
    for part in range(4):
        resid = resid + dot_nn(mixed_ref[pl.ds(part * rows, rows), :], wo_ref[part * 256 : (part + 1) * 256, :])
    resid_ref[...] = resid
    scale = lax.rsqrt(jnp.mean(resid * resid, axis=1, keepdims=True) + EPS)
    moe_in = (resid * scale * gain_ref[1:2, :]).astype(BF16)
    send_ref[:, :D] = moe_in
    logits = dot_nn(moe_in, wr_ref[...])
    lane = lax.broadcasted_iota(jnp.int32, (rows, LANES), 1)
    chosen = jnp.zeros((rows, LANES), jnp.bool_)
    for choice in range(TOPK):
        chosen = chosen | (ids_ref[:, choice : choice + 1] == lane)
    picked = jnp.where(chosen, logits, NEGATIVE)
    expo = jnp.exp(picked - jnp.max(picked, axis=1, keepdims=True))
    gates = expo / jnp.sum(expo, axis=1, keepdims=True)
    first = lax.broadcasted_iota(jnp.int32, (rows, rows), 0)
    second = lax.broadcasted_iota(jnp.int32, (rows, rows), 1)
    place = (first == order_ref[...]).astype(BF16)
    sooner = dot_nn(place, (second < first).astype(BF16)).astype(BF16)
    sooner = dot_nt(sooner, place).astype(BF16)
    slot = dot_nn(sooner, chosen.astype(BF16))
    kept = (chosen & (slot < CAP)).astype(F32)
    gates_ref[...] = gates
    kept_ref[...] = kept
    send_ref[:, D:] = dot_nn((gates * kept).astype(BF16), relabel(spot_ref[2])).astype(BF16)


def relabel(row):
    first = lax.broadcasted_iota(jnp.int32, (LANES, LANES), 0)
    second = lax.broadcasted_iota(jnp.int32, (LANES, LANES), 1)
    return (first == (second ^ (row * 4))).astype(BF16)


def route(spots, mixed, x, pack, gain, wr, ids, order):
    rows = x.shape[0]
    shapes = (
        jax.ShapeDtypeStruct((rows, D), F32),
        jax.ShapeDtypeStruct((rows, D + LANES), BF16),
        jax.ShapeDtypeStruct((rows, LANES), F32),
        jax.ShapeDtypeStruct((rows, LANES), F32),
        jax.ShapeDtypeStruct((D, D), BF16),
    )
    return pl.pallas_call(
        route_kernel,
        out_shape=shapes,
        in_specs=[in_smem()] + [in_vmem()] * 7,
        out_specs=tuple(in_vmem() for _ in shapes),
        compiler_params=pltpu.CompilerParams(vmem_limit_bytes=32 * MIB),
        cost_estimate=pl.CostEstimate(flops=10**9, bytes_accessed=5 * MIB, transcendentals=10**5),
    )(spots, mixed, x, pack, gain, wr, ids, order)


def expert_kernel(
    x_ref, g_ref, w0, w1, w2, w3, w4, w5, w6a, w6b, w7a, w7b,
    out_ref, back_ref, hg_ref, hu_ref, act_ref, out_acc, in_acc, gate_acc, held, sems,
):
    step = pl.program_id(0)
    count = held.shape[1]
    wide = count * LANES
    sources = ((w0,), (w1,), (w2,), (w3,), (w4,), (w5,), (w6a, w6b), (w7a, w7b))

    def fetch(at, slot):
        for k, parts in enumerate(sources):

            @pl.when(at == k)
            def _():
                size = count // len(parts)
                for i, part in enumerate(parts):
                    pltpu.make_async_copy(part, held.at[slot, pl.ds(i * size, size)], sems.at[slot]).start()

    @pl.when(step == 0)
    def _():
        fetch(step, 0)
        out_acc[...] = jnp.zeros_like(out_acc)
        in_acc[...] = jnp.zeros_like(in_acc)
        gate_acc[...] = jnp.zeros_like(gate_acc)

    now = lax.rem(step, 2)
    pltpu.make_async_copy(w0, held.at[now], sems.at[now]).wait()
    fetch(step + 1, 1 - now)

    join = lambda kind: jnp.concatenate([held[now, i, kind] for i in range(count)], axis=1)
    wg, wu, wd = join(0), join(1), join(2)
    x = x_ref[:, :D]
    expert = lax.broadcasted_iota(jnp.int32, (LANES, wide), 0)
    column = lax.broadcasted_iota(jnp.int32, (LANES, wide), 1)
    spread = (expert == step * count + column // LANES).astype(BF16)
    gate = dot_nn(x_ref[:, D:], spread)
    hidden_gate = dot_nn(x, wg)
    hidden_up = dot_nn(x, wu)
    act_grad = dot_nn(g_ref[...], wd)
    sigma = 0.5 * jnp.tanh(0.5 * hidden_gate) + 0.5
    swish = hidden_gate * sigma
    active = swish * hidden_up
    gate_acc[...] += dot_nt((active * act_grad).astype(BF16), spread)
    gated = (active * gate).astype(BF16)
    act_ref[...] = gated
    out_acc[...] += dot_nt(gated, wd)
    act_grad = act_grad * gate
    up_grad = (act_grad * swish).astype(BF16)
    gate_grad = (act_grad * hidden_up * (sigma + swish * (1.0 - sigma))).astype(BF16)
    hg_ref[...] = gate_grad
    hu_ref[...] = up_grad
    in_acc[...] += dot_nt(gate_grad, wg) + dot_nt(up_grad, wu)

    @pl.when(step == pl.num_programs(0) - 1)
    def _():
        out_ref[...] = out_acc[...].astype(BF16)
        back_ref[:, :D] = in_acc[...].astype(BF16)
        back_ref[:, D:] = gate_acc[...].astype(BF16)


def experts(x, g, weights):
    rows = x.shape[0]
    count = 4
    steps = 8
    wide = count * LANES
    hidden = pl.BlockSpec((rows, wide), lambda i: (0, i))
    whole = lambda width: pl.BlockSpec((rows, width), lambda i: (0, 0))
    return pl.pallas_call(
        expert_kernel,
        grid=(steps,),
        out_shape=(
            jax.ShapeDtypeStruct((rows, D), BF16),
            jax.ShapeDtypeStruct((rows, D + LANES), BF16),
        )
        + (jax.ShapeDtypeStruct((rows, steps * wide), BF16),) * 3,
        in_specs=[whole(D + LANES), whole(D)] + [pl.BlockSpec(memory_space=pl.ANY)] * 10,
        out_specs=(whole(D), whole(D + LANES), hidden, hidden, hidden),
        scratch_shapes=[
            pltpu.VMEM((rows, D), F32),
            pltpu.VMEM((rows, D), F32),
            pltpu.VMEM((rows, LANES), F32),
            pltpu.VMEM((2, count, 3, D, LANES), BF16),
            pltpu.SemaphoreType.DMA((2,)),
        ],
        compiler_params=pltpu.CompilerParams(vmem_limit_bytes=56 * MIB),
        cost_estimate=pl.CostEstimate(flops=20 * 10**9, bytes_accessed=32 * MIB, transcendentals=10**6),
    )(x, g, *weights)


def flip_kernel(x0, x1, x2, x3, g0, g1, g2, g3, xt_ref, gt_ref):
    rows = x0.shape[0]
    for at, (x, g) in enumerate(zip((x0, x1, x2, x3), (g0, g1, g2, g3))):
        xt_ref[:, at * rows : (at + 1) * rows] = x[:, :D].T
        gt_ref[:, at * rows : (at + 1) * rows] = g[...].T


def flip(xs, gs):
    seq = 4 * xs[0].shape[0]
    return pl.pallas_call(
        flip_kernel,
        out_shape=(jax.ShapeDtypeStruct((D, seq), BF16),) * 2,
        in_specs=[in_vmem()] * 8,
        out_specs=(in_vmem(),) * 2,
        compiler_params=pltpu.CompilerParams(vmem_limit_bytes=24 * MIB),
        cost_estimate=pl.CostEstimate(flops=10**9, bytes_accessed=8 * MIB, transcendentals=0),
    )(*xs, *gs)


def expert_wgrad_kernel(places, added, halved, *refs):
    xt_ref, gt_ref = refs[:2]
    hidden = refs[2:14]
    more = refs[14:]
    half = pl.program_id(0) % 2
    extra = more[0] if added else None
    outs = more[1:] if added else more
    for kind, left in enumerate((xt_ref, xt_ref, gt_ref)):
        joined = jnp.concatenate([part[...] for part in hidden[kind * 4 : kind * 4 + 4]], axis=0)
        product = dot_nn(left[...], joined)
        for i in range(2):
            piece = product[:, i * LANES : (i + 1) * LANES]
            if added:
                piece = piece + extra[0, i, kind].astype(F32)
            outs[0][0, i, kind] = piece.astype(BF16)


def expert_wgrads(flipped, hidden, places, extra=None):
    rows = hidden[0][0].shape[0]
    wide = 2 * LANES
    seq = flipped[0].shape[1]
    first = places[0] * 2
    jump = (places[1] - places[0]) * 2 if len(places) > 1 else 0
    lane = pl.BlockSpec((rows, wide), lambda i: (0, first + (i // 2) * jump + i % 2))
    whole = pl.BlockSpec((D, seq), lambda i: (0, 0))
    weight = pl.BlockSpec((1, 2, 3, D, LANES), lambda i: (i, 0, 0, 0, 0))
    steps = 2 * len(places)
    return pl.pallas_call(
        functools.partial(expert_wgrad_kernel, places, extra is not None, False),
        grid=(steps,),
        out_shape=jax.ShapeDtypeStruct((steps, 2, 3, D, LANES), BF16),
        in_specs=[whole] * 2 + [lane] * 12 + ([weight] if extra is not None else []),
        out_specs=weight,
        compiler_params=pltpu.CompilerParams(vmem_limit_bytes=32 * MIB),
        cost_estimate=pl.CostEstimate(
            flops=len(places) * 5 * 10**9, bytes_accessed=(4 + 6 * len(places)) * MIB, transcendentals=0
        ),
    )(*flipped, *hidden[0], *hidden[1], *hidden[2], *(() if extra is None else (extra,)))


def turn_kernel(
    spot_ref, back_ref, gates_ref, kept_ref, resid_ref, gain_ref, g_ref, wr_ref, wo_ref, send_ref,
    resid_grad_ref, branch_ref, mixed_grad_ref, small_ref,
):
    rows = resid_ref.shape[0]
    gates = gates_ref[...]
    gate_grad = dot_nn(back_ref[:, D:], relabel(spot_ref[2])) * kept_ref[...]
    logit_grad = gates * (gate_grad - jnp.sum(gates * gate_grad, axis=1, keepdims=True))
    logit_grad = logit_grad.astype(BF16)
    moe_grad = back_ref[:, :D].astype(F32) + dot_nt(logit_grad, wr_ref[...])
    resid = resid_ref[...]
    scale = lax.rsqrt(jnp.mean(resid * resid, axis=1, keepdims=True) + EPS)
    normed = resid * scale
    small_ref[LANES:, :] = jnp.broadcast_to(jnp.sum(moe_grad * normed, axis=0, keepdims=True), (8, D))
    small_ref[:LANES, :] = dot_tn(logit_grad, send_ref[:, :D])
    inner = moe_grad * gain_ref[1:2, :]
    grad = g_ref[...].astype(F32) + scale * (inner - normed * jnp.mean(inner * normed, axis=1, keepdims=True))
    resid_grad_ref[...] = grad
    branch = grad.astype(BF16)
    branch_ref[...] = branch
    for part in range(4):
        mixed_grad_ref[pl.ds(part * rows, rows), :] = dot_nt(
            branch, wo_ref[part * 256 : (part + 1) * 256, :]
        ).astype(BF16)


def turn(spots, back, gates, kept, resid, gain, g, wr, wo, send):
    rows = resid.shape[0]
    shapes = (
        jax.ShapeDtypeStruct((rows, D), F32),
        jax.ShapeDtypeStruct((rows, D), BF16),
        jax.ShapeDtypeStruct((4 * rows, 256), BF16),
        jax.ShapeDtypeStruct((LANES + 8, D), F32),
    )
    return pl.pallas_call(
        turn_kernel,
        out_shape=shapes,
        in_specs=[in_smem()] + [in_vmem()] * 9,
        out_specs=tuple(in_vmem() for _ in shapes),
        compiler_params=pltpu.CompilerParams(vmem_limit_bytes=32 * MIB),
        cost_estimate=pl.CostEstimate(flops=2 * 10**9, bytes_accessed=7 * MIB, transcendentals=10**5),
    )(spots, back, gates, kept, resid, gain, g, wr, wo, send)


def out_wgrad_kernel(mixed_ref, branch_ref, small_ref, pack_ref):
    rows = branch_ref.shape[0]
    for part in range(4):
        product = dot_tn(mixed_ref[pl.ds(part * rows, rows), :], branch_ref[...]).astype(BF16)
        pack_ref[2 * part, :LANES, :] = product[:LANES]
        pack_ref[2 * part + 1, :LANES, :] = product[LANES:]
    for row in range(8):
        span = pl.ds(row * LANES, LANES)
        for col in range(4):
            pack_ref[row, LANES:, col * 256 : col * 256 + LANES] = small_ref[col * 8 : col * 8 + 8, span].astype(BF16)
            pack_ref[row, LANES:, col * 256 + LANES : col * 256 + 256] = small_ref[LANES:, span].astype(BF16)


def out_wgrad(mixed, branch, small):
    return pl.pallas_call(
        out_wgrad_kernel,
        out_shape=jax.ShapeDtypeStruct((8, LANES + 8, D), BF16),
        in_specs=[in_vmem()] * 3,
        out_specs=in_vmem(),
        compiler_params=pltpu.CompilerParams(vmem_limit_bytes=24 * MIB),
        cost_estimate=pl.CostEstimate(flops=2 * 10**9, bytes_accessed=4 * MIB, transcendentals=0),
    )(mixed, branch, small)


def ring_gather(value, n_col):
    steps = [(i, (i + 1) % n_col) for i in range(n_col)]
    chunks = [value]
    for _ in range(n_col - 1):
        chunks.append(lax.ppermute(chunks[-1], "col", steps))
    return chunks


def ring_sum(parts, n_col):
    steps = [(i, (i + 1) % n_col) for i in range(n_col)]
    total = parts[1]
    for part in parts[2:] + parts[:1]:
        total = lax.ppermute(total, "col", steps).astype(F32) + part.astype(F32)
        if part is not parts[0]:
            total = total.astype(BF16)
    return total


CORE, ACROSS_X, ACROSS_Y = 1, 2, 4


def swap(value, mask):
    return lax.ppermute(value, "row", [(i, i ^ mask) for i in range(8)])


def gather_weights(own):
    from_x, from_y = swap(own, ACROSS_X), swap(own, ACROSS_Y)
    other = swap(own, CORE)
    half = own.shape[0] // 2
    far_a, far_b = swap(from_y[:half], ACROSS_X), swap(from_x[half:], ACROSS_Y)
    return (
        own, other, from_x, swap(from_x, CORE), from_y, swap(from_y, CORE),
        far_a, far_b, swap(far_a, CORE), swap(far_b, CORE),
    )


def sum_weights(flipped, hidden):
    p7 = expert_wgrads(flipped, hidden, (7,))
    r7 = swap(p7, CORE)
    p35 = expert_wgrads(flipped, hidden, (3, 5))
    r35 = swap(p35, CORE)
    q6 = expert_wgrads(flipped, hidden, (6,), r7)
    from_x, from_y = swap(q6[:1], ACROSS_X), swap(q6[1:], ACROSS_Y)
    p1 = expert_wgrads(flipped, hidden, (1,))
    r1 = swap(p1, CORE)
    q24 = expert_wgrads(flipped, hidden, (2, 4), r35)
    q2a, q2b, q4a, q4b = (q24[i : i + 1] for i in range(4))
    from_x2a, from_y4b = swap(q2a, ACROSS_X), swap(q4b, ACROSS_Y)
    add = lambda a, b: (a.astype(F32) + b.astype(F32)).astype(BF16)
    from_x2b = swap(add(q2b, from_y), ACROSS_X)
    from_y4a = swap(add(q4a, from_x), ACROSS_Y)
    q0 = expert_wgrads(flipped, hidden, (0,), r1)
    low = q0[0].astype(F32) + from_x2a[0].astype(F32) + from_y4a[0].astype(F32)
    high = q0[1].astype(F32) + from_x2b[0].astype(F32) + from_y4b[0].astype(F32)
    return low, high


def fast(
    block_in,
    attn_gain,
    moe_gain,
    w_query,
    w_key,
    w_value,
    w_out,
    w_router,
    w_gate,
    w_up,
    w_down,
    expert_ids,
    fill_order,
    prefix_len,
    out_grad,
):
    rows = block_in.shape[0]
    n_col = lax.axis_size("col")
    col = lax.axis_index("col")
    row = lax.axis_index("row")
    seq = rows * n_col
    spots = jnp.stack([col.astype(jnp.int32), prefix_len[0], row.astype(jnp.int32)])
    gains = jnp.concatenate([attn_gain, moe_gain, jnp.zeros((256,), BF16)])[None]
    pack_qkv = jnp.concatenate(
        [jnp.concatenate([w_query, w_key, w_value], axis=1), gains, jnp.zeros((7, 512), BF16)], axis=0
    )
    pack_qkv = lax.all_gather(pack_qkv, "row", axis=0)
    pack_out = jnp.concatenate([w_out, w_router.reshape(4, 256), jnp.zeros((4, 256), BF16)], axis=0)
    pack_out = lax.all_gather(pack_out, ("row", "col"), axis=0)
    wr = pack_out[:, LANES : LANES + 4].reshape(8, 4, LANES, 8).transpose(0, 2, 1, 3).reshape(D, E)
    wr = jnp.pad(wr, ((0, 0), (0, LANES - E)))
    cosine, sine = rope_tables(0, seq)
    cosine = jnp.tile(cosine, (1, 4))
    sine = jnp.concatenate([-sine, sine, -sine, sine], axis=1)

    weights = gather_weights(jnp.stack([w_gate, w_up, w_down], axis=1))
    x_chunks = ring_gather(block_in, n_col)
    attn_in, mixed, q, k, v, lse, w_qkv, gains = attend(spots, x_chunks, pack_qkv, cosine, sine)
    g_chunks = ring_gather(out_grad, n_col)
    mixed_own = lax.all_to_all(mixed, "col", split_axis=0, concat_axis=0, tiled=True)
    resid, send, gates, kept, wo = route(spots, mixed_own, block_in, pack_out, gains, wr, expert_ids, fill_order)

    send_chunks = ring_gather(send, n_col)
    results = [experts(x, g, weights) for x, g in zip(send_chunks, g_chunks)]
    back = ring_sum([result[1] for result in results], n_col).astype(BF16)
    resid_grad, branch, mixed_grad, small = turn(
        spots, back, gates, kept, resid, gains, out_grad, wr, wo, send
    )
    mixed_grads = lax.all_to_all(mixed_grad, "col", split_axis=0, concat_axis=0, tiled=True)
    qkv_wgrad, *back_parts = attend_back(
        spots, mixed_grads, mixed, q, k, v, lse, attn_in, w_qkv, cosine, sine, gains
    )
    attn_grad = ring_sum(back_parts, n_col)
    x_rows = block_in.astype(F32)
    scale = lax.rsqrt(jnp.mean(x_rows * x_rows, axis=1, keepdims=True) + EPS)
    normed = x_rows * scale
    inner = attn_grad * gains[:1]
    block_in_grad = resid_grad + scale * (inner - normed * jnp.mean(inner * normed, axis=1, keepdims=True))
    block_out = resid + ring_sum([result[0] for result in results], n_col)

    low, high = sum_weights(
        flip(send_chunks, g_chunks), [[result[kind] for result in results] for kind in (2, 3, 4)]
    )
    gate_sum, up_sum, down_sum = (jnp.concatenate([low[:, i], high[:, i]], axis=0) for i in range(3))

    out_sum = lax.psum_scatter(out_wgrad(mixed_own, branch, small), "row", scatter_dimension=0)
    out_sum = lax.psum_scatter(out_sum, "col", scatter_dimension=1, tiled=True).astype(F32)
    qkv_sum = lax.psum_scatter(qkv_wgrad, "row", scatter_dimension=0).astype(F32)
    gain_one_sum = lax.psum(qkv_sum[LANES, :LANES], "col")
    return (
        block_out,
        block_in_grad,
        gain_one_sum,
        out_sum[LANES, LANES:],
        qkv_sum[:LANES, :256],
        qkv_sum[:LANES, 256:384],
        qkv_sum[:LANES, 384:],
        out_sum[:LANES],
        out_sum[LANES:, :LANES].T,
        gate_sum,
        up_sum,
        down_sum,
    )


def takes_fast(mesh):
    n_row, n_col = mesh.shape["row"], mesh.shape["col"]
    return n_row == 8 and n_col == 4


def solution(mesh):
    in_specs = (
        P(("row", "col"), None),
        P("row"),
        P("row"),
        P("row", "col"),
        P("row", "col"),
        P("row", "col"),
        P("row", "col"),
        P("row", "col"),
        P("row", None, "col"),
        P("row", None, "col"),
        P("row", None, "col"),
        P(("row", "col"), None),
        P(("row", "col"), None),
        P("row"),
        P(("row", "col"), None),
    )
    out_specs = (
        P(("row", "col"), None),
        P(("row", "col"), None),
        P("row"),
        P("row"),
        P("row", "col"),
        P("row", "col"),
        P("row", "col"),
        P("row", "col"),
        P("row", "col"),
        P("row", None, "col"),
        P("row", None, "col"),
        P("row", None, "col"),
    )
    local = fast if takes_fast(mesh) else general
    return jax.shard_map(local, mesh=mesh, in_specs=in_specs, out_specs=out_specs, check_vma=False)
```

profile of v0, /device:TPU:20, one launch (start us, length us, event | category | flops | bytes accessed | tf_op | source)
XLA Modules:
  0.0 573.5 jit_solution(6510547891365735871)
XLA Ops:
  9.8 4.0 pad_maximum_fusion.w0
  18.4 11.5 %collective-permute-done.x1 = bf16[256,1024]{1,0:T(8,128)(2,1)S(1)} collective-permute-done((bf16[256,1024]{1,0:T(8,128)(2,1)S(1)}, bf16[256,1024]{1,0:T(8,128)(2,1)S(1)}, u32[]{:S(2)}, u32[]{:S(2)}) %collective-permute-start) | collective-permute-done | bytes 524320 | tf_op jit(solution)/shard_map/ppermute | solution.py:855
  33.6 11.3 %collective-permute-done.1.x2 = bf16[256,1024]{1,0:T(8,128)(2,1)} collective-permute-done((bf16[256,1024]{1,0:T(8,128)(2,1)S(1)}, bf16[256,1024]{1,0:T(8,128)(2,1)}, u32[]{:S(2)}, u32[]{:S(2)}) %collective-permute-start.1) | collective-permute-done | bytes 524320 | tf_op jit(solution)/shard_map/ppermute | solution.py:855
  50.8 39.1 %collective-permute-done.8.w4 = bf16[4,3,1024,128]{3,2,1,0:T(8,128)(2,1)} collective-permute-done((bf16[4,3,1024,128]{3,2,1,0:T(8,128)(2,1)}, bf16[4,3,1024,128]{3,2,1,0:T(8,128)(2,1)}, u32[]{:S(2)}, u32[]{:S(2)}) %collective-permute-start.8) | collective-permute-done | bytes 3145760 | tf_op jit(solution)/shard_map/ppermute | solution.py:873
  96.0 11.1 %shard_map.238 = (bf16[1024,1024]{1,0:T(8,128)(2,1)S(1)}, bf16[1024,256]{1,0:T(8,128)(2,1)}, bf16[4,1024,64]{2,1,0:T(8,128)(2,1)S(1)}, bf16[2,1024,64]{2,1,0:T(8...) custom-call(s32[3]{0:T(128)S(1)} %pad_add_fusion.spot_ref, ...), custom_call_target="tpu_custom_call" | custom-call | flops 4000000000 | bytes 8388608 | tf_op jit(solution)/shard_map/pallas_call | solution.py:482
  112.9 5.4 all-to-all-start
  119.7 20.7 %collective-permute-done.16.g_ref.g2 = bf16[256,1024]{1,0:T(8,128)(2,1)S(1)} collective-permute-done((bf16[256,1024]{1,0:T(8,128)(2,1)S(1)}, bf16[256,1024]{1,0:T(8,128)(2,1)S(1)}, u32[]{:S(2)}, u32[]{:S(2)}) %collective-permute-start.16) | collective-permute-done | bytes 524320 | tf_op jit(solution)/shard_map/ppermute | solution.py:855
  156.6 9.2 %collective-permute-done.3.x_ref.x1 = bf16[256,1152]{1,0:T(8,128)(2,1)S(1)} collective-permute-done((bf16[256,1152]{1,0:T(8,128)(2,1)S(1)}, bf16[256,1152]{1,0:T(8,128)(2,1)S(1)}, u32[]{:S(2)}, u32[]{:S(2)}) %collective-permute-start.3) | collective-permute-done | bytes 589856 | tf_op jit(solution)/shard_map/ppermute | solution.py:855
  166.1 13.4 %collective-permute-done.15.x_ref.x2 = bf16[256,1152]{1,0:T(8,128)(2,1)S(1)} collective-permute-done((bf16[256,1152]{1,0:T(8,128)(2,1)S(1)}, bf16[256,1152]{1,0:T(8,128)(2,1)S(1)}, u32[]{:S(2)}, u32[]{:S(2)}) %collective-permute-start.15) | collective-permute-done | bytes 589856 | tf_op jit(solution)/shard_map/ppermute | solution.py:855
  179.8 11.8 %collective-permute-done.11.w6b = bf16[2,3,1024,128]{3,2,1,0:T(8,128)(2,1)S(1)} collective-permute-done((bf16[2,3,1024,128]{3,2,1,0:T(8,128)(2,1)S(1)}, bf16[2,3,1024,128]{3,2,1,0:T(8,128)(2,1)S(1)}, u32[]{:S(2)}, u32[]{:S(2)}) %collective-permute-start.11) | collective-permute-done | bytes 1572896 | tf_op jit(solution)/shard_map/ppermute | solution.py:873
  201.0 21.7 %shard_map.240 = (bf16[256,1024]{1,0:T(8,128)(2,1)}, bf16[256,1152]{1,0:T(8,128)(2,1)}, bf16[256,4096]{1,0:T(8,128)(2,1)}, bf16[256,4096]{1,0:T(8,128)(2,1)}, bf16[256,4096]{1,0:T(8,128)(2,1)}) custom-call(bf16[256,1152]{1,0:T(8,128)(2,1)} %copy-done.37, bf16[256,1024]{1,0:T(8,128)(2,1)} %copy-done.44, bf16[4,3,1024,128]{3,2,1,0:T(8,128)(2,1)} %pad_maximum_fusion.w0, ...), custom_call_target="tpu_custom_call" | custom-call | flops 20000000000 | bytes 33554432 | tf_op jit(solution)/shard_map/pallas_call | solution.py:702
  223.4 4.3 collective-permute-start.21
  227.7 21.6 %shard_map.243 = (bf16[256,1024]{1,0:T(8,128)(2,1)}, bf16[256,1152]{1,0:T(8,128)(2,1)}, bf16[256,4096]{1,0:T(8,128)(2,1)}, bf16[256,4096]{1,0:T(8,128)(2,1)}, bf16[256,4096]{1,0:T(8,128)(2,1)}) custom-call(bf16[256,1152]{1,0:T(8,128)(2,1)} %copy-done.34, bf16[256,1024]{1,0:T(8,128)(2,1)} %g0.1, bf16[4,3,1024,128]{3,2,1,0:T(8,128)(2,1)} %pad_maximum_fusion.w0, ...), custom_call_target="tpu_custom_call" | custom-call | flops 20000000000 | bytes 33554432 | tf_op jit(solution)/shard_map/pallas_call | solution.py:702
  249.3 21.8 %shard_map.241 = (bf16[256,1024]{1,0:T(8,128)(2,1)}, bf16[256,1152]{1,0:T(8,128)(2,1)}, bf16[256,4096]{1,0:T(8,128)(2,1)}, bf16[256,4096]{1,0:T(8,128)(2,1)}, bf16[256,4096]{1,0:T(8,128)(2,1)}) custom-call(bf16[256,1152]{1,0:T(8,128)(2,1)} %copy-done.38, bf16[256,1024]{1,0:T(8,128)(2,1)} %copy-done.48, bf16[4,3,1024,128]{3,2,1,0:T(8,128)(2,1)} %pad_maximum_fusion.w0, ...), custom_call_target="tpu_custom_call" | custom-call | flops 20000000000 | bytes 33554432 | tf_op jit(solution)/shard_map/pallas_call | solution.py:702
  272.8 21.8 %shard_map.242 = (bf16[256,1024]{1,0:T(8,128)(2,1)}, bf16[256,1152]{1,0:T(8,128)(2,1)}, bf16[256,4096]{1,0:T(8,128)(2,1)}, bf16[256,4096]{1,0:T(8,128)(2,1)}, bf16[256,4096]{1,0:T(8,128)(2,1)}) custom-call(bf16[256,1152]{1,0:T(8,128)(2,1)} %copy-done.36, bf16[256,1024]{1,0:T(8,128)(2,1)} %copy-done.46, bf16[4,3,1024,128]{3,2,1,0:T(8,128)(2,1)} %pad_maximum_fusion.w0, ...), custom_call_target="tpu_custom_call" | custom-call | flops 20000000000 | bytes 33554432 | tf_op jit(solution)/shard_map/pallas_call | solution.py:702
  307.3 10.4 %shard_map.250 = bf16[4,2,3,1024,128]{4,3,2,1,0:T(8,128)(2,1)} custom-call(bf16[1024,1024]{1,0:T(8,128)(2,1)S(1)} %get-tuple-element.86.refs_0_, bf16[1024,1024]{1,0:T(8,128)(2,1)S(1)} %get-tuple-element.87.refs_1_, bf16[256,4096]{1,0:T(8,128)(2,1)S(1)} %copy-done.9, bf16[256,4096]{1,0:T(8,128)(2,1)S(1)} %copy-done.3, bf16[256,4096]{1,0:T(8,128)(2,1)S(1)} %copy-done.15, ...), custom_call_target="tpu_custom_call" | custom-call | flops 10000000000 | bytes 16777216 | tf_op jit(solution)/shard_map/pallas_call | solution.py:770
  323.3 6.7 %all-to-all-start.1 = ((bf16[4,256,256]{2,1,0:T(8,128)(2,1)}), bf16[4,256,256]{2,1,0:T(8,128)(2,1)S(1)}, u32[]{:S(2)}, u32[]{:S(2)}) async-start(bf16[4,256,256]{2,1,0:T(8,128)(2,1)} %bitcast.54), calls=%async_computation.1 | async-start | bytes 1048576 | tf_op jit(solution)/shard_map/all_to_all | solution.py:957
  344.3 6.1 %shard_map.252 = bf16[2,2,3,1024,128]{4,3,2,1,0:T(8,128)(2,1)} custom-call(bf16[1024,1024]{1,0:T(8,128)(2,1)S(1)} %get-tuple-element.86.refs_0_, bf16[1024,1024]{1,0:T(8,128)(2,1)S(1)} %copy-done.1, bf16[256,4096]{1,0:T(8,128)(2,1)S(1)} %copy-done.10, bf16[256,4096]{1,0:T(8,128)(2,1)S(1)} %copy-done.4, bf16[256,4096]{1,0:T(8,128)(2,1)S(1)} %copy-done.16, ...), custom_call_target="tpu_custom_call" | custom-call | flops 5000000000 | bytes 10485760 | tf_op jit(solution)/shard_map/pallas_call | solution.py:770
  350.6 6.1 %shard_map.248 = bf16[2,2,3,1024,128]{4,3,2,1,0:T(8,128)(2,1)} custom-call(bf16[1024,1024]{1,0:T(8,128)(2,1)S(1)} %get-tuple-element.86.refs_0_, bf16[1024,1024]{1,0:T(8,128)(2,1)S(1)} %copy-done.1, bf16[256,4096]{1,0:T(8,128)(2,1)S(1)} %copy-done.10, bf16[256,4096]{1,0:T(8,128)(2,1)S(1)} %copy-done.4, bf16[256,4096]{1,0:T(8,128)(2,1)S(1)} %copy-done.16, ...), custom_call_target="tpu_custom_call" | custom-call | flops 5000000000 | bytes 10485760 | tf_op jit(solution)/shard_map/pallas_call | solution.py:770
  367.7 16.0 %shard_map.245 = (bf16[8,136,512]{2,1,0:T(8,128)(2,1)}, bf16[256,1024]{1,0:T(8,128)(2,1)S(1)}, bf16[256,1024]{1,0:T(8,128)(2,1)S(1)}, bf16[256,1024]{1,0:T(8,128)(2,1)S(1)}, bf16[256,1024]{1,0:T(8,128)(2,1)S(1)}) custom-call(s32[3]{0:T(128)S(1)} %pad_add_fusion.spot_ref, bf16[1024,256]{1,0:T(8,128)(2,1)S(1)} %bitcast.53, ...), custom_call_target="tpu_custom_call" | custom-call | flops 10000000000 | bytes 14680064 | tf_op jit(solution)/shard_map/pallas_call | solution.py:559
  390.1 12.5 %collective-permute-done.20 = bf16[256,1024]{1,0:T(8,128)(2,1)S(1)} collective-permute-done((bf16[256,1024]{1,0:T(8,128)(2,1)S(1)}, bf16[256,1024]{1,0:T(8,128)(2,1)S(1)}, u32[]{:S(2)}, u32[]{:S(2)}) %collective-permute-start.20) | collective-permute-done | bytes 524320 | tf_op jit(solution)/shard_map/ppermute | solution.py:863
  403.8 9.0 %collective-permute-done.24 = bf16[256,1024]{1,0:T(8,128)(2,1)S(1)} collective-permute-done((bf16[256,1024]{1,0:T(8,128)(2,1)S(1)}, bf16[256,1024]{1,0:T(8,128)(2,1)S(1)}, u32[]{:S(2)}, u32[]{:S(2)}) %collective-permute-start.24) | collective-permute-done | bytes 524320 | tf_op jit(solution)/shard_map/ppermute | solution.py:863
  430.8 6.8 %shard_map.253 = bf16[2,2,3,1024,128]{4,3,2,1,0:T(8,128)(2,1)} custom-call(bf16[1024,1024]{1,0:T(8,128)(2,1)S(1)} %get-tuple-element.86.refs_0_, bf16[1024,1024]{1,0:T(8,128)(2,1)S(1)} %copy-done.2, bf16[256,4096]{1,0:T(8,128)(2,1)S(1)} %copy-done.11, bf16[256,4096]{1,0:T(8,128)(2,1)S(1)} %copy-done.5, bf16[256,4096]{1,0:T(8,128)(2,1)S(1)} %copy-done.17, ...), custom_call_target="tpu_custom_call" | custom-call | flops 5000000000 | bytes 10485760 | tf_op jit(solution)/shard_map/pallas_call | solution.py:770
  447.0 6.7 %shard_map.249 = bf16[2,2,3,1024,128]{4,3,2,1,0:T(8,128)(2,1)} custom-call(bf16[1024,1024]{1,0:T(8,128)(2,1)S(1)} %get-tuple-element.86.refs_0_, bf16[1024,1024]{1,0:T(8,128)(2,1)S(1)} %copy-done.2, bf16[256,4096]{1,0:T(8,128)(2,1)S(1)} %copy-done.11, bf16[256,4096]{1,0:T(8,128)(2,1)S(1)} %copy-done.5, bf16[256,4096]{1,0:T(8,128)(2,1)S(1)} %copy-done.17, ...), custom_call_target="tpu_custom_call" | custom-call | flops 5000000000 | bytes 10485760 | tf_op jit(solution)/shard_map/pallas_call | solution.py:770
  454.1 11.0 %shard_map.251 = bf16[4,2,3,1024,128]{4,3,2,1,0:T(8,128)(2,1)} custom-call(bf16[1024,1024]{1,0:T(8,128)(2,1)S(1)} %get-tuple-element.86.refs_0_, bf16[1024,1024]{1,0:T(8,128)(2,1)S(1)} %copy-done.2, bf16[256,4096]{1,0:T(8,128)(2,1)S(1)} %copy-done.11, bf16[256,4096]{1,0:T(8,128)(2,1)S(1)} %copy-done.5, bf16[256,4096]{1,0:T(8,128)(2,1)S(1)} %copy-done.17, ...), custom_call_target="tpu_custom_call" | custom-call | flops 10000000000 | bytes 16777216 | tf_op jit(solution)/shard_map/pallas_call | solution.py:770
  465.1 4.7 fusion.8
  471.4 18.8 %collective-permute-done.33 = bf16[1,2,3,1024,128]{4,3,2,1,0:T(8,128)(2,1)S(1)} collective-permute-done((bf16[1,2,3,1024,128]{4,3,2,1,0:T(8,128)(2,1)S(1)}, bf16[1,2,3,1024,128]{4,3,2,1,0:T(8,128)(2,1)S(1)}, u32[]{:S(2)}, u32[]{:S(2)}) %collective-permute-start.33) | collective-permute-done | bytes 1572896 | tf_op jit(solution)/shard_map/ppermute | solution.py:873
  504.3 7.9 %psum.7 = f32[128]{0:T(128)} all-reduce(f32[128]{0:T(128)S(1)} %slice_bitcast_fusion.8), channel_id=1, replica_groups=mesh['row'=8,'col'=4] {'col'}, use_global_device_ids=true, to_apply=%region_3.4 | all-reduce | flops 128 | bytes 1024 | tf_op jit(solution)/shard_map/psum | solution.py:977
  518.8 5.3 collective-permute-done.35
  524.1 6.8 %collective-permute-done.34 = bf16[1,2,3,1024,128]{4,3,2,1,0:T(8,128)(2,1)} collective-permute-done((bf16[1,2,3,1024,128]{4,3,2,1,0:T(8,128)(2,1)}, bf16[1,2,3,1024,128]{4,3,2,1,0:T(8,128)(2,1)}, u32[]{:S(2)}, u32[]{:S(2)}) %collective-permute-start.34) | collective-permute-done | bytes 1572896 | tf_op jit(solution)/shard_map/ppermute | solution.py:873
  533.5 22.5 %collective-permute-done.32 = bf16[1,2,3,1024,128]{4,3,1,2,0:T(8,128)(2,1)} collective-permute-done((bf16[1,2,3,1024,128]{4,3,1,2,0:T(8,128)(2,1)}, bf16[1,2,3,1024,128]{4,3,1,2,0:T(8,128)(2,1)}, u32[]{:S(2)}, u32[]{:S(2)}) %collective-permute-start.32) | collective-permute-done | bytes 1572896 | tf_op jit(solution)/shard_map/ppermute | solution.py:873
  556.0 4.2 collective-permute-done.29
  (331 shorter events, 167.6 us)
Async XLA Ops:
  7.2 87.4 %all-gather.5.cloned.1.call-start = ((), (), s32[]{:S(2)}) async-start(), calls=%async_computation.8 | async-start | bytes 1253376 | tf_op jit(solution)/shard_map/all_gather | solution.py:935
  9.7 131.2 %all-gather.7.cloned.1.call-start = ((), (), s32[]{:S(2)}) async-start(), calls=%async_computation.9 | async-start | bytes 2297856 | tf_op jit(solution)/shard_map/all_gather | solution.py:937
  13.7 76.1 %collective-permute-start.8 = (bf16[4,3,1024,128]{3,2,1,0:T(8,128)(2,1)}, bf16[4,3,1024,128]{3,2,1,0:T(8,128)(2,1)}, u32[]{:S(2)}, u32[]{:S(2)}) collective-permute-start(bf16[4,3,1024,128]{3,2,1,0:T(8,128)(2,1)} %pad_maximum_fusion.w0), channel_id=1, source_target_pairs={{0,16},{4,20},{8,24},{12,28},{16,0},{20,4},{24,8},{28,12},{1,17},{... | collective-permute-start | bytes 9437192 | tf_op jit(solution)/shard_map/ppermute | solution.py:873
  15.3 137.9 %collective-permute-start.6 = (bf16[4,3,1024,128]{3,2,1,0:T(8,128)(2,1)}, bf16[4,3,1024,128]{3,2,1,0:T(8,128)(2,1)}, u32[]{:S(2)}, u32[]{:S(2)}) collective-permute-start(bf16[4,3,1024,128]{3,2,1,0:T(8,128)(2,1)} %pad_maximum_fusion.w0), channel_id=1, source_target_pairs={{0,8},{4,12},{8,0},{12,4},{16,24},{20,28},{24,16},{28,20},{1,9},{5... | collective-permute-start | bytes 9437192 | tf_op jit(solution)/shard_map/ppermute | solution.py:873
  31.6 86.7 %collective-permute-start.4 = (bf16[256,1024]{1,0:T(8,128)(2,1)S(1)}, bf16[256,1024]{1,0:T(8,128)(2,1)S(1)}, u32[]{:S(2)}, u32[]{:S(2)}) collective-permute-start(bf16[256,1024]{1,0:T(8,128)(2,1)S(1)} %copy-done.39), channel_id=1, source_target_pairs={{0,1},{1,2},{2,3},{3,0},{4,5},{5,6},{6,7},{7,4},{8,9},{9,10},{10,1... | collective-permute-start | bytes 1572872 | tf_op jit(solution)/shard_map/ppermute | solution.py:855
  44.9 49.6 %collective-permute-start.2 = (bf16[256,1024]{1,0:T(8,128)(2,1)}, bf16[256,1024]{1,0:T(8,128)(2,1)}, u32[]{:S(2)}, u32[]{:S(2)}) collective-permute-start(bf16[256,1024]{1,0:T(8,128)(2,1)} %collective-permute-done.1.x2), channel_id=1, source_target_pairs={{0,1},{1,2},{2,3},{3,0},{4,5},{5,6},{6,7},{7,4},{8,9},{9,10},{10,1... | collective-permute-start | bytes 1572872 | tf_op jit(solution)/shard_map/ppermute | solution.py:855
  92.5 63.8 %collective-permute-start.10 = (bf16[2,3,1024,128]{3,2,1,0:T(8,128)(2,1)}, bf16[2,3,1024,128]{3,2,1,0:T(8,128)(2,1)}, u32[]{:S(2)}, u32[]{:S(2)}) collective-permute-start(bf16[2,3,1024,128]{3,2,1,0:T(8,128)(2,1)} %slice.101), channel_id=1, source_target_pairs={{0,8},{4,12},{8,0},{12,4},{16,24},{20,28},{24,16},{28,20},{1,9},{5... | collective-permute-start | bytes 4718600 | tf_op jit(solution)/shard_map/ppermute | solution.py:873
  112.9 32.9 %all-to-all-start = ((bf16[4,256,256]{2,1,0:T(8,128)(2,1)}), bf16[4,256,256]{2,1,0:T(8,128)(2,1)S(1)}, u32[]{:S(2)}, u32[]{:S(2)}) async-start(bf16[4,256,256]{2,1,0:T(8,128)(2,1)} %bitcast.4), calls=%async_computation | async-start | bytes 1048576 | tf_op jit(solution)/shard_map/all_to_all | solution.py:948
  118.3 22.2 %collective-permute-start.16 = (bf16[256,1024]{1,0:T(8,128)(2,1)S(1)}, bf16[256,1024]{1,0:T(8,128)(2,1)S(1)}, u32[]{:S(2)}, u32[]{:S(2)}) collective-permute-start(bf16[256,1024]{1,0:T(8,128)(2,1)S(1)} %collective-permute-done.4.g_ref.g1), channel_id=1, source_target_pairs={{0,1},{1,2},{2,3},{3,0},{4,5},{5,6},{6,7},{7,4},{8,9},{9,10},{10,1... | collective-permute-start | bytes 1572872 | tf_op jit(solution)/shard_map/ppermute | solution.py:855
  153.2 41.7 %collective-permute-start.5 = (bf16[4,3,1024,128]{3,2,1,0:T(8,128)(2,1)}, bf16[4,3,1024,128]{3,2,1,0:T(8,128)(2,1)S(1)}, u32[]{:S(2)}, u32[]{:S(2)}) collective-permute-start(bf16[4,3,1024,128]{3,2,1,0:T(8,128)(2,1)} %pad_maximum_fusion.w0), channel_id=1, source_target_pairs={{0,4},{4,0},{8,12},{12,8},{16,20},{20,16},{24,28},{28,24},{1,5},{5... | collective-permute-start | bytes 9437192 | tf_op jit(solution)/shard_map/ppermute | solution.py:873
  154.7 36.9 %collective-permute-start.11 = (bf16[2,3,1024,128]{3,2,1,0:T(8,128)(2,1)S(1)}, bf16[2,3,1024,128]{3,2,1,0:T(8,128)(2,1)S(1)}, u32[]{:S(2)}, u32[]{:S(2)}) collective-permute-start(bf16[2,3,1024,128]{3,2,1,0:T(8,128)(2,1)S(1)} %slice.102), channel_id=1, source_target_pairs={{0,16},{4,20},{8,24},{12,28},{16,0},{20,4},{24,8},{28,12},{1,17},{... | collective-permute-start | bytes 4718600 | tf_op jit(solution)/shard_map/ppermute | solution.py:873
  156.1 40.5 %collective-permute-start.7 = (bf16[4,3,1024,128]{3,2,1,0:T(8,128)(2,1)}, bf16[4,3,1024,128]{3,2,1,0:T(8,128)(2,1)S(1)}, u32[]{:S(2)}, u32[]{:S(2)}) collective-permute-start(bf16[4,3,1024,128]{3,2,1,0:T(8,128)(2,1)} %collective-permute-done.6.w2), channel_id=1, source_target_pairs={{0,4},{4,0},{8,12},{12,8},{16,20},{20,16},{24,28},{28,24},{1,5},{5... | collective-permute-start | bytes 9437192 | tf_op jit(solution)/shard_map/ppermute | solution.py:873
  156.3 41.9 %collective-permute-start.9 = (bf16[4,3,1024,128]{3,2,1,0:T(8,128)(2,1)}, bf16[4,3,1024,128]{3,2,1,0:T(8,128)(2,1)S(1)}, u32[]{:S(2)}, u32[]{:S(2)}) collective-permute-start(bf16[4,3,1024,128]{3,2,1,0:T(8,128)(2,1)} %collective-permute-done.8.w4), channel_id=1, source_target_pairs={{0,4},{4,0},{8,12},{12,8},{16,20},{20,16},{24,28},{28,24},{1,5},{5... | collective-permute-start | bytes 9437192 | tf_op jit(solution)/shard_map/ppermute | solution.py:873
  222.7 134.2 %collective-permute-start.14 = (bf16[256,1024]{1,0:T(8,128)(2,1)}, bf16[256,1024]{1,0:T(8,128)(2,1)}, u32[]{:S(2)}, u32[]{:S(2)}) collective-permute-start(bf16[256,1024]{1,0:T(8,128)(2,1)} %get-tuple-element.60), channel_id=1, source_target_pairs={{0,1},{1,2},{2,3},{3,0},{4,5},{5,6},{6,7},{7,4},{8,9},{9,10},{10,1... | collective-permute-start | bytes 1572872 | tf_op jit(solution)/shard_map/ppermute | solution.py:863
  223.4 47.7 %collective-permute-start.21 = (bf16[256,1152]{1,0:T(8,128)(2,1)}, bf16[256,1152]{1,0:T(8,128)(2,1)S(1)}, u32[]{:S(2)}, u32[]{:S(2)}) collective-permute-start(bf16[256,1152]{1,0:T(8,128)(2,1)} %get-tuple-element.64), channel_id=1, source_target_pairs={{0,1},{1,2},{2,3},{3,0},{4,5},{5,6},{6,7},{7,4},{8,9},{9,10},{10,1... | collective-permute-start | bytes 1769480 | tf_op jit(solution)/shard_map/ppermute | solution.py:863
  272.3 22.3 %collective-permute-start.22 = (bf16[256,1152]{1,0:T(8,128)(2,1)S(1)}, bf16[256,1152]{1,0:T(8,128)(2,1)}, u32[]{:S(2)}, u32[]{:S(2)}) collective-permute-start(bf16[256,1152]{1,0:T(8,128)(2,1)S(1)} %add_convert_fusion.4), channel_id=1, source_target_pairs={{0,1},{1,2},{2,3},{3,0},{4,5},{5,6},{6,7},{7,4},{8,9},{9,10},{10,1... | collective-permute-start | bytes 1769480 | tf_op jit(solution)/shard_map/ppermute | solution.py:863
  317.6 136.4 %collective-permute-start.28 = (bf16[4,2,3,1024,128]{4,3,2,1,0:T(8,128)(2,1)}, bf16[4,2,3,1024,128]{4,3,2,1,0:T(8,128)(2,1)}, u32[]{:S(2)}, u32[]{:S(2)}) collective-permute-start(bf16[4,2,3,1024,128]{4,3,2,1,0:T(8,128)(2,1)} %shard_map.250), channel_id=1, source_target_pairs={{0,4},{4,0},{8,12},{12,8},{16,20},{20,16},{24,28},{28,24},{1,5},{5... | collective-permute-start | bytes 18874376 | tf_op jit(solution)/shard_map/ppermute | solution.py:873
  323.3 37.4 %all-to-all-start.1 = ((bf16[4,256,256]{2,1,0:T(8,128)(2,1)}), bf16[4,256,256]{2,1,0:T(8,128)(2,1)S(1)}, u32[]{:S(2)}, u32[]{:S(2)}) async-start(bf16[4,256,256]{2,1,0:T(8,128)(2,1)} %bitcast.54), calls=%async_computation.1 | async-start | bytes 1048576 | tf_op jit(solution)/shard_map/all_to_all | solution.py:957
  330.0 165.8 %reduce-scatter.4.cloned.1.call-start = ((), (), s32[]{:S(2)}) async-start(), calls=%async_computation.5 | async-start | bytes 1253376 | tf_op jit(solution)/shard_map/reduce_scatter | solution.py:976
  350.4 66.0 %collective-permute-start.30 = (bf16[2,2,3,1024,128]{4,3,2,1,0:T(8,128)(2,1)}, bf16[2,2,3,1024,128]{4,3,2,1,0:T(8,128)(2,1)}, u32[]{:S(2)}, u32[]{:S(2)}) collective-permute-start(bf16[2,2,3,1024,128]{4,3,2,1,0:T(8,128)(2,1)} %shard_map.252), channel_id=1, source_target_pairs={{0,4},{4,0},{8,12},{12,8},{16,20},{20,16},{24,28},{28,24},{1,5},{5... | collective-permute-start | bytes 9437192 | tf_op jit(solution)/shard_map/ppermute | solution.py:873
  356.7 90.3 %collective-permute-start.27 = (bf16[2,2,3,1024,128]{4,3,2,1,0:T(8,128)(2,1)}, bf16[2,2,3,1024,128]{4,3,2,1,0:T(8,128)(2,1)}, u32[]{:S(2)}, u32[]{:S(2)}) collective-permute-start(bf16[2,2,3,1024,128]{4,3,2,1,0:T(8,128)(2,1)} %shard_map.248), channel_id=1, source_target_pairs={{0,4},{4,0},{8,12},{12,8},{16,20},{20,16},{24,28},{28,24},{1,5},{5... | collective-permute-start | bytes 9437192 | tf_op jit(solution)/shard_map/ppermute | solution.py:873
  359.0 27.2 %collective-permute-start.17 = (bf16[256,1024]{1,0:T(8,128)(2,1)}, bf16[256,1024]{1,0:T(8,128)(2,1)}, u32[]{:S(2)}, u32[]{:S(2)}) collective-permute-start(bf16[256,1024]{1,0:T(8,128)(2,1)} %add_convert_fusion.8), channel_id=1, source_target_pairs={{0,1},{1,2},{2,3},{3,0},{4,5},{5,6},{6,7},{7,4},{8,9},{9,10},{10,1... | collective-permute-start | bytes 1572872 | tf_op jit(solution)/shard_map/ppermute | solution.py:863
  386.1 111.3 %reduce-scatter.6.cloned.1.call-start = ((), (), s32[]{:S(2)}) async-start(), calls=%async_computation.6 | async-start | bytes 2506752 | tf_op jit(solution)/shard_map/reduce_scatter | solution.py:974
  388.1 24.7 %collective-permute-start.24 = (bf16[256,1024]{1,0:T(8,128)(2,1)S(1)}, bf16[256,1024]{1,0:T(8,128)(2,1)S(1)}, u32[]{:S(2)}, u32[]{:S(2)}) collective-permute-start(bf16[256,1024]{1,0:T(8,128)(2,1)S(1)} %copy-done.64), channel_id=1, source_target_pairs={{0,1},{1,2},{2,3},{3,0},{4,5},{5,6},{6,7},{7,4},{8,9},{9,10},{10,1... | collective-permute-start | bytes 1572872 | tf_op jit(solution)/shard_map/ppermute | solution.py:863
  413.8 23.8 %collective-permute-start.25 = (bf16[256,1024]{1,0:T(8,128)(2,1)}, bf16[256,1024]{1,0:T(8,128)(2,1)}, u32[]{:S(2)}, u32[]{:S(2)}) collective-permute-start(bf16[256,1024]{1,0:T(8,128)(2,1)} %add_convert_fusion.6), channel_id=1, source_target_pairs={{0,1},{1,2},{2,3},{3,0},{4,5},{5,6},{6,7},{7,4},{8,9},{9,10},{10,1... | collective-permute-start | bytes 1572872 | tf_op jit(solution)/shard_map/ppermute | solution.py:863
  416.3 98.9 %reduce-scatter.8.cloned.1.call-start = ((), (), s32[]{:S(2)}) async-start(), calls=%async_computation.7 | async-start | bytes 348160 | tf_op jit(solution)/shard_map/reduce_scatter | solution.py:975
  444.6 45.6 %collective-permute-start.33 = (bf16[1,2,3,1024,128]{4,3,2,1,0:T(8,128)(2,1)S(1)}, bf16[1,2,3,1024,128]{4,3,2,1,0:T(8,128)(2,1)S(1)}, u32[]{:S(2)}, u32[]{:S(2)}) collective-permute-start(bf16[1,2,3,1024,128]{4,3,2,1,0:T(8,128)(2,1)S(1)} %get-tuple-element.110), channel_id=1, source_target_pairs={{0,16},{4,20},{8,24},{12,28},{16,0},{20,4},{24,8},{28,12},{1,17},{... | collective-permute-start | bytes 4718600 | tf_op jit(solution)/shard_map/ppermute | solution.py:873
  446.5 50.9 %collective-permute-start.31 = (bf16[1,2,3,1024,128]{4,3,1,2,0:T(8,128)(2,1)}, bf16[1,2,3,1024,128]{4,3,1,2,0:T(8,128)(2,1)}, u32[]{:S(2)}, u32[]{:S(2)}) collective-permute-start(bf16[1,2,3,1024,128]{4,3,1,2,0:T(8,128)(2,1)} %copy.65), channel_id=1, source_target_pairs={{0,8},{4,12},{8,0},{12,4},{16,24},{20,28},{24,16},{28,20},{1,9},{5... | collective-permute-start | bytes 4718600 | tf_op jit(solution)/shard_map/ppermute | solution.py:873
  469.8 54.2 %collective-permute-start.35 = (bf16[1,2,3,1024,128]{4,3,2,1,0:T(8,128)(2,1)}, bf16[1,2,3,1024,128]{4,3,2,1,0:T(8,128)(2,1)}, u32[]{:S(2)}, u32[]{:S(2)}) collective-permute-start(bf16[1,2,3,1024,128]{4,3,2,1,0:T(8,128)(2,1)} %get-tuple-element.101), channel_id=1, source_target_pairs={{0,16},{4,20},{8,24},{12,28},{16,0},{20,4},{24,8},{28,12},{1,17},{... | collective-permute-start | bytes 4718600 | tf_op jit(solution)/shard_map/ppermute | solution.py:873
  493.2 37.6 %collective-permute-start.34 = (bf16[1,2,3,1024,128]{4,3,2,1,0:T(8,128)(2,1)}, bf16[1,2,3,1024,128]{4,3,2,1,0:T(8,128)(2,1)}, u32[]{:S(2)}, u32[]{:S(2)}) collective-permute-start(bf16[1,2,3,1024,128]{4,3,2,1,0:T(8,128)(2,1)} %add_convert_fusion), channel_id=1, source_target_pairs={{0,8},{4,12},{8,0},{12,4},{16,24},{20,28},{24,16},{28,20},{1,9},{5... | collective-permute-start | bytes 4718600 | tf_op jit(solution)/shard_map/ppermute | solution.py:873
  501.0 55.0 %collective-permute-start.32 = (bf16[1,2,3,1024,128]{4,3,1,2,0:T(8,128)(2,1)}, bf16[1,2,3,1024,128]{4,3,1,2,0:T(8,128)(2,1)}, u32[]{:S(2)}, u32[]{:S(2)}) collective-permute-start(bf16[1,2,3,1024,128]{4,3,1,2,0:T(8,128)(2,1)} %add_convert_fusion.1), channel_id=1, source_target_pairs={{0,16},{4,20},{8,24},{12,28},{16,0},{20,4},{24,8},{28,12},{1,17},{... | collective-permute-start | bytes 4718600 | tf_op jit(solution)/shard_map/ppermute | solution.py:873
  502.8 57.4 %collective-permute-start.29 = (bf16[1,2,3,1024,128]{4,3,1,2,0:T(8,128)(2,1)}, bf16[1,2,3,1024,128]{4,3,1,2,0:T(8,128)(2,1)}, u32[]{:S(2)}, u32[]{:S(2)}) collective-permute-start(bf16[1,2,3,1024,128]{4,3,1,2,0:T(8,128)(2,1)} %copy.63), channel_id=1, source_target_pairs={{0,8},{4,12},{8,0},{12,4},{16,24},{20,28},{24,16},{28,20},{1,9},{5... | collective-permute-start | bytes 4718600 | tf_op jit(solution)/shard_map/ppermute | solution.py:873
  (107 other events, 1138.9 us)
Sparse Core Ops, SparseCore 0:
  10.5 29.4 all-gather.4
  43.4 62.5 all-gather.6
  386.2 35.5 reduce-scatter.3
  425.0 51.0 reduce-scatter.5
  497.5 17.6 reduce-scatter.7
where the time goes:
time: 585 us; the launch traced here: 573 us
  waiting for transfers between devices  199 us (34%)
  Pallas kernels  167 us (29%)
  local copies, waits for them, and re-layouts  96.4 us (16%)
  starting transfers between devices  47.7 us (8%)
  other arithmetic  39.2 us (7%)
  between operations  15.6 us (3%)
  blocking collectives  7.91 us (1%)
    ppermute x18, waiting for transfers between devices, swap(): return lax.ppermute(value, 'row', [(i, i ^ mask) for i in range(8)])  109 us
    pallas_call x4, Pallas kernels, experts(): pl.pallas_call(expert_kernel, grid=(steps,), out_shape=(jax.ShapeDtypeStr...  86.9 us
    unnamed x197, local copies, waits for them, and re-layouts  75.5 us
    ppermute x9, waiting for transfers between devices, ring_gather(): chunks.append(lax.ppermute(chunks[-1], 'col', steps))  66.8 us
    pallas_call x6, Pallas kernels, expert_wgrads(): pl.pallas_call(functools.partial(expert_wgrad_kernel, places, extra is no...  47 us
    ppermute x9, waiting for transfers between devices, ring_sum(): total = lax.ppermute(total, 'col', steps).astype(F32) + part.astype(F32)  21.5 us
    pallas_call x1, Pallas kernels, attend_back(): pl.pallas_call(attend_back_kernel, out_shape=shapes, in_specs=[in_smem()]...  16 us
    ppermute x9, starting transfers between devices, ring_sum(): total = lax.ppermute(total, 'col', steps).astype(F32) + part.astype(F32)  13.3 us
  transfers between devices with their start and end apart: 43, of which 16 were waited for; matrix products, arithmetic and copies ran while one was open for 9% of the time, Pallas kernels for 25%

commit v1 on v0

--- a/solution.py
+++ b/solution.py
@@ -379,6 +379,12 @@
 BF16 = jnp.bfloat16
 MIB = 1024 * 1024
 LANES = 128
+VMEM_MOST = 60 * MIB
+COST_SCALE = 10**6
+
+
+def cost(microseconds):
+    return pl.CostEstimate(flops=int(microseconds * COST_SCALE), bytes_accessed=10**5, transcendentals=0)
 
 
 def dot_nn(a, b):
@@ -399,6 +405,16 @@
 
 def in_smem():
     return pl.BlockSpec(memory_space=pltpu.SMEM)
+
+
+def in_hbm():
+    return pl.BlockSpec(memory_space=pl.ANY)
+
+
+def behind(kernel, n_in, after):
+    if not after:
+        return kernel
+    return lambda *refs: kernel(*refs[:n_in], *refs[n_in + len(after) :])
 
 
 def partner(values):
@@ -413,7 +429,7 @@
 
 def attend_kernel(
     spot_ref, x0, x1, x2, x3, pack_ref, cos_ref, sin_ref,
-    attn_ref, mixed_ref, q_ref, k_ref, v_ref, lse_ref, w_ref, gain_ref,
+    attn_ref, q_ref, k_ref, v_ref, lse_ref, w_ref, gain_ref, mixed_ref,
 ):
     rows = x0.shape[0]
     col, prefix = spot_ref[0], spot_ref[1]
@@ -466,27 +482,27 @@
             mixed_ref[span, pair * LANES : (pair + 1) * LANES] = jnp.concatenate(outs, axis=1).astype(BF16)
 
 
-def attend(spots, chunks, pack, cosine, sine):
+def attend(spots, chunks, pack, cosine, sine, after=()):
     rows = chunks[0].shape[0]
     seq = 4 * rows
     shapes = (
         jax.ShapeDtypeStruct((seq, D), BF16),
-        jax.ShapeDtypeStruct((seq, 256), BF16),
         jax.ShapeDtypeStruct((4, seq, HD), BF16),
         jax.ShapeDtypeStruct((2, seq, HD), BF16),
         jax.ShapeDtypeStruct((2, seq, HD), BF16),
         jax.ShapeDtypeStruct((seq, 4), F32),
         jax.ShapeDtypeStruct((D, 512), BF16),
         jax.ShapeDtypeStruct((2, D), F32),
+        jax.ShapeDtypeStruct((seq, 256), BF16),
     )
     return pl.pallas_call(
-        attend_kernel,
+        behind(attend_kernel, 8, after),
         out_shape=shapes,
-        in_specs=[in_smem()] + [in_vmem()] * 7,
+        in_specs=[in_smem()] + [in_vmem()] * 7 + [in_hbm()] * len(after),
         out_specs=tuple(in_vmem() for _ in shapes),
-        compiler_params=pltpu.CompilerParams(vmem_limit_bytes=40 * MIB),
-        cost_estimate=pl.CostEstimate(flops=4 * 10**9, bytes_accessed=8 * MIB, transcendentals=3 * 10**6),
-    )(spots, *chunks, pack, cosine, sine)
+        compiler_params=pltpu.CompilerParams(vmem_limit_bytes=VMEM_MOST),
+        cost_estimate=cost(10),
+    )(spots, *chunks, pack, cosine, sine, *after)
 
 
 def attend_back_kernel(
@@ -551,15 +567,15 @@
         wgrad_ref[part, :LANES, :] = dot_tn(attn_ref[:, span], dqkv_ref[...]).astype(BF16)
 
 
-def attend_back(spots, grads, mixed, q, k, v, lse, attn_in, w_qkv, cosine, sine, gain):
+def attend_back(spots, grads, mixed, q, k, v, lse, attn_in, w_qkv, cosine, sine, gain, after=()):
     seq = attn_in.shape[0]
     shapes = (
         jax.ShapeDtypeStruct((8, 136, 512), BF16),
     ) + (jax.ShapeDtypeStruct((seq // 4, D), BF16),) * 4
     return pl.pallas_call(
-        attend_back_kernel,
+        behind(attend_back_kernel, 12, after),
         out_shape=shapes,
-        in_specs=[in_smem()] + [in_vmem()] * 11,
+        in_specs=[in_smem()] + [in_vmem()] * 11 + [in_hbm()] * len(after),
         out_specs=tuple(in_vmem() for _ in shapes),
         scratch_shapes=[
             pltpu.VMEM((seq, 512), BF16),
@@ -568,18 +584,23 @@
             pltpu.VMEM((seq, 256), F32),
             pltpu.VMEM((4, seq, HD), BF16),
         ],
-        compiler_params=pltpu.CompilerParams(vmem_limit_bytes=48 * MIB),
-        cost_estimate=pl.CostEstimate(flops=10 * 10**9, bytes_accessed=14 * MIB, transcendentals=3 * 10**6),
-    )(spots, grads, mixed, q, k, v, lse, attn_in, w_qkv, cosine, sine, gain)
+        compiler_params=pltpu.CompilerParams(vmem_limit_bytes=VMEM_MOST),
+        cost_estimate=cost(16),
+    )(spots, grads, mixed, q, k, v, lse, attn_in, w_qkv, cosine, sine, gain, *after)
 
 
 def route_kernel(
-    spot_ref, mixed_ref, x_ref, pack_ref, gain_ref, wr_ref, ids_ref, order_ref,
-    resid_ref, send_ref, gates_ref, kept_ref, wo_ref,
+    spot_ref, mixed_ref, x_ref, pack_ref, gain_ref, ids_ref, order_ref,
+    resid_ref, send_ref, gates_ref, kept_ref, wo_ref, wr_ref, wr_wide,
 ):
     rows = x_ref.shape[0]
-    for part in range(32):
-        wo_ref[pl.ds(part // 4 * LANES, LANES), pl.ds(part % 4 * 256, 256)] = pack_ref[part, :LANES, :]
+    wr_wide[...] = jnp.zeros_like(wr_wide)
+    for row in range(8):
+        span = pl.ds(row * LANES, LANES)
+        for col in range(4):
+            wo_ref[span, col * 256 : (col + 1) * 256] = pack_ref[4 * row + col, :LANES, :]
+            wr_wide[col * 8 : (col + 1) * 8, span] = pack_ref[4 * row + col, LANES:, :LANES].astype(F32)
+    wr_ref[...] = wr_wide[...].astype(BF16)
     resid = x_ref[...].astype(F32)
     for part in range(4):
         resid = resid + dot_nn(mixed_ref[pl.ds(part * rows, rows), :], wo_ref[part * 256 : (part + 1) * 256, :])
@@ -587,7 +608,7 @@
     scale = lax.rsqrt(jnp.mean(resid * resid, axis=1, keepdims=True) + EPS)
     moe_in = (resid * scale * gain_ref[1:2, :]).astype(BF16)
     send_ref[:, :D] = moe_in
-    logits = dot_nn(moe_in, wr_ref[...])
+    logits = dot_nt(moe_in, wr_ref[...])
     lane = lax.broadcasted_iota(jnp.int32, (rows, LANES), 1)
     chosen = jnp.zeros((rows, LANES), jnp.bool_)
     for choice in range(TOPK):
@@ -613,7 +634,7 @@
     return (first == (second ^ (row * 4))).astype(BF16)
 
 
-def route(spots, mixed, x, pack, gain, wr, ids, order):
+def route(spots, mixed, x, pack, gain, ids, order):
     rows = x.shape[0]
     shapes = (
         jax.ShapeDtypeStruct((rows, D), F32),
@@ -621,34 +642,34 @@
         jax.ShapeDtypeStruct((rows, LANES), F32),
         jax.ShapeDtypeStruct((rows, LANES), F32),
         jax.ShapeDtypeStruct((D, D), BF16),
+        jax.ShapeDtypeStruct((LANES, D), BF16),
     )
     return pl.pallas_call(
         route_kernel,
         out_shape=shapes,
-        in_specs=[in_smem()] + [in_vmem()] * 7,
+        in_specs=[in_smem()] + [in_vmem()] * 6,
         out_specs=tuple(in_vmem() for _ in shapes),
-        compiler_params=pltpu.CompilerParams(vmem_limit_bytes=32 * MIB),
-        cost_estimate=pl.CostEstimate(flops=10**9, bytes_accessed=5 * MIB, transcendentals=10**5),
-    )(spots, mixed, x, pack, gain, wr, ids, order)
-
-
-def expert_kernel(
-    x_ref, g_ref, w0, w1, w2, w3, w4, w5, w6a, w6b, w7a, w7b,
-    out_ref, back_ref, hg_ref, hu_ref, act_ref, out_acc, in_acc, gate_acc, held, sems,
-):
+        scratch_shapes=[pltpu.VMEM((LANES, D), F32)],
+        compiler_params=pltpu.CompilerParams(vmem_limit_bytes=VMEM_MOST),
+        cost_estimate=cost(2),
+    )(spots, mixed, x, pack, gain, ids, order)
+
+
+def expert_kernel(x_ref, g_ref, *refs):
+    weights, refs = refs[:10], refs[10:]
+    back_ref, hg_ref, hu_ref, act_ref, out_acc, in_acc, gate_acc, held, sems = refs
     step = pl.program_id(0)
     count = held.shape[1]
     wide = count * LANES
-    sources = ((w0,), (w1,), (w2,), (w3,), (w4,), (w5,), (w6a, w6b), (w7a, w7b))
 
     def fetch(at, slot):
-        for k, parts in enumerate(sources):
+        for k in range(8):
 
             @pl.when(at == k)
             def _():
-                size = count // len(parts)
-                for i, part in enumerate(parts):
-                    pltpu.make_async_copy(part, held.at[slot, pl.ds(i * size, size)], sems.at[slot]).start()
+                for i in range(2):
+                    half = weights[k].at[pl.ds(2 * i, 2)] if k < 6 else weights[2 * k - 6 + i]
+                    pltpu.make_async_copy(half, held.at[slot, pl.ds(2 * i, 2)], sems.at[slot, i]).start()
 
     @pl.when(step == 0)
     def _():
@@ -658,7 +679,8 @@
         gate_acc[...] = jnp.zeros_like(gate_acc)
 
     now = lax.rem(step, 2)
-    pltpu.make_async_copy(w0, held.at[now], sems.at[now]).wait()
+    for i in range(2):
+        pltpu.make_async_copy(weights[6], held.at[now, pl.ds(2 * i, 2)], sems.at[now, i]).wait()
     fetch(step + 1, 1 - now)
 
     join = lambda kind: jnp.concatenate([held[now, i, kind] for i in range(count)], axis=1)
@@ -687,12 +709,12 @@
 
     @pl.when(step == pl.num_programs(0) - 1)
     def _():
-        out_ref[...] = out_acc[...].astype(BF16)
         back_ref[:, :D] = in_acc[...].astype(BF16)
-        back_ref[:, D:] = gate_acc[...].astype(BF16)
-
-
-def experts(x, g, weights):
+        back_ref[:, D : 2 * D] = out_acc[...].astype(BF16)
+        back_ref[:, 2 * D :] = gate_acc[...].astype(BF16)
+
+
+def experts(x, g, weights, after=()):
     rows = x.shape[0]
     count = 4
     steps = 8
@@ -700,25 +722,25 @@
     hidden = pl.BlockSpec((rows, wide), lambda i: (0, i))
     whole = lambda width: pl.BlockSpec((rows, width), lambda i: (0, 0))
     return pl.pallas_call(
-        expert_kernel,
-        grid=(steps,),
-        out_shape=(
-            jax.ShapeDtypeStruct((rows, D), BF16),
-            jax.ShapeDtypeStruct((rows, D + LANES), BF16),
-        )
+        behind(expert_kernel, 12, after),
+        out_shape=(jax.ShapeDtypeStruct((rows, 2 * D + LANES), BF16),)
         + (jax.ShapeDtypeStruct((rows, steps * wide), BF16),) * 3,
-        in_specs=[whole(D + LANES), whole(D)] + [pl.BlockSpec(memory_space=pl.ANY)] * 10,
-        out_specs=(whole(D), whole(D + LANES), hidden, hidden, hidden),
-        scratch_shapes=[
-            pltpu.VMEM((rows, D), F32),
-            pltpu.VMEM((rows, D), F32),
-            pltpu.VMEM((rows, LANES), F32),
-            pltpu.VMEM((2, count, 3, D, LANES), BF16),
-            pltpu.SemaphoreType.DMA((2,)),
-        ],
-        compiler_params=pltpu.CompilerParams(vmem_limit_bytes=56 * MIB),
-        cost_estimate=pl.CostEstimate(flops=20 * 10**9, bytes_accessed=32 * MIB, transcendentals=10**6),
-    )(x, g, *weights)
+        grid_spec=pltpu.PrefetchScalarGridSpec(
+            num_scalar_prefetch=0,
+            grid=(steps,),
+            in_specs=[whole(D + LANES), whole(D)] + [in_hbm()] * (10 + len(after)),
+            out_specs=(whole(2 * D + LANES), hidden, hidden, hidden),
+            scratch_shapes=[
+                pltpu.VMEM((rows, D), F32),
+                pltpu.VMEM((rows, D), F32),
+                pltpu.VMEM((rows, LANES), F32),
+                pltpu.VMEM((2, count, 3, D, LANES), BF16),
+                pltpu.SemaphoreType.DMA((2, 2)),
+            ],
+        ),
+        compiler_params=pltpu.CompilerParams(vmem_limit_bytes=VMEM_MOST),
+        cost_estimate=cost(21),
+    )(x, g, *weights, *after)
 
 
 def flip_kernel(x0, x1, x2, x3, g0, g1, g2, g3, xt_ref, gt_ref):
@@ -728,68 +750,187 @@
         gt_ref[:, at * rows : (at + 1) * rows] = g[...].T
 
 
-def flip(xs, gs):
+def flip(xs, gs, after=()):
     seq = 4 * xs[0].shape[0]
     return pl.pallas_call(
-        flip_kernel,
+        behind(flip_kernel, 8, after),
         out_shape=(jax.ShapeDtypeStruct((D, seq), BF16),) * 2,
-        in_specs=[in_vmem()] * 8,
+        in_specs=[in_vmem()] * 8 + [in_hbm()] * len(after),
         out_specs=(in_vmem(),) * 2,
-        compiler_params=pltpu.CompilerParams(vmem_limit_bytes=24 * MIB),
-        cost_estimate=pl.CostEstimate(flops=10**9, bytes_accessed=8 * MIB, transcendentals=0),
-    )(*xs, *gs)
-
-
-def expert_wgrad_kernel(places, added, halved, *refs):
-    xt_ref, gt_ref = refs[:2]
-    hidden = refs[2:14]
-    more = refs[14:]
-    half = pl.program_id(0) % 2
-    extra = more[0] if added else None
-    outs = more[1:] if added else more
+        compiler_params=pltpu.CompilerParams(vmem_limit_bytes=VMEM_MOST),
+        cost_estimate=cost(2),
+    )(*xs, *gs, *after)
+
+
+def expert_wgrad_kernel(places, added, late, xt_ref, gt_ref, *refs):
+    hidden, refs = refs[:12], refs[12:]
+    count = len(places)
+    n_extra = len({place[0] for place in added if place}) + len(late)
+    plain = [k for k, place in enumerate(added) if not place]
+    extras, refs = refs[:n_extra], refs[n_extra:]
+    n_out = len({which for which, _ in places})
+    outs, refs = refs[:n_out], refs[n_out:]
+    held, out_sems, got, in_sems = refs
+    step = pl.program_id(0)
+    now = lax.rem(step, 2)
+
+    def fetch(at, slot):
+        for k, place in enumerate(added):
+            if not place:
+                continue
+            which, half = place
+
+            @pl.when(at == k)
+            def _():
+                pltpu.make_async_copy(extras[which].at[half], got.at[slot, 0], in_sems.at[slot, 0]).start()
+                if k in late:
+                    pltpu.make_async_copy(extras[late[k]].at[0], got.at[slot, 1], in_sems.at[slot, 1]).start()
+
+    if added:
+
+        @pl.when(step == 0)
+        def _():
+            fetch(step, 0)
+
+        fetch(step + 1, 1 - now)
+
+    def sent(slot):
+        pltpu.make_async_copy(held.at[slot], outs[0].at[0], out_sems.at[slot]).wait()
+
+    @pl.when(step >= 2)
+    def _():
+        sent(now)
+
+    first = functools.reduce(jnp.logical_and, [step != k for k in plain], step >= 0)
+    second = functools.reduce(jnp.logical_or, [step == k for k in late], False)
+    if added:
+
+        @pl.when(functools.reduce(jnp.logical_and, [step != k for k in plain], step >= 0))
+        def _():
+            pltpu.make_async_copy(extras[0].at[0], got.at[now, 0], in_sems.at[now, 0]).wait()
+
+        for k in late:
+
+            @pl.when(step == k)
+            def _():
+                pltpu.make_async_copy(extras[0].at[0], got.at[now, 1], in_sems.at[now, 1]).wait()
+
+
     for kind, left in enumerate((xt_ref, xt_ref, gt_ref)):
         joined = jnp.concatenate([part[...] for part in hidden[kind * 4 : kind * 4 + 4]], axis=0)
         product = dot_nn(left[...], joined)
         for i in range(2):
             piece = product[:, i * LANES : (i + 1) * LANES]
-            if added:
-                piece = piece + extra[0, i, kind].astype(F32)
-            outs[0][0, i, kind] = piece.astype(BF16)
-
-
-def expert_wgrads(flipped, hidden, places, extra=None):
+            if plain:
+                piece = piece + jnp.where(first, got[now, 0, i, kind].astype(F32), 0.0)
+            elif added:
+                piece = piece + got[now, 0, i, kind].astype(F32)
+            if late:
+                piece = piece + jnp.where(second, got[now, 1, i, kind].astype(F32), 0.0)
+            held[now, i, kind] = piece.astype(BF16)
+
+    for k, (which, half) in enumerate(places):
+
+        @pl.when(step == k)
+        def _():
+            pltpu.make_async_copy(held.at[now], outs[which].at[half], out_sems.at[now]).start()
+
+    @pl.when(step == count - 1)
+    def _():
+        sent(now)
+        if count > 1:
+            sent(1 - now)
+
+
+def expert_wgrads(flipped, hidden, entries, places, extras=(), added=(), late=None, after=(), time=None):
     rows = hidden[0][0].shape[0]
     wide = 2 * LANES
     seq = flipped[0].shape[1]
-    first = places[0] * 2
-    jump = (places[1] - places[0]) * 2 if len(places) > 1 else 0
-    lane = pl.BlockSpec((rows, wide), lambda i: (0, first + (i // 2) * jump + i % 2))
+    count = len(entries)
+
+    def entry(i):
+        place = entries[0]
+        for k in range(1, count):
+            place = jnp.where(i == k, entries[k], place)
+        return (0, place)
+
+    lane = pl.BlockSpec((rows, wide), entry)
     whole = pl.BlockSpec((D, seq), lambda i: (0, 0))
-    weight = pl.BlockSpec((1, 2, 3, D, LANES), lambda i: (i, 0, 0, 0, 0))
-    steps = 2 * len(places)
+    kernel = functools.partial(expert_wgrad_kernel, places, added, late or {})
+    sizes = [sum(which == o for which, _ in places) for o in range(max(which for which, _ in places) + 1)]
     return pl.pallas_call(
-        functools.partial(expert_wgrad_kernel, places, extra is not None, False),
-        grid=(steps,),
-        out_shape=jax.ShapeDtypeStruct((steps, 2, 3, D, LANES), BF16),
-        in_specs=[whole] * 2 + [lane] * 12 + ([weight] if extra is not None else []),
-        out_specs=weight,
-        compiler_params=pltpu.CompilerParams(vmem_limit_bytes=32 * MIB),
-        cost_estimate=pl.CostEstimate(
-            flops=len(places) * 5 * 10**9, bytes_accessed=(4 + 6 * len(places)) * MIB, transcendentals=0
-        ),
-    )(*flipped, *hidden[0], *hidden[1], *hidden[2], *(() if extra is None else (extra,)))
+        behind(kernel, 14 + len(extras), after),
+        grid=(count,),
+        out_shape=tuple(jax.ShapeDtypeStruct((size, 2, 3, D, LANES), BF16) for size in sizes),
+        in_specs=[whole] * 2 + [lane] * 12 + [in_hbm()] * (len(extras) + len(after)),
+        out_specs=(in_hbm(),) * len(sizes),
+        scratch_shapes=[
+            pltpu.VMEM((2, 2, 3, D, LANES), BF16),
+            pltpu.SemaphoreType.DMA((2,)),
+            pltpu.VMEM((2, 2, 2, 3, D, LANES), BF16),
+            pltpu.SemaphoreType.DMA((2, 2)),
+        ],
+        compiler_params=pltpu.CompilerParams(vmem_limit_bytes=VMEM_MOST),
+        cost_estimate=cost(time or 2.2 * count),
+    )(*flipped, *hidden[0], *hidden[1], *hidden[2], *extras, *after)
+
+
+def expert_total_kernel(own_ref, xa_ref, xb_ref, ya_ref, yb_ref, gate_ref, up_ref, down_ref):
+    for kind, out in enumerate((gate_ref, up_ref, down_ref)):
+        for half, (x_ref, y_ref) in enumerate(((xa_ref, ya_ref), (xb_ref, yb_ref))):
+            out[half, 0] = (
+                own_ref[half, 0, kind].astype(F32) + x_ref[0, 0, kind].astype(F32) + y_ref[0, 0, kind].astype(F32)
+            )
+
+
+def expert_total(after, own, *parts):
+    block = pl.BlockSpec((2, 1, 3, D, LANES), lambda i: (0, i, 0, 0, 0))
+    part = pl.BlockSpec((1, 1, 3, D, LANES), lambda i: (0, i, 0, 0, 0))
+    out = pl.BlockSpec((2, 1, D, LANES), lambda i: (0, i, 0, 0))
+    sums = pl.pallas_call(
+        behind(expert_total_kernel, 5, after),
+        grid=(2,),
+        out_shape=(jax.ShapeDtypeStruct((2, 2, D, LANES), F32),) * 3,
+        in_specs=[block] + [part] * 4 + [in_hbm()] * len(after),
+        out_specs=(out,) * 3,
+        compiler_params=pltpu.CompilerParams(vmem_limit_bytes=VMEM_MOST),
+        cost_estimate=cost(5),
+    )(own, *parts, *after)
+    return [total.reshape(4, D, LANES) for total in sums]
+
+
+def halves_kernel(x_ref, y_ref, low_ref, high_ref):
+    low_ref[...] = y_ref[...]
+    high_ref[...] = x_ref[...]
+
+
+def halves(from_x, from_y, after):
+    half = jax.ShapeDtypeStruct((2, 3, D, LANES), BF16)
+    first = pl.BlockSpec((1, 1, D, LANES), lambda i, j: (i, j, 0, 0))
+    second = pl.BlockSpec((1, 1, D, LANES), lambda i, j: (i + 2, j, 0, 0))
+    return pl.pallas_call(
+        behind(halves_kernel, 2, after),
+        grid=(2, 3),
+        out_shape=(half, half),
+        in_specs=[second, first] + [in_hbm()] * len(after),
+        out_specs=(first,) * 2,
+        compiler_params=pltpu.CompilerParams(vmem_limit_bytes=VMEM_MOST),
+        cost_estimate=cost(3),
+    )(from_x, from_y, *after)
 
 
 def turn_kernel(
-    spot_ref, back_ref, gates_ref, kept_ref, resid_ref, gain_ref, g_ref, wr_ref, wo_ref, send_ref,
-    resid_grad_ref, branch_ref, mixed_grad_ref, small_ref,
+    spot_ref, came_ref, back_ref, gates_ref, kept_ref, resid_ref, gain_ref, g_ref, wr_ref, wo_ref, send_ref,
+    out_ref, resid_grad_ref, branch_ref, mixed_grad_ref, small_ref,
 ):
     rows = resid_ref.shape[0]
     gates = gates_ref[...]
-    gate_grad = dot_nn(back_ref[:, D:], relabel(spot_ref[2])) * kept_ref[...]
+    both = lambda span: came_ref[:, span].astype(F32) + back_ref[:, span].astype(F32)
+    out_ref[...] = resid_ref[...] + both(slice(D, 2 * D))
+    gate_grad = dot_nn(both(slice(2 * D, None)).astype(BF16), relabel(spot_ref[2])) * kept_ref[...]
     logit_grad = gates * (gate_grad - jnp.sum(gates * gate_grad, axis=1, keepdims=True))
     logit_grad = logit_grad.astype(BF16)
-    moe_grad = back_ref[:, :D].astype(F32) + dot_nt(logit_grad, wr_ref[...])
+    moe_grad = both(slice(0, D)) + dot_nn(logit_grad, wr_ref[...])
     resid = resid_ref[...]
     scale = lax.rsqrt(jnp.mean(resid * resid, axis=1, keepdims=True) + EPS)
     normed = resid * scale
@@ -806,22 +947,23 @@
         ).astype(BF16)
 
 
-def turn(spots, back, gates, kept, resid, gain, g, wr, wo, send):
+def turn(spots, came, back, gates, kept, resid, gain, g, wr, wo, send, after=()):
     rows = resid.shape[0]
     shapes = (
+        jax.ShapeDtypeStruct((rows, D), F32),
         jax.ShapeDtypeStruct((rows, D), F32),
         jax.ShapeDtypeStruct((rows, D), BF16),
         jax.ShapeDtypeStruct((4 * rows, 256), BF16),
         jax.ShapeDtypeStruct((LANES + 8, D), F32),
     )
     return pl.pallas_call(
-        turn_kernel,
+        behind(turn_kernel, 11, after),
         out_shape=shapes,
-        in_specs=[in_smem()] + [in_vmem()] * 9,
+        in_specs=[in_smem()] + [in_vmem()] * 10 + [in_hbm()] * len(after),
         out_specs=tuple(in_vmem() for _ in shapes),
-        compiler_params=pltpu.CompilerParams(vmem_limit_bytes=32 * MIB),
-        cost_estimate=pl.CostEstimate(flops=2 * 10**9, bytes_accessed=7 * MIB, transcendentals=10**5),
-    )(spots, back, gates, kept, resid, gain, g, wr, wo, send)
+        compiler_params=pltpu.CompilerParams(vmem_limit_bytes=VMEM_MOST),
+        cost_estimate=cost(2),
+    )(spots, came, back, gates, kept, resid, gain, g, wr, wo, send, *after)
 
 
 def out_wgrad_kernel(mixed_ref, branch_ref, small_ref, pack_ref):
@@ -837,15 +979,15 @@
             pack_ref[row, LANES:, col * 256 + LANES : col * 256 + 256] = small_ref[LANES:, span].astype(BF16)
 
 
-def out_wgrad(mixed, branch, small):
+def out_wgrad(mixed, branch, small, after=()):
     return pl.pallas_call(
-        out_wgrad_kernel,
+        behind(out_wgrad_kernel, 3, after),
         out_shape=jax.ShapeDtypeStruct((8, LANES + 8, D), BF16),
-        in_specs=[in_vmem()] * 3,
+        in_specs=[in_vmem()] * 3 + [in_hbm()] * len(after),
         out_specs=in_vmem(),
-        compiler_params=pltpu.CompilerParams(vmem_limit_bytes=24 * MIB),
-        cost_estimate=pl.CostEstimate(flops=2 * 10**9, bytes_accessed=4 * MIB, transcendentals=0),
-    )(mixed, branch, small)
+        compiler_params=pltpu.CompilerParams(vmem_limit_bytes=VMEM_MOST),
+        cost_estimate=cost(3),
+    )(mixed, branch, small, *after)
 
 
 def ring_gather(value, n_col):
@@ -866,43 +1008,22 @@
     return total
 
 
+def shift_all(parts, n_col):
+    return [
+        lax.ppermute(part, "col", [(i, (i + s) % n_col) for i in range(n_col)]) if s else part
+        for s, part in enumerate(parts)
+    ]
+
+
+def hold(value, *until):
+    return lax.optimization_barrier((value, *until))[0]
+
+
 CORE, ACROSS_X, ACROSS_Y = 1, 2, 4
 
 
 def swap(value, mask):
     return lax.ppermute(value, "row", [(i, i ^ mask) for i in range(8)])
-
-
-def gather_weights(own):
-    from_x, from_y = swap(own, ACROSS_X), swap(own, ACROSS_Y)
-    other = swap(own, CORE)
-    half = own.shape[0] // 2
-    far_a, far_b = swap(from_y[:half], ACROSS_X), swap(from_x[half:], ACROSS_Y)
-    return (
-        own, other, from_x, swap(from_x, CORE), from_y, swap(from_y, CORE),
-        far_a, far_b, swap(far_a, CORE), swap(far_b, CORE),
-    )
-
-
-def sum_weights(flipped, hidden):
-    p7 = expert_wgrads(flipped, hidden, (7,))
-    r7 = swap(p7, CORE)
-    p35 = expert_wgrads(flipped, hidden, (3, 5))
-    r35 = swap(p35, CORE)
-    q6 = expert_wgrads(flipped, hidden, (6,), r7)
-    from_x, from_y = swap(q6[:1], ACROSS_X), swap(q6[1:], ACROSS_Y)
-    p1 = expert_wgrads(flipped, hidden, (1,))
-    r1 = swap(p1, CORE)
-    q24 = expert_wgrads(flipped, hidden, (2, 4), r35)
-    q2a, q2b, q4a, q4b = (q24[i : i + 1] for i in range(4))
-    from_x2a, from_y4b = swap(q2a, ACROSS_X), swap(q4b, ACROSS_Y)
-    add = lambda a, b: (a.astype(F32) + b.astype(F32)).astype(BF16)
-    from_x2b = swap(add(q2b, from_y), ACROSS_X)
-    from_y4a = swap(add(q4a, from_x), ACROSS_Y)
-    q0 = expert_wgrads(flipped, hidden, (0,), r1)
-    low = q0[0].astype(F32) + from_x2a[0].astype(F32) + from_y4a[0].astype(F32)
-    high = q0[1].astype(F32) + from_x2b[0].astype(F32) + from_y4b[0].astype(F32)
-    return low, high
 
 
 def fast(
@@ -933,48 +1054,90 @@
         [jnp.concatenate([w_query, w_key, w_value], axis=1), gains, jnp.zeros((7, 512), BF16)], axis=0
     )
     pack_qkv = lax.all_gather(pack_qkv, "row", axis=0)
-    pack_out = jnp.concatenate([w_out, w_router.reshape(4, 256), jnp.zeros((4, 256), BF16)], axis=0)
+    x_chunks = ring_gather(block_in, n_col)
+    own = jnp.stack([w_gate, w_up, w_down], axis=1)
+    from_x, from_y, other = swap(own, ACROSS_X), swap(own, ACROSS_Y), swap(own, CORE)
+    pack_out = jnp.concatenate([w_out, jnp.pad(w_router.T, ((0, 0), (0, 256 - LANES)))], axis=0)
     pack_out = lax.all_gather(pack_out, ("row", "col"), axis=0)
-    wr = pack_out[:, LANES : LANES + 4].reshape(8, 4, LANES, 8).transpose(0, 2, 1, 3).reshape(D, E)
-    wr = jnp.pad(wr, ((0, 0), (0, LANES - E)))
     cosine, sine = rope_tables(0, seq)
     cosine = jnp.tile(cosine, (1, 4))
     sine = jnp.concatenate([-sine, sine, -sine, sine], axis=1)
 
-    weights = gather_weights(jnp.stack([w_gate, w_up, w_down], axis=1))
-    x_chunks = ring_gather(block_in, n_col)
-    attn_in, mixed, q, k, v, lse, w_qkv, gains = attend(spots, x_chunks, pack_qkv, cosine, sine)
-    g_chunks = ring_gather(out_grad, n_col)
-    mixed_own = lax.all_to_all(mixed, "col", split_axis=0, concat_axis=0, tiled=True)
-    resid, send, gates, kept, wo = route(spots, mixed_own, block_in, pack_out, gains, wr, expert_ids, fill_order)
-
-    send_chunks = ring_gather(send, n_col)
-    results = [experts(x, g, weights) for x, g in zip(send_chunks, g_chunks)]
-    back = ring_sum([result[1] for result in results], n_col).astype(BF16)
-    resid_grad, branch, mixed_grad, small = turn(
-        spots, back, gates, kept, resid, gains, out_grad, wr, wo, send
+    attn_in, q, k, v, lse, w_qkv, gains, mixed_all = attend(spots, x_chunks, pack_qkv, cosine, sine, [other])
+    g_chunks = ring_gather(hold(out_grad, x_chunks[3]), n_col)
+    mixed_own = lax.all_to_all(mixed_all, "col", split_axis=0, concat_axis=0, tiled=True)
+    resid, send, gates, kept, wo, wr = route(
+        spots, mixed_own, block_in, pack_out, gains, expert_ids, fill_order
+    )
+    low, high = halves(from_x, from_y, [mixed_own])
+    far = swap(low, ACROSS_X), swap(high, ACROSS_Y)
+    weights = [own, other, from_x, swap(from_x, CORE), from_y, swap(from_y, CORE), *far]
+
+    send_chunks = [send, *ring_gather(hold(send, g_chunks[3]), n_col)[1:]]
+    weights += [swap(hold(part, send_chunks[3]), CORE) for part in far]
+    results, backs, back = {}, [], None
+    steps = [(i, (i + 1) % n_col) for i in range(n_col)]
+    order = (1, 2, 3, 0)
+    for at, chunk in enumerate(order):
+        after = [results[order[at - 1]][1]] if at else [send_chunks[3]]
+        if at >= 2:
+            after.append(backs[at - 2])
+        results[chunk] = experts(send_chunks[chunk], g_chunks[chunk], weights, after)
+        if chunk:
+            part = results[chunk][0]
+            back = part if back is None else (back.astype(F32) + part.astype(F32)).astype(BF16)
+            back = lax.ppermute(back, "col", steps)
+            backs.append(back)
+    results = [results[chunk] for chunk in range(n_col)]
+
+    flipped = flip(send_chunks, g_chunks, [results[2][1]])
+    hidden = [[result[kind] for result in results] for kind in (1, 2, 3)]
+    wgrads = functools.partial(expert_wgrads, flipped, hidden)
+    (p7,) = wgrads((14, 15), ((0, 0), (0, 1)), after=[backs[2]])
+    r7 = swap(p7, CORE)
+    block_out, resid_grad, branch, mixed_grad, small = turn(
+        spots, backs[2], results[0][0], gates, kept, resid, gains, out_grad, wr, wo, send, [p7]
     )
     mixed_grads = lax.all_to_all(mixed_grad, "col", split_axis=0, concat_axis=0, tiled=True)
+    (p53,) = wgrads((6, 7, 10, 11), tuple((0, i) for i in range(4)), after=[branch, r7])
+    r53 = swap(p53, CORE)
+    q6 = wgrads((12, 13), ((0, 0), (1, 0)), [r7], ((0, 0), (0, 1)), after=[p53])
+    far_x, far_y = swap(q6[0], ACROSS_X), swap(q6[1], ACROSS_Y)
+    pack = out_wgrad(mixed_own, branch, small, q6[:1])
+    out_sum = lax.psum_scatter(pack, "row", scatter_dimension=0, tiled=True)
+    q2a, q4b = wgrads((4, 9), ((0, 0), (1, 0)), [r53], ((0, 0), (0, 3)), after=[pack, mixed_grads])
+    x2a, y4b = swap(q2a, ACROSS_X), swap(q4b, ACROSS_Y)
+    q2b, q4a, p1 = wgrads(
+        (5, 8, 2, 3),
+        ((0, 0), (1, 0), (2, 0), (2, 1)),
+        [r53, far_y, far_x],
+        ((0, 1), (0, 2), None, None),
+        {0: 1, 1: 2},
+        [q2a],
+    )
+    r1 = swap(p1, CORE)
+    x2b, y4a = swap(q2b, ACROSS_X), swap(q4a, ACROSS_Y)
     qkv_wgrad, *back_parts = attend_back(
-        spots, mixed_grads, mixed, q, k, v, lse, attn_in, w_qkv, cosine, sine, gains
-    )
-    attn_grad = ring_sum(back_parts, n_col)
+        spots, mixed_grads, mixed_all, q, k, v, lse, attn_in, w_qkv, cosine, sine, gains, [q2b]
+    )
+    (q0,) = wgrads((0, 1), ((0, 0), (0, 1)), [r1], ((0, 0), (0, 1)), after=[qkv_wgrad])
+    moving = lax.ppermute(back_parts[1], "col", steps)
+    moving = (hold(moving, q0, x2a, y4b).astype(F32) + back_parts[2].astype(F32)).astype(BF16)
+    moving = lax.ppermute(moving, "col", steps)
+    moving = (moving.astype(F32) + back_parts[3].astype(F32)).astype(BF16)
+    third_step = moving
+    attn_grad = lax.ppermute(moving, "col", steps).astype(F32) + back_parts[0].astype(F32)
     x_rows = block_in.astype(F32)
     scale = lax.rsqrt(jnp.mean(x_rows * x_rows, axis=1, keepdims=True) + EPS)
     normed = x_rows * scale
     inner = attn_grad * gains[:1]
     block_in_grad = resid_grad + scale * (inner - normed * jnp.mean(inner * normed, axis=1, keepdims=True))
-    block_out = resid + ring_sum([result[0] for result in results], n_col)
-
-    low, high = sum_weights(
-        flip(send_chunks, g_chunks), [[result[kind] for result in results] for kind in (2, 3, 4)]
-    )
-    gate_sum, up_sum, down_sum = (jnp.concatenate([low[:, i], high[:, i]], axis=0) for i in range(3))
-
-    out_sum = lax.psum_scatter(out_wgrad(mixed_own, branch, small), "row", scatter_dimension=0)
-    out_sum = lax.psum_scatter(out_sum, "col", scatter_dimension=1, tiled=True).astype(F32)
-    qkv_sum = lax.psum_scatter(qkv_wgrad, "row", scatter_dimension=0).astype(F32)
-    gain_one_sum = lax.psum(qkv_sum[LANES, :LANES], "col")
+    gate_sum, up_sum, down_sum = expert_total([third_step], q0, x2a, x2b, y4a, y4b)
+
+    qkv_sum = lax.psum_scatter(qkv_wgrad, "row", scatter_dimension=0, tiled=True)[0].astype(F32)
+    out_sum = lax.psum_scatter(hold(out_sum, q2b), "col", scatter_dimension=2, tiled=True)[0].astype(F32)
+    gain_one = qkv_sum[LANES:, :LANES]
+    gain_one_sum = functools.reduce(jnp.add, shift_all([gain_one] * n_col, n_col))[0]
     return (
         block_out,
         block_in_grad,

time: 585 us -> 502 us (0.86)
  the two profiles are of different devices: /device:TPU:20 before, /device:TPU:0 now
where the time goes in v1:
time: 502 us; the launch traced here: 493 us
  Pallas kernels  209 us (42%)
  waiting for transfers between devices  174 us (35%)
  starting transfers between devices  36.4 us (7%)
  other arithmetic  21.8 us (4%)
  blocking collectives  19.6 us (4%)
  local copies, waits for them, and re-layouts  16 us (3%)
  between operations  15.4 us (3%)
    pallas_call x4, Pallas kernels, experts(): pl.pallas_call(behind(expert_kernel, 12, after), out_shape=(jax.ShapeDtyp...  86.9 us
    ppermute x9, waiting for transfers between devices, ring_gather(): chunks.append(lax.ppermute(chunks[-1], 'col', steps))  81.5 us
    pallas_call x6, Pallas kernels, expert_wgrads(): pl.pallas_call(behind(kernel, 14 + len(extras), after), grid=(count,), ou...  62.5 us
    ppermute x18, waiting for transfers between devices, swap(): return lax.ppermute(value, 'row', [(i, i ^ mask) for i in range(8)])  27.5 us
    reduce_scatter x1, waiting for transfers between devices, fast(): lax.psum_scatter(qkv_wgrad, 'row', scatter_dimension=0, tiled=True)[0]  25.5 us
    all_to_all x1, waiting for transfers between devices, fast(): lax.all_to_all(mixed_all, 'col', split_axis=0, concat_axis=0, tiled=True)  19.8 us
    all_to_all x1, blocking collectives, fast(): lax.all_to_all(mixed_grad, 'col', split_axis=0, concat_axis=0, tiled=True)  19.6 us
    ppermute x18, starting transfers between devices, swap(): return lax.ppermute(value, 'row', [(i, i ^ mask) for i in range(8)])  18.3 us
  transfers between devices with their start and end apart: 42, of which 20 were waited for; matrix products, arithmetic and copies ran while one was open for 5% of the time, Pallas kernels for 34%

profile of v1, /device:TPU:0, one launch (start us, length us, event | category | flops | bytes accessed | tf_op | source)
XLA Modules:
  0.0 492.9 jit_solution(14996895481144760626)
XLA Ops:
  19.7 11.5 %collective-permute-done.refs_2_ = bf16[256,1024]{1,0:T(8,128)(2,1)S(1)} collective-permute-done((bf16[256,1024]{1,0:T(8,128)(2,1)S(1)}, bf16[256,1024]{1,0:T(8,128)(2,1)S(1)}, u32[]{:S(2)}, u32[]{:S(2)}) %collective-permute-start) | collective-permute-done | bytes 524320 | tf_op jit(solution)/shard_map/ppermute | solution.py:997
  31.3 15.5 %collective-permute-done.1.refs_3_ = bf16[256,1024]{1,0:T(8,128)(2,1)S(1)} collective-permute-done((bf16[256,1024]{1,0:T(8,128)(2,1)S(1)}, bf16[256,1024]{1,0:T(8,128)(2,1)S(1)}, u32[]{:S(2)}, u32[]{:S(2)}) %collective-permute-start.1) | collective-permute-done | bytes 524320 | tf_op jit(solution)/shard_map/ppermute | solution.py:997
  46.8 15.5 %collective-permute-done.2.refs_4_ = bf16[256,1024]{1,0:T(8,128)(2,1)S(1)} collective-permute-done((bf16[256,1024]{1,0:T(8,128)(2,1)S(1)}, bf16[256,1024]{1,0:T(8,128)(2,1)S(1)}, u32[]{:S(2)}, u32[]{:S(2)}) %collective-permute-start.2) | collective-permute-done | bytes 524320 | tf_op jit(solution)/shard_map/ppermute | solution.py:997
  63.1 14.2 %collective-permute-done.4.refs_1_.refs_5_ = bf16[256,1024]{1,0:T(8,128)(2,1)} collective-permute-done((bf16[256,1024]{1,0:T(8,128)(2,1)S(1)}, bf16[256,1024]{1,0:T(8,128)(2,1)}, u32[]{:S(2)}, u32[]{:S(2)}) %collective-permute-start.4) | collective-permute-done | bytes 524320 | tf_op jit(solution)/shard_map/ppermute | solution.py:997
  88.8 12.1 %shard_map.238 = (bf16[1024,1024]{1,0:T(8,128)(2,1)}, bf16[4,1024,64]{2,1,0:T(8,128)(2,1)}, bf16[2,1024,64]{2,1,0:T(8,128)(2,1)}, bf16[2,1024,64]{2,1,0:T(8,128)...) custom-call(s32[3]{0:T(128)} %pad_add_fusion.refs_0_.spot_ref, ...), custom_call_target="tpu_custom_call" | custom-call | flops 10000000 | bytes 100000 | tf_op jit(solution)/shard_map/pallas_call | solution.py:498
  100.9 5.2 %all-to-all-start = ((bf16[4,256,256]{2,1,0:T(8,128)(2,1)}), bf16[4,256,256]{2,1,0:T(8,128)(2,1)}, u32[]{:S(2)}, u32[]{:S(2)}) async-start(bf16[4,256,256]{2,1,0:T(8,128)(2,1)} %bitcast.33), calls=%async_computation | async-start | bytes 1048576 | tf_op jit(solution)/shard_map/all_to_all | solution.py:1068
  109.4 19.8 %all-to-all-done = bf16[4,256,256]{2,1,0:T(8,128)(2,1)} async-done(((bf16[4,256,256]{2,1,0:T(8,128)(2,1)}), bf16[4,256,256]{2,1,0:T(8,128)(2,1)}, u32[]{:S(2)}, u32[]{:S(2)}) %all-to-all-start) | async-done | bytes 524320 | tf_op jit(solution)/shard_map/all_to_all | solution.py:1068
  129.2 5.0 %shard_map.239 = (f32[256,1024]{1,0:T(8,128)}, bf16[256,1152]{1,0:T(8,128)(2,1)}, f32[256,128]{1,0:T(8,128)}, f32[256,128]{1,0:T(8,128)}, bf16[1024,1024]{1,0:T(8,128)(2,1)}, /*index=5*/bf16[128,1024]{1,0:T(8,128)(2,1)}) custom-call(s32[3]{0:T(128)} %pad_add_fusion.refs_0_.spot_ref, bf16[1024,256]{1,0:T(8,128)(2,1)} %bitcast.8.mixed_ref.refs_2_.refs_0_, ...), custom_call_target="tpu_custom_call" | custom-call | flops 2000000 | bytes 100000 | tf_op jit(solution)/shard_map/pallas_call | solution.py:647
  134.3 5.2 %shard_map.240 = (bf16[2,3,1024,128]{3,2,1,0:T(8,128)(2,1)}, bf16[2,3,1024,128]{3,2,1,0:T(8,128)(2,1)}) custom-call(bf16[4,3,1024,128]{3,2,1,0:T(8,128)(2,1)} %collective-permute-done.8.refs_0_.refs_4_, bf16[4,3,1024,128]{3,2,1,0:T(8,128)(2,1)} %collective-permute-done.10.refs_1_.refs_6_, bf16[1024,256]{1,0:T(8,128)(2,1)} %bitcast.8.mixed_ref.refs_2_.refs_0_), custom_call_target="tpu_custom_call" | custom-call | flops 3000000 | bytes 100000 | tf_op jit(solution)/shard_map/pallas_call | solution.py:911
  140.8 7.2 %collective-permute-start.13 = (bf16[2,3,1024,128]{3,2,1,0:T(8,128)(2,1)}, bf16[2,3,1024,128]{3,2,1,0:T(8,128)(2,1)S(1)}, u32[]{:S(2)}, u32[]{:S(2)}) collective-permute-start(bf16[2,3,1024,128]{3,2,1,0:T(8,128)(2,1)} %get-tuple-element.78), channel_id=1, source_target_pairs={{0,16},{4,20},{8,24},{12,28},{16,0},{20,4},{24,8},{28,12},{1,17},{... | collective-permute-start | bytes 4718600 | tf_op jit(solution)/shard_map/ppermute | solution.py:1026
  149.5 16.4 %collective-permute-done.14.refs_0_.refs_2_ = bf16[256,1152]{1,0:T(8,128)(2,1)S(1)} collective-permute-done((bf16[256,1152]{1,0:T(8,128)(2,1)}, bf16[256,1152]{1,0:T(8,128)(2,1)S(1)}, u32[]{:S(2)}, u32[]{:S(2)}) %collective-permute-start.14) | collective-permute-done | bytes 589856 | tf_op jit(solution)/shard_map/ppermute | solution.py:997
  166.0 8.0 %collective-permute-done.12.refs_8_ = bf16[2,3,1024,128]{3,2,1,0:T(8,128)(2,1)S(1)} collective-permute-done((bf16[2,3,1024,128]{3,2,1,0:T(8,128)(2,1)}, bf16[2,3,1024,128]{3,2,1,0:T(8,128)(2,1)S(1)}, u32[]{:S(2)}, u32[]{:S(2)}) %collective-permute-start.12) | collective-permute-done | bytes 1572896 | tf_op jit(solution)/shard_map/ppermute | solution.py:1026
  174.0 7.3 %collective-permute-done.15.refs_12_.refs_0_.refs_3_ = bf16[256,1152]{1,0:T(8,128)(2,1)S(1)} collective-permute-done((bf16[256,1152]{1,0:T(8,128)(2,1)S(1)}, bf16[256,1152]{1,0:T(8,128)(2,1)S(1)}, u32[]{:S(2)}, u32[]{:S(2)}) %collective-permute-start.15) | collective-permute-done | bytes 589856 | tf_op jit(solution)/shard_map/ppermute | solution.py:997
  187.2 21.7 %shard_map.241 = (bf16[256,2176]{1,0:T(8,128)(2,1)}, bf16[256,4096]{1,0:T(8,128)(2,1)}, bf16[256,4096]{1,0:T(8,128)(2,1)}, bf16[256,4096]{1,0:T(8,128)(2,1)}) custom-call(bf16[256,1152]{1,0:T(8,128)(2,1)} %collective-permute-done.7.refs_0_.refs_1_, bf16[256,1024]{1,0:T(8,128)(2,1)} %collective-permute-done.4.refs_1_.refs_5_, ...), custom_call_target="tpu_custom_call" | custom-call | flops 21000000 | bytes 100000 | tf_op jit(solution)/shard_map/pallas_call | solution.py:724
  209.0 21.8 %shard_map.242 = (bf16[256,2176]{1,0:T(8,128)(2,1)}, bf16[256,4096]{1,0:T(8,128)(2,1)}, bf16[256,4096]{1,0:T(8,128)(2,1)}, bf16[256,4096]{1,0:T(8,128)(2,1)}) custom-call(bf16[256,1152]{1,0:T(8,128)(2,1)} %copy-done.13, bf16[256,1024]{1,0:T(8,128)(2,1)} %collective-permute-done.5.refs_1_.refs_6_, bf16[4,3,1024,128]{3,2,1,0:T(8,128)(2,1)} %copy-done, ...), custom_call_target="tpu_custom_call" | custom-call | flops 21000000 | bytes 100000 | tf_op jit(solution)/shard_map/pallas_call | solution.py:724
  230.7 6.8 %collective-permute-done.18.refs_13_ = bf16[256,2176]{1,0:T(8,128)(2,1)S(1)} collective-permute-done((bf16[256,2176]{1,0:T(8,128)(2,1)}, bf16[256,2176]{1,0:T(8,128)(2,1)S(1)}, u32[]{:S(2)}, u32[]{:S(2)}) %collective-permute-start.18) | collective-permute-done | bytes 1114144 | tf_op jit(solution)/shard_map/ppermute | solution.py:1089
  239.6 21.8 %shard_map.243 = (bf16[256,2176]{1,0:T(8,128)(2,1)}, bf16[256,4096]{1,0:T(8,128)(2,1)}, bf16[256,4096]{1,0:T(8,128)(2,1)}, bf16[256,4096]{1,0:T(8,128)(2,1)}) custom-call(bf16[256,1152]{1,0:T(8,128)(2,1)} %copy-done.8, bf16[256,1024]{1,0:T(8,128)(2,1)} %collective-permute-done.6.refs_1_.refs_7_, bf16[4,3,1024,128]{3,2,1,0:T(8,128)(2,1)} %copy-done, ...), custom_call_target="tpu_custom_call" | custom-call | flops 21000000 | bytes 100000 | tf_op jit(solution)/shard_map/pallas_call | solution.py:724
  261.3 5.8 %collective-permute-done.19.refs_13_ = bf16[256,2176]{1,0:T(8,128)(2,1)S(1)} collective-permute-done((bf16[256,2176]{1,0:T(8,128)(2,1)S(1)}, bf16[256,2176]{1,0:T(8,128)(2,1)S(1)}, u32[]{:S(2)}, u32[]{:S(2)}) %collective-permute-start.19) | collective-permute-done | bytes 1114144 | tf_op jit(solution)/shard_map/ppermute | solution.py:1089
  269.3 5.3 %shard_map.245 = (bf16[1024,1024]{1,0:T(8,128)(2,1)}, bf16[1024,1024]{1,0:T(8,128)(2,1)}) custom-call(bf16[256,1152]{1,0:T(8,128)(2,1)} %get-tuple-element.76.refs_0_.refs_10_, bf16[256,1152]{1,0:T(8,128)(2,1)} %collective-permute-done.7.refs_0_.refs_1_, bf16[256,1152]{1,0:T(8,128)(2,1)} %copy-done.13, bf16[256,1152]{1,0:T(8,128)(2,1)} %copy-done.8, ...), custom_call_target="tpu_custom_call" | custom-call | flops 2000000 | bytes 100000 | tf_op jit(solution)/shard_map/pallas_call | solution.py:755
  274.6 21.7 %shard_map.244 = (bf16[256,2176]{1,0:T(8,128)(2,1)}, bf16[256,4096]{1,0:T(8,128)(2,1)}, bf16[256,4096]{1,0:T(8,128)(2,1)}, bf16[256,4096]{1,0:T(8,128)(2,1)}) custom-call(bf16[256,1152]{1,0:T(8,128)(2,1)} %get-tuple-element.76.refs_0_.refs_10_, bf16[256,1024]{1,0:T(8,128)(2,1)} %refs_7_.1, bf16[4,3,1024,128]{3,2,1,0:T(8,128)(2,1)} %copy-done, ...), custom_call_target="tpu_custom_call" | custom-call | flops 21000000 | bytes 100000 | tf_op jit(solution)/shard_map/pallas_call | solution.py:724
  297.3 7.9 %shard_map.246.refs_11_ = bf16[2,2,3,1024,128]{4,3,2,1,0:T(8,128)(2,1)} custom-call(bf16[1024,1024]{1,0:T(8,128)(2,1)} %get-tuple-element.93.refs_0_, bf16[1024,1024]{1,0:T(8,128)(2,1)} %get-tuple-element.94.refs_1_, bf16[256,4096]{1,0:T(8,128)(2,1)} %get-tuple-element.95.refs_2_, bf16[256,4096]{1,0:T(8,128)(2,1)} %get-tuple-element.82.refs_12_.refs_3_, ...), custom_call_target="tpu_custom_call" | custom-call | flops 4400000 | bytes 100000 | tf_op jit(solution)/shard_map/pallas_call | solution.py:861
  305.4 6.0 %shard_map.247 = (f32[256,1024]{1,0:T(8,128)}, f32[256,1024]{1,0:T(8,128)}, bf16[256,1024]{1,0:T(8,128)(2,1)}, bf16[1024,256]{1,0:T(8,128)(2,1)}, f32[136,1024]{1,0:T(8,128)}) custom-call(s32[3]{0:T(128)} %pad_add_fusion.refs_0_.spot_ref, bf16[256,2176]{1,0:T(8,128)(2,1)} %copy-done.10, bf16[256,2176]{1,0:T(8,128)(2,1)} %get-tuple-element.87.refs_2_, ...), custom_call_target="tpu_custom_call" | custom-call | flops 2000000 | bytes 100000 | tf_op jit(solution)/shard_map/pallas_call | solution.py:959
  313.0 11.9 %shard_map.248.refs_15_ = bf16[4,2,3,1024,128]{4,3,2,1,0:T(8,128)(2,1)} custom-call(bf16[1024,1024]{1,0:T(8,128)(2,1)} %get-tuple-element.93.refs_0_, bf16[1024,1024]{1,0:T(8,128)(2,1)} %get-tuple-element.94.refs_1_, bf16[256,4096]{1,0:T(8,128)(2,1)} %get-tuple-element.95.refs_2_, bf16[256,4096]{1,0:T(8,128)(2,1)} %get-tuple-element.82.refs_12_.refs_3_, ...), custom_call_target="tpu_custom_call" | custom-call | flops 8800000 | bytes 100000 | tf_op jit(solution)/shard_map/pallas_call | solution.py:861
  325.4 9.4 %shard_map.249 = (bf16[1,2,3,1024,128]{4,3,2,1,0:T(8,128)(2,1)}, bf16[1,2,3,1024,128]{4,3,2,1,0:T(8,128)(2,1)}) custom-call(bf16[1024,1024]{1,0:T(8,128)(2,1)} %get-tuple-element.93.refs_0_, bf16[1024,1024]{1,0:T(8,128)(2,1)} %get-tuple-element.94.refs_1_, bf16[256,4096]{1,0:T(8,128)(2,1)} %get-tuple-element.95.refs_2_, ...), custom_call_target="tpu_custom_call" | custom-call | flops 4400000 | bytes 100000 | tf_op jit(solution)/shard_map/pallas_call | solution.py:861
  339.4 19.6 %all_to_all.22 = bf16[4,256,256]{2,1,0:T(8,128)(2,1)} all-to-all(bf16[4,256,256]{2,1,0:T(8,128)(2,1)S(1)} %bitcast.39), channel_id=1, replica_groups=mesh['row'=8,'col'=4] {'col'}, dimensions={0} | all-to-all | bytes 1048576 | tf_op jit(solution)/shard_map/all_to_all | solution.py:1101
  359.0 9.4 %shard_map.251 = (bf16[1,2,3,1024,128]{4,3,2,1,0:T(8,128)(2,1)}, bf16[1,2,3,1024,128]{4,3,2,1,0:T(8,128)(2,1)}) custom-call(bf16[1024,1024]{1,0:T(8,128)(2,1)} %get-tuple-element.93.refs_0_, bf16[1024,1024]{1,0:T(8,128)(2,1)} %get-tuple-element.94.refs_1_, bf16[256,4096]{1,0:T(8,128)(2,1)} %get-tuple-element.95.refs_2_, ...), custom_call_target="tpu_custom_call" | custom-call | flops 4400000 | bytes 100000 | tf_op jit(solution)/shard_map/pallas_call | solution.py:861
  368.4 12.5 %collective-permute-done.23.refs_15_ = bf16[1,2,3,1024,128]{4,3,2,1,0:T(8,128)(2,1)S(1)} collective-permute-done((bf16[1,2,3,1024,128]{4,3,2,1,0:T(8,128)(2,1)}, bf16[1,2,3,1024,128]{4,3,2,1,0:T(8,128)(2,1)S(1)}, u32[]{:S(2)}, u32[]{:S(2)}) %collective-permute-start.23) | collective-permute-done | bytes 1572896 | tf_op jit(solution)/shard_map/ppermute | solution.py:1026
  383.3 14.4 %shard_map.252 = (bf16[1,2,3,1024,128]{4,3,2,1,0:T(8,128)(2,1)}, bf16[1,2,3,1024,128]{4,3,2,1,0:T(8,128)(2,1)}, bf16[2,2,3,1024,128]{4,3,2,1,0:T(8,128)(2,1)}) custom-call(bf16[1024,1024]{1,0:T(8,128)(2,1)} %get-tuple-element.93.refs_0_, bf16[1024,1024]{1,0:T(8,128)(2,1)} %get-tuple-element.94.refs_1_, bf16[256,4096]{1,0:T(8,128)(2,1)} %get-tuple-element.95.refs_2_, ...), custom_call_target="tpu_custom_call" | custom-call | flops 8800000 | bytes 100000 | tf_op jit(solution)/shard_map/pallas_call | solution.py:861
  399.0 17.0 %shard_map.253 = (bf16[8,136,512]{2,1,0:T(8,128)(2,1)}, bf16[256,1024]{1,0:T(8,128)(2,1)}, bf16[256,1024]{1,0:T(8,128)(2,1)}, bf16[256,1024]{1,0:T(8,128)(2,1)}, bf16[256,1024]{1,0:T(8,128)(2,1)}) custom-call(s32[3]{0:T(128)} %pad_add_fusion.refs_0_.spot_ref, bf16[1024,256]{1,0:T(8,128)(2,1)} %bitcast.31, bf16[1024,256]{1,0:T(8,128)(2,1)} %get-tuple-element.72.refs_2_, ...), custom_call_target="tpu_custom_call" | custom-call | flops 16000000 | bytes 100000 | tf_op jit(solution)/shard_map/pallas_call | solution.py:575
  423.4 9.5 %shard_map.254.refs_0_ = bf16[2,2,3,1024,128]{4,3,2,1,0:T(8,128)(2,1)} custom-call(bf16[1024,1024]{1,0:T(8,128)(2,1)} %get-tuple-element.93.refs_0_, bf16[1024,1024]{1,0:T(8,128)(2,1)} %get-tuple-element.94.refs_1_, bf16[256,4096]{1,0:T(8,128)(2,1)} %get-tuple-element.95.refs_2_, bf16[256,4096]{1,0:T(8,128)(2,1)} %get-tuple-element.82.refs_12_.refs_3_, ...), custom_call_target="tpu_custom_call" | custom-call | flops 4400000 | bytes 100000 | tf_op jit(solution)/shard_map/pallas_call | solution.py:861
  437.9 25.5 %reduce-scatter.4.cloned.1.call-done = bf16[1,136,512]{2,1,0:T(8,128)(2,1)} async-done(((bf16[8,136,512]{2,1,0:T(8,128)(2,1)}), bf16[1,136,512]{2,1,0:T(8,128)(2,1)}) %reduce-scatter.4.cloned.1.call-update) | async-done | bytes 139280 | tf_op jit(solution)/shard_map/reduce_scatter | solution.py:1137
  473.7 5.9 %shard_map.255 = (f32[2,2,1024,128]{3,2,1,0:T(8,128)}, f32[2,2,1024,128]{3,2,1,0:T(8,128)}, f32[2,2,1024,128]{3,2,1,0:T(8,128)}) custom-call(bf16[2,2,3,1024,128]{4,3,2,1,0:T(8,128)(2,1)} %shard_map.254.refs_0_, bf16[1,2,3,1024,128]{4,3,2,1,0:T(8,128)(2,1)} %collective-permute-done.27.refs_1_, bf16[1,2,3,1024,128]{4,3,2,1,0:T(8,128)(2,1)} %collective-permute-done.34.refs_2_, ...), custom_call_target="tpu_custom_call" | custom-call | flops 5000000 | bytes 100000 | tf_op jit(solution)/shard_map/pallas_call | solution.py:890
  (169 shorter events, 80.7 us)
Async XLA Ops:
  7.2 81.6 %all-gather.5.cloned.1.call-start = ((), (), s32[]{:S(2)}) async-start(), calls=%async_computation.8 | async-start | bytes 1253376 | tf_op jit(solution)/shard_map/all_gather | solution.py:1056
  9.7 119.5 %all-gather.7.cloned.1.call-start = ((), (), s32[]{:S(2)}) async-start(), calls=%async_computation.9 | async-start | bytes 2297856 | tf_op jit(solution)/shard_map/all_gather | solution.py:1061
  13.6 75.2 %collective-permute-start.3 = (bf16[4,3,1024,128]{3,2,1,0:T(8,128)(2,1)S(1)}, bf16[4,3,1024,128]{3,2,1,0:T(8,128)(2,1)}, u32[]{:S(2)}, u32[]{:S(2)}) collective-permute-start(bf16[4,3,1024,128]{3,2,1,0:T(8,128)(2,1)S(1)} %pad_maximum_fusion.refs_2_), channel_id=1, source_target_pairs={{0,4},{4,0},{8,12},{12,8},{16,20},{20,16},{24,28},{28,24},{1,5},{5... | collective-permute-start | bytes 9437192 | tf_op jit(solution)/shard_map/ppermute | solution.py:1026
  14.1 17.2 %collective-permute-start = (bf16[256,1024]{1,0:T(8,128)(2,1)S(1)}, bf16[256,1024]{1,0:T(8,128)(2,1)S(1)}, u32[]{:S(2)}, u32[]{:S(2)}) collective-permute-start(bf16[256,1024]{1,0:T(8,128)(2,1)S(1)} %copy-done.5), channel_id=1, source_target_pairs={{0,1},{1,2},{2,3},{3,0},{4,5},{5,6},{6,7},{7,4},{8,9},{9,10},{10,1... | collective-permute-start | bytes 1572872 | tf_op jit(solution)/shard_map/ppermute | solution.py:997
  16.7 117.5 %collective-permute-start.8 = (bf16[4,3,1024,128]{3,2,1,0:T(8,128)(2,1)S(1)}, bf16[4,3,1024,128]{3,2,1,0:T(8,128)(2,1)}, u32[]{:S(2)}, u32[]{:S(2)}) collective-permute-start(bf16[4,3,1024,128]{3,2,1,0:T(8,128)(2,1)S(1)} %pad_maximum_fusion.refs_2_), channel_id=1, source_target_pairs={{0,8},{4,12},{8,0},{12,4},{16,24},{20,28},{24,16},{28,20},{1,9},{5... | collective-permute-start | bytes 9437192 | tf_op jit(solution)/shard_map/ppermute | solution.py:1026
  18.2 116.1 %collective-permute-start.10 = (bf16[4,3,1024,128]{3,2,1,0:T(8,128)(2,1)S(1)}, bf16[4,3,1024,128]{3,2,1,0:T(8,128)(2,1)}, u32[]{:S(2)}, u32[]{:S(2)}) collective-permute-start(bf16[4,3,1024,128]{3,2,1,0:T(8,128)(2,1)S(1)} %pad_maximum_fusion.refs_2_), channel_id=1, source_target_pairs={{0,16},{4,20},{8,24},{12,28},{16,0},{20,4},{24,8},{28,12},{1,17},{... | collective-permute-start | bytes 9437192 | tf_op jit(solution)/shard_map/ppermute | solution.py:1026
  31.3 15.5 %collective-permute-start.1 = (bf16[256,1024]{1,0:T(8,128)(2,1)S(1)}, bf16[256,1024]{1,0:T(8,128)(2,1)S(1)}, u32[]{:S(2)}, u32[]{:S(2)}) collective-permute-start(bf16[256,1024]{1,0:T(8,128)(2,1)S(1)} %collective-permute-done.refs_2_), channel_id=1, source_target_pairs={{0,1},{1,2},{2,3},{3,0},{4,5},{5,6},{6,7},{7,4},{8,9},{9,10},{10,1... | collective-permute-start | bytes 1572872 | tf_op jit(solution)/shard_map/ppermute | solution.py:997
  46.8 15.5 %collective-permute-start.2 = (bf16[256,1024]{1,0:T(8,128)(2,1)S(1)}, bf16[256,1024]{1,0:T(8,128)(2,1)S(1)}, u32[]{:S(2)}, u32[]{:S(2)}) collective-permute-start(bf16[256,1024]{1,0:T(8,128)(2,1)S(1)} %collective-permute-done.1.refs_3_), channel_id=1, source_target_pairs={{0,1},{1,2},{2,3},{3,0},{4,5},{5,6},{6,7},{7,4},{8,9},{9,10},{10,1... | collective-permute-start | bytes 1572872 | tf_op jit(solution)/shard_map/ppermute | solution.py:997
  77.3 28.8 %collective-permute-start.5 = (bf16[256,1024]{1,0:T(8,128)(2,1)}, bf16[256,1024]{1,0:T(8,128)(2,1)}, u32[]{:S(2)}, u32[]{:S(2)}) collective-permute-start(bf16[256,1024]{1,0:T(8,128)(2,1)} %collective-permute-done.4.refs_1_.refs_5_), channel_id=1, source_target_pairs={{0,1},{1,2},{2,3},{3,0},{4,5},{5,6},{6,7},{7,4},{8,9},{9,10},{10,1... | collective-permute-start | bytes 1572872 | tf_op jit(solution)/shard_map/ppermute | solution.py:997
  100.9 28.3 %all-to-all-start = ((bf16[4,256,256]{2,1,0:T(8,128)(2,1)}), bf16[4,256,256]{2,1,0:T(8,128)(2,1)}, u32[]{:S(2)}, u32[]{:S(2)}) async-start(bf16[4,256,256]{2,1,0:T(8,128)(2,1)} %bitcast.33), calls=%async_computation | async-start | bytes 1048576 | tf_op jit(solution)/shard_map/all_to_all | solution.py:1068
  106.1 292.6 %reduce-scatter.6.cloned.1.call-start = ((), (), s32[]{:S(2)}) async-start(), calls=%async_computation.6 | async-start | bytes 2506752 | tf_op jit(solution)/shard_map/reduce_scatter | solution.py:1107
  106.1 28.1 %collective-permute-start.6 = (bf16[256,1024]{1,0:T(8,128)(2,1)}, bf16[256,1024]{1,0:T(8,128)(2,1)}, u32[]{:S(2)}, u32[]{:S(2)}) collective-permute-start(bf16[256,1024]{1,0:T(8,128)(2,1)} %collective-permute-done.5.refs_1_.refs_6_), channel_id=1, source_target_pairs={{0,1},{1,2},{2,3},{3,0},{4,5},{5,6},{6,7},{7,4},{8,9},{9,10},{10,1... | collective-permute-start | bytes 1572872 | tf_op jit(solution)/shard_map/ppermute | solution.py:997
  139.5 34.4 %collective-permute-start.12 = (bf16[2,3,1024,128]{3,2,1,0:T(8,128)(2,1)}, bf16[2,3,1024,128]{3,2,1,0:T(8,128)(2,1)S(1)}, u32[]{:S(2)}, u32[]{:S(2)}) collective-permute-start(bf16[2,3,1024,128]{3,2,1,0:T(8,128)(2,1)} %get-tuple-element.77), channel_id=1, source_target_pairs={{0,8},{4,12},{8,0},{12,4},{16,24},{20,28},{24,16},{28,20},{1,9},{5... | collective-permute-start | bytes 4718600 | tf_op jit(solution)/shard_map/ppermute | solution.py:1026
  140.8 40.5 %collective-permute-start.13 = (bf16[2,3,1024,128]{3,2,1,0:T(8,128)(2,1)}, bf16[2,3,1024,128]{3,2,1,0:T(8,128)(2,1)S(1)}, u32[]{:S(2)}, u32[]{:S(2)}) collective-permute-start(bf16[2,3,1024,128]{3,2,1,0:T(8,128)(2,1)} %get-tuple-element.78), channel_id=1, source_target_pairs={{0,16},{4,20},{8,24},{12,28},{16,0},{20,4},{24,8},{28,12},{1,17},{... | collective-permute-start | bytes 4718600 | tf_op jit(solution)/shard_map/ppermute | solution.py:1026
  147.9 33.8 %collective-permute-start.9 = (bf16[4,3,1024,128]{3,2,1,0:T(8,128)(2,1)}, bf16[4,3,1024,128]{3,2,1,0:T(8,128)(2,1)S(1)}, u32[]{:S(2)}, u32[]{:S(2)}) collective-permute-start(bf16[4,3,1024,128]{3,2,1,0:T(8,128)(2,1)} %collective-permute-done.8.refs_0_.refs_4_), channel_id=1, source_target_pairs={{0,4},{4,0},{8,12},{12,8},{16,20},{20,16},{24,28},{28,24},{1,5},{5... | collective-permute-start | bytes 9437192 | tf_op jit(solution)/shard_map/ppermute | solution.py:1026
  147.9 33.8 %collective-permute-start.11 = (bf16[4,3,1024,128]{3,2,1,0:T(8,128)(2,1)}, bf16[4,3,1024,128]{3,2,1,0:T(8,128)(2,1)}, u32[]{:S(2)}, u32[]{:S(2)}) collective-permute-start(bf16[4,3,1024,128]{3,2,1,0:T(8,128)(2,1)} %collective-permute-done.10.refs_1_.refs_6_), channel_id=1, source_target_pairs={{0,4},{4,0},{8,12},{12,8},{16,20},{20,16},{24,28},{28,24},{1,5},{5... | collective-permute-start | bytes 9437192 | tf_op jit(solution)/shard_map/ppermute | solution.py:1026
  149.5 16.4 %collective-permute-start.14 = (bf16[256,1152]{1,0:T(8,128)(2,1)}, bf16[256,1152]{1,0:T(8,128)(2,1)S(1)}, u32[]{:S(2)}, u32[]{:S(2)}) collective-permute-start(bf16[256,1152]{1,0:T(8,128)(2,1)} %collective-permute-done.7.refs_0_.refs_1_), channel_id=1, source_target_pairs={{0,1},{1,2},{2,3},{3,0},{4,5},{5,6},{6,7},{7,4},{8,9},{9,10},{10,1... | collective-permute-start | bytes 1769480 | tf_op jit(solution)/shard_map/ppermute | solution.py:997
  208.9 28.7 %collective-permute-start.18 = (bf16[256,2176]{1,0:T(8,128)(2,1)}, bf16[256,2176]{1,0:T(8,128)(2,1)S(1)}, u32[]{:S(2)}, u32[]{:S(2)}) collective-permute-start(bf16[256,2176]{1,0:T(8,128)(2,1)} %get-tuple-element.81), channel_id=1, source_target_pairs={{0,1},{1,2},{2,3},{3,0},{4,5},{5,6},{6,7},{7,4},{8,9},{9,10},{10,1... | collective-permute-start | bytes 3342344 | tf_op jit(solution)/shard_map/ppermute | solution.py:1089
  239.5 27.6 %collective-permute-start.19 = (bf16[256,2176]{1,0:T(8,128)(2,1)S(1)}, bf16[256,2176]{1,0:T(8,128)(2,1)S(1)}, u32[]{:S(2)}, u32[]{:S(2)}) collective-permute-start(bf16[256,2176]{1,0:T(8,128)(2,1)S(1)} %add_convert_fusion.1), channel_id=1, source_target_pairs={{0,1},{1,2},{2,3},{3,0},{4,5},{5,6},{6,7},{7,4},{8,9},{9,10},{10,1... | collective-permute-start | bytes 3342344 | tf_op jit(solution)/shard_map/ppermute | solution.py:1089
  269.0 27.3 %collective-permute-start.20 = (bf16[256,2176]{1,0:T(8,128)(2,1)S(1)}, bf16[256,2176]{1,0:T(8,128)(2,1)S(1)}, u32[]{:S(2)}, u32[]{:S(2)}) collective-permute-start(bf16[256,2176]{1,0:T(8,128)(2,1)S(1)} %add_convert_fusion), channel_id=1, source_target_pairs={{0,1},{1,2},{2,3},{3,0},{4,5},{5,6},{6,7},{7,4},{8,9},{9,10},{10,1... | collective-permute-start | bytes 3342344 | tf_op jit(solution)/shard_map/ppermute | solution.py:1089
  324.9 34.2 %collective-permute-start.22 = (bf16[4,2,3,1024,128]{4,3,2,1,0:T(8,128)(2,1)}, bf16[4,2,3,1024,128]{4,3,2,1,0:T(8,128)(2,1)}, u32[]{:S(2)}, u32[]{:S(2)}) collective-permute-start(bf16[4,2,3,1024,128]{4,3,2,1,0:T(8,128)(2,1)} %shard_map.248.refs_15_), channel_id=1, source_target_pairs={{0,4},{4,0},{8,12},{12,8},{16,20},{20,16},{24,28},{28,24},{1,5},{5... | collective-permute-start | bytes 18874376 | tf_op jit(solution)/shard_map/ppermute | solution.py:1026
  338.3 82.0 %reduce-scatter.8.cloned.1.call-start = ((), (), s32[]{:S(2)}) async-start(), calls=%async_computation.7 | async-start | bytes 348160 | tf_op jit(solution)/shard_map/reduce_scatter | solution.py:1138
  338.4 42.6 %collective-permute-start.23 = (bf16[1,2,3,1024,128]{4,3,2,1,0:T(8,128)(2,1)}, bf16[1,2,3,1024,128]{4,3,2,1,0:T(8,128)(2,1)S(1)}, u32[]{:S(2)}, u32[]{:S(2)}) collective-permute-start(bf16[1,2,3,1024,128]{4,3,2,1,0:T(8,128)(2,1)} %get-tuple-element.114), channel_id=1, source_target_pairs={{0,16},{4,20},{8,24},{12,28},{16,0},{20,4},{24,8},{28,12},{1,17},{... | collective-permute-start | bytes 4718600 | tf_op jit(solution)/shard_map/ppermute | solution.py:1026
  338.5 42.6 %collective-permute-start.24 = (bf16[1,2,3,1024,128]{4,3,2,1,0:T(8,128)(2,1)}, bf16[1,2,3,1024,128]{4,3,2,1,0:T(8,128)(2,1)S(1)}, u32[]{:S(2)}, u32[]{:S(2)}) collective-permute-start(bf16[1,2,3,1024,128]{4,3,2,1,0:T(8,128)(2,1)} %get-tuple-element.115.refs_3_), channel_id=1, source_target_pairs={{0,8},{4,12},{8,0},{12,4},{16,24},{20,28},{24,16},{28,20},{1,9},{5... | collective-permute-start | bytes 4718600 | tf_op jit(solution)/shard_map/ppermute | solution.py:1026
  397.7 24.2 %collective-permute-start.26 = (bf16[2,2,3,1024,128]{4,3,2,1,0:T(8,128)(2,1)}, bf16[2,2,3,1024,128]{4,3,2,1,0:T(8,128)(2,1)}, u32[]{:S(2)}, u32[]{:S(2)}) collective-permute-start(bf16[2,2,3,1024,128]{4,3,2,1,0:T(8,128)(2,1)} %get-tuple-element.120), channel_id=1, source_target_pairs={{0,4},{4,0},{8,12},{12,8},{16,20},{20,16},{24,28},{28,24},{1,5},{5... | collective-permute-start | bytes 9437192 | tf_op jit(solution)/shard_map/ppermute | solution.py:1026
  397.8 37.4 %collective-permute-start.27 = (bf16[1,2,3,1024,128]{4,3,2,1,0:T(8,128)(2,1)S(1)}, bf16[1,2,3,1024,128]{4,3,2,1,0:T(8,128)(2,1)}, u32[]{:S(2)}, u32[]{:S(2)}) collective-permute-start(bf16[1,2,3,1024,128]{4,3,2,1,0:T(8,128)(2,1)S(1)} %copy-done.16), channel_id=1, source_target_pairs={{0,8},{4,12},{8,0},{12,4},{16,24},{20,28},{24,16},{28,20},{1,9},{5... | collective-permute-start | bytes 4718600 | tf_op jit(solution)/shard_map/ppermute | solution.py:1026
  397.9 37.6 %collective-permute-start.28 = (bf16[1,2,3,1024,128]{4,3,2,1,0:T(8,128)(2,1)}, bf16[1,2,3,1024,128]{4,3,2,1,0:T(8,128)(2,1)}, u32[]{:S(2)}, u32[]{:S(2)}) collective-permute-start(bf16[1,2,3,1024,128]{4,3,2,1,0:T(8,128)(2,1)} %get-tuple-element.122), channel_id=1, source_target_pairs={{0,16},{4,20},{8,24},{12,28},{16,0},{20,4},{24,8},{28,12},{1,17},{... | collective-permute-start | bytes 4718600 | tf_op jit(solution)/shard_map/ppermute | solution.py:1026
  398.7 64.7 %reduce-scatter.4.cloned.1.call-start = ((), (), s32[]{:S(2)}) async-start(), calls=%async_computation.5 | async-start | bytes 1253376 | tf_op jit(solution)/shard_map/reduce_scatter | solution.py:1137
  416.2 16.6 %collective-permute-start.25 = (bf16[256,1024]{1,0:T(8,128)(2,1)}, bf16[256,1024]{1,0:T(8,128)(2,1)}, u32[]{:S(2)}, u32[]{:S(2)}) collective-permute-start(bf16[256,1024]{1,0:T(8,128)(2,1)} %get-tuple-element.119), channel_id=1, source_target_pairs={{0,1},{1,2},{2,3},{3,0},{4,5},{5,6},{6,7},{7,4},{8,9},{9,10},{10,1... | collective-permute-start | bytes 1572872 | tf_op jit(solution)/shard_map/ppermute | solution.py:1124
  416.3 57.4 %collective-permute-start.34 = (bf16[1,2,3,1024,128]{4,3,2,1,0:T(8,128)(2,1)}, bf16[1,2,3,1024,128]{4,3,2,1,0:T(8,128)(2,1)}, u32[]{:S(2)}, u32[]{:S(2)}) collective-permute-start(bf16[1,2,3,1024,128]{4,3,2,1,0:T(8,128)(2,1)} %get-tuple-element.118.refs_12_), channel_id=1, source_target_pairs={{0,8},{4,12},{8,0},{12,4},{16,24},{20,28},{24,16},{28,20},{1,9},{5... | collective-permute-start | bytes 4718600 | tf_op jit(solution)/shard_map/ppermute | solution.py:1026
  421.9 51.8 %collective-permute-start.35 = (bf16[1,2,3,1024,128]{4,3,2,1,0:T(8,128)(2,1)}, bf16[1,2,3,1024,128]{4,3,2,1,0:T(8,128)(2,1)}, u32[]{:S(2)}, u32[]{:S(2)}) collective-permute-start(bf16[1,2,3,1024,128]{4,3,2,1,0:T(8,128)(2,1)} %get-tuple-element.128), channel_id=1, source_target_pairs={{0,16},{4,20},{8,24},{12,28},{16,0},{20,4},{24,8},{28,12},{1,17},{... | collective-permute-start | bytes 4718600 | tf_op jit(solution)/shard_map/ppermute | solution.py:1026
  436.7 31.0 %collective-permute-start.29 = (bf16[256,1024]{1,0:T(8,128)(2,1)S(1)}, bf16[256,1024]{1,0:T(8,128)(2,1)S(1)}, u32[]{:S(2)}, u32[]{:S(2)}) collective-permute-start(bf16[256,1024]{1,0:T(8,128)(2,1)S(1)} %add_convert_fusion.3), channel_id=1, source_target_pairs={{0,1},{1,2},{2,3},{3,0},{4,5},{5,6},{6,7},{7,4},{8,9},{9,10},{10,1... | collective-permute-start | bytes 1572872 | tf_op jit(solution)/shard_map/ppermute | solution.py:1126
  (38 other events, 440.7 us)
Sparse Core Ops, SparseCore 0:
  9.9 31.1 all-gather.4
  44.5 65.7 all-gather.6
  338.5 47.5 reduce-scatter.5
  398.8 21.5 reduce-scatter.7
  424.0 39.3 reduce-scatter.3

commit v2 on v1

--- a/solution.py
+++ b/solution.py
@@ -598,8 +598,8 @@
     for row in range(8):
         span = pl.ds(row * LANES, LANES)
         for col in range(4):
-            wo_ref[span, col * 256 : (col + 1) * 256] = pack_ref[4 * row + col, :LANES, :]
-            wr_wide[col * 8 : (col + 1) * 8, span] = pack_ref[4 * row + col, LANES:, :LANES].astype(F32)
+            wo_ref[span, col * 256 : (col + 1) * 256] = pack_ref[row, col, :LANES, :]
+            wr_wide[col * 8 : (col + 1) * 8, span] = pack_ref[row, col, LANES:, :LANES].astype(F32)
     wr_ref[...] = wr_wide[...].astype(BF16)
     resid = x_ref[...].astype(F32)
     for part in range(4):
@@ -634,7 +634,7 @@
     return (first == (second ^ (row * 4))).astype(BF16)
 
 
-def route(spots, mixed, x, pack, gain, ids, order):
+def route(spots, mixed, x, pack, gain, ids, order, after=()):
     rows = x.shape[0]
     shapes = (
         jax.ShapeDtypeStruct((rows, D), F32),
@@ -645,14 +645,14 @@
         jax.ShapeDtypeStruct((LANES, D), BF16),
     )
     return pl.pallas_call(
-        route_kernel,
+        behind(route_kernel, 7, after),
         out_shape=shapes,
-        in_specs=[in_smem()] + [in_vmem()] * 6,
+        in_specs=[in_smem()] + [in_vmem()] * 6 + [in_hbm()] * len(after),
         out_specs=tuple(in_vmem() for _ in shapes),
         scratch_shapes=[pltpu.VMEM((LANES, D), F32)],
         compiler_params=pltpu.CompilerParams(vmem_limit_bytes=VMEM_MOST),
         cost_estimate=cost(2),
-    )(spots, mixed, x, pack, gain, ids, order)
+    )(spots, mixed, x, pack, gain, ids, order, *after)
 
 
 def expert_kernel(x_ref, g_ref, *refs):
@@ -990,6 +990,24 @@
     )(mixed, branch, small, *after)
 
 
+def unpack_kernel(sum_ref, query_ref, key_ref, value_ref, gain_ref):
+    query_ref[...] = sum_ref[:LANES, :256].astype(F32)
+    key_ref[...] = sum_ref[:LANES, 256:384].astype(F32)
+    value_ref[...] = sum_ref[:LANES, 384:].astype(F32)
+    gain_ref[...] = sum_ref[LANES:, :LANES].astype(F32)
+
+
+def unpack(sums, after):
+    return pl.pallas_call(
+        behind(unpack_kernel, 1, after),
+        out_shape=tuple(jax.ShapeDtypeStruct(shape, F32) for shape in ((LANES, 256), (LANES, LANES), (LANES, LANES), (8, LANES))),
+        in_specs=[in_vmem()] + [in_hbm()] * len(after),
+        out_specs=(in_vmem(),) * 4,
+        compiler_params=pltpu.CompilerParams(vmem_limit_bytes=VMEM_MOST),
+        cost_estimate=cost(2),
+    )(sums, *after)
+
+
 def ring_gather(value, n_col):
     steps = [(i, (i + 1) % n_col) for i in range(n_col)]
     chunks = [value]
@@ -1053,28 +1071,32 @@
     pack_qkv = jnp.concatenate(
         [jnp.concatenate([w_query, w_key, w_value], axis=1), gains, jnp.zeros((7, 512), BF16)], axis=0
     )
+    pack_out = jnp.concatenate([w_out, jnp.pad(w_router.T, ((0, 0), (0, 256 - LANES)))], axis=0)
+    pack_out = lax.all_gather(pack_out, "col", axis=0)
     pack_qkv = lax.all_gather(pack_qkv, "row", axis=0)
-    x_chunks = ring_gather(block_in, n_col)
-    own = jnp.stack([w_gate, w_up, w_down], axis=1)
-    from_x, from_y, other = swap(own, ACROSS_X), swap(own, ACROSS_Y), swap(own, CORE)
-    pack_out = jnp.concatenate([w_out, jnp.pad(w_router.T, ((0, 0), (0, 256 - LANES)))], axis=0)
-    pack_out = lax.all_gather(pack_out, ("row", "col"), axis=0)
+    pack_out = lax.all_gather(pack_out, "row", axis=0)
     cosine, sine = rope_tables(0, seq)
     cosine = jnp.tile(cosine, (1, 4))
     sine = jnp.concatenate([-sine, sine, -sine, sine], axis=1)
+    ring = [(i, (i + 1) % n_col) for i in range(n_col)]
+    x_chunks = [block_in, lax.ppermute(block_in, "col", ring)]
+    x_chunks += ring_gather(hold(x_chunks[1], cosine, sine), n_col)[1:3]
+    own = jnp.stack([w_gate, w_up, w_down], axis=1)
+    from_x, from_y, other = swap(own, ACROSS_X), swap(own, ACROSS_Y), swap(own, CORE)
 
     attn_in, q, k, v, lse, w_qkv, gains, mixed_all = attend(spots, x_chunks, pack_qkv, cosine, sine, [other])
-    g_chunks = ring_gather(hold(out_grad, x_chunks[3]), n_col)
+    g_chunks = [out_grad, lax.ppermute(hold(out_grad, x_chunks[3]), "col", ring)]
+    g_chunks += ring_gather(hold(g_chunks[1], attn_in), n_col)[1:3]
     mixed_own = lax.all_to_all(mixed_all, "col", split_axis=0, concat_axis=0, tiled=True)
+    low, high = halves(from_x, from_y, [g_chunks[2]])
     resid, send, gates, kept, wo, wr = route(
-        spots, mixed_own, block_in, pack_out, gains, expert_ids, fill_order
-    )
-    low, high = halves(from_x, from_y, [mixed_own])
+        spots, mixed_own, block_in, pack_out, gains, expert_ids, fill_order, [low]
+    )
     far = swap(low, ACROSS_X), swap(high, ACROSS_Y)
     weights = [own, other, from_x, swap(from_x, CORE), from_y, swap(from_y, CORE), *far]
 
     send_chunks = [send, *ring_gather(hold(send, g_chunks[3]), n_col)[1:]]
-    weights += [swap(hold(part, send_chunks[3]), CORE) for part in far]
+    weights += [swap(hold(part, send_chunks[2]), CORE) for part in far]
     results, backs, back = {}, [], None
     steps = [(i, (i + 1) % n_col) for i in range(n_col)]
     order = (1, 2, 3, 0)
@@ -1082,6 +1104,9 @@
         after = [results[order[at - 1]][1]] if at else [send_chunks[3]]
         if at >= 2:
             after.append(backs[at - 2])
+        if at == 2:
+            flipped = flip(send_chunks, g_chunks, [results[2][1]])
+            after.append(flipped[0])
         results[chunk] = experts(send_chunks[chunk], g_chunks[chunk], weights, after)
         if chunk:
             part = results[chunk][0]
@@ -1090,7 +1115,6 @@
             backs.append(back)
     results = [results[chunk] for chunk in range(n_col)]
 
-    flipped = flip(send_chunks, g_chunks, [results[2][1]])
     hidden = [[result[kind] for result in results] for kind in (1, 2, 3)]
     wgrads = functools.partial(expert_wgrads, flipped, hidden)
     (p7,) = wgrads((14, 15), ((0, 0), (0, 1)), after=[backs[2]])
@@ -1126,7 +1150,8 @@
     moving = lax.ppermute(moving, "col", steps)
     moving = (moving.astype(F32) + back_parts[3].astype(F32)).astype(BF16)
     third_step = moving
-    attn_grad = lax.ppermute(moving, "col", steps).astype(F32) + back_parts[0].astype(F32)
+    last_step = lax.ppermute(moving, "col", steps)
+    attn_grad = last_step.astype(F32) + back_parts[0].astype(F32)
     x_rows = block_in.astype(F32)
     scale = lax.rsqrt(jnp.mean(x_rows * x_rows, axis=1, keepdims=True) + EPS)
     normed = x_rows * scale
@@ -1134,18 +1159,16 @@
     block_in_grad = resid_grad + scale * (inner - normed * jnp.mean(inner * normed, axis=1, keepdims=True))
     gate_sum, up_sum, down_sum = expert_total([third_step], q0, x2a, x2b, y4a, y4b)
 
-    qkv_sum = lax.psum_scatter(qkv_wgrad, "row", scatter_dimension=0, tiled=True)[0].astype(F32)
+    qkv_sum = lax.psum_scatter(qkv_wgrad, "row", scatter_dimension=0, tiled=True)[0]
+    *qkv_sums, gain_one = unpack(qkv_sum, [last_step])
     out_sum = lax.psum_scatter(hold(out_sum, q2b), "col", scatter_dimension=2, tiled=True)[0].astype(F32)
-    gain_one = qkv_sum[LANES:, :LANES]
     gain_one_sum = functools.reduce(jnp.add, shift_all([gain_one] * n_col, n_col))[0]
     return (
         block_out,
         block_in_grad,
         gain_one_sum,
         out_sum[LANES, LANES:],
-        qkv_sum[:LANES, :256],
-        qkv_sum[:LANES, 256:384],
-        qkv_sum[:LANES, 384:],
+        *qkv_sums,
         out_sum[:LANES],
         out_sum[LANES:, :LANES].T,
         gate_sum,

time: 502 us -> 489 us (0.974)
  waiting for transfers between devices: 174 us -> 167 us
    reduce_scatter x1, waiting for transfers between devices: 25.5 us -> 0.01 us  [fast(): lax.psum_scatter(qkv_wgrad, 'row', scatter_dimension=0, tiled=True)[0]]
    ppermute x18, waiting for transfers between devices: 27.5 us -> 49.6 us  [swap(): return lax.ppermute(value, 'row', [(i, i ^ mask) for i in range(8)])]
    all_to_all x1 -> x0, blocking collectives: 19.6 us -> none  [fast(): lax.all_to_all(mixed_grad, 'col', split_axis=0, concat_axis=0, tiled=True)]
    all_to_all x1, waiting for transfers between devices: 19.8 us -> 1.07 us  [fast(): lax.all_to_all(mixed_all, 'col', split_axis=0, concat_axis=0, tiled=True)]
    all_gather x0 -> x1, blocking collectives: none -> 16.1 us  [fast(): pack_out = lax.all_gather(pack_out, 'col', axis=0)]
    ppermute x1, waiting for transfers between devices: 0.01 us -> 13 us  [fast(): moving = lax.ppermute(moving, 'col', steps)]
    all_to_all x0 -> x1, waiting for transfers between devices: none -> 10.8 us  [fast(): lax.all_to_all(mixed_grad, 'col', split_axis=0, concat_axis=0, tiled=True)]
    ppermute x9 -> x7, waiting for transfers between devices: 81.5 us -> 73.4 us  [ring_gather(): chunks.append(lax.ppermute(chunks[-1], 'col', steps))]
  transfers between devices with their start and end apart: 42 -> 43, of which waited for: 20 -> 22; matrix products, arithmetic and copies ran while one was open for 5% -> 5% of each run, Pallas kernels for 34% -> 35%
where the time goes in v2:
time: 489 us; the launch traced here: 479 us
  Pallas kernels  211 us (43%)
  waiting for transfers between devices  167 us (34%)
  starting transfers between devices  31.4 us (6%)
  other arithmetic  21.3 us (4%)
  local copies, waits for them, and re-layouts  17.3 us (4%)
  blocking collectives  16.1 us (3%)
  between operations  15.4 us (3%)
    pallas_call x4, Pallas kernels, experts(): pl.pallas_call(behind(expert_kernel, 12, after), out_shape=(jax.ShapeDtyp...  86.9 us
    ppermute x7, waiting for transfers between devices, ring_gather(): chunks.append(lax.ppermute(chunks[-1], 'col', steps))  73.4 us
    pallas_call x6, Pallas kernels, expert_wgrads(): pl.pallas_call(behind(kernel, 14 + len(extras), after), grid=(count,), ou...  62.6 us
    ppermute x18, waiting for transfers between devices, swap(): return lax.ppermute(value, 'row', [(i, i ^ mask) for i in range(8)])  49.6 us
    pallas_call x1, Pallas kernels, attend_back(): pl.pallas_call(behind(attend_back_kernel, 12, after), out_shape=shapes, i...  17 us
    all_gather x1, blocking collectives, fast(): pack_out = lax.all_gather(pack_out, 'col', axis=0)  16.1 us
    ppermute x18, starting transfers between devices, swap(): return lax.ppermute(value, 'row', [(i, i ^ mask) for i in range(8)])  14.7 us
    ppermute x1, waiting for transfers between devices, fast(): moving = lax.ppermute(moving, 'col', steps)  13 us
  transfers between devices with their start and end apart: 43, of which 22 were waited for; matrix products, arithmetic and copies ran while one was open for 5% of the time, Pallas kernels for 35%

profile of v2, /device:TPU:0, one launch (start us, length us, event | category | flops | bytes accessed | tf_op | source)
XLA Modules:
  0.0 479.4 jit_solution(15887320258690828026)
XLA Ops:
  12.5 16.1 %all-gather.1 = bf16[544,256]{1,0:T(8,128)(2,1)} all-gather(bf16[136,256]{1,0:T(8,128)(2,1)S(1)} %fusion.9), channel_id=3, replica_groups=mesh['row'=8,'col'=4] {'col'}, dimensions={0}, use_global_device_ids=true | all-gather | bytes 348160 | tf_op jit(solution)/shard_map/all_gather | solution.py:1075
  46.1 12.3 %collective-permute-done.1.refs_3_ = bf16[256,1024]{1,0:T(8,128)(2,1)S(1)} collective-permute-done((bf16[256,1024]{1,0:T(8,128)(2,1)}, bf16[256,1024]{1,0:T(8,128)(2,1)S(1)}, u32[]{:S(2)}, u32[]{:S(2)}) %collective-permute-start.1) | collective-permute-done | bytes 524320 | tf_op jit(solution)/shard_map/ppermute | solution.py:1015
  59.2 11.2 %collective-permute-done.2.refs_4_ = bf16[256,1024]{1,0:T(8,128)(2,1)S(1)} collective-permute-done((bf16[256,1024]{1,0:T(8,128)(2,1)S(1)}, bf16[256,1024]{1,0:T(8,128)(2,1)S(1)}, u32[]{:S(2)}, u32[]{:S(2)}) %collective-permute-start.2) | collective-permute-done | bytes 524320 | tf_op jit(solution)/shard_map/ppermute | solution.py:1015
  74.5 12.1 %shard_map.238 = (bf16[1024,1024]{1,0:T(8,128)(2,1)}, bf16[4,1024,64]{2,1,0:T(8,128)(2,1)}, bf16[2,1024,64]{2,1,0:T(8,128)(2,1)}, bf16[2,1024,64]{2,1,0:T(8,128)...) custom-call(s32[3]{0:T(128)} %pad_add_fusion.refs_0_, ...), custom_call_target="tpu_custom_call" | custom-call | flops 10000000 | bytes 100000 | tf_op jit(solution)/shard_map/pallas_call | solution.py:498
  86.7 5.7 %all-to-all-start = ((bf16[4,256,256]{2,1,0:T(8,128)(2,1)}), bf16[4,256,256]{2,1,0:T(8,128)(2,1)}, u32[]{:S(2)}, u32[]{:S(2)}) async-start(bf16[4,256,256]{2,1,0:T(8,128)(2,1)} %bitcast.32), calls=%async_computation | async-start | bytes 1048576 | tf_op jit(solution)/shard_map/all_to_all | solution.py:1090
  92.4 11.3 %collective-permute-done.7.refs_2_.refs_1_.refs_6_ = bf16[256,1024]{1,0:T(8,128)(2,1)} collective-permute-done((bf16[256,1024]{1,0:T(8,128)(2,1)}, bf16[256,1024]{1,0:T(8,128)(2,1)}, u32[]{:S(2)}, u32[]{:S(2)}) %collective-permute-start.7) | collective-permute-done | bytes 524320 | tf_op jit(solution)/shard_map/ppermute | solution.py:1015
  110.1 5.2 %shard_map.239 = (bf16[2,3,1024,128]{3,2,1,0:T(8,128)(2,1)}, bf16[2,3,1024,128]{3,2,1,0:T(8,128)(2,1)}) custom-call(bf16[4,3,1024,128]{3,2,1,0:T(8,128)(2,1)} %collective-permute-done.4.refs_0_.refs_4_, bf16[4,3,1024,128]{3,2,1,0:T(8,128)(2,1)} %collective-permute-done.5.refs_1_.refs_6_, bf16[256,1024]{1,0:T(8,128)(2,1)} %collective-permute-done.7.refs_2_.refs_1_.refs_6_), custom_call_target="tpu_custom_call" | custom-call | flops 3000000 | bytes 100000 | tf_op jit(solution)/shard_map/pallas_call | solution.py:911
  119.8 5.0 %shard_map.240 = (f32[256,1024]{1,0:T(8,128)}, bf16[256,1152]{1,0:T(8,128)(2,1)}, f32[256,128]{1,0:T(8,128)}, f32[256,128]{1,0:T(8,128)}, bf16[1024,1024]{1,0:T(8,128)(2,1)}, /*index=5*/bf16[128,1024]{1,0:T(8,128)(2,1)}) custom-call(s32[3]{0:T(128)} %pad_add_fusion.refs_0_, bf16[1024,256]{1,0:T(8,128)(2,1)} %bitcast.8.refs_1_.refs_0_, ...), custom_call_target="tpu_custom_call" | custom-call | flops 2000000 | bytes 100000 | tf_op jit(solution)/shard_map/pallas_call | solution.py:647
  125.1 15.9 %collective-permute-done.9.refs_0_.refs_1_ = bf16[256,1152]{1,0:T(8,128)(2,1)S(1)} collective-permute-done((bf16[256,1152]{1,0:T(8,128)(2,1)}, bf16[256,1152]{1,0:T(8,128)(2,1)S(1)}, u32[]{:S(2)}, u32[]{:S(2)}) %collective-permute-start.9) | collective-permute-done | bytes 589856 | tf_op jit(solution)/shard_map/ppermute | solution.py:1015
  141.0 9.5 %collective-permute-done.13.refs_9_ = bf16[2,3,1024,128]{3,2,1,0:T(8,128)(2,1)} collective-permute-done((bf16[2,3,1024,128]{3,2,1,0:T(8,128)(2,1)}, bf16[2,3,1024,128]{3,2,1,0:T(8,128)(2,1)}, u32[]{:S(2)}, u32[]{:S(2)}) %collective-permute-start.13) | collective-permute-done | bytes 1572896 | tf_op jit(solution)/shard_map/ppermute | solution.py:1044
  150.5 5.5 %collective-permute-done.14.refs_0_.refs_2_ = bf16[256,1152]{1,0:T(8,128)(2,1)S(1)} collective-permute-done((bf16[256,1152]{1,0:T(8,128)(2,1)S(1)}, bf16[256,1152]{1,0:T(8,128)(2,1)S(1)}, u32[]{:S(2)}, u32[]{:S(2)}) %collective-permute-start.14) | collective-permute-done | bytes 589856 | tf_op jit(solution)/shard_map/ppermute | solution.py:1015
  156.6 17.1 %collective-permute-done.17.refs_12_.refs_3_.refs_0_ = bf16[256,1152]{1,0:T(8,128)(2,1)S(1)} collective-permute-done((bf16[256,1152]{1,0:T(8,128)(2,1)S(1)}, bf16[256,1152]{1,0:T(8,128)(2,1)S(1)}, u32[]{:S(2)}, u32[]{:S(2)}) %collective-permute-start.17) | collective-permute-done | bytes 589856 | tf_op jit(solution)/shard_map/ppermute | solution.py:1015
  176.2 21.6 %shard_map.241 = (bf16[256,2176]{1,0:T(8,128)(2,1)}, bf16[256,4096]{1,0:T(8,128)(2,1)}, bf16[256,4096]{1,0:T(8,128)(2,1)}, bf16[256,4096]{1,0:T(8,128)(2,1)}) custom-call(bf16[256,1152]{1,0:T(8,128)(2,1)} %copy-done.12, bf16[256,1024]{1,0:T(8,128)(2,1)} %collective-permute-done.6.refs_1_.refs_5_, bf16[4,3,1024,128]{3,2,1,0:T(8,128)(2,1)} %copy-done, ...), custom_call_target="tpu_custom_call" | custom-call | flops 21000000 | bytes 100000 | tf_op jit(solution)/shard_map/pallas_call | solution.py:724
  197.8 21.7 %shard_map.242 = (bf16[256,2176]{1,0:T(8,128)(2,1)}, bf16[256,4096]{1,0:T(8,128)(2,1)}, bf16[256,4096]{1,0:T(8,128)(2,1)}, bf16[256,4096]{1,0:T(8,128)(2,1)}) custom-call(bf16[256,1152]{1,0:T(8,128)(2,1)} %copy-done.11, bf16[256,1024]{1,0:T(8,128)(2,1)} %collective-permute-done.7.refs_2_.refs_1_.refs_6_, bf16[4,3,1024,128]{3,2,1,0:T(8,128)(2,1)} %copy-done, ...), custom_call_target="tpu_custom_call" | custom-call | flops 21000000 | bytes 100000 | tf_op jit(solution)/shard_map/pallas_call | solution.py:724
  219.6 6.0 %collective-permute-done.18.refs_13_ = bf16[256,2176]{1,0:T(8,128)(2,1)S(1)} collective-permute-done((bf16[256,2176]{1,0:T(8,128)(2,1)}, bf16[256,2176]{1,0:T(8,128)(2,1)S(1)}, u32[]{:S(2)}, u32[]{:S(2)}) %collective-permute-start.18) | collective-permute-done | bytes 1114144 | tf_op jit(solution)/shard_map/ppermute | solution.py:1114
  227.5 5.3 %shard_map.243 = (bf16[1024,1024]{1,0:T(8,128)(2,1)}, bf16[1024,1024]{1,0:T(8,128)(2,1)}) custom-call(bf16[256,1152]{1,0:T(8,128)(2,1)} %get-tuple-element.86.refs_0_.refs_10_, bf16[256,1152]{1,0:T(8,128)(2,1)} %copy-done.12, bf16[256,1152]{1,0:T(8,128)(2,1)} %copy-done.11, bf16[256,1152]{1,0:T(8,128)(2,1)} %copy-done.4, bf16[256,1024]{1,0:T(8,128)(2,1)} %refs_7_.1, ...), custom_call_target="tpu_custom_call" | custom-call | flops 2000000 | bytes 100000 | tf_op jit(solution)/shard_map/pallas_call | solution.py:755
  232.8 21.7 %shard_map.244 = (bf16[256,2176]{1,0:T(8,128)(2,1)}, bf16[256,4096]{1,0:T(8,128)(2,1)}, bf16[256,4096]{1,0:T(8,128)(2,1)}, bf16[256,4096]{1,0:T(8,128)(2,1)}) custom-call(bf16[256,1152]{1,0:T(8,128)(2,1)} %copy-done.4, bf16[256,1024]{1,0:T(8,128)(2,1)} %collective-permute-done.8.refs_7_.refs_1_, bf16[4,3,1024,128]{3,2,1,0:T(8,128)(2,1)} %copy-done, ...), custom_call_target="tpu_custom_call" | custom-call | flops 21000000 | bytes 100000 | tf_op jit(solution)/shard_map/pallas_call | solution.py:724
  256.7 21.7 %shard_map.245 = (bf16[256,2176]{1,0:T(8,128)(2,1)}, bf16[256,4096]{1,0:T(8,128)(2,1)}, bf16[256,4096]{1,0:T(8,128)(2,1)}, bf16[256,4096]{1,0:T(8,128)(2,1)}) custom-call(bf16[256,1152]{1,0:T(8,128)(2,1)} %get-tuple-element.86.refs_0_.refs_10_, bf16[256,1024]{1,0:T(8,128)(2,1)} %refs_7_.1, bf16[4,3,1024,128]{3,2,1,0:T(8,128)(2,1)} %copy-done, ...), custom_call_target="tpu_custom_call" | custom-call | flops 21000000 | bytes 100000 | tf_op jit(solution)/shard_map/pallas_call | solution.py:724
  278.5 4.8 %collective-permute-done.20.refs_14_.refs_1_ = bf16[256,2176]{1,0:T(8,128)(2,1)S(1)} collective-permute-done((bf16[256,2176]{1,0:T(8,128)(2,1)S(1)}, bf16[256,2176]{1,0:T(8,128)(2,1)S(1)}, u32[]{:S(2)}, u32[]{:S(2)}) %collective-permute-start.20) | collective-permute-done | bytes 1114144 | tf_op jit(solution)/shard_map/ppermute | solution.py:1114
  284.3 7.9 %shard_map.246.refs_11_ = bf16[2,2,3,1024,128]{4,3,2,1,0:T(8,128)(2,1)} custom-call(bf16[1024,1024]{1,0:T(8,128)(2,1)} %get-tuple-element.94.refs_14_.refs_0_, bf16[1024,1024]{1,0:T(8,128)(2,1)} %get-tuple-element.103.refs_1_, bf16[256,4096]{1,0:T(8,128)(2,1)} %get-tuple-element.104.refs_2_, bf16[256,4096]{1,0:T(8,128)(2,1)} %get-tuple-element.91.refs_12_.refs_3_, ...), custom_call_target="tpu_custom_call" | custom-call | flops 4400000 | bytes 100000 | tf_op jit(solution)/shard_map/pallas_call | solution.py:861
  292.3 6.0 %shard_map.247 = (f32[256,1024]{1,0:T(8,128)}, f32[256,1024]{1,0:T(8,128)}, bf16[256,1024]{1,0:T(8,128)(2,1)}, bf16[1024,256]{1,0:T(8,128)(2,1)}, f32[136,1024]{1,0:T(8,128)}) custom-call(s32[3]{0:T(128)} %pad_add_fusion.refs_0_, bf16[256,2176]{1,0:T(8,128)(2,1)} %copy-done.7, bf16[256,2176]{1,0:T(8,128)(2,1)} %get-tuple-element.97.refs_2_, ...), custom_call_target="tpu_custom_call" | custom-call | flops 2000000 | bytes 100000 | tf_op jit(solution)/shard_map/pallas_call | solution.py:959
  300.0 11.9 %shard_map.248.refs_15_ = bf16[4,2,3,1024,128]{4,3,2,1,0:T(8,128)(2,1)} custom-call(bf16[1024,1024]{1,0:T(8,128)(2,1)} %get-tuple-element.94.refs_14_.refs_0_, bf16[1024,1024]{1,0:T(8,128)(2,1)} %get-tuple-element.103.refs_1_, bf16[256,4096]{1,0:T(8,128)(2,1)} %get-tuple-element.104.refs_2_, bf16[256,4096]{1,0:T(8,128)(2,1)} %get-tuple-element.91.refs_12_.refs_3_, ...), custom_call_target="tpu_custom_call" | custom-call | flops 8800000 | bytes 100000 | tf_op jit(solution)/shard_map/pallas_call | solution.py:861
  312.4 9.4 %shard_map.249 = (bf16[1,2,3,1024,128]{4,3,2,1,0:T(8,128)(2,1)}, bf16[1,2,3,1024,128]{4,3,2,1,0:T(8,128)(2,1)}) custom-call(bf16[1024,1024]{1,0:T(8,128)(2,1)} %get-tuple-element.94.refs_14_.refs_0_, bf16[1024,1024]{1,0:T(8,128)(2,1)} %get-tuple-element.103.refs_1_, bf16[256,4096]{1,0:T(8,128)(2,1)} %get-tuple-element.104.refs_2_, ...), custom_call_target="tpu_custom_call" | custom-call | flops 4400000 | bytes 100000 | tf_op jit(solution)/shard_map/pallas_call | solution.py:861
  331.6 10.8 %all-to-all-done.1 = bf16[4,256,256]{2,1,0:T(8,128)(2,1)S(1)} async-done(((bf16[4,256,256]{2,1,0:T(8,128)(2,1)}), bf16[4,256,256]{2,1,0:T(8,128)(2,1)S(1)}, u32[]{:S(2)}, u32[]{:S(2)}) %all-to-all-start.1) | async-done | bytes 524320 | tf_op jit(solution)/shard_map/all_to_all | solution.py:1125
  343.2 9.6 %shard_map.251 = (bf16[1,2,3,1024,128]{4,3,2,1,0:T(8,128)(2,1)}, bf16[1,2,3,1024,128]{4,3,2,1,0:T(8,128)(2,1)}) custom-call(bf16[1024,1024]{1,0:T(8,128)(2,1)} %get-tuple-element.94.refs_14_.refs_0_, bf16[1024,1024]{1,0:T(8,128)(2,1)} %get-tuple-element.103.refs_1_, bf16[256,4096]{1,0:T(8,128)(2,1)} %get-tuple-element.104.refs_2_, ...), custom_call_target="tpu_custom_call" | custom-call | flops 4400000 | bytes 100000 | tf_op jit(solution)/shard_map/pallas_call | solution.py:861
  352.8 8.8 %collective-permute-done.23.refs_15_ = bf16[1,2,3,1024,128]{4,3,2,1,0:T(8,128)(2,1)S(1)} collective-permute-done((bf16[1,2,3,1024,128]{4,3,2,1,0:T(8,128)(2,1)}, bf16[1,2,3,1024,128]{4,3,2,1,0:T(8,128)(2,1)S(1)}, u32[]{:S(2)}, u32[]{:S(2)}) %collective-permute-start.23) | collective-permute-done | bytes 1572896 | tf_op jit(solution)/shard_map/ppermute | solution.py:1044
  364.0 14.3 %shard_map.252 = (bf16[1,2,3,1024,128]{4,3,2,1,0:T(8,128)(2,1)}, bf16[1,2,3,1024,128]{4,3,2,1,0:T(8,128)(2,1)}, bf16[2,2,3,1024,128]{4,3,2,1,0:T(8,128)(2,1)}) custom-call(bf16[1024,1024]{1,0:T(8,128)(2,1)} %get-tuple-element.94.refs_14_.refs_0_, bf16[1024,1024]{1,0:T(8,128)(2,1)} %get-tuple-element.103.refs_1_, ...), custom_call_target="tpu_custom_call" | custom-call | flops 8800000 | bytes 100000 | tf_op jit(solution)/shard_map/pallas_call | solution.py:861
  382.5 17.0 %shard_map.253 = (bf16[8,136,512]{2,1,0:T(8,128)(2,1)}, bf16[256,1024]{1,0:T(8,128)(2,1)}, bf16[256,1024]{1,0:T(8,128)(2,1)}, bf16[256,1024]{1,0:T(8,128)(2,1)}, bf16[256,1024]{1,0:T(8,128)(2,1)}) custom-call(s32[3]{0:T(128)} %pad_add_fusion.refs_0_, bf16[1024,256]{1,0:T(8,128)(2,1)} %bitcast.30, bf16[1024,256]{1,0:T(8,128)(2,1)} %get-tuple-element.79.refs_2_, ...), custom_call_target="tpu_custom_call" | custom-call | flops 16000000 | bytes 100000 | tf_op jit(solution)/shard_map/pallas_call | solution.py:575
  402.1 9.5 %shard_map.254.refs_0_ = bf16[2,2,3,1024,128]{4,3,2,1,0:T(8,128)(2,1)} custom-call(bf16[1024,1024]{1,0:T(8,128)(2,1)} %get-tuple-element.94.refs_14_.refs_0_, bf16[1024,1024]{1,0:T(8,128)(2,1)} %get-tuple-element.103.refs_1_, bf16[256,4096]{1,0:T(8,128)(2,1)} %get-tuple-element.104.refs_2_, bf16[256,4096]{1,0:T(8,128)(2,1)} %get-tuple-element.91.refs_12_.refs_3_, ...), custom_call_target="tpu_custom_call" | custom-call | flops 4400000 | bytes 100000 | tf_op jit(solution)/shard_map/pallas_call | solution.py:861
  420.9 13.0 %collective-permute-done.29 = bf16[256,1024]{1,0:T(8,128)(2,1)S(1)} collective-permute-done((bf16[256,1024]{1,0:T(8,128)(2,1)S(1)}, bf16[256,1024]{1,0:T(8,128)(2,1)S(1)}, u32[]{:S(2)}, u32[]{:S(2)}) %collective-permute-start.29) | collective-permute-done | bytes 524320 | tf_op jit(solution)/shard_map/ppermute | solution.py:1150
  436.1 18.3 %collective-permute-done.34.refs_2_ = bf16[1,2,3,1024,128]{4,3,2,1,0:T(8,128)(2,1)} collective-permute-done((bf16[1,2,3,1024,128]{4,3,2,1,0:T(8,128)(2,1)}, bf16[1,2,3,1024,128]{4,3,2,1,0:T(8,128)(2,1)}, u32[]{:S(2)}, u32[]{:S(2)}) %collective-permute-start.34) | collective-permute-done | bytes 1572896 | tf_op jit(solution)/shard_map/ppermute | solution.py:1044
  455.9 5.9 %shard_map.256 = (f32[2,2,1024,128]{3,2,1,0:T(8,128)}, f32[2,2,1024,128]{3,2,1,0:T(8,128)}, f32[2,2,1024,128]{3,2,1,0:T(8,128)}) custom-call(bf16[2,2,3,1024,128]{4,3,2,1,0:T(8,128)(2,1)} %shard_map.254.refs_0_, bf16[1,2,3,1024,128]{4,3,2,1,0:T(8,128)(2,1)} %collective-permute-done.27.refs_1_, bf16[1,2,3,1024,128]{4,3,2,1,0:T(8,128)(2,1)} %collective-permute-done.34.refs_2_, ...), custom_call_target="tpu_custom_call" | custom-call | flops 5000000 | bytes 100000 | tf_op jit(solution)/shard_map/pallas_call | solution.py:890
  (164 shorter events, 91.7 us)
Async XLA Ops:
  7.2 67.3 %all-gather.6.cloned.1.call-start = ((), (), s32[]{:S(2)}) async-start(), calls=%async_computation.8 | async-start | bytes 1253376 | tf_op jit(solution)/shard_map/all_gather | solution.py:1076
  9.7 109.1 %all-gather.8.cloned.1.call-start = ((), (), s32[]{:S(2)}) async-start(), calls=%async_computation.9 | async-start | bytes 2506752 | tf_op jit(solution)/shard_map/all_gather | solution.py:1077
  12.0 62.5 %collective-permute-start.3 = (bf16[4,3,1024,128]{3,2,1,0:T(8,128)(2,1)S(1)}, bf16[4,3,1024,128]{3,2,1,0:T(8,128)(2,1)}, u32[]{:S(2)}, u32[]{:S(2)}) collective-permute-start(bf16[4,3,1024,128]{3,2,1,0:T(8,128)(2,1)S(1)} %pad_maximum_fusion.refs_2_), channel_id=1, source_target_pairs={{0,4},{4,0},{8,12},{12,8},{16,20},{20,16},{24,28},{28,24},{1,5},{5... | collective-permute-start | bytes 9437192 | tf_op jit(solution)/shard_map/ppermute | solution.py:1044
  28.6 80.3 %collective-permute-start.4 = (bf16[4,3,1024,128]{3,2,1,0:T(8,128)(2,1)S(1)}, bf16[4,3,1024,128]{3,2,1,0:T(8,128)(2,1)}, u32[]{:S(2)}, u32[]{:S(2)}) collective-permute-start(bf16[4,3,1024,128]{3,2,1,0:T(8,128)(2,1)S(1)} %pad_maximum_fusion.refs_2_), channel_id=1, source_target_pairs={{0,8},{4,12},{8,0},{12,4},{16,24},{20,28},{24,16},{28,20},{1,9},{5... | collective-permute-start | bytes 9437192 | tf_op jit(solution)/shard_map/ppermute | solution.py:1044
  30.2 79.9 %collective-permute-start.5 = (bf16[4,3,1024,128]{3,2,1,0:T(8,128)(2,1)S(1)}, bf16[4,3,1024,128]{3,2,1,0:T(8,128)(2,1)}, u32[]{:S(2)}, u32[]{:S(2)}) collective-permute-start(bf16[4,3,1024,128]{3,2,1,0:T(8,128)(2,1)S(1)} %pad_maximum_fusion.refs_2_), channel_id=1, source_target_pairs={{0,16},{4,20},{8,24},{12,28},{16,0},{20,4},{24,8},{28,12},{1,17},{... | collective-permute-start | bytes 9437192 | tf_op jit(solution)/shard_map/ppermute | solution.py:1044
  86.7 17.1 %collective-permute-start.7 = (bf16[256,1024]{1,0:T(8,128)(2,1)}, bf16[256,1024]{1,0:T(8,128)(2,1)}, u32[]{:S(2)}, u32[]{:S(2)}) collective-permute-start(bf16[256,1024]{1,0:T(8,128)(2,1)} %collective-permute-done.6.refs_1_.refs_5_), channel_id=1, source_target_pairs={{0,1},{1,2},{2,3},{3,0},{4,5},{5,6},{6,7},{7,4},{8,9},{9,10},{10,1... | collective-permute-start | bytes 1572872 | tf_op jit(solution)/shard_map/ppermute | solution.py:1015
  86.7 33.1 %all-to-all-start = ((bf16[4,256,256]{2,1,0:T(8,128)(2,1)}), bf16[4,256,256]{2,1,0:T(8,128)(2,1)}, u32[]{:S(2)}, u32[]{:S(2)}) async-start(bf16[4,256,256]{2,1,0:T(8,128)(2,1)} %bitcast.32), calls=%async_computation | async-start | bytes 1048576 | tf_op jit(solution)/shard_map/all_to_all | solution.py:1090
  103.7 21.1 %collective-permute-start.8 = (bf16[256,1024]{1,0:T(8,128)(2,1)}, bf16[256,1024]{1,0:T(8,128)(2,1)}, u32[]{:S(2)}, u32[]{:S(2)}) collective-permute-start(bf16[256,1024]{1,0:T(8,128)(2,1)} %collective-permute-done.7.refs_2_.refs_1_.refs_6_), channel_id=1, source_target_pairs={{0,1},{1,2},{2,3},{3,0},{4,5},{5,6},{6,7},{7,4},{8,9},{9,10},{10,1... | collective-permute-start | bytes 1572872 | tf_op jit(solution)/shard_map/ppermute | solution.py:1015
  115.4 35.2 %collective-permute-start.13 = (bf16[2,3,1024,128]{3,2,1,0:T(8,128)(2,1)}, bf16[2,3,1024,128]{3,2,1,0:T(8,128)(2,1)}, u32[]{:S(2)}, u32[]{:S(2)}) collective-permute-start(bf16[2,3,1024,128]{3,2,1,0:T(8,128)(2,1)} %get-tuple-element.87), channel_id=1, source_target_pairs={{0,16},{4,20},{8,24},{12,28},{16,0},{20,4},{24,8},{28,12},{1,17},{... | collective-permute-start | bytes 4718600 | tf_op jit(solution)/shard_map/ppermute | solution.py:1044
  116.9 39.2 %collective-permute-start.12 = (bf16[2,3,1024,128]{3,2,1,0:T(8,128)(2,1)}, bf16[2,3,1024,128]{3,2,1,0:T(8,128)(2,1)}, u32[]{:S(2)}, u32[]{:S(2)}) collective-permute-start(bf16[2,3,1024,128]{3,2,1,0:T(8,128)(2,1)} %get-tuple-element.84.refs_7_), channel_id=1, source_target_pairs={{0,8},{4,12},{8,0},{12,4},{16,24},{20,28},{24,16},{28,20},{1,9},{5... | collective-permute-start | bytes 4718600 | tf_op jit(solution)/shard_map/ppermute | solution.py:1044
  117.4 56.3 %collective-permute-start.10 = (bf16[4,3,1024,128]{3,2,1,0:T(8,128)(2,1)}, bf16[4,3,1024,128]{3,2,1,0:T(8,128)(2,1)S(1)}, u32[]{:S(2)}, u32[]{:S(2)}) collective-permute-start(bf16[4,3,1024,128]{3,2,1,0:T(8,128)(2,1)} %collective-permute-done.4.refs_0_.refs_4_), channel_id=1, source_target_pairs={{0,4},{4,0},{8,12},{12,8},{16,20},{20,16},{24,28},{28,24},{1,5},{5... | collective-permute-start | bytes 9437192 | tf_op jit(solution)/shard_map/ppermute | solution.py:1044
  117.4 57.1 %collective-permute-start.11 = (bf16[4,3,1024,128]{3,2,1,0:T(8,128)(2,1)}, bf16[4,3,1024,128]{3,2,1,0:T(8,128)(2,1)}, u32[]{:S(2)}, u32[]{:S(2)}) collective-permute-start(bf16[4,3,1024,128]{3,2,1,0:T(8,128)(2,1)} %collective-permute-done.5.refs_1_.refs_6_), channel_id=1, source_target_pairs={{0,4},{4,0},{8,12},{12,8},{16,20},{20,16},{24,28},{28,24},{1,5},{5... | collective-permute-start | bytes 9437192 | tf_op jit(solution)/shard_map/ppermute | solution.py:1044
  124.8 16.2 %collective-permute-start.9 = (bf16[256,1152]{1,0:T(8,128)(2,1)}, bf16[256,1152]{1,0:T(8,128)(2,1)S(1)}, u32[]{:S(2)}, u32[]{:S(2)}) collective-permute-start(bf16[256,1152]{1,0:T(8,128)(2,1)} %get-tuple-element.86.refs_0_.refs_10_), channel_id=1, source_target_pairs={{0,1},{1,2},{2,3},{3,0},{4,5},{5,6},{6,7},{7,4},{8,9},{9,10},{10,1... | collective-permute-start | bytes 1769480 | tf_op jit(solution)/shard_map/ppermute | solution.py:1015
  156.1 18.5 %collective-permute-start.16 = (bf16[2,3,1024,128]{3,2,1,0:T(8,128)(2,1)}, bf16[2,3,1024,128]{3,2,1,0:T(8,128)(2,1)}, u32[]{:S(2)}, u32[]{:S(2)}) collective-permute-start(bf16[2,3,1024,128]{3,2,1,0:T(8,128)(2,1)} %collective-permute-done.13.refs_9_), channel_id=1, source_target_pairs={{0,4},{4,0},{8,12},{12,8},{16,20},{20,16},{24,28},{28,24},{1,5},{5... | collective-permute-start | bytes 4718600 | tf_op jit(solution)/shard_map/ppermute | solution.py:1044
  156.1 18.4 %collective-permute-start.15 = (bf16[2,3,1024,128]{3,2,1,0:T(8,128)(2,1)}, bf16[2,3,1024,128]{3,2,1,0:T(8,128)(2,1)}, u32[]{:S(2)}, u32[]{:S(2)}) collective-permute-start(bf16[2,3,1024,128]{3,2,1,0:T(8,128)(2,1)} %collective-permute-done.12.refs_8_), channel_id=1, source_target_pairs={{0,4},{4,0},{8,12},{12,8},{16,20},{20,16},{24,28},{28,24},{1,5},{5... | collective-permute-start | bytes 4718600 | tf_op jit(solution)/shard_map/ppermute | solution.py:1044
  156.6 17.1 %collective-permute-start.17 = (bf16[256,1152]{1,0:T(8,128)(2,1)S(1)}, bf16[256,1152]{1,0:T(8,128)(2,1)S(1)}, u32[]{:S(2)}, u32[]{:S(2)}) collective-permute-start(bf16[256,1152]{1,0:T(8,128)(2,1)S(1)} %collective-permute-done.14.refs_0_.refs_2_), channel_id=1, source_target_pairs={{0,1},{1,2},{2,3},{3,0},{4,5},{5,6},{6,7},{7,4},{8,9},{9,10},{10,1... | collective-permute-start | bytes 1769480 | tf_op jit(solution)/shard_map/ppermute | solution.py:1015
  197.8 27.8 %collective-permute-start.18 = (bf16[256,2176]{1,0:T(8,128)(2,1)}, bf16[256,2176]{1,0:T(8,128)(2,1)S(1)}, u32[]{:S(2)}, u32[]{:S(2)}) collective-permute-start(bf16[256,2176]{1,0:T(8,128)(2,1)} %get-tuple-element.90), channel_id=1, source_target_pairs={{0,1},{1,2},{2,3},{3,0},{4,5},{5,6},{6,7},{7,4},{8,9},{9,10},{10,1... | collective-permute-start | bytes 3342344 | tf_op jit(solution)/shard_map/ppermute | solution.py:1114
  227.5 27.1 %collective-permute-start.19 = (bf16[256,2176]{1,0:T(8,128)(2,1)S(1)}, bf16[256,2176]{1,0:T(8,128)(2,1)S(1)}, u32[]{:S(2)}, u32[]{:S(2)}) collective-permute-start(bf16[256,2176]{1,0:T(8,128)(2,1)S(1)} %add_convert_fusion.1), channel_id=1, source_target_pairs={{0,1},{1,2},{2,3},{3,0},{4,5},{5,6},{6,7},{7,4},{8,9},{9,10},{10,1... | collective-permute-start | bytes 3342344 | tf_op jit(solution)/shard_map/ppermute | solution.py:1114
  256.5 26.8 %collective-permute-start.20 = (bf16[256,2176]{1,0:T(8,128)(2,1)S(1)}, bf16[256,2176]{1,0:T(8,128)(2,1)S(1)}, u32[]{:S(2)}, u32[]{:S(2)}) collective-permute-start(bf16[256,2176]{1,0:T(8,128)(2,1)S(1)} %add_convert_fusion), channel_id=1, source_target_pairs={{0,1},{1,2},{2,3},{3,0},{4,5},{5,6},{6,7},{7,4},{8,9},{9,10},{10,1... | collective-permute-start | bytes 3342344 | tf_op jit(solution)/shard_map/ppermute | solution.py:1114
  311.8 30.5 %collective-permute-start.22 = (bf16[4,2,3,1024,128]{4,3,2,1,0:T(8,128)(2,1)}, bf16[4,2,3,1024,128]{4,3,2,1,0:T(8,128)(2,1)}, u32[]{:S(2)}, u32[]{:S(2)}) collective-permute-start(bf16[4,2,3,1024,128]{4,3,2,1,0:T(8,128)(2,1)} %shard_map.248.refs_15_), channel_id=1, source_target_pairs={{0,4},{4,0},{8,12},{12,8},{16,20},{20,16},{24,28},{28,24},{1,5},{5... | collective-permute-start | bytes 18874376 | tf_op jit(solution)/shard_map/ppermute | solution.py:1044
  321.7 39.8 %collective-permute-start.23 = (bf16[1,2,3,1024,128]{4,3,2,1,0:T(8,128)(2,1)}, bf16[1,2,3,1024,128]{4,3,2,1,0:T(8,128)(2,1)S(1)}, u32[]{:S(2)}, u32[]{:S(2)}) collective-permute-start(bf16[1,2,3,1024,128]{4,3,2,1,0:T(8,128)(2,1)} %get-tuple-element.122), channel_id=1, source_target_pairs={{0,16},{4,20},{8,24},{12,28},{16,0},{20,4},{24,8},{28,12},{1,17},{... | collective-permute-start | bytes 4718600 | tf_op jit(solution)/shard_map/ppermute | solution.py:1044
  322.0 42.0 %collective-permute-start.24 = (bf16[1,2,3,1024,128]{4,3,2,1,0:T(8,128)(2,1)}, bf16[1,2,3,1024,128]{4,3,2,1,0:T(8,128)(2,1)}, u32[]{:S(2)}, u32[]{:S(2)}) collective-permute-start(bf16[1,2,3,1024,128]{4,3,2,1,0:T(8,128)(2,1)} %get-tuple-element.123.refs_3_), channel_id=1, source_target_pairs={{0,8},{4,12},{8,0},{12,4},{16,24},{20,28},{24,16},{28,20},{1,9},{5... | collective-permute-start | bytes 4718600 | tf_op jit(solution)/shard_map/ppermute | solution.py:1044
  324.5 17.9 %all-to-all-start.1 = ((bf16[4,256,256]{2,1,0:T(8,128)(2,1)}), bf16[4,256,256]{2,1,0:T(8,128)(2,1)S(1)}, u32[]{:S(2)}, u32[]{:S(2)}) async-start(bf16[4,256,256]{2,1,0:T(8,128)(2,1)} %bitcast.12), calls=%async_computation.1 | async-start | bytes 1048576 | tf_op jit(solution)/shard_map/all_to_all | solution.py:1125
  328.0 54.3 %reduce-scatter.6.cloned.1.call-start = ((), (), s32[]{:S(2)}) async-start(), calls=%async_computation.6 | async-start | bytes 2506752 | tf_op jit(solution)/shard_map/reduce_scatter | solution.py:1131
  331.5 88.5 %reduce-scatter.8.cloned.1.call-start = ((), (), s32[]{:S(2)}) async-start(), calls=%async_computation.7 | async-start | bytes 348160 | tf_op jit(solution)/shard_map/reduce_scatter | solution.py:1164
  378.3 21.4 %collective-permute-start.26 = (bf16[2,2,3,1024,128]{4,3,2,1,0:T(8,128)(2,1)}, bf16[2,2,3,1024,128]{4,3,2,1,0:T(8,128)(2,1)S(1)}, u32[]{:S(2)}, u32[]{:S(2)}) collective-permute-start(bf16[2,2,3,1024,128]{4,3,2,1,0:T(8,128)(2,1)} %get-tuple-element.128), channel_id=1, source_target_pairs={{0,4},{4,0},{8,12},{12,8},{16,20},{20,16},{24,28},{28,24},{1,5},{5... | collective-permute-start | bytes 9437192 | tf_op jit(solution)/shard_map/ppermute | solution.py:1044
  378.4 38.1 %collective-permute-start.27 = (bf16[1,2,3,1024,128]{4,3,2,1,0:T(8,128)(2,1)}, bf16[1,2,3,1024,128]{4,3,2,1,0:T(8,128)(2,1)}, u32[]{:S(2)}, u32[]{:S(2)}) collective-permute-start(bf16[1,2,3,1024,128]{4,3,2,1,0:T(8,128)(2,1)} %get-tuple-element.125.refs_17_), channel_id=1, source_target_pairs={{0,8},{4,12},{8,0},{12,4},{16,24},{20,28},{24,16},{28,20},{1,9},{5... | collective-permute-start | bytes 4718600 | tf_op jit(solution)/shard_map/ppermute | solution.py:1044
  380.9 37.6 %collective-permute-start.28 = (bf16[1,2,3,1024,128]{4,3,2,1,0:T(8,128)(2,1)}, bf16[1,2,3,1024,128]{4,3,2,1,0:T(8,128)(2,1)}, u32[]{:S(2)}, u32[]{:S(2)}) collective-permute-start(bf16[1,2,3,1024,128]{4,3,2,1,0:T(8,128)(2,1)} %get-tuple-element.130), channel_id=1, source_target_pairs={{0,16},{4,20},{8,24},{12,28},{16,0},{20,4},{24,8},{28,12},{1,17},{... | collective-permute-start | bytes 4718600 | tf_op jit(solution)/shard_map/ppermute | solution.py:1044
  382.3 79.5 %reduce-scatter.4.cloned.1.call-start = ((), (), s32[]{:S(2)}) async-start(), calls=%async_computation.5 | async-start | bytes 1253376 | tf_op jit(solution)/shard_map/reduce_scatter | solution.py:1162
  399.6 54.8 %collective-permute-start.34 = (bf16[1,2,3,1024,128]{4,3,2,1,0:T(8,128)(2,1)}, bf16[1,2,3,1024,128]{4,3,2,1,0:T(8,128)(2,1)}, u32[]{:S(2)}, u32[]{:S(2)}) collective-permute-start(bf16[1,2,3,1024,128]{4,3,2,1,0:T(8,128)(2,1)} %get-tuple-element.126.refs_12_), channel_id=1, source_target_pairs={{0,8},{4,12},{8,0},{12,4},{16,24},{20,28},{24,16},{28,20},{1,9},{5... | collective-permute-start | bytes 4718600 | tf_op jit(solution)/shard_map/ppermute | solution.py:1044
  401.4 54.4 %collective-permute-start.35 = (bf16[1,2,3,1024,128]{4,3,2,1,0:T(8,128)(2,1)}, bf16[1,2,3,1024,128]{4,3,2,1,0:T(8,128)(2,1)}, u32[]{:S(2)}, u32[]{:S(2)}) collective-permute-start(bf16[1,2,3,1024,128]{4,3,2,1,0:T(8,128)(2,1)} %get-tuple-element.140), channel_id=1, source_target_pairs={{0,16},{4,20},{8,24},{12,28},{16,0},{20,4},{24,8},{28,12},{1,17},{... | collective-permute-start | bytes 4718600 | tf_op jit(solution)/shard_map/ppermute | solution.py:1044
  434.2 27.6 %collective-permute-start.30 = (bf16[256,1024]{1,0:T(8,128)(2,1)S(1)}, bf16[256,1024]{1,0:T(8,128)(2,1)S(1)}, u32[]{:S(2)}, u32[]{:S(2)}) collective-permute-start(bf16[256,1024]{1,0:T(8,128)(2,1)S(1)} %add_convert_fusion.2.refs_5_), channel_id=1, source_target_pairs={{0,1},{1,2},{2,3},{3,0},{4,5},{5,6},{6,7},{7,4},{8,9},{9,10},{10,1... | collective-permute-start | bytes 1572872 | tf_op jit(solution)/shard_map/ppermute | solution.py:1153
  (37 other events, 371.6 us)
Sparse Core Ops, SparseCore 0:
  10.5 29.4 all-gather.5
  41.8 37.7 all-gather.7
  332.1 45.0 reduce-scatter.5
  382.4 16.8 reduce-scatter.7
  402.4 39.5 reduce-scatter.3

commit v3 on v2

--- a/solution.py
+++ b/solution.py
@@ -842,7 +842,7 @@
             sent(1 - now)
 
 
-def expert_wgrads(flipped, hidden, entries, places, extras=(), added=(), late=None, after=(), time=None):
+def expert_wgrads(flipped, hidden, entries, places, extras=(), added=(), late=None, after=(), into=None, halves=None):
     rows = hidden[0][0].shape[0]
     wide = 2 * LANES
     seq = flipped[0].shape[1]
@@ -857,7 +857,9 @@
     lane = pl.BlockSpec((rows, wide), entry)
     whole = pl.BlockSpec((D, seq), lambda i: (0, 0))
     kernel = functools.partial(expert_wgrad_kernel, places, added, late or {})
-    sizes = [sum(which == o for which, _ in places) for o in range(max(which for which, _ in places) + 1)]
+    if into is not None:
+        after = [into, *after]
+    sizes = halves or [sum(which == o for which, _ in places) for o in range(max(which for which, _ in places) + 1)]
     return pl.pallas_call(
         behind(kernel, 14 + len(extras), after),
         grid=(count,),
@@ -871,7 +873,8 @@
             pltpu.SemaphoreType.DMA((2, 2)),
         ],
         compiler_params=pltpu.CompilerParams(vmem_limit_bytes=VMEM_MOST),
-        cost_estimate=cost(time or 2.2 * count),
+        cost_estimate=cost(2.2 * count),
+        input_output_aliases={} if into is None else {14 + len(extras): 0},
     )(*flipped, *hidden[0], *hidden[1], *hidden[2], *extras, *after)
 
 
@@ -1119,17 +1122,20 @@
     wgrads = functools.partial(expert_wgrads, flipped, hidden)
     (p7,) = wgrads((14, 15), ((0, 0), (0, 1)), after=[backs[2]])
     r7 = swap(p7, CORE)
-    block_out, resid_grad, branch, mixed_grad, small = turn(
-        spots, backs[2], results[0][0], gates, kept, resid, gains, out_grad, wr, wo, send, [p7]
-    )
-    mixed_grads = lax.all_to_all(mixed_grad, "col", split_axis=0, concat_axis=0, tiled=True)
-    (p53,) = wgrads((6, 7, 10, 11), tuple((0, i) for i in range(4)), after=[branch, r7])
+    (p5,) = wgrads((10, 11), ((0, 2), (0, 3)), after=[p7], halves=[4])
+    (p53,) = wgrads((6, 7), ((0, 0), (0, 1)), after=[r7], into=p5, halves=[4])
     r53 = swap(p53, CORE)
     q6 = wgrads((12, 13), ((0, 0), (1, 0)), [r7], ((0, 0), (0, 1)), after=[p53])
     far_x, far_y = swap(q6[0], ACROSS_X), swap(q6[1], ACROSS_Y)
-    pack = out_wgrad(mixed_own, branch, small, q6[:1])
+    block_out, resid_grad, branch, mixed_grad, small = turn(
+        spots, backs[2], results[0][0], gates, kept, resid, gains, out_grad, wr, wo, send, q6[:1]
+    )
+    mixed_grads = lax.all_to_all(mixed_grad, "col", split_axis=0, concat_axis=0, tiled=True)
+    pack = out_wgrad(mixed_own, branch, small)
     out_sum = lax.psum_scatter(pack, "row", scatter_dimension=0, tiled=True)
-    q2a, q4b = wgrads((4, 9), ((0, 0), (1, 0)), [r53], ((0, 0), (0, 3)), after=[pack, mixed_grads])
+    q2a, q4b = wgrads(
+        (4, 9), ((0, 0), (1, 0)), [r53], ((0, 0), (0, 3)), after=[pack, mixed_grads, far_x, far_y]
+    )
     x2a, y4b = swap(q2a, ACROSS_X), swap(q4b, ACROSS_Y)
     q2b, q4a, p1 = wgrads(
         (5, 8, 2, 3),

time: 489 us -> 502 us (1.027)
  starting transfers between devices: 31.4 us -> 41.4 us
    ppermute x3, starting transfers between devices: 0.35 us -> 10.3 us  [fast(): back = lax.ppermute(back, 'col', steps)]
    pallas_call x6 -> x7, Pallas kernels: 62.6 us -> 66.4 us  [expert_wgrads(): pl.pallas_call(behind(kernel, 14 + len(extras), after), grid=(count,), ou...]
  transfers between devices with their start and end apart: 43 -> 43, of which waited for: 22 -> 22; matrix products, arithmetic and copies ran while one was open for 5% -> 4% of each run, Pallas kernels for 35% -> 36%
where the time goes in v3:
time: 502 us; the launch traced here: 492 us
  Pallas kernels  215 us (43%)
  waiting for transfers between devices  166 us (33%)
  starting transfers between devices  41.4 us (8%)
  other arithmetic  21.3 us (4%)
  local copies, waits for them, and re-layouts  17.6 us (4%)
  blocking collectives  16.1 us (3%)
  between operations  15.4 us (3%)
    pallas_call x4, Pallas kernels, experts(): pl.pallas_call(behind(expert_kernel, 12, after), out_shape=(jax.ShapeDtyp...  86.9 us
    ppermute x7, waiting for transfers between devices, ring_gather(): chunks.append(lax.ppermute(chunks[-1], 'col', steps))  73.4 us
    pallas_call x7, Pallas kernels, expert_wgrads(): pl.pallas_call(behind(kernel, 14 + len(extras), after), grid=(count,), ou...  66.4 us
    ppermute x18, waiting for transfers between devices, swap(): return lax.ppermute(value, 'row', [(i, i ^ mask) for i in range(8)])  48.5 us
    pallas_call x1, Pallas kernels, attend_back(): pl.pallas_call(behind(attend_back_kernel, 12, after), out_shape=shapes, i...  17 us
    all_gather x1, blocking collectives, fast(): pack_out = lax.all_gather(pack_out, 'col', axis=0)  16.1 us
    ppermute x18, starting transfers between devices, swap(): return lax.ppermute(value, 'row', [(i, i ^ mask) for i in range(8)])  14.3 us
    ppermute x1, waiting for transfers between devices, fast(): moving = lax.ppermute(moving, 'col', steps)  13 us
  transfers between devices with their start and end apart: 43, of which 22 were waited for; matrix products, arithmetic and copies ran while one was open for 4% of the time, Pallas kernels for 36%

profile of v3, /device:TPU:0, one launch (start us, length us, event | category | flops | bytes accessed | tf_op | source)
XLA Modules:
  0.0 492.5 jit_solution(7120606896193910312)
XLA Ops:
  12.5 16.1 %all-gather.1 = bf16[544,256]{1,0:T(8,128)(2,1)} all-gather(bf16[136,256]{1,0:T(8,128)(2,1)S(1)} %fusion.9), channel_id=3, replica_groups=mesh['row'=8,'col'=4] {'col'}, dimensions={0}, use_global_device_ids=true | all-gather | bytes 348160 | tf_op jit(solution)/shard_map/all_gather | solution.py:1078
  46.1 12.3 %collective-permute-done.1.refs_3_ = bf16[256,1024]{1,0:T(8,128)(2,1)S(1)} collective-permute-done((bf16[256,1024]{1,0:T(8,128)(2,1)}, bf16[256,1024]{1,0:T(8,128)(2,1)S(1)}, u32[]{:S(2)}, u32[]{:S(2)}) %collective-permute-start.1) | collective-permute-done | bytes 524320 | tf_op jit(solution)/shard_map/ppermute | solution.py:1018
  59.2 11.2 %collective-permute-done.2.refs_4_ = bf16[256,1024]{1,0:T(8,128)(2,1)S(1)} collective-permute-done((bf16[256,1024]{1,0:T(8,128)(2,1)S(1)}, bf16[256,1024]{1,0:T(8,128)(2,1)S(1)}, u32[]{:S(2)}, u32[]{:S(2)}) %collective-permute-start.2) | collective-permute-done | bytes 524320 | tf_op jit(solution)/shard_map/ppermute | solution.py:1018
  74.5 12.1 %shard_map.238 = (bf16[1024,1024]{1,0:T(8,128)(2,1)}, bf16[4,1024,64]{2,1,0:T(8,128)(2,1)}, bf16[2,1024,64]{2,1,0:T(8,128)(2,1)}, bf16[2,1024,64]{2,1,0:T(8,128)...) custom-call(s32[3]{0:T(128)} %pad_add_fusion.refs_0_, ...), custom_call_target="tpu_custom_call" | custom-call | flops 10000000 | bytes 100000 | tf_op jit(solution)/shard_map/pallas_call | solution.py:498
  86.7 5.7 %all-to-all-start = ((bf16[4,256,256]{2,1,0:T(8,128)(2,1)}), bf16[4,256,256]{2,1,0:T(8,128)(2,1)}, u32[]{:S(2)}, u32[]{:S(2)}) async-start(bf16[4,256,256]{2,1,0:T(8,128)(2,1)} %bitcast.30), calls=%async_computation | async-start | bytes 1048576 | tf_op jit(solution)/shard_map/all_to_all | solution.py:1093
  92.4 11.3 %collective-permute-done.7.refs_2_.refs_1_.refs_6_ = bf16[256,1024]{1,0:T(8,128)(2,1)} collective-permute-done((bf16[256,1024]{1,0:T(8,128)(2,1)}, bf16[256,1024]{1,0:T(8,128)(2,1)}, u32[]{:S(2)}, u32[]{:S(2)}) %collective-permute-start.7) | collective-permute-done | bytes 524320 | tf_op jit(solution)/shard_map/ppermute | solution.py:1018
  110.1 5.2 %shard_map.239 = (bf16[2,3,1024,128]{3,2,1,0:T(8,128)(2,1)}, bf16[2,3,1024,128]{3,2,1,0:T(8,128)(2,1)}) custom-call(bf16[4,3,1024,128]{3,2,1,0:T(8,128)(2,1)} %collective-permute-done.4.refs_0_.refs_4_, bf16[4,3,1024,128]{3,2,1,0:T(8,128)(2,1)} %collective-permute-done.5.refs_1_.refs_6_, bf16[256,1024]{1,0:T(8,128)(2,1)} %collective-permute-done.7.refs_2_.refs_1_.refs_6_), custom_call_target="tpu_custom_call" | custom-call | flops 3000000 | bytes 100000 | tf_op jit(solution)/shard_map/pallas_call | solution.py:914
  125.1 15.9 %collective-permute-done.9.refs_0_.refs_1_ = bf16[256,1152]{1,0:T(8,128)(2,1)S(1)} collective-permute-done((bf16[256,1152]{1,0:T(8,128)(2,1)}, bf16[256,1152]{1,0:T(8,128)(2,1)S(1)}, u32[]{:S(2)}, u32[]{:S(2)}) %collective-permute-start.9) | collective-permute-done | bytes 589856 | tf_op jit(solution)/shard_map/ppermute | solution.py:1018
  141.0 9.5 %collective-permute-done.13.refs_9_ = bf16[2,3,1024,128]{3,2,1,0:T(8,128)(2,1)} collective-permute-done((bf16[2,3,1024,128]{3,2,1,0:T(8,128)(2,1)}, bf16[2,3,1024,128]{3,2,1,0:T(8,128)(2,1)}, u32[]{:S(2)}, u32[]{:S(2)}) %collective-permute-start.13) | collective-permute-done | bytes 1572896 | tf_op jit(solution)/shard_map/ppermute | solution.py:1047
  150.5 5.5 %collective-permute-done.14.refs_0_.refs_2_ = bf16[256,1152]{1,0:T(8,128)(2,1)S(1)} collective-permute-done((bf16[256,1152]{1,0:T(8,128)(2,1)S(1)}, bf16[256,1152]{1,0:T(8,128)(2,1)S(1)}, u32[]{:S(2)}, u32[]{:S(2)}) %collective-permute-start.14) | collective-permute-done | bytes 589856 | tf_op jit(solution)/shard_map/ppermute | solution.py:1018
  156.6 17.1 %collective-permute-done.17.refs_12_.refs_3_.refs_0_ = bf16[256,1152]{1,0:T(8,128)(2,1)S(1)} collective-permute-done((bf16[256,1152]{1,0:T(8,128)(2,1)S(1)}, bf16[256,1152]{1,0:T(8,128)(2,1)S(1)}, u32[]{:S(2)}, u32[]{:S(2)}) %collective-permute-start.17) | collective-permute-done | bytes 589856 | tf_op jit(solution)/shard_map/ppermute | solution.py:1018
  176.2 21.6 %shard_map.241 = (bf16[256,2176]{1,0:T(8,128)(2,1)}, bf16[256,4096]{1,0:T(8,128)(2,1)}, bf16[256,4096]{1,0:T(8,128)(2,1)}, bf16[256,4096]{1,0:T(8,128)(2,1)}) custom-call(bf16[256,1152]{1,0:T(8,128)(2,1)} %copy-done.13, bf16[256,1024]{1,0:T(8,128)(2,1)} %collective-permute-done.6.refs_1_.refs_5_, bf16[4,3,1024,128]{3,2,1,0:T(8,128)(2,1)} %copy-done, ...), custom_call_target="tpu_custom_call" | custom-call | flops 21000000 | bytes 100000 | tf_op jit(solution)/shard_map/pallas_call | solution.py:724
  197.9 21.7 %shard_map.242 = (bf16[256,2176]{1,0:T(8,128)(2,1)}, bf16[256,4096]{1,0:T(8,128)(2,1)}, bf16[256,4096]{1,0:T(8,128)(2,1)}, bf16[256,4096]{1,0:T(8,128)(2,1)}) custom-call(bf16[256,1152]{1,0:T(8,128)(2,1)} %copy-done.12, bf16[256,1024]{1,0:T(8,128)(2,1)} %collective-permute-done.7.refs_2_.refs_1_.refs_6_, bf16[4,3,1024,128]{3,2,1,0:T(8,128)(2,1)} %copy-done, ...), custom_call_target="tpu_custom_call" | custom-call | flops 21000000 | bytes 100000 | tf_op jit(solution)/shard_map/pallas_call | solution.py:724
  219.6 6.0 %collective-permute-done.18.refs_13_ = bf16[256,2176]{1,0:T(8,128)(2,1)S(1)} collective-permute-done((bf16[256,2176]{1,0:T(8,128)(2,1)}, bf16[256,2176]{1,0:T(8,128)(2,1)S(1)}, u32[]{:S(2)}, u32[]{:S(2)}) %collective-permute-start.18) | collective-permute-done | bytes 1114144 | tf_op jit(solution)/shard_map/ppermute | solution.py:1117
  227.5 5.3 %shard_map.243 = (bf16[1024,1024]{1,0:T(8,128)(2,1)}, bf16[1024,1024]{1,0:T(8,128)(2,1)}) custom-call(bf16[256,1152]{1,0:T(8,128)(2,1)} %get-tuple-element.86.refs_0_.refs_10_, bf16[256,1152]{1,0:T(8,128)(2,1)} %copy-done.13, bf16[256,1152]{1,0:T(8,128)(2,1)} %copy-done.12, bf16[256,1152]{1,0:T(8,128)(2,1)} %copy-done.6, bf16[256,1024]{1,0:T(8,128)(2,1)} %refs_7_.1, ...), custom_call_target="tpu_custom_call" | custom-call | flops 2000000 | bytes 100000 | tf_op jit(solution)/shard_map/pallas_call | solution.py:755
  232.8 21.7 %shard_map.244 = (bf16[256,2176]{1,0:T(8,128)(2,1)}, bf16[256,4096]{1,0:T(8,128)(2,1)}, bf16[256,4096]{1,0:T(8,128)(2,1)}, bf16[256,4096]{1,0:T(8,128)(2,1)}) custom-call(bf16[256,1152]{1,0:T(8,128)(2,1)} %copy-done.6, bf16[256,1024]{1,0:T(8,128)(2,1)} %collective-permute-done.8.refs_7_.refs_1_, bf16[4,3,1024,128]{3,2,1,0:T(8,128)(2,1)} %copy-done, ...), custom_call_target="tpu_custom_call" | custom-call | flops 21000000 | bytes 100000 | tf_op jit(solution)/shard_map/pallas_call | solution.py:724
  256.5 10.2 %collective-permute-start.20 = (bf16[256,2176]{1,0:T(8,128)(2,1)S(1)}, bf16[256,2176]{1,0:T(8,128)(2,1)S(1)}, u32[]{:S(2)}, u32[]{:S(2)}) collective-permute-start(bf16[256,2176]{1,0:T(8,128)(2,1)S(1)} %add_convert_fusion), channel_id=1, source_target_pairs={{0,1},{1,2},{2,3},{3,0},{4,5},{5,6},{6,7},{7,4},{8,9},{9,10},{10,1... | collective-permute-start | bytes 3342344 | tf_op jit(solution)/shard_map/ppermute | solution.py:1117
  266.7 21.7 %shard_map.245 = (bf16[256,2176]{1,0:T(8,128)(2,1)}, bf16[256,4096]{1,0:T(8,128)(2,1)}, bf16[256,4096]{1,0:T(8,128)(2,1)}, bf16[256,4096]{1,0:T(8,128)(2,1)}) custom-call(bf16[256,1152]{1,0:T(8,128)(2,1)} %get-tuple-element.86.refs_0_.refs_10_, bf16[256,1024]{1,0:T(8,128)(2,1)} %refs_7_.1, bf16[4,3,1024,128]{3,2,1,0:T(8,128)(2,1)} %copy-done, ...), custom_call_target="tpu_custom_call" | custom-call | flops 21000000 | bytes 100000 | tf_op jit(solution)/shard_map/pallas_call | solution.py:724
  294.2 8.0 %shard_map.246.refs_14_ = bf16[2,2,3,1024,128]{4,3,2,1,0:T(8,128)(2,1)} custom-call(bf16[1024,1024]{1,0:T(8,128)(2,1)} %get-tuple-element.94.refs_14_.refs_0_, bf16[1024,1024]{1,0:T(8,128)(2,1)} %get-tuple-element.103.refs_1_, bf16[256,4096]{1,0:T(8,128)(2,1)} %get-tuple-element.104.refs_2_, bf16[256,4096]{1,0:T(8,128)(2,1)} %get-tuple-element.91.refs_12_.refs_3_, ...), custom_call_target="tpu_custom_call" | custom-call | flops 4400000 | bytes 100000 | tf_op jit(solution)/shard_map/pallas_call | solution.py:863
  302.3 8.0 %shard_map.247.refs_14_ = bf16[4,2,3,1024,128]{4,3,2,1,0:T(8,128)(2,1)} custom-call(bf16[1024,1024]{1,0:T(8,128)(2,1)} %get-tuple-element.94.refs_14_.refs_0_, bf16[1024,1024]{1,0:T(8,128)(2,1)} %get-tuple-element.103.refs_1_, bf16[256,4096]{1,0:T(8,128)(2,1)} %get-tuple-element.104.refs_2_, bf16[256,4096]{1,0:T(8,128)(2,1)} %get-tuple-element.91.refs_12_.refs_3_, ...), custom_call_target="tpu_custom_call" | custom-call | flops 4400000 | bytes 100000 | tf_op jit(solution)/shard_map/pallas_call | solution.py:863
  311.9 7.9 %shard_map.248.refs_15_ = bf16[4,2,3,1024,128]{4,3,2,1,0:T(8,128)(2,1)} custom-call(bf16[1024,1024]{1,0:T(8,128)(2,1)} %get-tuple-element.94.refs_14_.refs_0_, bf16[1024,1024]{1,0:T(8,128)(2,1)} %get-tuple-element.103.refs_1_, bf16[256,4096]{1,0:T(8,128)(2,1)} %get-tuple-element.104.refs_2_, ...), custom_call_target="tpu_custom_call", output_to_operand_aliasing={{}: (14, {})} | custom-call | flops 4400000 | bytes 100000 | tf_op jit(solution)/shard_map/pallas_call | solution.py:863
  320.4 9.4 %shard_map.249 = (bf16[1,2,3,1024,128]{4,3,2,1,0:T(8,128)(2,1)}, bf16[1,2,3,1024,128]{4,3,2,1,0:T(8,128)(2,1)}) custom-call(bf16[1024,1024]{1,0:T(8,128)(2,1)} %get-tuple-element.94.refs_14_.refs_0_, bf16[1024,1024]{1,0:T(8,128)(2,1)} %get-tuple-element.103.refs_1_, bf16[256,4096]{1,0:T(8,128)(2,1)} %get-tuple-element.104.refs_2_, ...), custom_call_target="tpu_custom_call" | custom-call | flops 4400000 | bytes 100000 | tf_op jit(solution)/shard_map/pallas_call | solution.py:863
  332.5 6.0 %shard_map.250 = (f32[256,1024]{1,0:T(8,128)}, f32[256,1024]{1,0:T(8,128)}, bf16[256,1024]{1,0:T(8,128)(2,1)}, bf16[1024,256]{1,0:T(8,128)(2,1)}, f32[136,1024]{1,0:T(8,128)}) custom-call(s32[3]{0:T(128)} %pad_add_fusion.refs_0_, bf16[256,2176]{1,0:T(8,128)(2,1)} %copy-done.8, bf16[256,2176]{1,0:T(8,128)(2,1)} %get-tuple-element.97.refs_2_, ...), custom_call_target="tpu_custom_call" | custom-call | flops 2000000 | bytes 100000 | tf_op jit(solution)/shard_map/pallas_call | solution.py:962
  346.3 10.9 %all-to-all-done.1 = bf16[4,256,256]{2,1,0:T(8,128)(2,1)} async-done(((bf16[4,256,256]{2,1,0:T(8,128)(2,1)}), bf16[4,256,256]{2,1,0:T(8,128)(2,1)}, u32[]{:S(2)}, u32[]{:S(2)}) %all-to-all-start.1) | async-done | bytes 524320 | tf_op jit(solution)/shard_map/all_to_all | solution.py:1133
  357.1 9.2 %collective-permute-done.23.refs_18_.refs_15_ = bf16[1,2,3,1024,128]{4,3,2,1,0:T(8,128)(2,1)S(1)} collective-permute-done((bf16[1,2,3,1024,128]{4,3,2,1,0:T(8,128)(2,1)}, bf16[1,2,3,1024,128]{4,3,2,1,0:T(8,128)(2,1)S(1)}, u32[]{:S(2)}, u32[]{:S(2)}) %collective-permute-start.23) | collective-permute-done | bytes 1572896 | tf_op jit(solution)/shard_map/ppermute | solution.py:1047
  368.2 9.5 %shard_map.252 = (bf16[1,2,3,1024,128]{4,3,2,1,0:T(8,128)(2,1)}, bf16[1,2,3,1024,128]{4,3,2,1,0:T(8,128)(2,1)}) custom-call(bf16[1024,1024]{1,0:T(8,128)(2,1)} %get-tuple-element.94.refs_14_.refs_0_, bf16[1024,1024]{1,0:T(8,128)(2,1)} %get-tuple-element.103.refs_1_, bf16[256,4096]{1,0:T(8,128)(2,1)} %get-tuple-element.104.refs_2_, ...), custom_call_target="tpu_custom_call" | custom-call | flops 4400000 | bytes 100000 | tf_op jit(solution)/shard_map/pallas_call | solution.py:863
  377.6 14.2 %shard_map.253 = (bf16[1,2,3,1024,128]{4,3,2,1,0:T(8,128)(2,1)}, bf16[1,2,3,1024,128]{4,3,2,1,0:T(8,128)(2,1)}, bf16[2,2,3,1024,128]{4,3,2,1,0:T(8,128)(2,1)}) custom-call(bf16[1024,1024]{1,0:T(8,128)(2,1)} %get-tuple-element.94.refs_14_.refs_0_, bf16[1024,1024]{1,0:T(8,128)(2,1)} %get-tuple-element.103.refs_1_, ...), custom_call_target="tpu_custom_call" | custom-call | flops 8800000 | bytes 100000 | tf_op jit(solution)/shard_map/pallas_call | solution.py:863
  395.6 17.0 %shard_map.254 = (bf16[8,136,512]{2,1,0:T(8,128)(2,1)}, bf16[256,1024]{1,0:T(8,128)(2,1)}, bf16[256,1024]{1,0:T(8,128)(2,1)}, bf16[256,1024]{1,0:T(8,128)(2,1)}, bf16[256,1024]{1,0:T(8,128)(2,1)}) custom-call(s32[3]{0:T(128)} %pad_add_fusion.refs_0_, bf16[1024,256]{1,0:T(8,128)(2,1)} %bitcast.13.refs_16_.refs_1_, ...), custom_call_target="tpu_custom_call" | custom-call | flops 16000000 | bytes 100000 | tf_op jit(solution)/shard_map/pallas_call | solution.py:575
  415.2 9.4 %shard_map.255.refs_0_ = bf16[2,2,3,1024,128]{4,3,2,1,0:T(8,128)(2,1)} custom-call(bf16[1024,1024]{1,0:T(8,128)(2,1)} %get-tuple-element.94.refs_14_.refs_0_, bf16[1024,1024]{1,0:T(8,128)(2,1)} %get-tuple-element.103.refs_1_, bf16[256,4096]{1,0:T(8,128)(2,1)} %get-tuple-element.104.refs_2_, bf16[256,4096]{1,0:T(8,128)(2,1)} %get-tuple-element.91.refs_12_.refs_3_, ...), custom_call_target="tpu_custom_call" | custom-call | flops 4400000 | bytes 100000 | tf_op jit(solution)/shard_map/pallas_call | solution.py:863
  434.0 13.0 %collective-permute-done.29 = bf16[256,1024]{1,0:T(8,128)(2,1)S(1)} collective-permute-done((bf16[256,1024]{1,0:T(8,128)(2,1)S(1)}, bf16[256,1024]{1,0:T(8,128)(2,1)S(1)}, u32[]{:S(2)}, u32[]{:S(2)}) %collective-permute-start.29) | collective-permute-done | bytes 524320 | tf_op jit(solution)/shard_map/ppermute | solution.py:1156
  449.2 18.3 %collective-permute-done.34.refs_2_ = bf16[1,2,3,1024,128]{4,3,2,1,0:T(8,128)(2,1)} collective-permute-done((bf16[1,2,3,1024,128]{4,3,2,1,0:T(8,128)(2,1)}, bf16[1,2,3,1024,128]{4,3,2,1,0:T(8,128)(2,1)}, u32[]{:S(2)}, u32[]{:S(2)}) %collective-permute-start.34) | collective-permute-done | bytes 1572896 | tf_op jit(solution)/shard_map/ppermute | solution.py:1047
  469.0 5.9 %shard_map.257 = (f32[2,2,1024,128]{3,2,1,0:T(8,128)}, f32[2,2,1024,128]{3,2,1,0:T(8,128)}, f32[2,2,1024,128]{3,2,1,0:T(8,128)}) custom-call(bf16[2,2,3,1024,128]{4,3,2,1,0:T(8,128)(2,1)} %shard_map.255.refs_0_, bf16[1,2,3,1024,128]{4,3,2,1,0:T(8,128)(2,1)} %collective-permute-done.27.refs_1_, bf16[1,2,3,1024,128]{4,3,2,1,0:T(8,128)(2,1)} %collective-permute-done.34.refs_2_, ...), custom_call_target="tpu_custom_call" | custom-call | flops 5000000 | bytes 100000 | tf_op jit(solution)/shard_map/pallas_call | solution.py:893
  (165 shorter events, 100.1 us)
Async XLA Ops:
  7.2 67.3 %all-gather.6.cloned.1.call-start = ((), (), s32[]{:S(2)}) async-start(), calls=%async_computation.8 | async-start | bytes 1253376 | tf_op jit(solution)/shard_map/all_gather | solution.py:1079
  9.7 109.1 %all-gather.8.cloned.1.call-start = ((), (), s32[]{:S(2)}) async-start(), calls=%async_computation.9 | async-start | bytes 2506752 | tf_op jit(solution)/shard_map/all_gather | solution.py:1080
  12.0 62.5 %collective-permute-start.3 = (bf16[4,3,1024,128]{3,2,1,0:T(8,128)(2,1)S(1)}, bf16[4,3,1024,128]{3,2,1,0:T(8,128)(2,1)}, u32[]{:S(2)}, u32[]{:S(2)}) collective-permute-start(bf16[4,3,1024,128]{3,2,1,0:T(8,128)(2,1)S(1)} %pad_maximum_fusion.refs_2_), channel_id=1, source_target_pairs={{0,4},{4,0},{8,12},{12,8},{16,20},{20,16},{24,28},{28,24},{1,5},{5... | collective-permute-start | bytes 9437192 | tf_op jit(solution)/shard_map/ppermute | solution.py:1047
  28.6 80.3 %collective-permute-start.4 = (bf16[4,3,1024,128]{3,2,1,0:T(8,128)(2,1)S(1)}, bf16[4,3,1024,128]{3,2,1,0:T(8,128)(2,1)}, u32[]{:S(2)}, u32[]{:S(2)}) collective-permute-start(bf16[4,3,1024,128]{3,2,1,0:T(8,128)(2,1)S(1)} %pad_maximum_fusion.refs_2_), channel_id=1, source_target_pairs={{0,8},{4,12},{8,0},{12,4},{16,24},{20,28},{24,16},{28,20},{1,9},{5... | collective-permute-start | bytes 9437192 | tf_op jit(solution)/shard_map/ppermute | solution.py:1047
  30.2 79.9 %collective-permute-start.5 = (bf16[4,3,1024,128]{3,2,1,0:T(8,128)(2,1)S(1)}, bf16[4,3,1024,128]{3,2,1,0:T(8,128)(2,1)}, u32[]{:S(2)}, u32[]{:S(2)}) collective-permute-start(bf16[4,3,1024,128]{3,2,1,0:T(8,128)(2,1)S(1)} %pad_maximum_fusion.refs_2_), channel_id=1, source_target_pairs={{0,16},{4,20},{8,24},{12,28},{16,0},{20,4},{24,8},{28,12},{1,17},{... | collective-permute-start | bytes 9437192 | tf_op jit(solution)/shard_map/ppermute | solution.py:1047
  86.6 17.1 %collective-permute-start.7 = (bf16[256,1024]{1,0:T(8,128)(2,1)}, bf16[256,1024]{1,0:T(8,128)(2,1)}, u32[]{:S(2)}, u32[]{:S(2)}) collective-permute-start(bf16[256,1024]{1,0:T(8,128)(2,1)} %collective-permute-done.6.refs_1_.refs_5_), channel_id=1, source_target_pairs={{0,1},{1,2},{2,3},{3,0},{4,5},{5,6},{6,7},{7,4},{8,9},{9,10},{10,1... | collective-permute-start | bytes 1572872 | tf_op jit(solution)/shard_map/ppermute | solution.py:1018
  86.7 33.1 %all-to-all-start = ((bf16[4,256,256]{2,1,0:T(8,128)(2,1)}), bf16[4,256,256]{2,1,0:T(8,128)(2,1)}, u32[]{:S(2)}, u32[]{:S(2)}) async-start(bf16[4,256,256]{2,1,0:T(8,128)(2,1)} %bitcast.30), calls=%async_computation | async-start | bytes 1048576 | tf_op jit(solution)/shard_map/all_to_all | solution.py:1093
  103.8 21.0 %collective-permute-start.8 = (bf16[256,1024]{1,0:T(8,128)(2,1)}, bf16[256,1024]{1,0:T(8,128)(2,1)}, u32[]{:S(2)}, u32[]{:S(2)}) collective-permute-start(bf16[256,1024]{1,0:T(8,128)(2,1)} %collective-permute-done.7.refs_2_.refs_1_.refs_6_), channel_id=1, source_target_pairs={{0,1},{1,2},{2,3},{3,0},{4,5},{5,6},{6,7},{7,4},{8,9},{9,10},{10,1... | collective-permute-start | bytes 1572872 | tf_op jit(solution)/shard_map/ppermute | solution.py:1018
  115.4 35.2 %collective-permute-start.13 = (bf16[2,3,1024,128]{3,2,1,0:T(8,128)(2,1)}, bf16[2,3,1024,128]{3,2,1,0:T(8,128)(2,1)}, u32[]{:S(2)}, u32[]{:S(2)}) collective-permute-start(bf16[2,3,1024,128]{3,2,1,0:T(8,128)(2,1)} %get-tuple-element.87), channel_id=1, source_target_pairs={{0,16},{4,20},{8,24},{12,28},{16,0},{20,4},{24,8},{28,12},{1,17},{... | collective-permute-start | bytes 4718600 | tf_op jit(solution)/shard_map/ppermute | solution.py:1047
  116.9 39.2 %collective-permute-start.12 = (bf16[2,3,1024,128]{3,2,1,0:T(8,128)(2,1)}, bf16[2,3,1024,128]{3,2,1,0:T(8,128)(2,1)}, u32[]{:S(2)}, u32[]{:S(2)}) collective-permute-start(bf16[2,3,1024,128]{3,2,1,0:T(8,128)(2,1)} %get-tuple-element.84.refs_7_), channel_id=1, source_target_pairs={{0,8},{4,12},{8,0},{12,4},{16,24},{20,28},{24,16},{28,20},{1,9},{5... | collective-permute-start | bytes 4718600 | tf_op jit(solution)/shard_map/ppermute | solution.py:1047
  117.4 56.3 %collective-permute-start.10 = (bf16[4,3,1024,128]{3,2,1,0:T(8,128)(2,1)}, bf16[4,3,1024,128]{3,2,1,0:T(8,128)(2,1)S(1)}, u32[]{:S(2)}, u32[]{:S(2)}) collective-permute-start(bf16[4,3,1024,128]{3,2,1,0:T(8,128)(2,1)} %collective-permute-done.4.refs_0_.refs_4_), channel_id=1, source_target_pairs={{0,4},{4,0},{8,12},{12,8},{16,20},{20,16},{24,28},{28,24},{1,5},{5... | collective-permute-start | bytes 9437192 | tf_op jit(solution)/shard_map/ppermute | solution.py:1047
  117.4 57.1 %collective-permute-start.11 = (bf16[4,3,1024,128]{3,2,1,0:T(8,128)(2,1)}, bf16[4,3,1024,128]{3,2,1,0:T(8,128)(2,1)}, u32[]{:S(2)}, u32[]{:S(2)}) collective-permute-start(bf16[4,3,1024,128]{3,2,1,0:T(8,128)(2,1)} %collective-permute-done.5.refs_1_.refs_6_), channel_id=1, source_target_pairs={{0,4},{4,0},{8,12},{12,8},{16,20},{20,16},{24,28},{28,24},{1,5},{5... | collective-permute-start | bytes 9437192 | tf_op jit(solution)/shard_map/ppermute | solution.py:1047
  124.8 16.2 %collective-permute-start.9 = (bf16[256,1152]{1,0:T(8,128)(2,1)}, bf16[256,1152]{1,0:T(8,128)(2,1)S(1)}, u32[]{:S(2)}, u32[]{:S(2)}) collective-permute-start(bf16[256,1152]{1,0:T(8,128)(2,1)} %get-tuple-element.86.refs_0_.refs_10_), channel_id=1, source_target_pairs={{0,1},{1,2},{2,3},{3,0},{4,5},{5,6},{6,7},{7,4},{8,9},{9,10},{10,1... | collective-permute-start | bytes 1769480 | tf_op jit(solution)/shard_map/ppermute | solution.py:1018
  156.1 18.5 %collective-permute-start.16 = (bf16[2,3,1024,128]{3,2,1,0:T(8,128)(2,1)}, bf16[2,3,1024,128]{3,2,1,0:T(8,128)(2,1)}, u32[]{:S(2)}, u32[]{:S(2)}) collective-permute-start(bf16[2,3,1024,128]{3,2,1,0:T(8,128)(2,1)} %collective-permute-done.13.refs_9_), channel_id=1, source_target_pairs={{0,4},{4,0},{8,12},{12,8},{16,20},{20,16},{24,28},{28,24},{1,5},{5... | collective-permute-start | bytes 4718600 | tf_op jit(solution)/shard_map/ppermute | solution.py:1047
  156.1 18.4 %collective-permute-start.15 = (bf16[2,3,1024,128]{3,2,1,0:T(8,128)(2,1)}, bf16[2,3,1024,128]{3,2,1,0:T(8,128)(2,1)}, u32[]{:S(2)}, u32[]{:S(2)}) collective-permute-start(bf16[2,3,1024,128]{3,2,1,0:T(8,128)(2,1)} %collective-permute-done.12.refs_8_), channel_id=1, source_target_pairs={{0,4},{4,0},{8,12},{12,8},{16,20},{20,16},{24,28},{28,24},{1,5},{5... | collective-permute-start | bytes 4718600 | tf_op jit(solution)/shard_map/ppermute | solution.py:1047
  156.6 17.1 %collective-permute-start.17 = (bf16[256,1152]{1,0:T(8,128)(2,1)S(1)}, bf16[256,1152]{1,0:T(8,128)(2,1)S(1)}, u32[]{:S(2)}, u32[]{:S(2)}) collective-permute-start(bf16[256,1152]{1,0:T(8,128)(2,1)S(1)} %collective-permute-done.14.refs_0_.refs_2_), channel_id=1, source_target_pairs={{0,1},{1,2},{2,3},{3,0},{4,5},{5,6},{6,7},{7,4},{8,9},{9,10},{10,1... | collective-permute-start | bytes 1769480 | tf_op jit(solution)/shard_map/ppermute | solution.py:1018
  197.8 27.8 %collective-permute-start.18 = (bf16[256,2176]{1,0:T(8,128)(2,1)}, bf16[256,2176]{1,0:T(8,128)(2,1)S(1)}, u32[]{:S(2)}, u32[]{:S(2)}) collective-permute-start(bf16[256,2176]{1,0:T(8,128)(2,1)} %get-tuple-element.90), channel_id=1, source_target_pairs={{0,1},{1,2},{2,3},{3,0},{4,5},{5,6},{6,7},{7,4},{8,9},{9,10},{10,1... | collective-permute-start | bytes 3342344 | tf_op jit(solution)/shard_map/ppermute | solution.py:1117
  227.5 27.1 %collective-permute-start.19 = (bf16[256,2176]{1,0:T(8,128)(2,1)S(1)}, bf16[256,2176]{1,0:T(8,128)(2,1)S(1)}, u32[]{:S(2)}, u32[]{:S(2)}) collective-permute-start(bf16[256,2176]{1,0:T(8,128)(2,1)S(1)} %add_convert_fusion.1), channel_id=1, source_target_pairs={{0,1},{1,2},{2,3},{3,0},{4,5},{5,6},{6,7},{7,4},{8,9},{9,10},{10,1... | collective-permute-start | bytes 3342344 | tf_op jit(solution)/shard_map/ppermute | solution.py:1117
  256.5 36.7 %collective-permute-start.20 = (bf16[256,2176]{1,0:T(8,128)(2,1)S(1)}, bf16[256,2176]{1,0:T(8,128)(2,1)S(1)}, u32[]{:S(2)}, u32[]{:S(2)}) collective-permute-start(bf16[256,2176]{1,0:T(8,128)(2,1)S(1)} %add_convert_fusion), channel_id=1, source_target_pairs={{0,1},{1,2},{2,3},{3,0},{4,5},{5,6},{6,7},{7,4},{8,9},{9,10},{10,1... | collective-permute-start | bytes 3342344 | tf_op jit(solution)/shard_map/ppermute | solution.py:1117
  319.9 47.2 %collective-permute-start.22 = (bf16[4,2,3,1024,128]{4,3,2,1,0:T(8,128)(2,1)}, bf16[4,2,3,1024,128]{4,3,2,1,0:T(8,128)(2,1)}, u32[]{:S(2)}, u32[]{:S(2)}) collective-permute-start(bf16[4,2,3,1024,128]{4,3,2,1,0:T(8,128)(2,1)} %shard_map.248.refs_15_), channel_id=1, source_target_pairs={{0,4},{4,0},{8,12},{12,8},{16,20},{20,16},{24,28},{28,24},{1,5},{5... | collective-permute-start | bytes 18874376 | tf_op jit(solution)/shard_map/ppermute | solution.py:1047
  329.8 36.6 %collective-permute-start.23 = (bf16[1,2,3,1024,128]{4,3,2,1,0:T(8,128)(2,1)}, bf16[1,2,3,1024,128]{4,3,2,1,0:T(8,128)(2,1)S(1)}, u32[]{:S(2)}, u32[]{:S(2)}) collective-permute-start(bf16[1,2,3,1024,128]{4,3,2,1,0:T(8,128)(2,1)} %get-tuple-element.122), channel_id=1, source_target_pairs={{0,16},{4,20},{8,24},{12,28},{16,0},{20,4},{24,8},{28,12},{1,17},{... | collective-permute-start | bytes 4718600 | tf_op jit(solution)/shard_map/ppermute | solution.py:1047
  330.1 37.0 %collective-permute-start.24 = (bf16[1,2,3,1024,128]{4,3,2,1,0:T(8,128)(2,1)}, bf16[1,2,3,1024,128]{4,3,2,1,0:T(8,128)(2,1)S(1)}, u32[]{:S(2)}, u32[]{:S(2)}) collective-permute-start(bf16[1,2,3,1024,128]{4,3,2,1,0:T(8,128)(2,1)} %get-tuple-element.113.refs_11_), channel_id=1, source_target_pairs={{0,8},{4,12},{8,0},{12,4},{16,24},{20,28},{24,16},{28,20},{1,9},{5... | collective-permute-start | bytes 4718600 | tf_op jit(solution)/shard_map/ppermute | solution.py:1047
  338.5 18.6 %all-to-all-start.1 = ((bf16[4,256,256]{2,1,0:T(8,128)(2,1)}), bf16[4,256,256]{2,1,0:T(8,128)(2,1)}, u32[]{:S(2)}, u32[]{:S(2)}) async-start(bf16[4,256,256]{2,1,0:T(8,128)(2,1)} %bitcast.37), calls=%async_computation.1 | async-start | bytes 1048576 | tf_op jit(solution)/shard_map/all_to_all | solution.py:1133
  342.7 52.7 %reduce-scatter.6.cloned.1.call-start = ((), (), s32[]{:S(2)}) async-start(), calls=%async_computation.6 | async-start | bytes 2506752 | tf_op jit(solution)/shard_map/reduce_scatter | solution.py:1135
  346.2 86.9 %reduce-scatter.8.cloned.1.call-start = ((), (), s32[]{:S(2)}) async-start(), calls=%async_computation.7 | async-start | bytes 348160 | tf_op jit(solution)/shard_map/reduce_scatter | solution.py:1170
  391.9 21.3 %collective-permute-start.26 = (bf16[2,2,3,1024,128]{4,3,2,1,0:T(8,128)(2,1)}, bf16[2,2,3,1024,128]{4,3,2,1,0:T(8,128)(2,1)S(1)}, u32[]{:S(2)}, u32[]{:S(2)}) collective-permute-start(bf16[2,2,3,1024,128]{4,3,2,1,0:T(8,128)(2,1)} %get-tuple-element.128), channel_id=1, source_target_pairs={{0,4},{4,0},{8,12},{12,8},{16,20},{20,16},{24,28},{28,24},{1,5},{5... | collective-permute-start | bytes 9437192 | tf_op jit(solution)/shard_map/ppermute | solution.py:1047
  392.0 37.6 %collective-permute-start.27 = (bf16[1,2,3,1024,128]{4,3,2,1,0:T(8,128)(2,1)}, bf16[1,2,3,1024,128]{4,3,2,1,0:T(8,128)(2,1)}, u32[]{:S(2)}, u32[]{:S(2)}) collective-permute-start(bf16[1,2,3,1024,128]{4,3,2,1,0:T(8,128)(2,1)} %get-tuple-element.125.refs_17_), channel_id=1, source_target_pairs={{0,8},{4,12},{8,0},{12,4},{16,24},{20,28},{24,16},{28,20},{1,9},{5... | collective-permute-start | bytes 4718600 | tf_op jit(solution)/shard_map/ppermute | solution.py:1047
  394.0 37.6 %collective-permute-start.28 = (bf16[1,2,3,1024,128]{4,3,2,1,0:T(8,128)(2,1)}, bf16[1,2,3,1024,128]{4,3,2,1,0:T(8,128)(2,1)}, u32[]{:S(2)}, u32[]{:S(2)}) collective-permute-start(bf16[1,2,3,1024,128]{4,3,2,1,0:T(8,128)(2,1)} %get-tuple-element.130), channel_id=1, source_target_pairs={{0,16},{4,20},{8,24},{12,28},{16,0},{20,4},{24,8},{28,12},{1,17},{... | collective-permute-start | bytes 4718600 | tf_op jit(solution)/shard_map/ppermute | solution.py:1047
  395.4 79.5 %reduce-scatter.4.cloned.1.call-start = ((), (), s32[]{:S(2)}) async-start(), calls=%async_computation.5 | async-start | bytes 1253376 | tf_op jit(solution)/shard_map/reduce_scatter | solution.py:1168
  412.6 54.9 %collective-permute-start.34 = (bf16[1,2,3,1024,128]{4,3,2,1,0:T(8,128)(2,1)}, bf16[1,2,3,1024,128]{4,3,2,1,0:T(8,128)(2,1)}, u32[]{:S(2)}, u32[]{:S(2)}) collective-permute-start(bf16[1,2,3,1024,128]{4,3,2,1,0:T(8,128)(2,1)} %get-tuple-element.126.refs_12_), channel_id=1, source_target_pairs={{0,8},{4,12},{8,0},{12,4},{16,24},{20,28},{24,16},{28,20},{1,9},{5... | collective-permute-start | bytes 4718600 | tf_op jit(solution)/shard_map/ppermute | solution.py:1047
  414.8 54.1 %collective-permute-start.35 = (bf16[1,2,3,1024,128]{4,3,2,1,0:T(8,128)(2,1)}, bf16[1,2,3,1024,128]{4,3,2,1,0:T(8,128)(2,1)}, u32[]{:S(2)}, u32[]{:S(2)}) collective-permute-start(bf16[1,2,3,1024,128]{4,3,2,1,0:T(8,128)(2,1)} %get-tuple-element.140), channel_id=1, source_target_pairs={{0,16},{4,20},{8,24},{12,28},{16,0},{20,4},{24,8},{28,12},{1,17},{... | collective-permute-start | bytes 4718600 | tf_op jit(solution)/shard_map/ppermute | solution.py:1047
  447.3 27.6 %collective-permute-start.30 = (bf16[256,1024]{1,0:T(8,128)(2,1)S(1)}, bf16[256,1024]{1,0:T(8,128)(2,1)S(1)}, u32[]{:S(2)}, u32[]{:S(2)}) collective-permute-start(bf16[256,1024]{1,0:T(8,128)(2,1)S(1)} %add_convert_fusion.2.refs_5_), channel_id=1, source_target_pairs={{0,1},{1,2},{2,3},{3,0},{4,5},{5,6},{6,7},{7,4},{8,9},{9,10},{10,1... | collective-permute-start | bytes 1572872 | tf_op jit(solution)/shard_map/ppermute | solution.py:1159
  (37 other events, 379.9 us)
Sparse Core Ops, SparseCore 0:
  10.5 29.4 all-gather.5
  41.8 37.7 all-gather.7
  346.8 42.3 reduce-scatter.5
  395.5 17.9 reduce-scatter.7
  416.5 39.2 reduce-scatter.3

commit v4 on v3

--- a/solution.py
+++ b/solution.py
@@ -1133,19 +1133,16 @@
     mixed_grads = lax.all_to_all(mixed_grad, "col", split_axis=0, concat_axis=0, tiled=True)
     pack = out_wgrad(mixed_own, branch, small)
     out_sum = lax.psum_scatter(pack, "row", scatter_dimension=0, tiled=True)
-    q2a, q4b = wgrads(
-        (4, 9), ((0, 0), (1, 0)), [r53], ((0, 0), (0, 3)), after=[pack, mixed_grads, far_x, far_y]
-    )
+    q2a, q4b, p1 = wgrads(
+        (4, 9, 2, 3),
+        ((0, 0), (1, 0), (2, 0), (2, 1)),
+        [r53],
+        ((0, 0), (0, 3), None, None),
+        after=[pack, mixed_grads, far_x, far_y],
+    )
+    r1 = swap(p1, CORE)
     x2a, y4b = swap(q2a, ACROSS_X), swap(q4b, ACROSS_Y)
-    q2b, q4a, p1 = wgrads(
-        (5, 8, 2, 3),
-        ((0, 0), (1, 0), (2, 0), (2, 1)),
-        [r53, far_y, far_x],
-        ((0, 1), (0, 2), None, None),
-        {0: 1, 1: 2},
-        [q2a],
-    )
-    r1 = swap(p1, CORE)
+    q2b, q4a = wgrads((5, 8), ((0, 0), (1, 0)), [r53, far_y, far_x], ((0, 1), (0, 2)), {0: 1, 1: 2}, [q2a])
     x2b, y4a = swap(q2b, ACROSS_X), swap(q4a, ACROSS_Y)
     qkv_wgrad, *back_parts = attend_back(
         spots, mixed_grads, mixed_all, q, k, v, lse, attn_in, w_qkv, cosine, sine, gains, [q2b]

time: 502 us -> 493 us (0.982)
  waiting for transfers between devices: 166 us -> 157 us
    ppermute x18, waiting for transfers between devices: 48.5 us -> 39.4 us  [swap(): return lax.ppermute(value, 'row', [(i, i ^ mask) for i in range(8)])]
  transfers between devices with their start and end apart: 43 -> 43, of which waited for: 22 -> 19; matrix products, arithmetic and copies ran while one was open for 4% -> 5% of each run, Pallas kernels for 36% -> 36%
where the time goes in v4:
time: 493 us; the launch traced here: 484 us
  Pallas kernels  215 us (44%)
  waiting for transfers between devices  157 us (32%)
  starting transfers between devices  41.9 us (8%)
  other arithmetic  21.3 us (4%)
  local copies, waits for them, and re-layouts  17.6 us (4%)
  blocking collectives  16.1 us (3%)
  between operations  15.4 us (3%)
    pallas_call x4, Pallas kernels, experts(): pl.pallas_call(behind(expert_kernel, 12, after), out_shape=(jax.ShapeDtyp...  86.9 us
    ppermute x7, waiting for transfers between devices, ring_gather(): chunks.append(lax.ppermute(chunks[-1], 'col', steps))  73.4 us
    pallas_call x7, Pallas kernels, expert_wgrads(): pl.pallas_call(behind(kernel, 14 + len(extras), after), grid=(count,), ou...  66.1 us
    ppermute x18, waiting for transfers between devices, swap(): return lax.ppermute(value, 'row', [(i, i ^ mask) for i in range(8)])  39.4 us
    pallas_call x1, Pallas kernels, attend_back(): pl.pallas_call(behind(attend_back_kernel, 12, after), out_shape=shapes, i...  17 us
    all_gather x1, blocking collectives, fast(): pack_out = lax.all_gather(pack_out, 'col', axis=0)  16.1 us
    ppermute x18, starting transfers between devices, swap(): return lax.ppermute(value, 'row', [(i, i ^ mask) for i in range(8)])  14.4 us
    ppermute x1, waiting for transfers between devices, fast(): moving = lax.ppermute(moving, 'col', steps)  13.5 us
  transfers between devices with their start and end apart: 43, of which 19 were waited for; matrix products, arithmetic and copies ran while one was open for 5% of the time, Pallas kernels for 36%

profile of v4, /device:TPU:0, one launch (start us, length us, event | category | flops | bytes accessed | tf_op | source)
XLA Modules:
  0.0 484.0 jit_solution(5422332807284037579)
XLA Ops:
  12.5 16.1 %all-gather.1 = bf16[544,256]{1,0:T(8,128)(2,1)} all-gather(bf16[136,256]{1,0:T(8,128)(2,1)S(1)} %fusion.9), channel_id=3, replica_groups=mesh['row'=8,'col'=4] {'col'}, dimensions={0}, use_global_device_ids=true | all-gather | bytes 348160 | tf_op jit(solution)/shard_map/all_gather | solution.py:1078
  46.1 12.3 %collective-permute-done.1.refs_3_ = bf16[256,1024]{1,0:T(8,128)(2,1)S(1)} collective-permute-done((bf16[256,1024]{1,0:T(8,128)(2,1)}, bf16[256,1024]{1,0:T(8,128)(2,1)S(1)}, u32[]{:S(2)}, u32[]{:S(2)}) %collective-permute-start.1) | collective-permute-done | bytes 524320 | tf_op jit(solution)/shard_map/ppermute | solution.py:1018
  59.2 11.2 %collective-permute-done.2.refs_4_ = bf16[256,1024]{1,0:T(8,128)(2,1)S(1)} collective-permute-done((bf16[256,1024]{1,0:T(8,128)(2,1)S(1)}, bf16[256,1024]{1,0:T(8,128)(2,1)S(1)}, u32[]{:S(2)}, u32[]{:S(2)}) %collective-permute-start.2) | collective-permute-done | bytes 524320 | tf_op jit(solution)/shard_map/ppermute | solution.py:1018
  74.5 12.1 %shard_map.238 = (bf16[1024,1024]{1,0:T(8,128)(2,1)}, bf16[4,1024,64]{2,1,0:T(8,128)(2,1)}, bf16[2,1024,64]{2,1,0:T(8,128)(2,1)}, bf16[2,1024,64]{2,1,0:T(8,128)...) custom-call(s32[3]{0:T(128)} %pad_add_fusion.refs_0_, ...), custom_call_target="tpu_custom_call" | custom-call | flops 10000000 | bytes 100000 | tf_op jit(solution)/shard_map/pallas_call | solution.py:498
  86.7 5.7 %all-to-all-start = ((bf16[4,256,256]{2,1,0:T(8,128)(2,1)}), bf16[4,256,256]{2,1,0:T(8,128)(2,1)}, u32[]{:S(2)}, u32[]{:S(2)}) async-start(bf16[4,256,256]{2,1,0:T(8,128)(2,1)} %bitcast.30), calls=%async_computation | async-start | bytes 1048576 | tf_op jit(solution)/shard_map/all_to_all | solution.py:1093
  92.4 11.3 %collective-permute-done.7.refs_2_.refs_1_.refs_6_ = bf16[256,1024]{1,0:T(8,128)(2,1)} collective-permute-done((bf16[256,1024]{1,0:T(8,128)(2,1)}, bf16[256,1024]{1,0:T(8,128)(2,1)}, u32[]{:S(2)}, u32[]{:S(2)}) %collective-permute-start.7) | collective-permute-done | bytes 524320 | tf_op jit(solution)/shard_map/ppermute | solution.py:1018
  110.1 5.2 %shard_map.239 = (bf16[2,3,1024,128]{3,2,1,0:T(8,128)(2,1)}, bf16[2,3,1024,128]{3,2,1,0:T(8,128)(2,1)}) custom-call(bf16[4,3,1024,128]{3,2,1,0:T(8,128)(2,1)} %collective-permute-done.4.refs_0_.refs_4_, bf16[4,3,1024,128]{3,2,1,0:T(8,128)(2,1)} %collective-permute-done.5.refs_1_.refs_6_, bf16[256,1024]{1,0:T(8,128)(2,1)} %collective-permute-done.7.refs_2_.refs_1_.refs_6_), custom_call_target="tpu_custom_call" | custom-call | flops 3000000 | bytes 100000 | tf_op jit(solution)/shard_map/pallas_call | solution.py:914
  125.1 15.9 %collective-permute-done.9.refs_0_.refs_1_ = bf16[256,1152]{1,0:T(8,128)(2,1)S(1)} collective-permute-done((bf16[256,1152]{1,0:T(8,128)(2,1)}, bf16[256,1152]{1,0:T(8,128)(2,1)S(1)}, u32[]{:S(2)}, u32[]{:S(2)}) %collective-permute-start.9) | collective-permute-done | bytes 589856 | tf_op jit(solution)/shard_map/ppermute | solution.py:1018
  141.0 9.5 %collective-permute-done.13.refs_9_ = bf16[2,3,1024,128]{3,2,1,0:T(8,128)(2,1)} collective-permute-done((bf16[2,3,1024,128]{3,2,1,0:T(8,128)(2,1)}, bf16[2,3,1024,128]{3,2,1,0:T(8,128)(2,1)}, u32[]{:S(2)}, u32[]{:S(2)}) %collective-permute-start.13) | collective-permute-done | bytes 1572896 | tf_op jit(solution)/shard_map/ppermute | solution.py:1047
  150.5 5.5 %collective-permute-done.14.refs_0_.refs_2_ = bf16[256,1152]{1,0:T(8,128)(2,1)S(1)} collective-permute-done((bf16[256,1152]{1,0:T(8,128)(2,1)S(1)}, bf16[256,1152]{1,0:T(8,128)(2,1)S(1)}, u32[]{:S(2)}, u32[]{:S(2)}) %collective-permute-start.14) | collective-permute-done | bytes 589856 | tf_op jit(solution)/shard_map/ppermute | solution.py:1018
  156.6 17.1 %collective-permute-done.17.refs_12_.refs_3_.refs_0_ = bf16[256,1152]{1,0:T(8,128)(2,1)S(1)} collective-permute-done((bf16[256,1152]{1,0:T(8,128)(2,1)S(1)}, bf16[256,1152]{1,0:T(8,128)(2,1)S(1)}, u32[]{:S(2)}, u32[]{:S(2)}) %collective-permute-start.17) | collective-permute-done | bytes 589856 | tf_op jit(solution)/shard_map/ppermute | solution.py:1018
  176.2 21.6 %shard_map.241 = (bf16[256,2176]{1,0:T(8,128)(2,1)}, bf16[256,4096]{1,0:T(8,128)(2,1)}, bf16[256,4096]{1,0:T(8,128)(2,1)}, bf16[256,4096]{1,0:T(8,128)(2,1)}) custom-call(bf16[256,1152]{1,0:T(8,128)(2,1)} %copy-done.13, bf16[256,1024]{1,0:T(8,128)(2,1)} %collective-permute-done.6.refs_1_.refs_5_, bf16[4,3,1024,128]{3,2,1,0:T(8,128)(2,1)} %copy-done, ...), custom_call_target="tpu_custom_call" | custom-call | flops 21000000 | bytes 100000 | tf_op jit(solution)/shard_map/pallas_call | solution.py:724
  197.9 21.7 %shard_map.242 = (bf16[256,2176]{1,0:T(8,128)(2,1)}, bf16[256,4096]{1,0:T(8,128)(2,1)}, bf16[256,4096]{1,0:T(8,128)(2,1)}, bf16[256,4096]{1,0:T(8,128)(2,1)}) custom-call(bf16[256,1152]{1,0:T(8,128)(2,1)} %copy-done.12, bf16[256,1024]{1,0:T(8,128)(2,1)} %collective-permute-done.7.refs_2_.refs_1_.refs_6_, bf16[4,3,1024,128]{3,2,1,0:T(8,128)(2,1)} %copy-done, ...), custom_call_target="tpu_custom_call" | custom-call | flops 21000000 | bytes 100000 | tf_op jit(solution)/shard_map/pallas_call | solution.py:724
  219.6 6.0 %collective-permute-done.18.refs_13_ = bf16[256,2176]{1,0:T(8,128)(2,1)S(1)} collective-permute-done((bf16[256,2176]{1,0:T(8,128)(2,1)}, bf16[256,2176]{1,0:T(8,128)(2,1)S(1)}, u32[]{:S(2)}, u32[]{:S(2)}) %collective-permute-start.18) | collective-permute-done | bytes 1114144 | tf_op jit(solution)/shard_map/ppermute | solution.py:1117
  227.5 5.3 %shard_map.243 = (bf16[1024,1024]{1,0:T(8,128)(2,1)}, bf16[1024,1024]{1,0:T(8,128)(2,1)}) custom-call(bf16[256,1152]{1,0:T(8,128)(2,1)} %get-tuple-element.86.refs_0_.refs_10_, bf16[256,1152]{1,0:T(8,128)(2,1)} %copy-done.13, bf16[256,1152]{1,0:T(8,128)(2,1)} %copy-done.12, bf16[256,1152]{1,0:T(8,128)(2,1)} %copy-done.6, bf16[256,1024]{1,0:T(8,128)(2,1)} %refs_7_.1, ...), custom_call_target="tpu_custom_call" | custom-call | flops 2000000 | bytes 100000 | tf_op jit(solution)/shard_map/pallas_call | solution.py:755
  232.8 21.7 %shard_map.244 = (bf16[256,2176]{1,0:T(8,128)(2,1)}, bf16[256,4096]{1,0:T(8,128)(2,1)}, bf16[256,4096]{1,0:T(8,128)(2,1)}, bf16[256,4096]{1,0:T(8,128)(2,1)}) custom-call(bf16[256,1152]{1,0:T(8,128)(2,1)} %copy-done.6, bf16[256,1024]{1,0:T(8,128)(2,1)} %collective-permute-done.8.refs_7_.refs_1_, bf16[4,3,1024,128]{3,2,1,0:T(8,128)(2,1)} %copy-done, ...), custom_call_target="tpu_custom_call" | custom-call | flops 21000000 | bytes 100000 | tf_op jit(solution)/shard_map/pallas_call | solution.py:724
  256.5 10.1 %collective-permute-start.20 = (bf16[256,2176]{1,0:T(8,128)(2,1)S(1)}, bf16[256,2176]{1,0:T(8,128)(2,1)S(1)}, u32[]{:S(2)}, u32[]{:S(2)}) collective-permute-start(bf16[256,2176]{1,0:T(8,128)(2,1)S(1)} %add_convert_fusion), channel_id=1, source_target_pairs={{0,1},{1,2},{2,3},{3,0},{4,5},{5,6},{6,7},{7,4},{8,9},{9,10},{10,1... | collective-permute-start | bytes 3342344 | tf_op jit(solution)/shard_map/ppermute | solution.py:1117
  266.6 21.7 %shard_map.245 = (bf16[256,2176]{1,0:T(8,128)(2,1)}, bf16[256,4096]{1,0:T(8,128)(2,1)}, bf16[256,4096]{1,0:T(8,128)(2,1)}, bf16[256,4096]{1,0:T(8,128)(2,1)}) custom-call(bf16[256,1152]{1,0:T(8,128)(2,1)} %get-tuple-element.86.refs_0_.refs_10_, bf16[256,1024]{1,0:T(8,128)(2,1)} %refs_7_.1, bf16[4,3,1024,128]{3,2,1,0:T(8,128)(2,1)} %copy-done, ...), custom_call_target="tpu_custom_call" | custom-call | flops 21000000 | bytes 100000 | tf_op jit(solution)/shard_map/pallas_call | solution.py:724
  294.2 8.0 %shard_map.246.refs_14_ = bf16[2,2,3,1024,128]{4,3,2,1,0:T(8,128)(2,1)} custom-call(bf16[1024,1024]{1,0:T(8,128)(2,1)} %get-tuple-element.94.refs_14_.refs_0_, bf16[1024,1024]{1,0:T(8,128)(2,1)} %get-tuple-element.103.refs_1_, bf16[256,4096]{1,0:T(8,128)(2,1)} %get-tuple-element.104.refs_2_, bf16[256,4096]{1,0:T(8,128)(2,1)} %get-tuple-element.91.refs_12_.refs_3_, ...), custom_call_target="tpu_custom_call" | custom-call | flops 4400000 | bytes 100000 | tf_op jit(solution)/shard_map/pallas_call | solution.py:863
  302.2 8.0 %shard_map.247.refs_14_ = bf16[4,2,3,1024,128]{4,3,2,1,0:T(8,128)(2,1)} custom-call(bf16[1024,1024]{1,0:T(8,128)(2,1)} %get-tuple-element.94.refs_14_.refs_0_, bf16[1024,1024]{1,0:T(8,128)(2,1)} %get-tuple-element.103.refs_1_, bf16[256,4096]{1,0:T(8,128)(2,1)} %get-tuple-element.104.refs_2_, bf16[256,4096]{1,0:T(8,128)(2,1)} %get-tuple-element.91.refs_12_.refs_3_, ...), custom_call_target="tpu_custom_call" | custom-call | flops 4400000 | bytes 100000 | tf_op jit(solution)/shard_map/pallas_call | solution.py:863
  311.9 7.9 %shard_map.248.refs_15_ = bf16[4,2,3,1024,128]{4,3,2,1,0:T(8,128)(2,1)} custom-call(bf16[1024,1024]{1,0:T(8,128)(2,1)} %get-tuple-element.94.refs_14_.refs_0_, bf16[1024,1024]{1,0:T(8,128)(2,1)} %get-tuple-element.103.refs_1_, bf16[256,4096]{1,0:T(8,128)(2,1)} %get-tuple-element.104.refs_2_, ...), custom_call_target="tpu_custom_call", output_to_operand_aliasing={{}: (14, {})} | custom-call | flops 4400000 | bytes 100000 | tf_op jit(solution)/shard_map/pallas_call | solution.py:863
  320.4 9.4 %shard_map.249 = (bf16[1,2,3,1024,128]{4,3,2,1,0:T(8,128)(2,1)}, bf16[1,2,3,1024,128]{4,3,2,1,0:T(8,128)(2,1)}) custom-call(bf16[1024,1024]{1,0:T(8,128)(2,1)} %get-tuple-element.94.refs_14_.refs_0_, bf16[1024,1024]{1,0:T(8,128)(2,1)} %get-tuple-element.103.refs_1_, bf16[256,4096]{1,0:T(8,128)(2,1)} %get-tuple-element.104.refs_2_, ...), custom_call_target="tpu_custom_call" | custom-call | flops 4400000 | bytes 100000 | tf_op jit(solution)/shard_map/pallas_call | solution.py:863
  332.5 6.0 %shard_map.250 = (f32[256,1024]{1,0:T(8,128)}, f32[256,1024]{1,0:T(8,128)}, bf16[256,1024]{1,0:T(8,128)(2,1)}, bf16[1024,256]{1,0:T(8,128)(2,1)}, f32[136,1024]{1,0:T(8,128)}) custom-call(s32[3]{0:T(128)} %pad_add_fusion.refs_0_, bf16[256,2176]{1,0:T(8,128)(2,1)} %copy-done.8, bf16[256,2176]{1,0:T(8,128)(2,1)} %get-tuple-element.97.refs_2_, ...), custom_call_target="tpu_custom_call" | custom-call | flops 2000000 | bytes 100000 | tf_op jit(solution)/shard_map/pallas_call | solution.py:962
  346.2 10.9 %all-to-all-done.1 = bf16[4,256,256]{2,1,0:T(8,128)(2,1)} async-done(((bf16[4,256,256]{2,1,0:T(8,128)(2,1)}), bf16[4,256,256]{2,1,0:T(8,128)(2,1)}, u32[]{:S(2)}, u32[]{:S(2)}) %all-to-all-start.1) | async-done | bytes 524320 | tf_op jit(solution)/shard_map/all_to_all | solution.py:1133
  357.1 9.2 %collective-permute-done.23.refs_18_.refs_15_ = bf16[1,2,3,1024,128]{4,3,2,1,0:T(8,128)(2,1)S(1)} collective-permute-done((bf16[1,2,3,1024,128]{4,3,2,1,0:T(8,128)(2,1)}, bf16[1,2,3,1024,128]{4,3,2,1,0:T(8,128)(2,1)S(1)}, u32[]{:S(2)}, u32[]{:S(2)}) %collective-permute-start.23) | collective-permute-done | bytes 1572896 | tf_op jit(solution)/shard_map/ppermute | solution.py:1047
  368.1 13.3 %shard_map.252 = (bf16[1,2,3,1024,128]{4,3,2,1,0:T(8,128)(2,1)}, bf16[1,2,3,1024,128]{4,3,2,1,0:T(8,128)(2,1)}, bf16[2,2,3,1024,128]{4,3,2,1,0:T(8,128)(2,1)}) custom-call(bf16[1024,1024]{1,0:T(8,128)(2,1)} %get-tuple-element.94.refs_14_.refs_0_, bf16[1024,1024]{1,0:T(8,128)(2,1)} %get-tuple-element.103.refs_1_, ...), custom_call_target="tpu_custom_call" | custom-call | flops 8800000 | bytes 100000 | tf_op jit(solution)/shard_map/pallas_call | solution.py:863
  384.9 10.1 %shard_map.253 = (bf16[1,2,3,1024,128]{4,3,2,1,0:T(8,128)(2,1)}, bf16[1,2,3,1024,128]{4,3,2,1,0:T(8,128)(2,1)}) custom-call(bf16[1024,1024]{1,0:T(8,128)(2,1)} %get-tuple-element.94.refs_14_.refs_0_, bf16[1024,1024]{1,0:T(8,128)(2,1)} %get-tuple-element.103.refs_1_, bf16[256,4096]{1,0:T(8,128)(2,1)} %get-tuple-element.104.refs_2_, ...), custom_call_target="tpu_custom_call" | custom-call | flops 4400000 | bytes 100000 | tf_op jit(solution)/shard_map/pallas_call | solution.py:863
  395.3 17.0 %shard_map.254 = (bf16[8,136,512]{2,1,0:T(8,128)(2,1)}, bf16[256,1024]{1,0:T(8,128)(2,1)}, bf16[256,1024]{1,0:T(8,128)(2,1)}, bf16[256,1024]{1,0:T(8,128)(2,1)}, bf16[256,1024]{1,0:T(8,128)(2,1)}) custom-call(s32[3]{0:T(128)} %pad_add_fusion.refs_0_, bf16[1024,256]{1,0:T(8,128)(2,1)} %bitcast.13.refs_16_.refs_1_, ...), custom_call_target="tpu_custom_call" | custom-call | flops 16000000 | bytes 100000 | tf_op jit(solution)/shard_map/pallas_call | solution.py:575
  415.0 9.4 %shard_map.255.refs_0_ = bf16[2,2,3,1024,128]{4,3,2,1,0:T(8,128)(2,1)} custom-call(bf16[1024,1024]{1,0:T(8,128)(2,1)} %get-tuple-element.94.refs_14_.refs_0_, bf16[1024,1024]{1,0:T(8,128)(2,1)} %get-tuple-element.103.refs_1_, bf16[256,4096]{1,0:T(8,128)(2,1)} %get-tuple-element.104.refs_2_, bf16[256,4096]{1,0:T(8,128)(2,1)} %get-tuple-element.91.refs_12_.refs_3_, ...), custom_call_target="tpu_custom_call" | custom-call | flops 4400000 | bytes 100000 | tf_op jit(solution)/shard_map/pallas_call | solution.py:863
  430.6 13.5 %collective-permute-done.29 = bf16[256,1024]{1,0:T(8,128)(2,1)S(1)} collective-permute-done((bf16[256,1024]{1,0:T(8,128)(2,1)S(1)}, bf16[256,1024]{1,0:T(8,128)(2,1)S(1)}, u32[]{:S(2)}, u32[]{:S(2)}) %collective-permute-start.29) | collective-permute-done | bytes 524320 | tf_op jit(solution)/shard_map/ppermute | solution.py:1153
  446.3 13.8 %collective-permute-done.34.refs_2_ = bf16[1,2,3,1024,128]{4,3,2,1,0:T(8,128)(2,1)} collective-permute-done((bf16[1,2,3,1024,128]{4,3,2,1,0:T(8,128)(2,1)}, bf16[1,2,3,1024,128]{4,3,2,1,0:T(8,128)(2,1)}, u32[]{:S(2)}, u32[]{:S(2)}) %collective-permute-start.34) | collective-permute-done | bytes 1572896 | tf_op jit(solution)/shard_map/ppermute | solution.py:1047
  460.1 5.8 %shard_map.257 = (f32[2,2,1024,128]{3,2,1,0:T(8,128)}, f32[2,2,1024,128]{3,2,1,0:T(8,128)}, f32[2,2,1024,128]{3,2,1,0:T(8,128)}) custom-call(bf16[2,2,3,1024,128]{4,3,2,1,0:T(8,128)(2,1)} %shard_map.255.refs_0_, bf16[1,2,3,1024,128]{4,3,2,1,0:T(8,128)(2,1)} %collective-permute-done.27.refs_1_, bf16[1,2,3,1024,128]{4,3,2,1,0:T(8,128)(2,1)} %collective-permute-done.34.refs_2_, ...), custom_call_target="tpu_custom_call" | custom-call | flops 5000000 | bytes 100000 | tf_op jit(solution)/shard_map/pallas_call | solution.py:893
  (165 shorter events, 96.0 us)
Async XLA Ops:
  7.2 67.3 %all-gather.6.cloned.1.call-start = ((), (), s32[]{:S(2)}) async-start(), calls=%async_computation.8 | async-start | bytes 1253376 | tf_op jit(solution)/shard_map/all_gather | solution.py:1079
  9.7 109.1 %all-gather.8.cloned.1.call-start = ((), (), s32[]{:S(2)}) async-start(), calls=%async_computation.9 | async-start | bytes 2506752 | tf_op jit(solution)/shard_map/all_gather | solution.py:1080
  12.0 62.5 %collective-permute-start.3 = (bf16[4,3,1024,128]{3,2,1,0:T(8,128)(2,1)S(1)}, bf16[4,3,1024,128]{3,2,1,0:T(8,128)(2,1)}, u32[]{:S(2)}, u32[]{:S(2)}) collective-permute-start(bf16[4,3,1024,128]{3,2,1,0:T(8,128)(2,1)S(1)} %pad_maximum_fusion.refs_2_), channel_id=1, source_target_pairs={{0,4},{4,0},{8,12},{12,8},{16,20},{20,16},{24,28},{28,24},{1,5},{5... | collective-permute-start | bytes 9437192 | tf_op jit(solution)/shard_map/ppermute | solution.py:1047
  28.6 80.3 %collective-permute-start.4 = (bf16[4,3,1024,128]{3,2,1,0:T(8,128)(2,1)S(1)}, bf16[4,3,1024,128]{3,2,1,0:T(8,128)(2,1)}, u32[]{:S(2)}, u32[]{:S(2)}) collective-permute-start(bf16[4,3,1024,128]{3,2,1,0:T(8,128)(2,1)S(1)} %pad_maximum_fusion.refs_2_), channel_id=1, source_target_pairs={{0,8},{4,12},{8,0},{12,4},{16,24},{20,28},{24,16},{28,20},{1,9},{5... | collective-permute-start | bytes 9437192 | tf_op jit(solution)/shard_map/ppermute | solution.py:1047
  30.2 79.9 %collective-permute-start.5 = (bf16[4,3,1024,128]{3,2,1,0:T(8,128)(2,1)S(1)}, bf16[4,3,1024,128]{3,2,1,0:T(8,128)(2,1)}, u32[]{:S(2)}, u32[]{:S(2)}) collective-permute-start(bf16[4,3,1024,128]{3,2,1,0:T(8,128)(2,1)S(1)} %pad_maximum_fusion.refs_2_), channel_id=1, source_target_pairs={{0,16},{4,20},{8,24},{12,28},{16,0},{20,4},{24,8},{28,12},{1,17},{... | collective-permute-start | bytes 9437192 | tf_op jit(solution)/shard_map/ppermute | solution.py:1047
  86.6 17.1 %collective-permute-start.7 = (bf16[256,1024]{1,0:T(8,128)(2,1)}, bf16[256,1024]{1,0:T(8,128)(2,1)}, u32[]{:S(2)}, u32[]{:S(2)}) collective-permute-start(bf16[256,1024]{1,0:T(8,128)(2,1)} %collective-permute-done.6.refs_1_.refs_5_), channel_id=1, source_target_pairs={{0,1},{1,2},{2,3},{3,0},{4,5},{5,6},{6,7},{7,4},{8,9},{9,10},{10,1... | collective-permute-start | bytes 1572872 | tf_op jit(solution)/shard_map/ppermute | solution.py:1018
  86.7 33.1 %all-to-all-start = ((bf16[4,256,256]{2,1,0:T(8,128)(2,1)}), bf16[4,256,256]{2,1,0:T(8,128)(2,1)}, u32[]{:S(2)}, u32[]{:S(2)}) async-start(bf16[4,256,256]{2,1,0:T(8,128)(2,1)} %bitcast.30), calls=%async_computation | async-start | bytes 1048576 | tf_op jit(solution)/shard_map/all_to_all | solution.py:1093
  103.8 21.0 %collective-permute-start.8 = (bf16[256,1024]{1,0:T(8,128)(2,1)}, bf16[256,1024]{1,0:T(8,128)(2,1)}, u32[]{:S(2)}, u32[]{:S(2)}) collective-permute-start(bf16[256,1024]{1,0:T(8,128)(2,1)} %collective-permute-done.7.refs_2_.refs_1_.refs_6_), channel_id=1, source_target_pairs={{0,1},{1,2},{2,3},{3,0},{4,5},{5,6},{6,7},{7,4},{8,9},{9,10},{10,1... | collective-permute-start | bytes 1572872 | tf_op jit(solution)/shard_map/ppermute | solution.py:1018
  115.4 35.2 %collective-permute-start.13 = (bf16[2,3,1024,128]{3,2,1,0:T(8,128)(2,1)}, bf16[2,3,1024,128]{3,2,1,0:T(8,128)(2,1)}, u32[]{:S(2)}, u32[]{:S(2)}) collective-permute-start(bf16[2,3,1024,128]{3,2,1,0:T(8,128)(2,1)} %get-tuple-element.87), channel_id=1, source_target_pairs={{0,16},{4,20},{8,24},{12,28},{16,0},{20,4},{24,8},{28,12},{1,17},{... | collective-permute-start | bytes 4718600 | tf_op jit(solution)/shard_map/ppermute | solution.py:1047
  116.9 39.2 %collective-permute-start.12 = (bf16[2,3,1024,128]{3,2,1,0:T(8,128)(2,1)}, bf16[2,3,1024,128]{3,2,1,0:T(8,128)(2,1)}, u32[]{:S(2)}, u32[]{:S(2)}) collective-permute-start(bf16[2,3,1024,128]{3,2,1,0:T(8,128)(2,1)} %get-tuple-element.84.refs_7_), channel_id=1, source_target_pairs={{0,8},{4,12},{8,0},{12,4},{16,24},{20,28},{24,16},{28,20},{1,9},{5... | collective-permute-start | bytes 4718600 | tf_op jit(solution)/shard_map/ppermute | solution.py:1047
  117.4 56.3 %collective-permute-start.10 = (bf16[4,3,1024,128]{3,2,1,0:T(8,128)(2,1)}, bf16[4,3,1024,128]{3,2,1,0:T(8,128)(2,1)S(1)}, u32[]{:S(2)}, u32[]{:S(2)}) collective-permute-start(bf16[4,3,1024,128]{3,2,1,0:T(8,128)(2,1)} %collective-permute-done.4.refs_0_.refs_4_), channel_id=1, source_target_pairs={{0,4},{4,0},{8,12},{12,8},{16,20},{20,16},{24,28},{28,24},{1,5},{5... | collective-permute-start | bytes 9437192 | tf_op jit(solution)/shard_map/ppermute | solution.py:1047
  117.4 57.1 %collective-permute-start.11 = (bf16[4,3,1024,128]{3,2,1,0:T(8,128)(2,1)}, bf16[4,3,1024,128]{3,2,1,0:T(8,128)(2,1)}, u32[]{:S(2)}, u32[]{:S(2)}) collective-permute-start(bf16[4,3,1024,128]{3,2,1,0:T(8,128)(2,1)} %collective-permute-done.5.refs_1_.refs_6_), channel_id=1, source_target_pairs={{0,4},{4,0},{8,12},{12,8},{16,20},{20,16},{24,28},{28,24},{1,5},{5... | collective-permute-start | bytes 9437192 | tf_op jit(solution)/shard_map/ppermute | solution.py:1047
  124.8 16.2 %collective-permute-start.9 = (bf16[256,1152]{1,0:T(8,128)(2,1)}, bf16[256,1152]{1,0:T(8,128)(2,1)S(1)}, u32[]{:S(2)}, u32[]{:S(2)}) collective-permute-start(bf16[256,1152]{1,0:T(8,128)(2,1)} %get-tuple-element.86.refs_0_.refs_10_), channel_id=1, source_target_pairs={{0,1},{1,2},{2,3},{3,0},{4,5},{5,6},{6,7},{7,4},{8,9},{9,10},{10,1... | collective-permute-start | bytes 1769480 | tf_op jit(solution)/shard_map/ppermute | solution.py:1018
  156.1 18.5 %collective-permute-start.16 = (bf16[2,3,1024,128]{3,2,1,0:T(8,128)(2,1)}, bf16[2,3,1024,128]{3,2,1,0:T(8,128)(2,1)}, u32[]{:S(2)}, u32[]{:S(2)}) collective-permute-start(bf16[2,3,1024,128]{3,2,1,0:T(8,128)(2,1)} %collective-permute-done.13.refs_9_), channel_id=1, source_target_pairs={{0,4},{4,0},{8,12},{12,8},{16,20},{20,16},{24,28},{28,24},{1,5},{5... | collective-permute-start | bytes 4718600 | tf_op jit(solution)/shard_map/ppermute | solution.py:1047
  156.1 18.4 %collective-permute-start.15 = (bf16[2,3,1024,128]{3,2,1,0:T(8,128)(2,1)}, bf16[2,3,1024,128]{3,2,1,0:T(8,128)(2,1)}, u32[]{:S(2)}, u32[]{:S(2)}) collective-permute-start(bf16[2,3,1024,128]{3,2,1,0:T(8,128)(2,1)} %collective-permute-done.12.refs_8_), channel_id=1, source_target_pairs={{0,4},{4,0},{8,12},{12,8},{16,20},{20,16},{24,28},{28,24},{1,5},{5... | collective-permute-start | bytes 4718600 | tf_op jit(solution)/shard_map/ppermute | solution.py:1047
  156.6 17.1 %collective-permute-start.17 = (bf16[256,1152]{1,0:T(8,128)(2,1)S(1)}, bf16[256,1152]{1,0:T(8,128)(2,1)S(1)}, u32[]{:S(2)}, u32[]{:S(2)}) collective-permute-start(bf16[256,1152]{1,0:T(8,128)(2,1)S(1)} %collective-permute-done.14.refs_0_.refs_2_), channel_id=1, source_target_pairs={{0,1},{1,2},{2,3},{3,0},{4,5},{5,6},{6,7},{7,4},{8,9},{9,10},{10,1... | collective-permute-start | bytes 1769480 | tf_op jit(solution)/shard_map/ppermute | solution.py:1018
  197.8 27.8 %collective-permute-start.18 = (bf16[256,2176]{1,0:T(8,128)(2,1)}, bf16[256,2176]{1,0:T(8,128)(2,1)S(1)}, u32[]{:S(2)}, u32[]{:S(2)}) collective-permute-start(bf16[256,2176]{1,0:T(8,128)(2,1)} %get-tuple-element.90), channel_id=1, source_target_pairs={{0,1},{1,2},{2,3},{3,0},{4,5},{5,6},{6,7},{7,4},{8,9},{9,10},{10,1... | collective-permute-start | bytes 3342344 | tf_op jit(solution)/shard_map/ppermute | solution.py:1117
  227.5 27.1 %collective-permute-start.19 = (bf16[256,2176]{1,0:T(8,128)(2,1)S(1)}, bf16[256,2176]{1,0:T(8,128)(2,1)S(1)}, u32[]{:S(2)}, u32[]{:S(2)}) collective-permute-start(bf16[256,2176]{1,0:T(8,128)(2,1)S(1)} %add_convert_fusion.1), channel_id=1, source_target_pairs={{0,1},{1,2},{2,3},{3,0},{4,5},{5,6},{6,7},{7,4},{8,9},{9,10},{10,1... | collective-permute-start | bytes 3342344 | tf_op jit(solution)/shard_map/ppermute | solution.py:1117
  256.5 36.7 %collective-permute-start.20 = (bf16[256,2176]{1,0:T(8,128)(2,1)S(1)}, bf16[256,2176]{1,0:T(8,128)(2,1)S(1)}, u32[]{:S(2)}, u32[]{:S(2)}) collective-permute-start(bf16[256,2176]{1,0:T(8,128)(2,1)S(1)} %add_convert_fusion), channel_id=1, source_target_pairs={{0,1},{1,2},{2,3},{3,0},{4,5},{5,6},{6,7},{7,4},{8,9},{9,10},{10,1... | collective-permute-start | bytes 3342344 | tf_op jit(solution)/shard_map/ppermute | solution.py:1117
  319.8 47.2 %collective-permute-start.22 = (bf16[4,2,3,1024,128]{4,3,2,1,0:T(8,128)(2,1)}, bf16[4,2,3,1024,128]{4,3,2,1,0:T(8,128)(2,1)}, u32[]{:S(2)}, u32[]{:S(2)}) collective-permute-start(bf16[4,2,3,1024,128]{4,3,2,1,0:T(8,128)(2,1)} %shard_map.248.refs_15_), channel_id=1, source_target_pairs={{0,4},{4,0},{8,12},{12,8},{16,20},{20,16},{24,28},{28,24},{1,5},{5... | collective-permute-start | bytes 18874376 | tf_op jit(solution)/shard_map/ppermute | solution.py:1047
  329.7 36.6 %collective-permute-start.23 = (bf16[1,2,3,1024,128]{4,3,2,1,0:T(8,128)(2,1)}, bf16[1,2,3,1024,128]{4,3,2,1,0:T(8,128)(2,1)S(1)}, u32[]{:S(2)}, u32[]{:S(2)}) collective-permute-start(bf16[1,2,3,1024,128]{4,3,2,1,0:T(8,128)(2,1)} %get-tuple-element.122), channel_id=1, source_target_pairs={{0,16},{4,20},{8,24},{12,28},{16,0},{20,4},{24,8},{28,12},{1,17},{... | collective-permute-start | bytes 4718600 | tf_op jit(solution)/shard_map/ppermute | solution.py:1047
  330.0 37.0 %collective-permute-start.24 = (bf16[1,2,3,1024,128]{4,3,2,1,0:T(8,128)(2,1)}, bf16[1,2,3,1024,128]{4,3,2,1,0:T(8,128)(2,1)S(1)}, u32[]{:S(2)}, u32[]{:S(2)}) collective-permute-start(bf16[1,2,3,1024,128]{4,3,2,1,0:T(8,128)(2,1)} %get-tuple-element.113.refs_11_), channel_id=1, source_target_pairs={{0,8},{4,12},{8,0},{12,4},{16,24},{20,28},{24,16},{28,20},{1,9},{5... | collective-permute-start | bytes 4718600 | tf_op jit(solution)/shard_map/ppermute | solution.py:1047
  338.5 18.6 %all-to-all-start.1 = ((bf16[4,256,256]{2,1,0:T(8,128)(2,1)}), bf16[4,256,256]{2,1,0:T(8,128)(2,1)}, u32[]{:S(2)}, u32[]{:S(2)}) async-start(bf16[4,256,256]{2,1,0:T(8,128)(2,1)} %bitcast.37), calls=%async_computation.1 | async-start | bytes 1048576 | tf_op jit(solution)/shard_map/all_to_all | solution.py:1133
  342.6 52.4 %reduce-scatter.6.cloned.1.call-start = ((), (), s32[]{:S(2)}) async-start(), calls=%async_computation.6 | async-start | bytes 2506752 | tf_op jit(solution)/shard_map/reduce_scatter | solution.py:1135
  346.2 83.6 %reduce-scatter.8.cloned.1.call-start = ((), (), s32[]{:S(2)}) async-start(), calls=%async_computation.7 | async-start | bytes 348160 | tf_op jit(solution)/shard_map/reduce_scatter | solution.py:1167
  381.4 31.5 %collective-permute-start.26 = (bf16[2,2,3,1024,128]{4,3,2,1,0:T(8,128)(2,1)}, bf16[2,2,3,1024,128]{4,3,2,1,0:T(8,128)(2,1)S(1)}, u32[]{:S(2)}, u32[]{:S(2)}) collective-permute-start(bf16[2,2,3,1024,128]{4,3,2,1,0:T(8,128)(2,1)} %get-tuple-element.128), channel_id=1, source_target_pairs={{0,4},{4,0},{8,12},{12,8},{16,20},{20,16},{24,28},{28,24},{1,5},{5... | collective-permute-start | bytes 9437192 | tf_op jit(solution)/shard_map/ppermute | solution.py:1047
  381.5 46.7 %collective-permute-start.27 = (bf16[1,2,3,1024,128]{4,3,2,1,0:T(8,128)(2,1)}, bf16[1,2,3,1024,128]{4,3,2,1,0:T(8,128)(2,1)}, u32[]{:S(2)}, u32[]{:S(2)}) collective-permute-start(bf16[1,2,3,1024,128]{4,3,2,1,0:T(8,128)(2,1)} %get-tuple-element.125.refs_17_), channel_id=1, source_target_pairs={{0,8},{4,12},{8,0},{12,4},{16,24},{20,28},{24,16},{28,20},{1,9},{5... | collective-permute-start | bytes 4718600 | tf_op jit(solution)/shard_map/ppermute | solution.py:1047
  383.6 44.6 %collective-permute-start.28 = (bf16[1,2,3,1024,128]{4,3,2,1,0:T(8,128)(2,1)}, bf16[1,2,3,1024,128]{4,3,2,1,0:T(8,128)(2,1)}, u32[]{:S(2)}, u32[]{:S(2)}) collective-permute-start(bf16[1,2,3,1024,128]{4,3,2,1,0:T(8,128)(2,1)} %get-tuple-element.130), channel_id=1, source_target_pairs={{0,16},{4,20},{8,24},{12,28},{16,0},{20,4},{24,8},{28,12},{1,17},{... | collective-permute-start | bytes 4718600 | tf_op jit(solution)/shard_map/ppermute | solution.py:1047
  395.1 70.9 %reduce-scatter.4.cloned.1.call-start = ((), (), s32[]{:S(2)}) async-start(), calls=%async_computation.5 | async-start | bytes 1253376 | tf_op jit(solution)/shard_map/reduce_scatter | solution.py:1165
  412.3 47.7 %collective-permute-start.34 = (bf16[1,2,3,1024,128]{4,3,2,1,0:T(8,128)(2,1)}, bf16[1,2,3,1024,128]{4,3,2,1,0:T(8,128)(2,1)}, u32[]{:S(2)}, u32[]{:S(2)}) collective-permute-start(bf16[1,2,3,1024,128]{4,3,2,1,0:T(8,128)(2,1)} %get-tuple-element.126.refs_12_), channel_id=1, source_target_pairs={{0,8},{4,12},{8,0},{12,4},{16,24},{20,28},{24,16},{28,20},{1,9},{5... | collective-permute-start | bytes 4718600 | tf_op jit(solution)/shard_map/ppermute | solution.py:1047
  414.6 45.5 %collective-permute-start.35 = (bf16[1,2,3,1024,128]{4,3,2,1,0:T(8,128)(2,1)}, bf16[1,2,3,1024,128]{4,3,2,1,0:T(8,128)(2,1)}, u32[]{:S(2)}, u32[]{:S(2)}) collective-permute-start(bf16[1,2,3,1024,128]{4,3,2,1,0:T(8,128)(2,1)} %get-tuple-element.140), channel_id=1, source_target_pairs={{0,16},{4,20},{8,24},{12,28},{16,0},{20,4},{24,8},{28,12},{1,17},{... | collective-permute-start | bytes 4718600 | tf_op jit(solution)/shard_map/ppermute | solution.py:1047
  444.3 21.6 %collective-permute-start.30 = (bf16[256,1024]{1,0:T(8,128)(2,1)S(1)}, bf16[256,1024]{1,0:T(8,128)(2,1)S(1)}, u32[]{:S(2)}, u32[]{:S(2)}) collective-permute-start(bf16[256,1024]{1,0:T(8,128)(2,1)S(1)} %add_convert_fusion.2.refs_5_), channel_id=1, source_target_pairs={{0,1},{1,2},{2,3},{3,0},{4,5},{5,6},{6,7},{7,4},{8,9},{9,10},{10,1... | collective-permute-start | bytes 1572872 | tf_op jit(solution)/shard_map/ppermute | solution.py:1156
  (37 other events, 357.0 us)
Sparse Core Ops, SparseCore 0:
  10.5 29.4 all-gather.5
  41.8 37.7 all-gather.7
  346.8 45.3 reduce-scatter.5
  395.2 18.9 reduce-scatter.7
  417.3 39.3 reduce-scatter.3

commit v5 on v4

--- a/solution.py
+++ b/solution.py
@@ -1133,16 +1133,16 @@
     mixed_grads = lax.all_to_all(mixed_grad, "col", split_axis=0, concat_axis=0, tiled=True)
     pack = out_wgrad(mixed_own, branch, small)
     out_sum = lax.psum_scatter(pack, "row", scatter_dimension=0, tiled=True)
-    q2a, q4b, p1 = wgrads(
-        (4, 9, 2, 3),
-        ((0, 0), (1, 0), (2, 0), (2, 1)),
-        [r53],
-        ((0, 0), (0, 3), None, None),
-        after=[pack, mixed_grads, far_x, far_y],
-    )
+    q2a, q4b, q2b, q4a, p1 = wgrads(
+        (4, 9, 5, 8, 2, 3),
+        ((0, 0), (1, 0), (2, 0), (3, 0), (4, 0), (4, 1)),
+        [r53, far_y, far_x],
+        ((0, 0), (0, 3), (0, 1), (0, 2), None, None),
+        {2: 1, 3: 2},
+        [pack, mixed_grads],
+    )
+    x2a, y4b = swap(q2a, ACROSS_X), swap(q4b, ACROSS_Y)
     r1 = swap(p1, CORE)
-    x2a, y4b = swap(q2a, ACROSS_X), swap(q4b, ACROSS_Y)
-    q2b, q4a = wgrads((5, 8), ((0, 0), (1, 0)), [r53, far_y, far_x], ((0, 1), (0, 2)), {0: 1, 1: 2}, [q2a])
     x2b, y4a = swap(q2b, ACROSS_X), swap(q4a, ACROSS_Y)
     qkv_wgrad, *back_parts = attend_back(
         spots, mixed_grads, mixed_all, q, k, v, lse, attn_in, w_qkv, cosine, sine, gains, [q2b]

time: 493 us -> 487 us (0.988)
  starting transfers between devices: 41.9 us -> 32.1 us
  waiting for transfers between devices: 157 us -> 165 us
  Pallas kernels: 215 us -> 210 us
    ppermute x18, waiting for transfers between devices: 39.4 us -> 49.4 us  [swap(): return lax.ppermute(value, 'row', [(i, i ^ mask) for i in range(8)])]
    ppermute x3, starting transfers between devices: 10.2 us -> 0.35 us  [fast(): back = lax.ppermute(back, 'col', steps)]
    pallas_call x7 -> x6, Pallas kernels: 66.1 us -> 61.9 us  [expert_wgrads(): pl.pallas_call(behind(kernel, 14 + len(extras), after), grid=(count,), ou...]
  transfers between devices with their start and end apart: 43 -> 43, of which waited for: 19 -> 22; matrix products, arithmetic and copies ran while one was open for 5% -> 5% of each run, Pallas kernels for 36% -> 36%
where the time goes in v5:
time: 487 us; the launch traced here: 478 us
  Pallas kernels  210 us (43%)
  waiting for transfers between devices  165 us (34%)
  starting transfers between devices  32.1 us (7%)
  other arithmetic  21.3 us (4%)
  local copies, waits for them, and re-layouts  17 us (3%)
  blocking collectives  16.1 us (3%)
  between operations  15.4 us (3%)
    pallas_call x4, Pallas kernels, experts(): pl.pallas_call(behind(expert_kernel, 12, after), out_shape=(jax.ShapeDtyp...  86.9 us
    ppermute x7, waiting for transfers between devices, ring_gather(): chunks.append(lax.ppermute(chunks[-1], 'col', steps))  73.4 us
    pallas_call x6, Pallas kernels, expert_wgrads(): pl.pallas_call(behind(kernel, 14 + len(extras), after), grid=(count,), ou...  61.9 us
    ppermute x18, waiting for transfers between devices, swap(): return lax.ppermute(value, 'row', [(i, i ^ mask) for i in range(8)])  49.4 us
    pallas_call x1, Pallas kernels, attend_back(): pl.pallas_call(behind(attend_back_kernel, 12, after), out_shape=shapes, i...  17 us
    all_gather x1, blocking collectives, fast(): pack_out = lax.all_gather(pack_out, 'col', axis=0)  16.1 us
    ppermute x18, starting transfers between devices, swap(): return lax.ppermute(value, 'row', [(i, i ^ mask) for i in range(8)])  15.3 us
    ppermute x1, waiting for transfers between devices, fast(): moving = lax.ppermute(moving, 'col', steps)  13 us
  transfers between devices with their start and end apart: 43, of which 22 were waited for; matrix products, arithmetic and copies ran while one was open for 5% of the time, Pallas kernels for 36%

profile of v5, /device:TPU:0, one launch (start us, length us, event | category | flops | bytes accessed | tf_op | source)
XLA Modules:
  0.0 477.7 jit_solution(1694470198951157207)
XLA Ops:
  12.5 16.1 %all-gather.1 = bf16[544,256]{1,0:T(8,128)(2,1)} all-gather(bf16[136,256]{1,0:T(8,128)(2,1)S(1)} %fusion.9), channel_id=3, replica_groups=mesh['row'=8,'col'=4] {'col'}, dimensions={0}, use_global_device_ids=true | all-gather | bytes 348160 | tf_op jit(solution)/shard_map/all_gather | solution.py:1078
  46.1 12.3 %collective-permute-done.1.refs_3_ = bf16[256,1024]{1,0:T(8,128)(2,1)S(1)} collective-permute-done((bf16[256,1024]{1,0:T(8,128)(2,1)}, bf16[256,1024]{1,0:T(8,128)(2,1)S(1)}, u32[]{:S(2)}, u32[]{:S(2)}) %collective-permute-start.1) | collective-permute-done | bytes 524320 | tf_op jit(solution)/shard_map/ppermute | solution.py:1018
  59.2 11.2 %collective-permute-done.2.refs_4_ = bf16[256,1024]{1,0:T(8,128)(2,1)S(1)} collective-permute-done((bf16[256,1024]{1,0:T(8,128)(2,1)S(1)}, bf16[256,1024]{1,0:T(8,128)(2,1)S(1)}, u32[]{:S(2)}, u32[]{:S(2)}) %collective-permute-start.2) | collective-permute-done | bytes 524320 | tf_op jit(solution)/shard_map/ppermute | solution.py:1018
  74.5 12.1 %shard_map.238 = (bf16[1024,1024]{1,0:T(8,128)(2,1)}, bf16[4,1024,64]{2,1,0:T(8,128)(2,1)}, bf16[2,1024,64]{2,1,0:T(8,128)(2,1)}, bf16[2,1024,64]{2,1,0:T(8,128)...) custom-call(s32[3]{0:T(128)} %pad_add_fusion.refs_0_, ...), custom_call_target="tpu_custom_call" | custom-call | flops 10000000 | bytes 100000 | tf_op jit(solution)/shard_map/pallas_call | solution.py:498
  86.7 5.7 %all-to-all-start = ((bf16[4,256,256]{2,1,0:T(8,128)(2,1)}), bf16[4,256,256]{2,1,0:T(8,128)(2,1)}, u32[]{:S(2)}, u32[]{:S(2)}) async-start(bf16[4,256,256]{2,1,0:T(8,128)(2,1)} %bitcast.32), calls=%async_computation | async-start | bytes 1048576 | tf_op jit(solution)/shard_map/all_to_all | solution.py:1093
  92.4 11.3 %collective-permute-done.7.refs_2_.refs_1_.refs_6_ = bf16[256,1024]{1,0:T(8,128)(2,1)} collective-permute-done((bf16[256,1024]{1,0:T(8,128)(2,1)}, bf16[256,1024]{1,0:T(8,128)(2,1)}, u32[]{:S(2)}, u32[]{:S(2)}) %collective-permute-start.7) | collective-permute-done | bytes 524320 | tf_op jit(solution)/shard_map/ppermute | solution.py:1018
  110.1 5.2 %shard_map.239 = (bf16[2,3,1024,128]{3,2,1,0:T(8,128)(2,1)}, bf16[2,3,1024,128]{3,2,1,0:T(8,128)(2,1)}) custom-call(bf16[4,3,1024,128]{3,2,1,0:T(8,128)(2,1)} %collective-permute-done.4.refs_0_.refs_4_, bf16[4,3,1024,128]{3,2,1,0:T(8,128)(2,1)} %collective-permute-done.5.refs_1_.refs_6_, bf16[256,1024]{1,0:T(8,128)(2,1)} %collective-permute-done.7.refs_2_.refs_1_.refs_6_), custom_call_target="tpu_custom_call" | custom-call | flops 3000000 | bytes 100000 | tf_op jit(solution)/shard_map/pallas_call | solution.py:914
  119.8 5.0 %shard_map.240 = (f32[256,1024]{1,0:T(8,128)}, bf16[256,1152]{1,0:T(8,128)(2,1)}, f32[256,128]{1,0:T(8,128)}, f32[256,128]{1,0:T(8,128)}, bf16[1024,1024]{1,0:T(8,128)(2,1)}, /*index=5*/bf16[128,1024]{1,0:T(8,128)(2,1)}) custom-call(s32[3]{0:T(128)} %pad_add_fusion.refs_0_, bf16[1024,256]{1,0:T(8,128)(2,1)} %bitcast.8.refs_1_.mixed_ref, ...), custom_call_target="tpu_custom_call" | custom-call | flops 2000000 | bytes 100000 | tf_op jit(solution)/shard_map/pallas_call | solution.py:647
  125.1 15.9 %collective-permute-done.9.refs_0_.refs_1_ = bf16[256,1152]{1,0:T(8,128)(2,1)S(1)} collective-permute-done((bf16[256,1152]{1,0:T(8,128)(2,1)}, bf16[256,1152]{1,0:T(8,128)(2,1)S(1)}, u32[]{:S(2)}, u32[]{:S(2)}) %collective-permute-start.9) | collective-permute-done | bytes 589856 | tf_op jit(solution)/shard_map/ppermute | solution.py:1018
  141.0 9.5 %collective-permute-done.13.refs_9_ = bf16[2,3,1024,128]{3,2,1,0:T(8,128)(2,1)} collective-permute-done((bf16[2,3,1024,128]{3,2,1,0:T(8,128)(2,1)}, bf16[2,3,1024,128]{3,2,1,0:T(8,128)(2,1)}, u32[]{:S(2)}, u32[]{:S(2)}) %collective-permute-start.13) | collective-permute-done | bytes 1572896 | tf_op jit(solution)/shard_map/ppermute | solution.py:1047
  150.5 5.5 %collective-permute-done.14.refs_0_.refs_2_ = bf16[256,1152]{1,0:T(8,128)(2,1)S(1)} collective-permute-done((bf16[256,1152]{1,0:T(8,128)(2,1)S(1)}, bf16[256,1152]{1,0:T(8,128)(2,1)S(1)}, u32[]{:S(2)}, u32[]{:S(2)}) %collective-permute-start.14) | collective-permute-done | bytes 589856 | tf_op jit(solution)/shard_map/ppermute | solution.py:1018
  156.6 17.1 %collective-permute-done.17.refs_12_.refs_3_.refs_0_ = bf16[256,1152]{1,0:T(8,128)(2,1)S(1)} collective-permute-done((bf16[256,1152]{1,0:T(8,128)(2,1)S(1)}, bf16[256,1152]{1,0:T(8,128)(2,1)S(1)}, u32[]{:S(2)}, u32[]{:S(2)}) %collective-permute-start.17) | collective-permute-done | bytes 589856 | tf_op jit(solution)/shard_map/ppermute | solution.py:1018
  176.2 21.6 %shard_map.241 = (bf16[256,2176]{1,0:T(8,128)(2,1)}, bf16[256,4096]{1,0:T(8,128)(2,1)}, bf16[256,4096]{1,0:T(8,128)(2,1)}, bf16[256,4096]{1,0:T(8,128)(2,1)}) custom-call(bf16[256,1152]{1,0:T(8,128)(2,1)} %copy-done.12, bf16[256,1024]{1,0:T(8,128)(2,1)} %collective-permute-done.6.refs_1_.refs_5_, bf16[4,3,1024,128]{3,2,1,0:T(8,128)(2,1)} %copy-done, ...), custom_call_target="tpu_custom_call" | custom-call | flops 21000000 | bytes 100000 | tf_op jit(solution)/shard_map/pallas_call | solution.py:724
  197.9 21.7 %shard_map.242 = (bf16[256,2176]{1,0:T(8,128)(2,1)}, bf16[256,4096]{1,0:T(8,128)(2,1)}, bf16[256,4096]{1,0:T(8,128)(2,1)}, bf16[256,4096]{1,0:T(8,128)(2,1)}) custom-call(bf16[256,1152]{1,0:T(8,128)(2,1)} %copy-done.11, bf16[256,1024]{1,0:T(8,128)(2,1)} %collective-permute-done.7.refs_2_.refs_1_.refs_6_, bf16[4,3,1024,128]{3,2,1,0:T(8,128)(2,1)} %copy-done, ...), custom_call_target="tpu_custom_call" | custom-call | flops 21000000 | bytes 100000 | tf_op jit(solution)/shard_map/pallas_call | solution.py:724
  219.6 6.0 %collective-permute-done.18.refs_13_ = bf16[256,2176]{1,0:T(8,128)(2,1)S(1)} collective-permute-done((bf16[256,2176]{1,0:T(8,128)(2,1)}, bf16[256,2176]{1,0:T(8,128)(2,1)S(1)}, u32[]{:S(2)}, u32[]{:S(2)}) %collective-permute-start.18) | collective-permute-done | bytes 1114144 | tf_op jit(solution)/shard_map/ppermute | solution.py:1117
  227.5 5.3 %shard_map.243 = (bf16[1024,1024]{1,0:T(8,128)(2,1)}, bf16[1024,1024]{1,0:T(8,128)(2,1)}) custom-call(bf16[256,1152]{1,0:T(8,128)(2,1)} %get-tuple-element.86.refs_0_.refs_10_, bf16[256,1152]{1,0:T(8,128)(2,1)} %copy-done.12, bf16[256,1152]{1,0:T(8,128)(2,1)} %copy-done.11, bf16[256,1152]{1,0:T(8,128)(2,1)} %copy-done.4, bf16[256,1024]{1,0:T(8,128)(2,1)} %refs_7_.1, ...), custom_call_target="tpu_custom_call" | custom-call | flops 2000000 | bytes 100000 | tf_op jit(solution)/shard_map/pallas_call | solution.py:755
  232.8 21.8 %shard_map.244 = (bf16[256,2176]{1,0:T(8,128)(2,1)}, bf16[256,4096]{1,0:T(8,128)(2,1)}, bf16[256,4096]{1,0:T(8,128)(2,1)}, bf16[256,4096]{1,0:T(8,128)(2,1)}) custom-call(bf16[256,1152]{1,0:T(8,128)(2,1)} %copy-done.4, bf16[256,1024]{1,0:T(8,128)(2,1)} %collective-permute-done.8.refs_7_.refs_1_, bf16[4,3,1024,128]{3,2,1,0:T(8,128)(2,1)} %copy-done, ...), custom_call_target="tpu_custom_call" | custom-call | flops 21000000 | bytes 100000 | tf_op jit(solution)/shard_map/pallas_call | solution.py:724
  256.8 21.8 %shard_map.245 = (bf16[256,2176]{1,0:T(8,128)(2,1)}, bf16[256,4096]{1,0:T(8,128)(2,1)}, bf16[256,4096]{1,0:T(8,128)(2,1)}, bf16[256,4096]{1,0:T(8,128)(2,1)}) custom-call(bf16[256,1152]{1,0:T(8,128)(2,1)} %get-tuple-element.86.refs_0_.refs_10_, bf16[256,1024]{1,0:T(8,128)(2,1)} %refs_7_.1, bf16[4,3,1024,128]{3,2,1,0:T(8,128)(2,1)} %copy-done, ...), custom_call_target="tpu_custom_call" | custom-call | flops 21000000 | bytes 100000 | tf_op jit(solution)/shard_map/pallas_call | solution.py:724
  278.5 4.8 %collective-permute-done.20.refs_14_.refs_1_ = bf16[256,2176]{1,0:T(8,128)(2,1)S(1)} collective-permute-done((bf16[256,2176]{1,0:T(8,128)(2,1)S(1)}, bf16[256,2176]{1,0:T(8,128)(2,1)S(1)}, u32[]{:S(2)}, u32[]{:S(2)}) %collective-permute-start.20) | collective-permute-done | bytes 1114144 | tf_op jit(solution)/shard_map/ppermute | solution.py:1117
  284.4 8.0 %shard_map.246.refs_14_ = bf16[2,2,3,1024,128]{4,3,2,1,0:T(8,128)(2,1)} custom-call(bf16[1024,1024]{1,0:T(8,128)(2,1)} %get-tuple-element.94.refs_14_.refs_0_, bf16[1024,1024]{1,0:T(8,128)(2,1)} %get-tuple-element.103.refs_1_, bf16[256,4096]{1,0:T(8,128)(2,1)} %get-tuple-element.104.refs_2_, bf16[256,4096]{1,0:T(8,128)(2,1)} %get-tuple-element.91.refs_12_.refs_3_, ...), custom_call_target="tpu_custom_call" | custom-call | flops 4400000 | bytes 100000 | tf_op jit(solution)/shard_map/pallas_call | solution.py:863
  292.4 8.1 %shard_map.247.refs_14_ = bf16[4,2,3,1024,128]{4,3,2,1,0:T(8,128)(2,1)} custom-call(bf16[1024,1024]{1,0:T(8,128)(2,1)} %get-tuple-element.94.refs_14_.refs_0_, bf16[1024,1024]{1,0:T(8,128)(2,1)} %get-tuple-element.103.refs_1_, bf16[256,4096]{1,0:T(8,128)(2,1)} %get-tuple-element.104.refs_2_, bf16[256,4096]{1,0:T(8,128)(2,1)} %get-tuple-element.91.refs_12_.refs_3_, ...), custom_call_target="tpu_custom_call" | custom-call | flops 4400000 | bytes 100000 | tf_op jit(solution)/shard_map/pallas_call | solution.py:863
  302.1 7.9 %shard_map.248.refs_15_ = bf16[4,2,3,1024,128]{4,3,2,1,0:T(8,128)(2,1)} custom-call(bf16[1024,1024]{1,0:T(8,128)(2,1)} %get-tuple-element.94.refs_14_.refs_0_, bf16[1024,1024]{1,0:T(8,128)(2,1)} %get-tuple-element.103.refs_1_, bf16[256,4096]{1,0:T(8,128)(2,1)} %get-tuple-element.104.refs_2_, ...), custom_call_target="tpu_custom_call", output_to_operand_aliasing={{}: (14, {})} | custom-call | flops 4400000 | bytes 100000 | tf_op jit(solution)/shard_map/pallas_call | solution.py:863
  310.6 9.4 %shard_map.249 = (bf16[1,2,3,1024,128]{4,3,2,1,0:T(8,128)(2,1)}, bf16[1,2,3,1024,128]{4,3,2,1,0:T(8,128)(2,1)}) custom-call(bf16[1024,1024]{1,0:T(8,128)(2,1)} %get-tuple-element.94.refs_14_.refs_0_, bf16[1024,1024]{1,0:T(8,128)(2,1)} %get-tuple-element.103.refs_1_, bf16[256,4096]{1,0:T(8,128)(2,1)} %get-tuple-element.104.refs_2_, ...), custom_call_target="tpu_custom_call" | custom-call | flops 4400000 | bytes 100000 | tf_op jit(solution)/shard_map/pallas_call | solution.py:863
  322.7 6.0 %shard_map.250 = (f32[256,1024]{1,0:T(8,128)}, f32[256,1024]{1,0:T(8,128)}, bf16[256,1024]{1,0:T(8,128)(2,1)}, bf16[1024,256]{1,0:T(8,128)(2,1)}, f32[136,1024]{1,0:T(8,128)}) custom-call(s32[3]{0:T(128)} %pad_add_fusion.refs_0_, bf16[256,2176]{1,0:T(8,128)(2,1)} %copy-done.7, bf16[256,2176]{1,0:T(8,128)(2,1)} %get-tuple-element.97.refs_2_, ...), custom_call_target="tpu_custom_call" | custom-call | flops 2000000 | bytes 100000 | tf_op jit(solution)/shard_map/pallas_call | solution.py:962
  335.8 10.8 %all-to-all-done.1 = bf16[4,256,256]{2,1,0:T(8,128)(2,1)S(1)} async-done(((bf16[4,256,256]{2,1,0:T(8,128)(2,1)}), bf16[4,256,256]{2,1,0:T(8,128)(2,1)S(1)}, u32[]{:S(2)}, u32[]{:S(2)}) %all-to-all-start.1) | async-done | bytes 524320 | tf_op jit(solution)/shard_map/all_to_all | solution.py:1133
  346.6 10.0 %collective-permute-done.23.refs_15_ = bf16[1,2,3,1024,128]{4,3,2,1,0:T(8,128)(2,1)S(1)} collective-permute-done((bf16[1,2,3,1024,128]{4,3,2,1,0:T(8,128)(2,1)}, bf16[1,2,3,1024,128]{4,3,2,1,0:T(8,128)(2,1)S(1)}, u32[]{:S(2)}, u32[]{:S(2)}) %collective-permute-start.23) | collective-permute-done | bytes 1572896 | tf_op jit(solution)/shard_map/ppermute | solution.py:1047
  357.7 19.2 %shard_map.252 = (bf16[1,2,3,1024,128]{4,3,2,1,0:T(8,128)(2,1)}, bf16[1,2,3,1024,128]{4,3,2,1,0:T(8,128)(2,1)}, bf16[1,2,3,1024,128]{4,3,2,1,0:T(8,128)(2,1)}, b...) custom-call(bf16[1024,1024]{1,0:T(8,128)(2,1)} %get-tuple-element.94.refs_14_.refs_0_, ...), custom_call_target="tpu_custom_call" | custom-call | flops 13200000 | bytes 100000 | tf_op jit(solution)/shard_map/pallas_call | solution.py:863
  380.5 17.0 %shard_map.253 = (bf16[8,136,512]{2,1,0:T(8,128)(2,1)}, bf16[256,1024]{1,0:T(8,128)(2,1)}, bf16[256,1024]{1,0:T(8,128)(2,1)}, bf16[256,1024]{1,0:T(8,128)(2,1)}, bf16[256,1024]{1,0:T(8,128)(2,1)}) custom-call(s32[3]{0:T(128)} %pad_add_fusion.refs_0_, bf16[1024,256]{1,0:T(8,128)(2,1)} %bitcast.30, bf16[1024,256]{1,0:T(8,128)(2,1)} %get-tuple-element.79.refs_2_, ...), custom_call_target="tpu_custom_call" | custom-call | flops 16000000 | bytes 100000 | tf_op jit(solution)/shard_map/pallas_call | solution.py:575
  401.3 9.4 %shard_map.254.refs_0_ = bf16[2,2,3,1024,128]{4,3,2,1,0:T(8,128)(2,1)} custom-call(bf16[1024,1024]{1,0:T(8,128)(2,1)} %get-tuple-element.94.refs_14_.refs_0_, bf16[1024,1024]{1,0:T(8,128)(2,1)} %get-tuple-element.103.refs_1_, bf16[256,4096]{1,0:T(8,128)(2,1)} %get-tuple-element.104.refs_2_, bf16[256,4096]{1,0:T(8,128)(2,1)} %get-tuple-element.91.refs_12_.refs_3_, ...), custom_call_target="tpu_custom_call" | custom-call | flops 4400000 | bytes 100000 | tf_op jit(solution)/shard_map/pallas_call | solution.py:863
  419.2 13.0 %collective-permute-done.29 = bf16[256,1024]{1,0:T(8,128)(2,1)S(1)} collective-permute-done((bf16[256,1024]{1,0:T(8,128)(2,1)S(1)}, bf16[256,1024]{1,0:T(8,128)(2,1)S(1)}, u32[]{:S(2)}, u32[]{:S(2)}) %collective-permute-start.29) | collective-permute-done | bytes 524320 | tf_op jit(solution)/shard_map/ppermute | solution.py:1153
  434.4 18.3 %collective-permute-done.34.refs_2_ = bf16[1,2,3,1024,128]{4,3,2,1,0:T(8,128)(2,1)} collective-permute-done((bf16[1,2,3,1024,128]{4,3,2,1,0:T(8,128)(2,1)}, bf16[1,2,3,1024,128]{4,3,2,1,0:T(8,128)(2,1)}, u32[]{:S(2)}, u32[]{:S(2)}) %collective-permute-start.34) | collective-permute-done | bytes 1572896 | tf_op jit(solution)/shard_map/ppermute | solution.py:1047
  454.2 5.9 %shard_map.256 = (f32[2,2,1024,128]{3,2,1,0:T(8,128)}, f32[2,2,1024,128]{3,2,1,0:T(8,128)}, f32[2,2,1024,128]{3,2,1,0:T(8,128)}) custom-call(bf16[2,2,3,1024,128]{4,3,2,1,0:T(8,128)(2,1)} %shard_map.254.refs_0_, bf16[1,2,3,1024,128]{4,3,2,1,0:T(8,128)(2,1)} %collective-permute-done.27.refs_1_, bf16[1,2,3,1024,128]{4,3,2,1,0:T(8,128)(2,1)} %collective-permute-done.34.refs_2_, ...), custom_call_target="tpu_custom_call" | custom-call | flops 5000000 | bytes 100000 | tf_op jit(solution)/shard_map/pallas_call | solution.py:893
  (164 shorter events, 89.5 us)
Async XLA Ops:
  7.2 67.3 %all-gather.6.cloned.1.call-start = ((), (), s32[]{:S(2)}) async-start(), calls=%async_computation.8 | async-start | bytes 1253376 | tf_op jit(solution)/shard_map/all_gather | solution.py:1079
  9.7 109.1 %all-gather.8.cloned.1.call-start = ((), (), s32[]{:S(2)}) async-start(), calls=%async_computation.9 | async-start | bytes 2506752 | tf_op jit(solution)/shard_map/all_gather | solution.py:1080
  12.0 62.5 %collective-permute-start.3 = (bf16[4,3,1024,128]{3,2,1,0:T(8,128)(2,1)S(1)}, bf16[4,3,1024,128]{3,2,1,0:T(8,128)(2,1)}, u32[]{:S(2)}, u32[]{:S(2)}) collective-permute-start(bf16[4,3,1024,128]{3,2,1,0:T(8,128)(2,1)S(1)} %pad_maximum_fusion.refs_2_), channel_id=1, source_target_pairs={{0,4},{4,0},{8,12},{12,8},{16,20},{20,16},{24,28},{28,24},{1,5},{5... | collective-permute-start | bytes 9437192 | tf_op jit(solution)/shard_map/ppermute | solution.py:1047
  28.6 80.3 %collective-permute-start.4 = (bf16[4,3,1024,128]{3,2,1,0:T(8,128)(2,1)S(1)}, bf16[4,3,1024,128]{3,2,1,0:T(8,128)(2,1)}, u32[]{:S(2)}, u32[]{:S(2)}) collective-permute-start(bf16[4,3,1024,128]{3,2,1,0:T(8,128)(2,1)S(1)} %pad_maximum_fusion.refs_2_), channel_id=1, source_target_pairs={{0,8},{4,12},{8,0},{12,4},{16,24},{20,28},{24,16},{28,20},{1,9},{5... | collective-permute-start | bytes 9437192 | tf_op jit(solution)/shard_map/ppermute | solution.py:1047
  30.2 79.9 %collective-permute-start.5 = (bf16[4,3,1024,128]{3,2,1,0:T(8,128)(2,1)S(1)}, bf16[4,3,1024,128]{3,2,1,0:T(8,128)(2,1)}, u32[]{:S(2)}, u32[]{:S(2)}) collective-permute-start(bf16[4,3,1024,128]{3,2,1,0:T(8,128)(2,1)S(1)} %pad_maximum_fusion.refs_2_), channel_id=1, source_target_pairs={{0,16},{4,20},{8,24},{12,28},{16,0},{20,4},{24,8},{28,12},{1,17},{... | collective-permute-start | bytes 9437192 | tf_op jit(solution)/shard_map/ppermute | solution.py:1047
  86.6 17.1 %collective-permute-start.7 = (bf16[256,1024]{1,0:T(8,128)(2,1)}, bf16[256,1024]{1,0:T(8,128)(2,1)}, u32[]{:S(2)}, u32[]{:S(2)}) collective-permute-start(bf16[256,1024]{1,0:T(8,128)(2,1)} %collective-permute-done.6.refs_1_.refs_5_), channel_id=1, source_target_pairs={{0,1},{1,2},{2,3},{3,0},{4,5},{5,6},{6,7},{7,4},{8,9},{9,10},{10,1... | collective-permute-start | bytes 1572872 | tf_op jit(solution)/shard_map/ppermute | solution.py:1018
  86.7 33.1 %all-to-all-start = ((bf16[4,256,256]{2,1,0:T(8,128)(2,1)}), bf16[4,256,256]{2,1,0:T(8,128)(2,1)}, u32[]{:S(2)}, u32[]{:S(2)}) async-start(bf16[4,256,256]{2,1,0:T(8,128)(2,1)} %bitcast.32), calls=%async_computation | async-start | bytes 1048576 | tf_op jit(solution)/shard_map/all_to_all | solution.py:1093
  103.7 21.0 %collective-permute-start.8 = (bf16[256,1024]{1,0:T(8,128)(2,1)}, bf16[256,1024]{1,0:T(8,128)(2,1)}, u32[]{:S(2)}, u32[]{:S(2)}) collective-permute-start(bf16[256,1024]{1,0:T(8,128)(2,1)} %collective-permute-done.7.refs_2_.refs_1_.refs_6_), channel_id=1, source_target_pairs={{0,1},{1,2},{2,3},{3,0},{4,5},{5,6},{6,7},{7,4},{8,9},{9,10},{10,1... | collective-permute-start | bytes 1572872 | tf_op jit(solution)/shard_map/ppermute | solution.py:1018
  115.4 35.2 %collective-permute-start.13 = (bf16[2,3,1024,128]{3,2,1,0:T(8,128)(2,1)}, bf16[2,3,1024,128]{3,2,1,0:T(8,128)(2,1)}, u32[]{:S(2)}, u32[]{:S(2)}) collective-permute-start(bf16[2,3,1024,128]{3,2,1,0:T(8,128)(2,1)} %get-tuple-element.87), channel_id=1, source_target_pairs={{0,16},{4,20},{8,24},{12,28},{16,0},{20,4},{24,8},{28,12},{1,17},{... | collective-permute-start | bytes 4718600 | tf_op jit(solution)/shard_map/ppermute | solution.py:1047
  116.9 39.2 %collective-permute-start.12 = (bf16[2,3,1024,128]{3,2,1,0:T(8,128)(2,1)}, bf16[2,3,1024,128]{3,2,1,0:T(8,128)(2,1)}, u32[]{:S(2)}, u32[]{:S(2)}) collective-permute-start(bf16[2,3,1024,128]{3,2,1,0:T(8,128)(2,1)} %get-tuple-element.84.refs_7_), channel_id=1, source_target_pairs={{0,8},{4,12},{8,0},{12,4},{16,24},{20,28},{24,16},{28,20},{1,9},{5... | collective-permute-start | bytes 4718600 | tf_op jit(solution)/shard_map/ppermute | solution.py:1047
  117.4 56.3 %collective-permute-start.10 = (bf16[4,3,1024,128]{3,2,1,0:T(8,128)(2,1)}, bf16[4,3,1024,128]{3,2,1,0:T(8,128)(2,1)S(1)}, u32[]{:S(2)}, u32[]{:S(2)}) collective-permute-start(bf16[4,3,1024,128]{3,2,1,0:T(8,128)(2,1)} %collective-permute-done.4.refs_0_.refs_4_), channel_id=1, source_target_pairs={{0,4},{4,0},{8,12},{12,8},{16,20},{20,16},{24,28},{28,24},{1,5},{5... | collective-permute-start | bytes 9437192 | tf_op jit(solution)/shard_map/ppermute | solution.py:1047
  117.4 57.1 %collective-permute-start.11 = (bf16[4,3,1024,128]{3,2,1,0:T(8,128)(2,1)}, bf16[4,3,1024,128]{3,2,1,0:T(8,128)(2,1)}, u32[]{:S(2)}, u32[]{:S(2)}) collective-permute-start(bf16[4,3,1024,128]{3,2,1,0:T(8,128)(2,1)} %collective-permute-done.5.refs_1_.refs_6_), channel_id=1, source_target_pairs={{0,4},{4,0},{8,12},{12,8},{16,20},{20,16},{24,28},{28,24},{1,5},{5... | collective-permute-start | bytes 9437192 | tf_op jit(solution)/shard_map/ppermute | solution.py:1047
  124.8 16.2 %collective-permute-start.9 = (bf16[256,1152]{1,0:T(8,128)(2,1)}, bf16[256,1152]{1,0:T(8,128)(2,1)S(1)}, u32[]{:S(2)}, u32[]{:S(2)}) collective-permute-start(bf16[256,1152]{1,0:T(8,128)(2,1)} %get-tuple-element.86.refs_0_.refs_10_), channel_id=1, source_target_pairs={{0,1},{1,2},{2,3},{3,0},{4,5},{5,6},{6,7},{7,4},{8,9},{9,10},{10,1... | collective-permute-start | bytes 1769480 | tf_op jit(solution)/shard_map/ppermute | solution.py:1018
  156.1 18.5 %collective-permute-start.16 = (bf16[2,3,1024,128]{3,2,1,0:T(8,128)(2,1)}, bf16[2,3,1024,128]{3,2,1,0:T(8,128)(2,1)}, u32[]{:S(2)}, u32[]{:S(2)}) collective-permute-start(bf16[2,3,1024,128]{3,2,1,0:T(8,128)(2,1)} %collective-permute-done.13.refs_9_), channel_id=1, source_target_pairs={{0,4},{4,0},{8,12},{12,8},{16,20},{20,16},{24,28},{28,24},{1,5},{5... | collective-permute-start | bytes 4718600 | tf_op jit(solution)/shard_map/ppermute | solution.py:1047
  156.1 18.4 %collective-permute-start.15 = (bf16[2,3,1024,128]{3,2,1,0:T(8,128)(2,1)}, bf16[2,3,1024,128]{3,2,1,0:T(8,128)(2,1)}, u32[]{:S(2)}, u32[]{:S(2)}) collective-permute-start(bf16[2,3,1024,128]{3,2,1,0:T(8,128)(2,1)} %collective-permute-done.12.refs_8_), channel_id=1, source_target_pairs={{0,4},{4,0},{8,12},{12,8},{16,20},{20,16},{24,28},{28,24},{1,5},{5... | collective-permute-start | bytes 4718600 | tf_op jit(solution)/shard_map/ppermute | solution.py:1047
  156.6 17.1 %collective-permute-start.17 = (bf16[256,1152]{1,0:T(8,128)(2,1)S(1)}, bf16[256,1152]{1,0:T(8,128)(2,1)S(1)}, u32[]{:S(2)}, u32[]{:S(2)}) collective-permute-start(bf16[256,1152]{1,0:T(8,128)(2,1)S(1)} %collective-permute-done.14.refs_0_.refs_2_), channel_id=1, source_target_pairs={{0,1},{1,2},{2,3},{3,0},{4,5},{5,6},{6,7},{7,4},{8,9},{9,10},{10,1... | collective-permute-start | bytes 1769480 | tf_op jit(solution)/shard_map/ppermute | solution.py:1018
  197.8 27.8 %collective-permute-start.18 = (bf16[256,2176]{1,0:T(8,128)(2,1)}, bf16[256,2176]{1,0:T(8,128)(2,1)S(1)}, u32[]{:S(2)}, u32[]{:S(2)}) collective-permute-start(bf16[256,2176]{1,0:T(8,128)(2,1)} %get-tuple-element.90), channel_id=1, source_target_pairs={{0,1},{1,2},{2,3},{3,0},{4,5},{5,6},{6,7},{7,4},{8,9},{9,10},{10,1... | collective-permute-start | bytes 3342344 | tf_op jit(solution)/shard_map/ppermute | solution.py:1117
  227.5 27.1 %collective-permute-start.19 = (bf16[256,2176]{1,0:T(8,128)(2,1)S(1)}, bf16[256,2176]{1,0:T(8,128)(2,1)S(1)}, u32[]{:S(2)}, u32[]{:S(2)}) collective-permute-start(bf16[256,2176]{1,0:T(8,128)(2,1)S(1)} %add_convert_fusion.1), channel_id=1, source_target_pairs={{0,1},{1,2},{2,3},{3,0},{4,5},{5,6},{6,7},{7,4},{8,9},{9,10},{10,1... | collective-permute-start | bytes 3342344 | tf_op jit(solution)/shard_map/ppermute | solution.py:1117
  256.5 26.8 %collective-permute-start.20 = (bf16[256,2176]{1,0:T(8,128)(2,1)S(1)}, bf16[256,2176]{1,0:T(8,128)(2,1)S(1)}, u32[]{:S(2)}, u32[]{:S(2)}) collective-permute-start(bf16[256,2176]{1,0:T(8,128)(2,1)S(1)} %add_convert_fusion), channel_id=1, source_target_pairs={{0,1},{1,2},{2,3},{3,0},{4,5},{5,6},{6,7},{7,4},{8,9},{9,10},{10,1... | collective-permute-start | bytes 3342344 | tf_op jit(solution)/shard_map/ppermute | solution.py:1117
  310.0 47.3 %collective-permute-start.22 = (bf16[4,2,3,1024,128]{4,3,2,1,0:T(8,128)(2,1)}, bf16[4,2,3,1024,128]{4,3,2,1,0:T(8,128)(2,1)}, u32[]{:S(2)}, u32[]{:S(2)}) collective-permute-start(bf16[4,2,3,1024,128]{4,3,2,1,0:T(8,128)(2,1)} %shard_map.248.refs_15_), channel_id=1, source_target_pairs={{0,4},{4,0},{8,12},{12,8},{16,20},{20,16},{24,28},{28,24},{1,5},{5... | collective-permute-start | bytes 18874376 | tf_op jit(solution)/shard_map/ppermute | solution.py:1047
  320.0 36.6 %collective-permute-start.23 = (bf16[1,2,3,1024,128]{4,3,2,1,0:T(8,128)(2,1)}, bf16[1,2,3,1024,128]{4,3,2,1,0:T(8,128)(2,1)S(1)}, u32[]{:S(2)}, u32[]{:S(2)}) collective-permute-start(bf16[1,2,3,1024,128]{4,3,2,1,0:T(8,128)(2,1)} %get-tuple-element.122), channel_id=1, source_target_pairs={{0,16},{4,20},{8,24},{12,28},{16,0},{20,4},{24,8},{28,12},{1,17},{... | collective-permute-start | bytes 4718600 | tf_op jit(solution)/shard_map/ppermute | solution.py:1047
  320.3 37.0 %collective-permute-start.24 = (bf16[1,2,3,1024,128]{4,3,2,1,0:T(8,128)(2,1)}, bf16[1,2,3,1024,128]{4,3,2,1,0:T(8,128)(2,1)}, u32[]{:S(2)}, u32[]{:S(2)}) collective-permute-start(bf16[1,2,3,1024,128]{4,3,2,1,0:T(8,128)(2,1)} %get-tuple-element.113.refs_11_), channel_id=1, source_target_pairs={{0,8},{4,12},{8,0},{12,4},{16,24},{20,28},{24,16},{28,20},{1,9},{5... | collective-permute-start | bytes 4718600 | tf_op jit(solution)/shard_map/ppermute | solution.py:1047
  328.7 17.9 %all-to-all-start.1 = ((bf16[4,256,256]{2,1,0:T(8,128)(2,1)}), bf16[4,256,256]{2,1,0:T(8,128)(2,1)S(1)}, u32[]{:S(2)}, u32[]{:S(2)}) async-start(bf16[4,256,256]{2,1,0:T(8,128)(2,1)} %bitcast.39), calls=%async_computation.1 | async-start | bytes 1048576 | tf_op jit(solution)/shard_map/all_to_all | solution.py:1133
  332.2 48.1 %reduce-scatter.6.cloned.1.call-start = ((), (), s32[]{:S(2)}) async-start(), calls=%async_computation.6 | async-start | bytes 2506752 | tf_op jit(solution)/shard_map/reduce_scatter | solution.py:1135
  335.7 82.6 %reduce-scatter.8.cloned.1.call-start = ((), (), s32[]{:S(2)}) async-start(), calls=%async_computation.7 | async-start | bytes 348160 | tf_op jit(solution)/shard_map/reduce_scatter | solution.py:1167
  376.9 22.1 %collective-permute-start.26 = (bf16[2,2,3,1024,128]{4,3,2,1,0:T(8,128)(2,1)}, bf16[2,2,3,1024,128]{4,3,2,1,0:T(8,128)(2,1)S(1)}, u32[]{:S(2)}, u32[]{:S(2)}) collective-permute-start(bf16[2,2,3,1024,128]{4,3,2,1,0:T(8,128)(2,1)} %get-tuple-element.127), channel_id=1, source_target_pairs={{0,4},{4,0},{8,12},{12,8},{16,20},{20,16},{24,28},{28,24},{1,5},{5... | collective-permute-start | bytes 9437192 | tf_op jit(solution)/shard_map/ppermute | solution.py:1047
  377.0 37.8 %collective-permute-start.27 = (bf16[1,2,3,1024,128]{4,3,2,1,0:T(8,128)(2,1)}, bf16[1,2,3,1024,128]{4,3,2,1,0:T(8,128)(2,1)}, u32[]{:S(2)}, u32[]{:S(2)}) collective-permute-start(bf16[1,2,3,1024,128]{4,3,2,1,0:T(8,128)(2,1)} %get-tuple-element.129), channel_id=1, source_target_pairs={{0,8},{4,12},{8,0},{12,4},{16,24},{20,28},{24,16},{28,20},{1,9},{5... | collective-permute-start | bytes 4718600 | tf_op jit(solution)/shard_map/ppermute | solution.py:1047
  379.2 37.6 %collective-permute-start.28 = (bf16[1,2,3,1024,128]{4,3,2,1,0:T(8,128)(2,1)}, bf16[1,2,3,1024,128]{4,3,2,1,0:T(8,128)(2,1)}, u32[]{:S(2)}, u32[]{:S(2)}) collective-permute-start(bf16[1,2,3,1024,128]{4,3,2,1,0:T(8,128)(2,1)} %get-tuple-element.130), channel_id=1, source_target_pairs={{0,16},{4,20},{8,24},{12,28},{16,0},{20,4},{24,8},{28,12},{1,17},{... | collective-permute-start | bytes 4718600 | tf_op jit(solution)/shard_map/ppermute | solution.py:1047
  380.3 79.8 %reduce-scatter.4.cloned.1.call-start = ((), (), s32[]{:S(2)}) async-start(), calls=%async_computation.5 | async-start | bytes 1253376 | tf_op jit(solution)/shard_map/reduce_scatter | solution.py:1165
  397.5 55.1 %collective-permute-start.34 = (bf16[1,2,3,1024,128]{4,3,2,1,0:T(8,128)(2,1)}, bf16[1,2,3,1024,128]{4,3,2,1,0:T(8,128)(2,1)}, u32[]{:S(2)}, u32[]{:S(2)}) collective-permute-start(bf16[1,2,3,1024,128]{4,3,2,1,0:T(8,128)(2,1)} %get-tuple-element.125.refs_12_), channel_id=1, source_target_pairs={{0,8},{4,12},{8,0},{12,4},{16,24},{20,28},{24,16},{28,20},{1,9},{5... | collective-permute-start | bytes 4718600 | tf_op jit(solution)/shard_map/ppermute | solution.py:1047
  400.7 53.5 %collective-permute-start.35 = (bf16[1,2,3,1024,128]{4,3,2,1,0:T(8,128)(2,1)}, bf16[1,2,3,1024,128]{4,3,2,1,0:T(8,128)(2,1)}, u32[]{:S(2)}, u32[]{:S(2)}) collective-permute-start(bf16[1,2,3,1024,128]{4,3,2,1,0:T(8,128)(2,1)} %get-tuple-element.140), channel_id=1, source_target_pairs={{0,16},{4,20},{8,24},{12,28},{16,0},{20,4},{24,8},{28,12},{1,17},{... | collective-permute-start | bytes 4718600 | tf_op jit(solution)/shard_map/ppermute | solution.py:1047
  432.5 27.6 %collective-permute-start.30 = (bf16[256,1024]{1,0:T(8,128)(2,1)S(1)}, bf16[256,1024]{1,0:T(8,128)(2,1)S(1)}, u32[]{:S(2)}, u32[]{:S(2)}) collective-permute-start(bf16[256,1024]{1,0:T(8,128)(2,1)S(1)} %add_convert_fusion.2.refs_5_), channel_id=1, source_target_pairs={{0,1},{1,2},{2,3},{3,0},{4,5},{5,6},{6,7},{7,4},{8,9},{9,10},{10,1... | collective-permute-start | bytes 1572872 | tf_op jit(solution)/shard_map/ppermute | solution.py:1156
  (37 other events, 376.6 us)
Sparse Core Ops, SparseCore 0:
  10.5 29.4 all-gather.5
  41.8 37.7 all-gather.7
  336.3 42.3 reduce-scatter.5
  380.9 19.9 reduce-scatter.7
  403.9 39.3 reduce-scatter.3

commit v6 on v5

--- a/solution.py
+++ b/solution.py
@@ -1160,16 +1160,16 @@
     normed = x_rows * scale
     inner = attn_grad * gains[:1]
     block_in_grad = resid_grad + scale * (inner - normed * jnp.mean(inner * normed, axis=1, keepdims=True))
-    gate_sum, up_sum, down_sum = expert_total([third_step], q0, x2a, x2b, y4a, y4b)
 
     qkv_sum = lax.psum_scatter(qkv_wgrad, "row", scatter_dimension=0, tiled=True)[0]
     *qkv_sums, gain_one = unpack(qkv_sum, [last_step])
     out_sum = lax.psum_scatter(hold(out_sum, q2b), "col", scatter_dimension=2, tiled=True)[0].astype(F32)
-    gain_one_sum = functools.reduce(jnp.add, shift_all([gain_one] * n_col, n_col))[0]
+    gain_one_sum = functools.reduce(jnp.add, shift_all([gain_one] * n_col, n_col))
+    gate_sum, up_sum, down_sum = expert_total([block_in_grad, gain_one_sum], q0, x2a, x2b, y4a, y4b)
     return (
         block_out,
         block_in_grad,
-        gain_one_sum,
+        gain_one_sum[0],
         out_sum[LANES, LANES:],
         *qkv_sums,
         out_sum[:LANES],

time: 487 us -> 482 us (0.990)
  waiting for transfers between devices: 165 us -> 160 us
    ppermute x18, waiting for transfers between devices: 49.4 us -> 29 us  [swap(): return lax.ppermute(value, 'row', [(i, i ^ mask) for i in range(8)])]
    reduce_scatter x1, waiting for transfers between devices: 0.01 us -> 6.69 us  [fast(): lax.psum_scatter(qkv_wgrad, 'row', scatter_dimension=0, tiled=True)[0]]
    ppermute x1, waiting for transfers between devices: 0.01 us -> 5.8 us  [fast(): last_step = lax.ppermute(moving, 'col', steps)]
    unnamed x53 -> x55, local copies, waits for them, and re-layouts: 10.4 us -> 8.75 us
  transfers between devices with their start and end apart: 43 -> 43, of which waited for: 22 -> 22; matrix products, arithmetic and copies ran while one was open for 5% -> 5% of each run, Pallas kernels for 36% -> 35%
where the time goes in v6:
time: 482 us; the launch traced here: 473 us
  Pallas kernels  210 us (44%)
  waiting for transfers between devices  160 us (33%)
  starting transfers between devices  31.8 us (7%)
  other arithmetic  24 us (5%)
  blocking collectives  16.1 us (3%)
  between operations  15.3 us (3%)
  local copies, waits for them, and re-layouts  15.2 us (3%)
    pallas_call x4, Pallas kernels, experts(): pl.pallas_call(behind(expert_kernel, 12, after), out_shape=(jax.ShapeDtyp...  86.9 us
    ppermute x7, waiting for transfers between devices, ring_gather(): chunks.append(lax.ppermute(chunks[-1], 'col', steps))  73.4 us
    pallas_call x6, Pallas kernels, expert_wgrads(): pl.pallas_call(behind(kernel, 14 + len(extras), after), grid=(count,), ou...  62 us
    ppermute x18, waiting for transfers between devices, swap(): return lax.ppermute(value, 'row', [(i, i ^ mask) for i in range(8)])  29 us
    pallas_call x1, Pallas kernels, attend_back(): pl.pallas_call(behind(attend_back_kernel, 12, after), out_shape=shapes, i...  17 us
    all_gather x1, blocking collectives, fast(): pack_out = lax.all_gather(pack_out, 'col', axis=0)  16.1 us
    ppermute x18, starting transfers between devices, swap(): return lax.ppermute(value, 'row', [(i, i ^ mask) for i in range(8)])  15.1 us
    ppermute x1, waiting for transfers between devices, fast(): moving = lax.ppermute(moving, 'col', steps)  12.3 us
  transfers between devices with their start and end apart: 43, of which 22 were waited for; matrix products, arithmetic and copies ran while one was open for 5% of the time, Pallas kernels for 35%

profile of v6, /device:TPU:0, one launch (start us, length us, event | category | flops | bytes accessed | tf_op | source)
XLA Modules:
  0.0 473.1 jit_solution(2599779283457511411)
XLA Ops:
  12.5 16.1 %all-gather.1 = bf16[544,256]{1,0:T(8,128)(2,1)} all-gather(bf16[136,256]{1,0:T(8,128)(2,1)S(1)} %fusion.9), channel_id=3, replica_groups=mesh['row'=8,'col'=4] {'col'}, dimensions={0}, use_global_device_ids=true | all-gather | bytes 348160 | tf_op jit(solution)/shard_map/all_gather | solution.py:1078
  46.1 12.3 %collective-permute-done.1.refs_3_ = bf16[256,1024]{1,0:T(8,128)(2,1)S(1)} collective-permute-done((bf16[256,1024]{1,0:T(8,128)(2,1)}, bf16[256,1024]{1,0:T(8,128)(2,1)S(1)}, u32[]{:S(2)}, u32[]{:S(2)}) %collective-permute-start.1) | collective-permute-done | bytes 524320 | tf_op jit(solution)/shard_map/ppermute | solution.py:1018
  59.2 11.2 %collective-permute-done.2.refs_4_ = bf16[256,1024]{1,0:T(8,128)(2,1)S(1)} collective-permute-done((bf16[256,1024]{1,0:T(8,128)(2,1)S(1)}, bf16[256,1024]{1,0:T(8,128)(2,1)S(1)}, u32[]{:S(2)}, u32[]{:S(2)}) %collective-permute-start.2) | collective-permute-done | bytes 524320 | tf_op jit(solution)/shard_map/ppermute | solution.py:1018
  74.5 12.1 %shard_map.238 = (bf16[1024,1024]{1,0:T(8,128)(2,1)}, bf16[4,1024,64]{2,1,0:T(8,128)(2,1)}, bf16[2,1024,64]{2,1,0:T(8,128)(2,1)}, bf16[2,1024,64]{2,1,0:T(8,128)...) custom-call(s32[3]{0:T(128)} %pad_add_fusion.refs_0_, ...), custom_call_target="tpu_custom_call" | custom-call | flops 10000000 | bytes 100000 | tf_op jit(solution)/shard_map/pallas_call | solution.py:498
  86.7 5.7 %all-to-all-start = ((bf16[4,256,256]{2,1,0:T(8,128)(2,1)}), bf16[4,256,256]{2,1,0:T(8,128)(2,1)}, u32[]{:S(2)}, u32[]{:S(2)}) async-start(bf16[4,256,256]{2,1,0:T(8,128)(2,1)} %bitcast.32), calls=%async_computation | async-start | bytes 1048576 | tf_op jit(solution)/shard_map/all_to_all | solution.py:1093
  92.4 11.3 %collective-permute-done.7.refs_2_.refs_1_.refs_6_ = bf16[256,1024]{1,0:T(8,128)(2,1)} collective-permute-done((bf16[256,1024]{1,0:T(8,128)(2,1)}, bf16[256,1024]{1,0:T(8,128)(2,1)}, u32[]{:S(2)}, u32[]{:S(2)}) %collective-permute-start.7) | collective-permute-done | bytes 524320 | tf_op jit(solution)/shard_map/ppermute | solution.py:1018
  110.1 5.2 %shard_map.239 = (bf16[2,3,1024,128]{3,2,1,0:T(8,128)(2,1)}, bf16[2,3,1024,128]{3,2,1,0:T(8,128)(2,1)}) custom-call(bf16[4,3,1024,128]{3,2,1,0:T(8,128)(2,1)} %collective-permute-done.4.refs_0_.refs_4_, bf16[4,3,1024,128]{3,2,1,0:T(8,128)(2,1)} %collective-permute-done.5.refs_1_.refs_6_, bf16[256,1024]{1,0:T(8,128)(2,1)} %collective-permute-done.7.refs_2_.refs_1_.refs_6_), custom_call_target="tpu_custom_call" | custom-call | flops 3000000 | bytes 100000 | tf_op jit(solution)/shard_map/pallas_call | solution.py:914
  125.1 15.9 %collective-permute-done.9.refs_0_.refs_1_ = bf16[256,1152]{1,0:T(8,128)(2,1)S(1)} collective-permute-done((bf16[256,1152]{1,0:T(8,128)(2,1)}, bf16[256,1152]{1,0:T(8,128)(2,1)S(1)}, u32[]{:S(2)}, u32[]{:S(2)}) %collective-permute-start.9) | collective-permute-done | bytes 589856 | tf_op jit(solution)/shard_map/ppermute | solution.py:1018
  141.0 9.5 %collective-permute-done.13.refs_9_ = bf16[2,3,1024,128]{3,2,1,0:T(8,128)(2,1)} collective-permute-done((bf16[2,3,1024,128]{3,2,1,0:T(8,128)(2,1)}, bf16[2,3,1024,128]{3,2,1,0:T(8,128)(2,1)}, u32[]{:S(2)}, u32[]{:S(2)}) %collective-permute-start.13) | collective-permute-done | bytes 1572896 | tf_op jit(solution)/shard_map/ppermute | solution.py:1047
  150.5 5.5 %collective-permute-done.14.refs_0_.refs_2_ = bf16[256,1152]{1,0:T(8,128)(2,1)S(1)} collective-permute-done((bf16[256,1152]{1,0:T(8,128)(2,1)S(1)}, bf16[256,1152]{1,0:T(8,128)(2,1)S(1)}, u32[]{:S(2)}, u32[]{:S(2)}) %collective-permute-start.14) | collective-permute-done | bytes 589856 | tf_op jit(solution)/shard_map/ppermute | solution.py:1018
  156.6 17.1 %collective-permute-done.17.refs_12_.refs_3_.refs_0_ = bf16[256,1152]{1,0:T(8,128)(2,1)S(1)} collective-permute-done((bf16[256,1152]{1,0:T(8,128)(2,1)S(1)}, bf16[256,1152]{1,0:T(8,128)(2,1)S(1)}, u32[]{:S(2)}, u32[]{:S(2)}) %collective-permute-start.17) | collective-permute-done | bytes 589856 | tf_op jit(solution)/shard_map/ppermute | solution.py:1018
  176.2 21.6 %shard_map.241 = (bf16[256,2176]{1,0:T(8,128)(2,1)}, bf16[256,4096]{1,0:T(8,128)(2,1)}, bf16[256,4096]{1,0:T(8,128)(2,1)}, bf16[256,4096]{1,0:T(8,128)(2,1)}) custom-call(bf16[256,1152]{1,0:T(8,128)(2,1)} %copy-done.11, bf16[256,1024]{1,0:T(8,128)(2,1)} %collective-permute-done.6.refs_1_.refs_5_, bf16[4,3,1024,128]{3,2,1,0:T(8,128)(2,1)} %copy-done, ...), custom_call_target="tpu_custom_call" | custom-call | flops 21000000 | bytes 100000 | tf_op jit(solution)/shard_map/pallas_call | solution.py:724
  197.8 21.7 %shard_map.242 = (bf16[256,2176]{1,0:T(8,128)(2,1)}, bf16[256,4096]{1,0:T(8,128)(2,1)}, bf16[256,4096]{1,0:T(8,128)(2,1)}, bf16[256,4096]{1,0:T(8,128)(2,1)}) custom-call(bf16[256,1152]{1,0:T(8,128)(2,1)} %copy-done.10, bf16[256,1024]{1,0:T(8,128)(2,1)} %collective-permute-done.7.refs_2_.refs_1_.refs_6_, bf16[4,3,1024,128]{3,2,1,0:T(8,128)(2,1)} %copy-done, ...), custom_call_target="tpu_custom_call" | custom-call | flops 21000000 | bytes 100000 | tf_op jit(solution)/shard_map/pallas_call | solution.py:724
  219.6 6.0 %collective-permute-done.18.refs_13_ = bf16[256,2176]{1,0:T(8,128)(2,1)S(1)} collective-permute-done((bf16[256,2176]{1,0:T(8,128)(2,1)}, bf16[256,2176]{1,0:T(8,128)(2,1)S(1)}, u32[]{:S(2)}, u32[]{:S(2)}) %collective-permute-start.18) | collective-permute-done | bytes 1114144 | tf_op jit(solution)/shard_map/ppermute | solution.py:1117
  227.5 5.3 %shard_map.243 = (bf16[1024,1024]{1,0:T(8,128)(2,1)}, bf16[1024,1024]{1,0:T(8,128)(2,1)}) custom-call(bf16[256,1152]{1,0:T(8,128)(2,1)} %get-tuple-element.86.refs_0_.refs_10_, bf16[256,1152]{1,0:T(8,128)(2,1)} %copy-done.11, bf16[256,1152]{1,0:T(8,128)(2,1)} %copy-done.10, bf16[256,1152]{1,0:T(8,128)(2,1)} %copy-done.4, bf16[256,1024]{1,0:T(8,128)(2,1)} %refs_7_.1, ...), custom_call_target="tpu_custom_call" | custom-call | flops 2000000 | bytes 100000 | tf_op jit(solution)/shard_map/pallas_call | solution.py:755
  232.8 21.7 %shard_map.244 = (bf16[256,2176]{1,0:T(8,128)(2,1)}, bf16[256,4096]{1,0:T(8,128)(2,1)}, bf16[256,4096]{1,0:T(8,128)(2,1)}, bf16[256,4096]{1,0:T(8,128)(2,1)}) custom-call(bf16[256,1152]{1,0:T(8,128)(2,1)} %copy-done.4, bf16[256,1024]{1,0:T(8,128)(2,1)} %collective-permute-done.8.refs_7_.refs_1_, bf16[4,3,1024,128]{3,2,1,0:T(8,128)(2,1)} %copy-done, ...), custom_call_target="tpu_custom_call" | custom-call | flops 21000000 | bytes 100000 | tf_op jit(solution)/shard_map/pallas_call | solution.py:724
  256.7 21.7 %shard_map.245 = (bf16[256,2176]{1,0:T(8,128)(2,1)}, bf16[256,4096]{1,0:T(8,128)(2,1)}, bf16[256,4096]{1,0:T(8,128)(2,1)}, bf16[256,4096]{1,0:T(8,128)(2,1)}) custom-call(bf16[256,1152]{1,0:T(8,128)(2,1)} %get-tuple-element.86.refs_0_.refs_10_, bf16[256,1024]{1,0:T(8,128)(2,1)} %refs_7_.1, bf16[4,3,1024,128]{3,2,1,0:T(8,128)(2,1)} %copy-done, ...), custom_call_target="tpu_custom_call" | custom-call | flops 21000000 | bytes 100000 | tf_op jit(solution)/shard_map/pallas_call | solution.py:724
  284.3 8.0 %shard_map.246.refs_14_ = bf16[2,2,3,1024,128]{4,3,2,1,0:T(8,128)(2,1)} custom-call(bf16[1024,1024]{1,0:T(8,128)(2,1)} %get-tuple-element.94.refs_14_.refs_0_, bf16[1024,1024]{1,0:T(8,128)(2,1)} %get-tuple-element.103.refs_1_, bf16[256,4096]{1,0:T(8,128)(2,1)} %get-tuple-element.104.refs_2_, bf16[256,4096]{1,0:T(8,128)(2,1)} %get-tuple-element.91.refs_12_.refs_3_, ...), custom_call_target="tpu_custom_call" | custom-call | flops 4400000 | bytes 100000 | tf_op jit(solution)/shard_map/pallas_call | solution.py:863
  292.3 8.0 %shard_map.247.refs_14_ = bf16[4,2,3,1024,128]{4,3,2,1,0:T(8,128)(2,1)} custom-call(bf16[1024,1024]{1,0:T(8,128)(2,1)} %get-tuple-element.94.refs_14_.refs_0_, bf16[1024,1024]{1,0:T(8,128)(2,1)} %get-tuple-element.103.refs_1_, bf16[256,4096]{1,0:T(8,128)(2,1)} %get-tuple-element.104.refs_2_, bf16[256,4096]{1,0:T(8,128)(2,1)} %get-tuple-element.91.refs_12_.refs_3_, ...), custom_call_target="tpu_custom_call" | custom-call | flops 4400000 | bytes 100000 | tf_op jit(solution)/shard_map/pallas_call | solution.py:863
  302.0 7.9 %shard_map.248.refs_15_ = bf16[4,2,3,1024,128]{4,3,2,1,0:T(8,128)(2,1)} custom-call(bf16[1024,1024]{1,0:T(8,128)(2,1)} %get-tuple-element.94.refs_14_.refs_0_, bf16[1024,1024]{1,0:T(8,128)(2,1)} %get-tuple-element.103.refs_1_, bf16[256,4096]{1,0:T(8,128)(2,1)} %get-tuple-element.104.refs_2_, ...), custom_call_target="tpu_custom_call", output_to_operand_aliasing={{}: (14, {})} | custom-call | flops 4400000 | bytes 100000 | tf_op jit(solution)/shard_map/pallas_call | solution.py:863
  310.5 9.4 %shard_map.249 = (bf16[1,2,3,1024,128]{4,3,2,1,0:T(8,128)(2,1)}, bf16[1,2,3,1024,128]{4,3,2,1,0:T(8,128)(2,1)}) custom-call(bf16[1024,1024]{1,0:T(8,128)(2,1)} %get-tuple-element.94.refs_14_.refs_0_, bf16[1024,1024]{1,0:T(8,128)(2,1)} %get-tuple-element.103.refs_1_, bf16[256,4096]{1,0:T(8,128)(2,1)} %get-tuple-element.104.refs_2_, ...), custom_call_target="tpu_custom_call" | custom-call | flops 4400000 | bytes 100000 | tf_op jit(solution)/shard_map/pallas_call | solution.py:863
  322.6 6.0 %shard_map.250 = (f32[256,1024]{1,0:T(8,128)}, f32[256,1024]{1,0:T(8,128)}, bf16[256,1024]{1,0:T(8,128)(2,1)}, bf16[1024,256]{1,0:T(8,128)(2,1)}, f32[136,1024]{1,0:T(8,128)}) custom-call(s32[3]{0:T(128)} %pad_add_fusion.refs_0_, bf16[256,2176]{1,0:T(8,128)(2,1)} %copy-done.7, bf16[256,2176]{1,0:T(8,128)(2,1)} %get-tuple-element.97.refs_2_, ...), custom_call_target="tpu_custom_call" | custom-call | flops 2000000 | bytes 100000 | tf_op jit(solution)/shard_map/pallas_call | solution.py:962
  335.7 10.8 %all-to-all-done.1 = bf16[4,256,256]{2,1,0:T(8,128)(2,1)S(1)} async-done(((bf16[4,256,256]{2,1,0:T(8,128)(2,1)}), bf16[4,256,256]{2,1,0:T(8,128)(2,1)S(1)}, u32[]{:S(2)}, u32[]{:S(2)}) %all-to-all-start.1) | async-done | bytes 524320 | tf_op jit(solution)/shard_map/all_to_all | solution.py:1133
  346.5 10.0 %collective-permute-done.23.refs_15_ = bf16[1,2,3,1024,128]{4,3,2,1,0:T(8,128)(2,1)S(1)} collective-permute-done((bf16[1,2,3,1024,128]{4,3,2,1,0:T(8,128)(2,1)}, bf16[1,2,3,1024,128]{4,3,2,1,0:T(8,128)(2,1)S(1)}, u32[]{:S(2)}, u32[]{:S(2)}) %collective-permute-start.23) | collective-permute-done | bytes 1572896 | tf_op jit(solution)/shard_map/ppermute | solution.py:1047
  357.6 19.2 %shard_map.252 = (bf16[1,2,3,1024,128]{4,3,2,1,0:T(8,128)(2,1)}, bf16[1,2,3,1024,128]{4,3,2,1,0:T(8,128)(2,1)}, bf16[1,2,3,1024,128]{4,3,2,1,0:T(8,128)(2,1)}, b...) custom-call(bf16[1024,1024]{1,0:T(8,128)(2,1)} %get-tuple-element.94.refs_14_.refs_0_, ...), custom_call_target="tpu_custom_call" | custom-call | flops 13200000 | bytes 100000 | tf_op jit(solution)/shard_map/pallas_call | solution.py:863
  380.5 17.0 %shard_map.253 = (bf16[8,136,512]{2,1,0:T(8,128)(2,1)}, bf16[256,1024]{1,0:T(8,128)(2,1)}, bf16[256,1024]{1,0:T(8,128)(2,1)}, bf16[256,1024]{1,0:T(8,128)(2,1)}, bf16[256,1024]{1,0:T(8,128)(2,1)}) custom-call(s32[3]{0:T(128)} %pad_add_fusion.refs_0_, bf16[1024,256]{1,0:T(8,128)(2,1)} %bitcast.30, bf16[1024,256]{1,0:T(8,128)(2,1)} %get-tuple-element.79.refs_2_, ...), custom_call_target="tpu_custom_call" | custom-call | flops 16000000 | bytes 100000 | tf_op jit(solution)/shard_map/pallas_call | solution.py:575
  397.5 9.5 %shard_map.254.refs_0_ = bf16[2,2,3,1024,128]{4,3,2,1,0:T(8,128)(2,1)} custom-call(bf16[1024,1024]{1,0:T(8,128)(2,1)} %get-tuple-element.94.refs_14_.refs_0_, bf16[1024,1024]{1,0:T(8,128)(2,1)} %get-tuple-element.103.refs_1_, bf16[256,4096]{1,0:T(8,128)(2,1)} %get-tuple-element.104.refs_2_, bf16[256,4096]{1,0:T(8,128)(2,1)} %get-tuple-element.91.refs_12_.refs_3_, ...), custom_call_target="tpu_custom_call" | custom-call | flops 4400000 | bytes 100000 | tf_op jit(solution)/shard_map/pallas_call | solution.py:863
  407.0 6.1 %collective-permute-done.25 = bf16[256,1024]{1,0:T(8,128)(2,1)S(1)} collective-permute-done((bf16[256,1024]{1,0:T(8,128)(2,1)}, bf16[256,1024]{1,0:T(8,128)(2,1)S(1)}, u32[]{:S(2)}, u32[]{:S(2)}) %collective-permute-start.25) | collective-permute-done | bytes 524320 | tf_op jit(solution)/shard_map/ppermute | solution.py:1151
  421.0 12.3 %collective-permute-done.29 = bf16[256,1024]{1,0:T(8,128)(2,1)} collective-permute-done((bf16[256,1024]{1,0:T(8,128)(2,1)}, bf16[256,1024]{1,0:T(8,128)(2,1)}, u32[]{:S(2)}, u32[]{:S(2)}) %collective-permute-start.29) | collective-permute-done | bytes 524320 | tf_op jit(solution)/shard_map/ppermute | solution.py:1153
  437.1 6.7 %reduce-scatter.4.cloned.1.call-done = bf16[1,136,512]{2,1,0:T(8,128)(2,1)} async-done(((bf16[8,136,512]{2,1,0:T(8,128)(2,1)}), bf16[1,136,512]{2,1,0:T(8,128)(2,1)}) %reduce-scatter.4.cloned.1.call-update) | async-done | bytes 139280 | tf_op jit(solution)/shard_map/reduce_scatter | solution.py:1164
  443.8 5.8 %collective-permute-done.30.refs_1_ = bf16[256,1024]{1,0:T(8,128)(2,1)S(1)} collective-permute-done((bf16[256,1024]{1,0:T(8,128)(2,1)}, bf16[256,1024]{1,0:T(8,128)(2,1)S(1)}, u32[]{:S(2)}, u32[]{:S(2)}) %collective-permute-start.30) | collective-permute-done | bytes 524320 | tf_op jit(solution)/shard_map/ppermute | solution.py:1156
  460.3 5.8 %shard_map.256 = (f32[2,2,1024,128]{3,2,1,0:T(8,128)}, f32[2,2,1024,128]{3,2,1,0:T(8,128)}, f32[2,2,1024,128]{3,2,1,0:T(8,128)}) custom-call(bf16[2,2,3,1024,128]{4,3,2,1,0:T(8,128)(2,1)} %shard_map.254.refs_0_, bf16[1,2,3,1024,128]{4,3,2,1,0:T(8,128)(2,1)} %copy-done.14, bf16[1,2,3,1024,128]{4,3,2,1,0:T(8,128)(2,1)} %collective-permute-done.34.refs_2_, ...), custom_call_target="tpu_custom_call" | custom-call | flops 5000000 | bytes 100000 | tf_op jit(solution)/shard_map/pallas_call | solution.py:893
  (166 shorter events, 95.1 us)
Async XLA Ops:
  7.2 67.3 %all-gather.6.cloned.1.call-start = ((), (), s32[]{:S(2)}) async-start(), calls=%async_computation.8 | async-start | bytes 1253376 | tf_op jit(solution)/shard_map/all_gather | solution.py:1079
  9.7 109.1 %all-gather.8.cloned.1.call-start = ((), (), s32[]{:S(2)}) async-start(), calls=%async_computation.9 | async-start | bytes 2506752 | tf_op jit(solution)/shard_map/all_gather | solution.py:1080
  12.0 62.5 %collective-permute-start.3 = (bf16[4,3,1024,128]{3,2,1,0:T(8,128)(2,1)S(1)}, bf16[4,3,1024,128]{3,2,1,0:T(8,128)(2,1)}, u32[]{:S(2)}, u32[]{:S(2)}) collective-permute-start(bf16[4,3,1024,128]{3,2,1,0:T(8,128)(2,1)S(1)} %pad_maximum_fusion.refs_2_), channel_id=1, source_target_pairs={{0,4},{4,0},{8,12},{12,8},{16,20},{20,16},{24,28},{28,24},{1,5},{5... | collective-permute-start | bytes 9437192 | tf_op jit(solution)/shard_map/ppermute | solution.py:1047
  28.6 80.3 %collective-permute-start.4 = (bf16[4,3,1024,128]{3,2,1,0:T(8,128)(2,1)S(1)}, bf16[4,3,1024,128]{3,2,1,0:T(8,128)(2,1)}, u32[]{:S(2)}, u32[]{:S(2)}) collective-permute-start(bf16[4,3,1024,128]{3,2,1,0:T(8,128)(2,1)S(1)} %pad_maximum_fusion.refs_2_), channel_id=1, source_target_pairs={{0,8},{4,12},{8,0},{12,4},{16,24},{20,28},{24,16},{28,20},{1,9},{5... | collective-permute-start | bytes 9437192 | tf_op jit(solution)/shard_map/ppermute | solution.py:1047
  30.2 79.9 %collective-permute-start.5 = (bf16[4,3,1024,128]{3,2,1,0:T(8,128)(2,1)S(1)}, bf16[4,3,1024,128]{3,2,1,0:T(8,128)(2,1)}, u32[]{:S(2)}, u32[]{:S(2)}) collective-permute-start(bf16[4,3,1024,128]{3,2,1,0:T(8,128)(2,1)S(1)} %pad_maximum_fusion.refs_2_), channel_id=1, source_target_pairs={{0,16},{4,20},{8,24},{12,28},{16,0},{20,4},{24,8},{28,12},{1,17},{... | collective-permute-start | bytes 9437192 | tf_op jit(solution)/shard_map/ppermute | solution.py:1047
  86.7 17.1 %collective-permute-start.7 = (bf16[256,1024]{1,0:T(8,128)(2,1)}, bf16[256,1024]{1,0:T(8,128)(2,1)}, u32[]{:S(2)}, u32[]{:S(2)}) collective-permute-start(bf16[256,1024]{1,0:T(8,128)(2,1)} %collective-permute-done.6.refs_1_.refs_5_), channel_id=1, source_target_pairs={{0,1},{1,2},{2,3},{3,0},{4,5},{5,6},{6,7},{7,4},{8,9},{9,10},{10,1... | collective-permute-start | bytes 1572872 | tf_op jit(solution)/shard_map/ppermute | solution.py:1018
  86.7 33.1 %all-to-all-start = ((bf16[4,256,256]{2,1,0:T(8,128)(2,1)}), bf16[4,256,256]{2,1,0:T(8,128)(2,1)}, u32[]{:S(2)}, u32[]{:S(2)}) async-start(bf16[4,256,256]{2,1,0:T(8,128)(2,1)} %bitcast.32), calls=%async_computation | async-start | bytes 1048576 | tf_op jit(solution)/shard_map/all_to_all | solution.py:1093
  103.7 21.1 %collective-permute-start.8 = (bf16[256,1024]{1,0:T(8,128)(2,1)}, bf16[256,1024]{1,0:T(8,128)(2,1)}, u32[]{:S(2)}, u32[]{:S(2)}) collective-permute-start(bf16[256,1024]{1,0:T(8,128)(2,1)} %collective-permute-done.7.refs_2_.refs_1_.refs_6_), channel_id=1, source_target_pairs={{0,1},{1,2},{2,3},{3,0},{4,5},{5,6},{6,7},{7,4},{8,9},{9,10},{10,1... | collective-permute-start | bytes 1572872 | tf_op jit(solution)/shard_map/ppermute | solution.py:1018
  115.4 35.2 %collective-permute-start.13 = (bf16[2,3,1024,128]{3,2,1,0:T(8,128)(2,1)}, bf16[2,3,1024,128]{3,2,1,0:T(8,128)(2,1)}, u32[]{:S(2)}, u32[]{:S(2)}) collective-permute-start(bf16[2,3,1024,128]{3,2,1,0:T(8,128)(2,1)} %get-tuple-element.87), channel_id=1, source_target_pairs={{0,16},{4,20},{8,24},{12,28},{16,0},{20,4},{24,8},{28,12},{1,17},{... | collective-permute-start | bytes 4718600 | tf_op jit(solution)/shard_map/ppermute | solution.py:1047
  116.9 39.2 %collective-permute-start.12 = (bf16[2,3,1024,128]{3,2,1,0:T(8,128)(2,1)}, bf16[2,3,1024,128]{3,2,1,0:T(8,128)(2,1)}, u32[]{:S(2)}, u32[]{:S(2)}) collective-permute-start(bf16[2,3,1024,128]{3,2,1,0:T(8,128)(2,1)} %get-tuple-element.84.refs_7_), channel_id=1, source_target_pairs={{0,8},{4,12},{8,0},{12,4},{16,24},{20,28},{24,16},{28,20},{1,9},{5... | collective-permute-start | bytes 4718600 | tf_op jit(solution)/shard_map/ppermute | solution.py:1047
  117.4 56.3 %collective-permute-start.10 = (bf16[4,3,1024,128]{3,2,1,0:T(8,128)(2,1)}, bf16[4,3,1024,128]{3,2,1,0:T(8,128)(2,1)S(1)}, u32[]{:S(2)}, u32[]{:S(2)}) collective-permute-start(bf16[4,3,1024,128]{3,2,1,0:T(8,128)(2,1)} %collective-permute-done.4.refs_0_.refs_4_), channel_id=1, source_target_pairs={{0,4},{4,0},{8,12},{12,8},{16,20},{20,16},{24,28},{28,24},{1,5},{5... | collective-permute-start | bytes 9437192 | tf_op jit(solution)/shard_map/ppermute | solution.py:1047
  117.4 57.1 %collective-permute-start.11 = (bf16[4,3,1024,128]{3,2,1,0:T(8,128)(2,1)}, bf16[4,3,1024,128]{3,2,1,0:T(8,128)(2,1)}, u32[]{:S(2)}, u32[]{:S(2)}) collective-permute-start(bf16[4,3,1024,128]{3,2,1,0:T(8,128)(2,1)} %collective-permute-done.5.refs_1_.refs_6_), channel_id=1, source_target_pairs={{0,4},{4,0},{8,12},{12,8},{16,20},{20,16},{24,28},{28,24},{1,5},{5... | collective-permute-start | bytes 9437192 | tf_op jit(solution)/shard_map/ppermute | solution.py:1047
  124.8 16.2 %collective-permute-start.9 = (bf16[256,1152]{1,0:T(8,128)(2,1)}, bf16[256,1152]{1,0:T(8,128)(2,1)S(1)}, u32[]{:S(2)}, u32[]{:S(2)}) collective-permute-start(bf16[256,1152]{1,0:T(8,128)(2,1)} %get-tuple-element.86.refs_0_.refs_10_), channel_id=1, source_target_pairs={{0,1},{1,2},{2,3},{3,0},{4,5},{5,6},{6,7},{7,4},{8,9},{9,10},{10,1... | collective-permute-start | bytes 1769480 | tf_op jit(solution)/shard_map/ppermute | solution.py:1018
  156.1 18.5 %collective-permute-start.16 = (bf16[2,3,1024,128]{3,2,1,0:T(8,128)(2,1)}, bf16[2,3,1024,128]{3,2,1,0:T(8,128)(2,1)}, u32[]{:S(2)}, u32[]{:S(2)}) collective-permute-start(bf16[2,3,1024,128]{3,2,1,0:T(8,128)(2,1)} %collective-permute-done.13.refs_9_), channel_id=1, source_target_pairs={{0,4},{4,0},{8,12},{12,8},{16,20},{20,16},{24,28},{28,24},{1,5},{5... | collective-permute-start | bytes 4718600 | tf_op jit(solution)/shard_map/ppermute | solution.py:1047
  156.1 18.4 %collective-permute-start.15 = (bf16[2,3,1024,128]{3,2,1,0:T(8,128)(2,1)}, bf16[2,3,1024,128]{3,2,1,0:T(8,128)(2,1)}, u32[]{:S(2)}, u32[]{:S(2)}) collective-permute-start(bf16[2,3,1024,128]{3,2,1,0:T(8,128)(2,1)} %collective-permute-done.12.refs_8_), channel_id=1, source_target_pairs={{0,4},{4,0},{8,12},{12,8},{16,20},{20,16},{24,28},{28,24},{1,5},{5... | collective-permute-start | bytes 4718600 | tf_op jit(solution)/shard_map/ppermute | solution.py:1047
  156.6 17.1 %collective-permute-start.17 = (bf16[256,1152]{1,0:T(8,128)(2,1)S(1)}, bf16[256,1152]{1,0:T(8,128)(2,1)S(1)}, u32[]{:S(2)}, u32[]{:S(2)}) collective-permute-start(bf16[256,1152]{1,0:T(8,128)(2,1)S(1)} %collective-permute-done.14.refs_0_.refs_2_), channel_id=1, source_target_pairs={{0,1},{1,2},{2,3},{3,0},{4,5},{5,6},{6,7},{7,4},{8,9},{9,10},{10,1... | collective-permute-start | bytes 1769480 | tf_op jit(solution)/shard_map/ppermute | solution.py:1018
  197.8 27.8 %collective-permute-start.18 = (bf16[256,2176]{1,0:T(8,128)(2,1)}, bf16[256,2176]{1,0:T(8,128)(2,1)S(1)}, u32[]{:S(2)}, u32[]{:S(2)}) collective-permute-start(bf16[256,2176]{1,0:T(8,128)(2,1)} %get-tuple-element.90), channel_id=1, source_target_pairs={{0,1},{1,2},{2,3},{3,0},{4,5},{5,6},{6,7},{7,4},{8,9},{9,10},{10,1... | collective-permute-start | bytes 3342344 | tf_op jit(solution)/shard_map/ppermute | solution.py:1117
  227.5 27.1 %collective-permute-start.19 = (bf16[256,2176]{1,0:T(8,128)(2,1)S(1)}, bf16[256,2176]{1,0:T(8,128)(2,1)S(1)}, u32[]{:S(2)}, u32[]{:S(2)}) collective-permute-start(bf16[256,2176]{1,0:T(8,128)(2,1)S(1)} %add_convert_fusion.1), channel_id=1, source_target_pairs={{0,1},{1,2},{2,3},{3,0},{4,5},{5,6},{6,7},{7,4},{8,9},{9,10},{10,1... | collective-permute-start | bytes 3342344 | tf_op jit(solution)/shard_map/ppermute | solution.py:1117
  256.5 26.8 %collective-permute-start.20 = (bf16[256,2176]{1,0:T(8,128)(2,1)S(1)}, bf16[256,2176]{1,0:T(8,128)(2,1)S(1)}, u32[]{:S(2)}, u32[]{:S(2)}) collective-permute-start(bf16[256,2176]{1,0:T(8,128)(2,1)S(1)} %add_convert_fusion), channel_id=1, source_target_pairs={{0,1},{1,2},{2,3},{3,0},{4,5},{5,6},{6,7},{7,4},{8,9},{9,10},{10,1... | collective-permute-start | bytes 3342344 | tf_op jit(solution)/shard_map/ppermute | solution.py:1117
  309.9 47.3 %collective-permute-start.22 = (bf16[4,2,3,1024,128]{4,3,2,1,0:T(8,128)(2,1)}, bf16[4,2,3,1024,128]{4,3,2,1,0:T(8,128)(2,1)}, u32[]{:S(2)}, u32[]{:S(2)}) collective-permute-start(bf16[4,2,3,1024,128]{4,3,2,1,0:T(8,128)(2,1)} %shard_map.248.refs_15_), channel_id=1, source_target_pairs={{0,4},{4,0},{8,12},{12,8},{16,20},{20,16},{24,28},{28,24},{1,5},{5... | collective-permute-start | bytes 18874376 | tf_op jit(solution)/shard_map/ppermute | solution.py:1047
  319.9 36.6 %collective-permute-start.23 = (bf16[1,2,3,1024,128]{4,3,2,1,0:T(8,128)(2,1)}, bf16[1,2,3,1024,128]{4,3,2,1,0:T(8,128)(2,1)S(1)}, u32[]{:S(2)}, u32[]{:S(2)}) collective-permute-start(bf16[1,2,3,1024,128]{4,3,2,1,0:T(8,128)(2,1)} %get-tuple-element.122), channel_id=1, source_target_pairs={{0,16},{4,20},{8,24},{12,28},{16,0},{20,4},{24,8},{28,12},{1,17},{... | collective-permute-start | bytes 4718600 | tf_op jit(solution)/shard_map/ppermute | solution.py:1047
  320.2 37.1 %collective-permute-start.24 = (bf16[1,2,3,1024,128]{4,3,2,1,0:T(8,128)(2,1)}, bf16[1,2,3,1024,128]{4,3,2,1,0:T(8,128)(2,1)}, u32[]{:S(2)}, u32[]{:S(2)}) collective-permute-start(bf16[1,2,3,1024,128]{4,3,2,1,0:T(8,128)(2,1)} %get-tuple-element.113.refs_11_), channel_id=1, source_target_pairs={{0,8},{4,12},{8,0},{12,4},{16,24},{20,28},{24,16},{28,20},{1,9},{5... | collective-permute-start | bytes 4718600 | tf_op jit(solution)/shard_map/ppermute | solution.py:1047
  328.6 17.9 %all-to-all-start.1 = ((bf16[4,256,256]{2,1,0:T(8,128)(2,1)}), bf16[4,256,256]{2,1,0:T(8,128)(2,1)S(1)}, u32[]{:S(2)}, u32[]{:S(2)}) async-start(bf16[4,256,256]{2,1,0:T(8,128)(2,1)} %bitcast.39), calls=%async_computation.1 | async-start | bytes 1048576 | tf_op jit(solution)/shard_map/all_to_all | solution.py:1133
  332.1 48.1 %reduce-scatter.6.cloned.1.call-start = ((), (), s32[]{:S(2)}) async-start(), calls=%async_computation.6 | async-start | bytes 2506752 | tf_op jit(solution)/shard_map/reduce_scatter | solution.py:1135
  335.6 84.4 %reduce-scatter.8.cloned.1.call-start = ((), (), s32[]{:S(2)}) async-start(), calls=%async_computation.7 | async-start | bytes 348160 | tf_op jit(solution)/shard_map/reduce_scatter | solution.py:1166
  376.9 20.6 %collective-permute-start.26 = (bf16[2,2,3,1024,128]{4,3,2,1,0:T(8,128)(2,1)}, bf16[2,2,3,1024,128]{4,3,2,1,0:T(8,128)(2,1)}, u32[]{:S(2)}, u32[]{:S(2)}) collective-permute-start(bf16[2,2,3,1024,128]{4,3,2,1,0:T(8,128)(2,1)} %get-tuple-element.127), channel_id=1, source_target_pairs={{0,4},{4,0},{8,12},{12,8},{16,20},{20,16},{24,28},{28,24},{1,5},{5... | collective-permute-start | bytes 9437192 | tf_op jit(solution)/shard_map/ppermute | solution.py:1047
  376.9 37.4 %collective-permute-start.27 = (bf16[1,2,3,1024,128]{4,3,2,1,0:T(8,128)(2,1)}, bf16[1,2,3,1024,128]{4,3,2,1,0:T(8,128)(2,1)S(1)}, u32[]{:S(2)}, u32[]{:S(2)}) collective-permute-start(bf16[1,2,3,1024,128]{4,3,2,1,0:T(8,128)(2,1)} %get-tuple-element.129), channel_id=1, source_target_pairs={{0,8},{4,12},{8,0},{12,4},{16,24},{20,28},{24,16},{28,20},{1,9},{5... | collective-permute-start | bytes 4718600 | tf_op jit(solution)/shard_map/ppermute | solution.py:1047
  379.1 36.8 %collective-permute-start.28 = (bf16[1,2,3,1024,128]{4,3,2,1,0:T(8,128)(2,1)}, bf16[1,2,3,1024,128]{4,3,2,1,0:T(8,128)(2,1)}, u32[]{:S(2)}, u32[]{:S(2)}) collective-permute-start(bf16[1,2,3,1024,128]{4,3,2,1,0:T(8,128)(2,1)} %get-tuple-element.130), channel_id=1, source_target_pairs={{0,16},{4,20},{8,24},{12,28},{16,0},{20,4},{24,8},{28,12},{1,17},{... | collective-permute-start | bytes 4718600 | tf_op jit(solution)/shard_map/ppermute | solution.py:1047
  380.2 63.6 %reduce-scatter.4.cloned.1.call-start = ((), (), s32[]{:S(2)}) async-start(), calls=%async_computation.5 | async-start | bytes 1253376 | tf_op jit(solution)/shard_map/reduce_scatter | solution.py:1164
  397.4 15.7 %collective-permute-start.25 = (bf16[256,1024]{1,0:T(8,128)(2,1)}, bf16[256,1024]{1,0:T(8,128)(2,1)S(1)}, u32[]{:S(2)}, u32[]{:S(2)}) collective-permute-start(bf16[256,1024]{1,0:T(8,128)(2,1)} %get-tuple-element.126), channel_id=1, source_target_pairs={{0,1},{1,2},{2,3},{3,0},{4,5},{5,6},{6,7},{7,4},{8,9},{9,10},{10,1... | collective-permute-start | bytes 1572872 | tf_op jit(solution)/shard_map/ppermute | solution.py:1151
  418.2 42.0 %collective-permute-start.34 = (bf16[1,2,3,1024,128]{4,3,2,1,0:T(8,128)(2,1)}, bf16[1,2,3,1024,128]{4,3,2,1,0:T(8,128)(2,1)}, u32[]{:S(2)}, u32[]{:S(2)}) collective-permute-start(bf16[1,2,3,1024,128]{4,3,2,1,0:T(8,128)(2,1)} %get-tuple-element.125.refs_12_), channel_id=1, source_target_pairs={{0,8},{4,12},{8,0},{12,4},{16,24},{20,28},{24,16},{28,20},{1,9},{5... | collective-permute-start | bytes 4718600 | tf_op jit(solution)/shard_map/ppermute | solution.py:1047
  419.0 41.2 %collective-permute-start.35 = (bf16[1,2,3,1024,128]{4,3,2,1,0:T(8,128)(2,1)}, bf16[1,2,3,1024,128]{4,3,2,1,0:T(8,128)(2,1)}, u32[]{:S(2)}, u32[]{:S(2)}) collective-permute-start(bf16[1,2,3,1024,128]{4,3,2,1,0:T(8,128)(2,1)} %get-tuple-element.140), channel_id=1, source_target_pairs={{0,16},{4,20},{8,24},{12,28},{16,0},{20,4},{24,8},{28,12},{1,17},{... | collective-permute-start | bytes 4718600 | tf_op jit(solution)/shard_map/ppermute | solution.py:1047
  (38 other events, 408.8 us)
Sparse Core Ops, SparseCore 0:
  10.5 29.4 all-gather.5
  41.8 37.7 all-gather.7
  336.3 42.4 reduce-scatter.5
  380.8 19.8 reduce-scatter.7
  404.4 39.3 reduce-scatter.3

commit v7 on v6

--- a/solution.py
+++ b/solution.py
@@ -1149,9 +1149,9 @@
     )
     (q0,) = wgrads((0, 1), ((0, 0), (0, 1)), [r1], ((0, 0), (0, 1)), after=[qkv_wgrad])
     moving = lax.ppermute(back_parts[1], "col", steps)
-    moving = (hold(moving, q0, x2a, y4b).astype(F32) + back_parts[2].astype(F32)).astype(BF16)
+    moving = (hold(moving, x2a, y4b).astype(F32) + back_parts[2].astype(F32)).astype(BF16)
     moving = lax.ppermute(moving, "col", steps)
-    moving = (moving.astype(F32) + back_parts[3].astype(F32)).astype(BF16)
+    moving = (hold(moving, q0).astype(F32) + back_parts[3].astype(F32)).astype(BF16)
     third_step = moving
     last_step = lax.ppermute(moving, "col", steps)
     attn_grad = last_step.astype(F32) + back_parts[0].astype(F32)

time: 482 us -> 500 us (1.037)
  blocking collectives: 16.1 us -> 33.6 us
    all_to_all x0 -> x1, blocking collectives: none -> 17.5 us  [fast(): lax.all_to_all(mixed_grad, 'col', split_axis=0, concat_axis=0, tiled=True)]
    ppermute x18, waiting for transfers between devices: 29 us -> 43 us  [swap(): return lax.ppermute(value, 'row', [(i, i ^ mask) for i in range(8)])]
    all_to_all x1 -> x0, waiting for transfers between devices: 10.8 us -> none  [fast(): lax.all_to_all(mixed_grad, 'col', split_axis=0, concat_axis=0, tiled=True)]
    ppermute x1, waiting for transfers between devices: 12.3 us -> 2.57 us  [fast(): moving = lax.ppermute(moving, 'col', steps)]
    ppermute x1, waiting for transfers between devices: 6.12 us -> 15.7 us  [fast(): moving = lax.ppermute(back_parts[1], 'col', steps)]
  transfers between devices with their start and end apart: 43 -> 42, of which waited for: 22 -> 22; matrix products, arithmetic and copies ran while one was open for 5% -> 5% of each run, Pallas kernels for 35% -> 34%
where the time goes in v7:
time: 500 us; the launch traced here: 491 us
  Pallas kernels  210 us (42%)
  waiting for transfers between devices  163 us (33%)
  blocking collectives  33.6 us (7%)
  starting transfers between devices  29.1 us (6%)
  other arithmetic  23.2 us (5%)
  local copies, waits for them, and re-layouts  15.9 us (3%)
  between operations  15.3 us (3%)
    pallas_call x4, Pallas kernels, experts(): pl.pallas_call(behind(expert_kernel, 12, after), out_shape=(jax.ShapeDtyp...  87 us
    ppermute x7, waiting for transfers between devices, ring_gather(): chunks.append(lax.ppermute(chunks[-1], 'col', steps))  73.4 us
    pallas_call x6, Pallas kernels, expert_wgrads(): pl.pallas_call(behind(kernel, 14 + len(extras), after), grid=(count,), ou...  61.8 us
    ppermute x18, waiting for transfers between devices, swap(): return lax.ppermute(value, 'row', [(i, i ^ mask) for i in range(8)])  43 us
    all_to_all x1, blocking collectives, fast(): lax.all_to_all(mixed_grad, 'col', split_axis=0, concat_axis=0, tiled=True)  17.5 us
    pallas_call x1, Pallas kernels, attend_back(): pl.pallas_call(behind(attend_back_kernel, 12, after), out_shape=shapes, i...  17 us
    all_gather x1, blocking collectives, fast(): pack_out = lax.all_gather(pack_out, 'col', axis=0)  16.1 us
    ppermute x18, starting transfers between devices, swap(): return lax.ppermute(value, 'row', [(i, i ^ mask) for i in range(8)])  15.9 us
  transfers between devices with their start and end apart: 42, of which 22 were waited for; matrix products, arithmetic and copies ran while one was open for 5% of the time, Pallas kernels for 34%

profile of v7, /device:TPU:0, one launch (start us, length us, event | category | flops | bytes accessed | tf_op | source)
XLA Modules:
  0.0 490.5 jit_solution(1365066843991914803)
XLA Ops:
  12.5 16.1 %all-gather.1 = bf16[544,256]{1,0:T(8,128)(2,1)} all-gather(bf16[136,256]{1,0:T(8,128)(2,1)S(1)} %fusion.9), channel_id=3, replica_groups=mesh['row'=8,'col'=4] {'col'}, dimensions={0}, use_global_device_ids=true | all-gather | bytes 348160 | tf_op jit(solution)/shard_map/all_gather | solution.py:1078
  46.1 12.3 %collective-permute-done.1.refs_3_ = bf16[256,1024]{1,0:T(8,128)(2,1)S(1)} collective-permute-done((bf16[256,1024]{1,0:T(8,128)(2,1)}, bf16[256,1024]{1,0:T(8,128)(2,1)S(1)}, u32[]{:S(2)}, u32[]{:S(2)}) %collective-permute-start.1) | collective-permute-done | bytes 524320 | tf_op jit(solution)/shard_map/ppermute | solution.py:1018
  59.2 11.2 %collective-permute-done.2.refs_4_ = bf16[256,1024]{1,0:T(8,128)(2,1)S(1)} collective-permute-done((bf16[256,1024]{1,0:T(8,128)(2,1)S(1)}, bf16[256,1024]{1,0:T(8,128)(2,1)S(1)}, u32[]{:S(2)}, u32[]{:S(2)}) %collective-permute-start.2) | collective-permute-done | bytes 524320 | tf_op jit(solution)/shard_map/ppermute | solution.py:1018
  74.5 12.1 %shard_map.238 = (bf16[1024,1024]{1,0:T(8,128)(2,1)}, bf16[4,1024,64]{2,1,0:T(8,128)(2,1)}, bf16[2,1024,64]{2,1,0:T(8,128)(2,1)}, bf16[2,1024,64]{2,1,0:T(8,128)...) custom-call(s32[3]{0:T(128)} %pad_add_fusion.refs_0_, ...), custom_call_target="tpu_custom_call" | custom-call | flops 10000000 | bytes 100000 | tf_op jit(solution)/shard_map/pallas_call | solution.py:498
  86.7 5.7 %all-to-all-start = ((bf16[4,256,256]{2,1,0:T(8,128)(2,1)}), bf16[4,256,256]{2,1,0:T(8,128)(2,1)}, u32[]{:S(2)}, u32[]{:S(2)}) async-start(bf16[4,256,256]{2,1,0:T(8,128)(2,1)} %bitcast.32), calls=%async_computation | async-start | bytes 1048576 | tf_op jit(solution)/shard_map/all_to_all | solution.py:1093
  92.4 11.3 %collective-permute-done.7.refs_2_.refs_1_.refs_6_ = bf16[256,1024]{1,0:T(8,128)(2,1)} collective-permute-done((bf16[256,1024]{1,0:T(8,128)(2,1)}, bf16[256,1024]{1,0:T(8,128)(2,1)}, u32[]{:S(2)}, u32[]{:S(2)}) %collective-permute-start.7) | collective-permute-done | bytes 524320 | tf_op jit(solution)/shard_map/ppermute | solution.py:1018
  110.1 5.2 %shard_map.239 = (bf16[2,3,1024,128]{3,2,1,0:T(8,128)(2,1)}, bf16[2,3,1024,128]{3,2,1,0:T(8,128)(2,1)}) custom-call(bf16[4,3,1024,128]{3,2,1,0:T(8,128)(2,1)} %collective-permute-done.4.refs_0_.refs_4_, bf16[4,3,1024,128]{3,2,1,0:T(8,128)(2,1)} %collective-permute-done.5.refs_1_.refs_6_, bf16[256,1024]{1,0:T(8,128)(2,1)} %collective-permute-done.7.refs_2_.refs_1_.refs_6_), custom_call_target="tpu_custom_call" | custom-call | flops 3000000 | bytes 100000 | tf_op jit(solution)/shard_map/pallas_call | solution.py:914
  119.8 5.0 %shard_map.240 = (f32[256,1024]{1,0:T(8,128)}, bf16[256,1152]{1,0:T(8,128)(2,1)}, f32[256,128]{1,0:T(8,128)}, f32[256,128]{1,0:T(8,128)}, bf16[1024,1024]{1,0:T(8,128)(2,1)}, /*index=5*/bf16[128,1024]{1,0:T(8,128)(2,1)}) custom-call(s32[3]{0:T(128)} %pad_add_fusion.refs_0_, bf16[1024,256]{1,0:T(8,128)(2,1)} %bitcast.8.refs_1_.mixed_ref, ...), custom_call_target="tpu_custom_call" | custom-call | flops 2000000 | bytes 100000 | tf_op jit(solution)/shard_map/pallas_call | solution.py:647
  125.1 15.9 %collective-permute-done.9.refs_0_.refs_1_ = bf16[256,1152]{1,0:T(8,128)(2,1)S(1)} collective-permute-done((bf16[256,1152]{1,0:T(8,128)(2,1)}, bf16[256,1152]{1,0:T(8,128)(2,1)S(1)}, u32[]{:S(2)}, u32[]{:S(2)}) %collective-permute-start.9) | collective-permute-done | bytes 589856 | tf_op jit(solution)/shard_map/ppermute | solution.py:1018
  141.0 9.5 %collective-permute-done.13.refs_9_ = bf16[2,3,1024,128]{3,2,1,0:T(8,128)(2,1)} collective-permute-done((bf16[2,3,1024,128]{3,2,1,0:T(8,128)(2,1)}, bf16[2,3,1024,128]{3,2,1,0:T(8,128)(2,1)}, u32[]{:S(2)}, u32[]{:S(2)}) %collective-permute-start.13) | collective-permute-done | bytes 1572896 | tf_op jit(solution)/shard_map/ppermute | solution.py:1047
  150.5 5.5 %collective-permute-done.14.refs_0_.refs_2_ = bf16[256,1152]{1,0:T(8,128)(2,1)S(1)} collective-permute-done((bf16[256,1152]{1,0:T(8,128)(2,1)S(1)}, bf16[256,1152]{1,0:T(8,128)(2,1)S(1)}, u32[]{:S(2)}, u32[]{:S(2)}) %collective-permute-start.14) | collective-permute-done | bytes 589856 | tf_op jit(solution)/shard_map/ppermute | solution.py:1018
  156.6 17.1 %collective-permute-done.17.refs_12_.refs_3_.refs_0_ = bf16[256,1152]{1,0:T(8,128)(2,1)S(1)} collective-permute-done((bf16[256,1152]{1,0:T(8,128)(2,1)S(1)}, bf16[256,1152]{1,0:T(8,128)(2,1)S(1)}, u32[]{:S(2)}, u32[]{:S(2)}) %collective-permute-start.17) | collective-permute-done | bytes 589856 | tf_op jit(solution)/shard_map/ppermute | solution.py:1018
  176.1 21.7 %shard_map.241 = (bf16[256,2176]{1,0:T(8,128)(2,1)}, bf16[256,4096]{1,0:T(8,128)(2,1)}, bf16[256,4096]{1,0:T(8,128)(2,1)}, bf16[256,4096]{1,0:T(8,128)(2,1)}) custom-call(bf16[256,1152]{1,0:T(8,128)(2,1)} %copy-done.10, bf16[256,1024]{1,0:T(8,128)(2,1)} %collective-permute-done.6.refs_1_.refs_5_, bf16[4,3,1024,128]{3,2,1,0:T(8,128)(2,1)} %copy-done, ...), custom_call_target="tpu_custom_call" | custom-call | flops 21000000 | bytes 100000 | tf_op jit(solution)/shard_map/pallas_call | solution.py:724
  197.9 21.7 %shard_map.242 = (bf16[256,2176]{1,0:T(8,128)(2,1)}, bf16[256,4096]{1,0:T(8,128)(2,1)}, bf16[256,4096]{1,0:T(8,128)(2,1)}, bf16[256,4096]{1,0:T(8,128)(2,1)}) custom-call(bf16[256,1152]{1,0:T(8,128)(2,1)} %copy-done.9, bf16[256,1024]{1,0:T(8,128)(2,1)} %collective-permute-done.7.refs_2_.refs_1_.refs_6_, bf16[4,3,1024,128]{3,2,1,0:T(8,128)(2,1)} %copy-done, ...), custom_call_target="tpu_custom_call" | custom-call | flops 21000000 | bytes 100000 | tf_op jit(solution)/shard_map/pallas_call | solution.py:724
  219.6 6.0 %collective-permute-done.18.refs_13_ = bf16[256,2176]{1,0:T(8,128)(2,1)S(1)} collective-permute-done((bf16[256,2176]{1,0:T(8,128)(2,1)}, bf16[256,2176]{1,0:T(8,128)(2,1)S(1)}, u32[]{:S(2)}, u32[]{:S(2)}) %collective-permute-start.18) | collective-permute-done | bytes 1114144 | tf_op jit(solution)/shard_map/ppermute | solution.py:1117
  227.6 5.3 %shard_map.243 = (bf16[1024,1024]{1,0:T(8,128)(2,1)}, bf16[1024,1024]{1,0:T(8,128)(2,1)}) custom-call(bf16[256,1152]{1,0:T(8,128)(2,1)} %get-tuple-element.87.refs_0_.refs_10_, bf16[256,1152]{1,0:T(8,128)(2,1)} %copy-done.10, bf16[256,1152]{1,0:T(8,128)(2,1)} %copy-done.9, bf16[256,1152]{1,0:T(8,128)(2,1)} %copy-done.4, bf16[256,1024]{1,0:T(8,128)(2,1)} %refs_7_.1, ...), custom_call_target="tpu_custom_call" | custom-call | flops 2000000 | bytes 100000 | tf_op jit(solution)/shard_map/pallas_call | solution.py:755
  232.8 21.8 %shard_map.244 = (bf16[256,2176]{1,0:T(8,128)(2,1)}, bf16[256,4096]{1,0:T(8,128)(2,1)}, bf16[256,4096]{1,0:T(8,128)(2,1)}, bf16[256,4096]{1,0:T(8,128)(2,1)}) custom-call(bf16[256,1152]{1,0:T(8,128)(2,1)} %copy-done.4, bf16[256,1024]{1,0:T(8,128)(2,1)} %collective-permute-done.8.refs_7_.refs_1_, bf16[4,3,1024,128]{3,2,1,0:T(8,128)(2,1)} %copy-done, ...), custom_call_target="tpu_custom_call" | custom-call | flops 21000000 | bytes 100000 | tf_op jit(solution)/shard_map/pallas_call | solution.py:724
  256.8 21.8 %shard_map.245 = (bf16[256,2176]{1,0:T(8,128)(2,1)}, bf16[256,4096]{1,0:T(8,128)(2,1)}, bf16[256,4096]{1,0:T(8,128)(2,1)}, bf16[256,4096]{1,0:T(8,128)(2,1)}) custom-call(bf16[256,1152]{1,0:T(8,128)(2,1)} %get-tuple-element.87.refs_0_.refs_10_, bf16[256,1024]{1,0:T(8,128)(2,1)} %refs_7_.1, bf16[4,3,1024,128]{3,2,1,0:T(8,128)(2,1)} %copy-done, ...), custom_call_target="tpu_custom_call" | custom-call | flops 21000000 | bytes 100000 | tf_op jit(solution)/shard_map/pallas_call | solution.py:724
  278.6 4.8 collective-permute-done.20.refs_14_.refs_1_
  284.3 8.0 %shard_map.246.refs_14_ = bf16[2,2,3,1024,128]{4,3,2,1,0:T(8,128)(2,1)} custom-call(bf16[1024,1024]{1,0:T(8,128)(2,1)} %get-tuple-element.95.refs_14_.refs_0_, bf16[1024,1024]{1,0:T(8,128)(2,1)} %get-tuple-element.104.refs_1_, bf16[256,4096]{1,0:T(8,128)(2,1)} %get-tuple-element.105.refs_2_, bf16[256,4096]{1,0:T(8,128)(2,1)} %get-tuple-element.92.refs_12_.refs_3_, ...), custom_call_target="tpu_custom_call" | custom-call | flops 4400000 | bytes 100000 | tf_op jit(solution)/shard_map/pallas_call | solution.py:863
  292.4 8.0 %shard_map.247.refs_14_ = bf16[4,2,3,1024,128]{4,3,2,1,0:T(8,128)(2,1)} custom-call(bf16[1024,1024]{1,0:T(8,128)(2,1)} %get-tuple-element.95.refs_14_.refs_0_, bf16[1024,1024]{1,0:T(8,128)(2,1)} %get-tuple-element.104.refs_1_, bf16[256,4096]{1,0:T(8,128)(2,1)} %get-tuple-element.105.refs_2_, bf16[256,4096]{1,0:T(8,128)(2,1)} %get-tuple-element.92.refs_12_.refs_3_, ...), custom_call_target="tpu_custom_call" | custom-call | flops 4400000 | bytes 100000 | tf_op jit(solution)/shard_map/pallas_call | solution.py:863
  302.1 7.9 %shard_map.248.refs_15_ = bf16[4,2,3,1024,128]{4,3,2,1,0:T(8,128)(2,1)} custom-call(bf16[1024,1024]{1,0:T(8,128)(2,1)} %get-tuple-element.95.refs_14_.refs_0_, bf16[1024,1024]{1,0:T(8,128)(2,1)} %get-tuple-element.104.refs_1_, bf16[256,4096]{1,0:T(8,128)(2,1)} %get-tuple-element.105.refs_2_, ...), custom_call_target="tpu_custom_call", output_to_operand_aliasing={{}: (14, {})} | custom-call | flops 4400000 | bytes 100000 | tf_op jit(solution)/shard_map/pallas_call | solution.py:863
  310.6 9.4 %shard_map.249 = (bf16[1,2,3,1024,128]{4,3,2,1,0:T(8,128)(2,1)}, bf16[1,2,3,1024,128]{4,3,2,1,0:T(8,128)(2,1)}) custom-call(bf16[1024,1024]{1,0:T(8,128)(2,1)} %get-tuple-element.95.refs_14_.refs_0_, bf16[1024,1024]{1,0:T(8,128)(2,1)} %get-tuple-element.104.refs_1_, bf16[256,4096]{1,0:T(8,128)(2,1)} %get-tuple-element.105.refs_2_, ...), custom_call_target="tpu_custom_call" | custom-call | flops 4400000 | bytes 100000 | tf_op jit(solution)/shard_map/pallas_call | solution.py:863
  320.0 6.0 %shard_map.250 = (f32[256,1024]{1,0:T(8,128)}, f32[256,1024]{1,0:T(8,128)}, bf16[256,1024]{1,0:T(8,128)(2,1)}, bf16[1024,256]{1,0:T(8,128)(2,1)}, f32[136,1024]{1,0:T(8,128)}) custom-call(s32[3]{0:T(128)} %pad_add_fusion.refs_0_, bf16[256,2176]{1,0:T(8,128)(2,1)} %copy-done.6, bf16[256,2176]{1,0:T(8,128)(2,1)} %get-tuple-element.98.refs_2_, ...), custom_call_target="tpu_custom_call" | custom-call | flops 2000000 | bytes 100000 | tf_op jit(solution)/shard_map/pallas_call | solution.py:962
  332.3 17.5 %all_to_all.22 = bf16[4,256,256]{2,1,0:T(8,128)(2,1)} all-to-all(bf16[4,256,256]{2,1,0:T(8,128)(2,1)S(1)} %bitcast.39), channel_id=1, replica_groups=mesh['row'=8,'col'=4] {'col'}, dimensions={0} | all-to-all | bytes 1048576 | tf_op jit(solution)/shard_map/all_to_all | solution.py:1133
  349.8 22.4 %collective-permute-done.23.refs_15_ = bf16[1,2,3,1024,128]{4,3,2,1,0:T(8,128)(2,1)S(1)} collective-permute-done((bf16[1,2,3,1024,128]{4,3,2,1,0:T(8,128)(2,1)}, bf16[1,2,3,1024,128]{4,3,2,1,0:T(8,128)(2,1)S(1)}, u32[]{:S(2)}, u32[]{:S(2)}) %collective-permute-start.23) | collective-permute-done | bytes 1572896 | tf_op jit(solution)/shard_map/ppermute | solution.py:1047
  376.0 19.0 %shard_map.252 = (bf16[1,2,3,1024,128]{4,3,2,1,0:T(8,128)(2,1)}, bf16[1,2,3,1024,128]{4,3,2,1,0:T(8,128)(2,1)}, bf16[1,2,3,1024,128]{4,3,2,1,0:T(8,128)(2,1)}, b...) custom-call(bf16[1024,1024]{1,0:T(8,128)(2,1)} %get-tuple-element.95.refs_14_.refs_0_, ...), custom_call_target="tpu_custom_call" | custom-call | flops 13200000 | bytes 100000 | tf_op jit(solution)/shard_map/pallas_call | solution.py:863
  399.1 17.0 %shard_map.253 = (bf16[8,136,512]{2,1,0:T(8,128)(2,1)}, bf16[256,1024]{1,0:T(8,128)(2,1)}, bf16[256,1024]{1,0:T(8,128)(2,1)}, bf16[256,1024]{1,0:T(8,128)(2,1)}, bf16[256,1024]{1,0:T(8,128)(2,1)}) custom-call(s32[3]{0:T(128)} %pad_add_fusion.refs_0_, bf16[1024,256]{1,0:T(8,128)(2,1)} %bitcast.30, bf16[1024,256]{1,0:T(8,128)(2,1)} %get-tuple-element.80.refs_2_, ...), custom_call_target="tpu_custom_call" | custom-call | flops 16000000 | bytes 100000 | tf_op jit(solution)/shard_map/pallas_call | solution.py:575
  416.2 15.7 %collective-permute-done.25 = bf16[256,1024]{1,0:T(8,128)(2,1)S(1)} collective-permute-done((bf16[256,1024]{1,0:T(8,128)(2,1)}, bf16[256,1024]{1,0:T(8,128)(2,1)S(1)}, u32[]{:S(2)}, u32[]{:S(2)}) %collective-permute-start.25) | collective-permute-done | bytes 524320 | tf_op jit(solution)/shard_map/ppermute | solution.py:1151
  439.5 9.5 %shard_map.254.refs_0_ = bf16[2,2,3,1024,128]{4,3,2,1,0:T(8,128)(2,1)} custom-call(bf16[1024,1024]{1,0:T(8,128)(2,1)} %get-tuple-element.95.refs_14_.refs_0_, bf16[1024,1024]{1,0:T(8,128)(2,1)} %get-tuple-element.104.refs_1_, bf16[256,4096]{1,0:T(8,128)(2,1)} %get-tuple-element.105.refs_2_, bf16[256,4096]{1,0:T(8,128)(2,1)} %get-tuple-element.92.refs_12_.refs_3_, ...), custom_call_target="tpu_custom_call" | custom-call | flops 4400000 | bytes 100000 | tf_op jit(solution)/shard_map/pallas_call | solution.py:863
  458.1 8.9 %collective-permute-done.30.refs_1_ = bf16[256,1024]{1,0:T(8,128)(2,1)S(1)} collective-permute-done((bf16[256,1024]{1,0:T(8,128)(2,1)S(1)}, bf16[256,1024]{1,0:T(8,128)(2,1)S(1)}, u32[]{:S(2)}, u32[]{:S(2)}) %collective-permute-start.30) | collective-permute-done | bytes 524320 | tf_op jit(solution)/shard_map/ppermute | solution.py:1156
  477.7 5.8 %shard_map.256 = (f32[2,2,1024,128]{3,2,1,0:T(8,128)}, f32[2,2,1024,128]{3,2,1,0:T(8,128)}, f32[2,2,1024,128]{3,2,1,0:T(8,128)}) custom-call(bf16[2,2,3,1024,128]{4,3,2,1,0:T(8,128)(2,1)} %shard_map.254.refs_0_, bf16[1,2,3,1024,128]{4,3,2,1,0:T(8,128)(2,1)} %copy-done.14, bf16[1,2,3,1024,128]{4,3,2,1,0:T(8,128)(2,1)} %collective-permute-done.34.refs_2_, ...), custom_call_target="tpu_custom_call" | custom-call | flops 5000000 | bytes 100000 | tf_op jit(solution)/shard_map/pallas_call | solution.py:893
  (163 shorter events, 90.2 us)
Async XLA Ops:
  7.2 67.3 %all-gather.6.cloned.1.call-start = ((), (), s32[]{:S(2)}) async-start(), calls=%async_computation.8 | async-start | bytes 1253376 | tf_op jit(solution)/shard_map/all_gather | solution.py:1079
  9.7 109.1 %all-gather.8.cloned.1.call-start = ((), (), s32[]{:S(2)}) async-start(), calls=%async_computation.9 | async-start | bytes 2506752 | tf_op jit(solution)/shard_map/all_gather | solution.py:1080
  12.0 62.5 %collective-permute-start.3 = (bf16[4,3,1024,128]{3,2,1,0:T(8,128)(2,1)S(1)}, bf16[4,3,1024,128]{3,2,1,0:T(8,128)(2,1)}, u32[]{:S(2)}, u32[]{:S(2)}) collective-permute-start(bf16[4,3,1024,128]{3,2,1,0:T(8,128)(2,1)S(1)} %pad_maximum_fusion.refs_2_), channel_id=1, source_target_pairs={{0,4},{4,0},{8,12},{12,8},{16,20},{20,16},{24,28},{28,24},{1,5},{5... | collective-permute-start | bytes 9437192 | tf_op jit(solution)/shard_map/ppermute | solution.py:1047
  28.6 80.3 %collective-permute-start.4 = (bf16[4,3,1024,128]{3,2,1,0:T(8,128)(2,1)S(1)}, bf16[4,3,1024,128]{3,2,1,0:T(8,128)(2,1)}, u32[]{:S(2)}, u32[]{:S(2)}) collective-permute-start(bf16[4,3,1024,128]{3,2,1,0:T(8,128)(2,1)S(1)} %pad_maximum_fusion.refs_2_), channel_id=1, source_target_pairs={{0,8},{4,12},{8,0},{12,4},{16,24},{20,28},{24,16},{28,20},{1,9},{5... | collective-permute-start | bytes 9437192 | tf_op jit(solution)/shard_map/ppermute | solution.py:1047
  30.2 79.9 %collective-permute-start.5 = (bf16[4,3,1024,128]{3,2,1,0:T(8,128)(2,1)S(1)}, bf16[4,3,1024,128]{3,2,1,0:T(8,128)(2,1)}, u32[]{:S(2)}, u32[]{:S(2)}) collective-permute-start(bf16[4,3,1024,128]{3,2,1,0:T(8,128)(2,1)S(1)} %pad_maximum_fusion.refs_2_), channel_id=1, source_target_pairs={{0,16},{4,20},{8,24},{12,28},{16,0},{20,4},{24,8},{28,12},{1,17},{... | collective-permute-start | bytes 9437192 | tf_op jit(solution)/shard_map/ppermute | solution.py:1047
  71.2 15.4 %collective-permute-start.6 = (bf16[256,1024]{1,0:T(8,128)(2,1)}, bf16[256,1024]{1,0:T(8,128)(2,1)}, u32[]{:S(2)}, u32[]{:S(2)}) collective-permute-start(bf16[256,1024]{1,0:T(8,128)(2,1)} %refs_7_.1), channel_id=1, source_target_pairs={{0,1},{1,2},{2,3},{3,0},{4,5},{5,6},{6,7},{7,4},{8,9},{9,10},{10,1... | collective-permute-start | bytes 1572872 | tf_op jit(solution)/shard_map/ppermute | solution.py:1091
  86.6 17.1 %collective-permute-start.7 = (bf16[256,1024]{1,0:T(8,128)(2,1)}, bf16[256,1024]{1,0:T(8,128)(2,1)}, u32[]{:S(2)}, u32[]{:S(2)}) collective-permute-start(bf16[256,1024]{1,0:T(8,128)(2,1)} %collective-permute-done.6.refs_1_.refs_5_), channel_id=1, source_target_pairs={{0,1},{1,2},{2,3},{3,0},{4,5},{5,6},{6,7},{7,4},{8,9},{9,10},{10,1... | collective-permute-start | bytes 1572872 | tf_op jit(solution)/shard_map/ppermute | solution.py:1018
  86.7 33.1 %all-to-all-start = ((bf16[4,256,256]{2,1,0:T(8,128)(2,1)}), bf16[4,256,256]{2,1,0:T(8,128)(2,1)}, u32[]{:S(2)}, u32[]{:S(2)}) async-start(bf16[4,256,256]{2,1,0:T(8,128)(2,1)} %bitcast.32), calls=%async_computation | async-start | bytes 1048576 | tf_op jit(solution)/shard_map/all_to_all | solution.py:1093
  92.4 306.4 %reduce-scatter.6.cloned.1.call-start = ((), (), s32[]{:S(2)}) async-start(), calls=%async_computation.6 | async-start | bytes 2506752 | tf_op jit(solution)/shard_map/reduce_scatter | solution.py:1135
  103.7 21.0 %collective-permute-start.8 = (bf16[256,1024]{1,0:T(8,128)(2,1)}, bf16[256,1024]{1,0:T(8,128)(2,1)}, u32[]{:S(2)}, u32[]{:S(2)}) collective-permute-start(bf16[256,1024]{1,0:T(8,128)(2,1)} %collective-permute-done.7.refs_2_.refs_1_.refs_6_), channel_id=1, source_target_pairs={{0,1},{1,2},{2,3},{3,0},{4,5},{5,6},{6,7},{7,4},{8,9},{9,10},{10,1... | collective-permute-start | bytes 1572872 | tf_op jit(solution)/shard_map/ppermute | solution.py:1018
  115.4 35.2 %collective-permute-start.13 = (bf16[2,3,1024,128]{3,2,1,0:T(8,128)(2,1)}, bf16[2,3,1024,128]{3,2,1,0:T(8,128)(2,1)}, u32[]{:S(2)}, u32[]{:S(2)}) collective-permute-start(bf16[2,3,1024,128]{3,2,1,0:T(8,128)(2,1)} %get-tuple-element.88), channel_id=1, source_target_pairs={{0,16},{4,20},{8,24},{12,28},{16,0},{20,4},{24,8},{28,12},{1,17},{... | collective-permute-start | bytes 4718600 | tf_op jit(solution)/shard_map/ppermute | solution.py:1047
  116.9 39.2 %collective-permute-start.12 = (bf16[2,3,1024,128]{3,2,1,0:T(8,128)(2,1)}, bf16[2,3,1024,128]{3,2,1,0:T(8,128)(2,1)}, u32[]{:S(2)}, u32[]{:S(2)}) collective-permute-start(bf16[2,3,1024,128]{3,2,1,0:T(8,128)(2,1)} %get-tuple-element.85.refs_7_), channel_id=1, source_target_pairs={{0,8},{4,12},{8,0},{12,4},{16,24},{20,28},{24,16},{28,20},{1,9},{5... | collective-permute-start | bytes 4718600 | tf_op jit(solution)/shard_map/ppermute | solution.py:1047
  117.4 56.3 %collective-permute-start.10 = (bf16[4,3,1024,128]{3,2,1,0:T(8,128)(2,1)}, bf16[4,3,1024,128]{3,2,1,0:T(8,128)(2,1)S(1)}, u32[]{:S(2)}, u32[]{:S(2)}) collective-permute-start(bf16[4,3,1024,128]{3,2,1,0:T(8,128)(2,1)} %collective-permute-done.4.refs_0_.refs_4_), channel_id=1, source_target_pairs={{0,4},{4,0},{8,12},{12,8},{16,20},{20,16},{24,28},{28,24},{1,5},{5... | collective-permute-start | bytes 9437192 | tf_op jit(solution)/shard_map/ppermute | solution.py:1047
  117.4 57.1 %collective-permute-start.11 = (bf16[4,3,1024,128]{3,2,1,0:T(8,128)(2,1)}, bf16[4,3,1024,128]{3,2,1,0:T(8,128)(2,1)}, u32[]{:S(2)}, u32[]{:S(2)}) collective-permute-start(bf16[4,3,1024,128]{3,2,1,0:T(8,128)(2,1)} %collective-permute-done.5.refs_1_.refs_6_), channel_id=1, source_target_pairs={{0,4},{4,0},{8,12},{12,8},{16,20},{20,16},{24,28},{28,24},{1,5},{5... | collective-permute-start | bytes 9437192 | tf_op jit(solution)/shard_map/ppermute | solution.py:1047
  124.8 16.2 %collective-permute-start.9 = (bf16[256,1152]{1,0:T(8,128)(2,1)}, bf16[256,1152]{1,0:T(8,128)(2,1)S(1)}, u32[]{:S(2)}, u32[]{:S(2)}) collective-permute-start(bf16[256,1152]{1,0:T(8,128)(2,1)} %get-tuple-element.87.refs_0_.refs_10_), channel_id=1, source_target_pairs={{0,1},{1,2},{2,3},{3,0},{4,5},{5,6},{6,7},{7,4},{8,9},{9,10},{10,1... | collective-permute-start | bytes 1769480 | tf_op jit(solution)/shard_map/ppermute | solution.py:1018
  156.0 18.5 %collective-permute-start.16 = (bf16[2,3,1024,128]{3,2,1,0:T(8,128)(2,1)}, bf16[2,3,1024,128]{3,2,1,0:T(8,128)(2,1)}, u32[]{:S(2)}, u32[]{:S(2)}) collective-permute-start(bf16[2,3,1024,128]{3,2,1,0:T(8,128)(2,1)} %collective-permute-done.13.refs_9_), channel_id=1, source_target_pairs={{0,4},{4,0},{8,12},{12,8},{16,20},{20,16},{24,28},{28,24},{1,5},{5... | collective-permute-start | bytes 4718600 | tf_op jit(solution)/shard_map/ppermute | solution.py:1047
  156.1 18.4 %collective-permute-start.15 = (bf16[2,3,1024,128]{3,2,1,0:T(8,128)(2,1)}, bf16[2,3,1024,128]{3,2,1,0:T(8,128)(2,1)}, u32[]{:S(2)}, u32[]{:S(2)}) collective-permute-start(bf16[2,3,1024,128]{3,2,1,0:T(8,128)(2,1)} %collective-permute-done.12.refs_8_), channel_id=1, source_target_pairs={{0,4},{4,0},{8,12},{12,8},{16,20},{20,16},{24,28},{28,24},{1,5},{5... | collective-permute-start | bytes 4718600 | tf_op jit(solution)/shard_map/ppermute | solution.py:1047
  156.6 17.1 %collective-permute-start.17 = (bf16[256,1152]{1,0:T(8,128)(2,1)S(1)}, bf16[256,1152]{1,0:T(8,128)(2,1)S(1)}, u32[]{:S(2)}, u32[]{:S(2)}) collective-permute-start(bf16[256,1152]{1,0:T(8,128)(2,1)S(1)} %collective-permute-done.14.refs_0_.refs_2_), channel_id=1, source_target_pairs={{0,1},{1,2},{2,3},{3,0},{4,5},{5,6},{6,7},{7,4},{8,9},{9,10},{10,1... | collective-permute-start | bytes 1769480 | tf_op jit(solution)/shard_map/ppermute | solution.py:1018
  197.8 27.8 %collective-permute-start.18 = (bf16[256,2176]{1,0:T(8,128)(2,1)}, bf16[256,2176]{1,0:T(8,128)(2,1)S(1)}, u32[]{:S(2)}, u32[]{:S(2)}) collective-permute-start(bf16[256,2176]{1,0:T(8,128)(2,1)} %get-tuple-element.91), channel_id=1, source_target_pairs={{0,1},{1,2},{2,3},{3,0},{4,5},{5,6},{6,7},{7,4},{8,9},{9,10},{10,1... | collective-permute-start | bytes 3342344 | tf_op jit(solution)/shard_map/ppermute | solution.py:1117
  227.5 27.1 %collective-permute-start.19 = (bf16[256,2176]{1,0:T(8,128)(2,1)S(1)}, bf16[256,2176]{1,0:T(8,128)(2,1)S(1)}, u32[]{:S(2)}, u32[]{:S(2)}) collective-permute-start(bf16[256,2176]{1,0:T(8,128)(2,1)S(1)} %add_convert_fusion.1), channel_id=1, source_target_pairs={{0,1},{1,2},{2,3},{3,0},{4,5},{5,6},{6,7},{7,4},{8,9},{9,10},{10,1... | collective-permute-start | bytes 3342344 | tf_op jit(solution)/shard_map/ppermute | solution.py:1117
  256.5 26.8 %collective-permute-start.20 = (bf16[256,2176]{1,0:T(8,128)(2,1)S(1)}, bf16[256,2176]{1,0:T(8,128)(2,1)S(1)}, u32[]{:S(2)}, u32[]{:S(2)}) collective-permute-start(bf16[256,2176]{1,0:T(8,128)(2,1)S(1)} %add_convert_fusion), channel_id=1, source_target_pairs={{0,1},{1,2},{2,3},{3,0},{4,5},{5,6},{6,7},{7,4},{8,9},{9,10},{10,1... | collective-permute-start | bytes 3342344 | tf_op jit(solution)/shard_map/ppermute | solution.py:1117
  310.0 64.8 %collective-permute-start.22 = (bf16[4,2,3,1024,128]{4,3,2,1,0:T(8,128)(2,1)}, bf16[4,2,3,1024,128]{4,3,2,1,0:T(8,128)(2,1)}, u32[]{:S(2)}, u32[]{:S(2)}) collective-permute-start(bf16[4,2,3,1024,128]{4,3,2,1,0:T(8,128)(2,1)} %shard_map.248.refs_15_), channel_id=1, source_target_pairs={{0,4},{4,0},{8,12},{12,8},{16,20},{20,16},{24,28},{28,24},{1,5},{5... | collective-permute-start | bytes 18874376 | tf_op jit(solution)/shard_map/ppermute | solution.py:1047
  329.6 109.0 %reduce-scatter.8.cloned.1.call-start = ((), (), s32[]{:S(2)}) async-start(), calls=%async_computation.7 | async-start | bytes 348160 | tf_op jit(solution)/shard_map/reduce_scatter | solution.py:1166
  329.6 42.6 %collective-permute-start.23 = (bf16[1,2,3,1024,128]{4,3,2,1,0:T(8,128)(2,1)}, bf16[1,2,3,1024,128]{4,3,2,1,0:T(8,128)(2,1)S(1)}, u32[]{:S(2)}, u32[]{:S(2)}) collective-permute-start(bf16[1,2,3,1024,128]{4,3,2,1,0:T(8,128)(2,1)} %get-tuple-element.123), channel_id=1, source_target_pairs={{0,16},{4,20},{8,24},{12,28},{16,0},{20,4},{24,8},{28,12},{1,17},{... | collective-permute-start | bytes 4718600 | tf_op jit(solution)/shard_map/ppermute | solution.py:1047
  329.9 45.0 %collective-permute-start.24 = (bf16[1,2,3,1024,128]{4,3,2,1,0:T(8,128)(2,1)}, bf16[1,2,3,1024,128]{4,3,2,1,0:T(8,128)(2,1)S(1)}, u32[]{:S(2)}, u32[]{:S(2)}) collective-permute-start(bf16[1,2,3,1024,128]{4,3,2,1,0:T(8,128)(2,1)} %get-tuple-element.114.refs_11_), channel_id=1, source_target_pairs={{0,8},{4,12},{8,0},{12,4},{16,24},{20,28},{24,16},{28,20},{1,9},{5... | collective-permute-start | bytes 4718600 | tf_op jit(solution)/shard_map/ppermute | solution.py:1047
  395.0 44.5 %collective-permute-start.29 = (bf16[2,2,3,1024,128]{4,3,2,1,0:T(8,128)(2,1)}, bf16[2,2,3,1024,128]{4,3,2,1,0:T(8,128)(2,1)}, u32[]{:S(2)}, u32[]{:S(2)}) collective-permute-start(bf16[2,2,3,1024,128]{4,3,2,1,0:T(8,128)(2,1)} %get-tuple-element.132), channel_id=1, source_target_pairs={{0,4},{4,0},{8,12},{12,8},{16,20},{20,16},{24,28},{28,24},{1,5},{5... | collective-permute-start | bytes 9437192 | tf_op jit(solution)/shard_map/ppermute | solution.py:1047
  395.1 37.6 %collective-permute-start.26 = (bf16[1,2,3,1024,128]{4,3,2,1,0:T(8,128)(2,1)}, bf16[1,2,3,1024,128]{4,3,2,1,0:T(8,128)(2,1)S(1)}, u32[]{:S(2)}, u32[]{:S(2)}) collective-permute-start(bf16[1,2,3,1024,128]{4,3,2,1,0:T(8,128)(2,1)} %get-tuple-element.128), channel_id=1, source_target_pairs={{0,8},{4,12},{8,0},{12,4},{16,24},{20,28},{24,16},{28,20},{1,9},{5... | collective-permute-start | bytes 4718600 | tf_op jit(solution)/shard_map/ppermute | solution.py:1047
  397.5 36.8 %collective-permute-start.27 = (bf16[1,2,3,1024,128]{4,3,2,1,0:T(8,128)(2,1)}, bf16[1,2,3,1024,128]{4,3,2,1,0:T(8,128)(2,1)}, u32[]{:S(2)}, u32[]{:S(2)}) collective-permute-start(bf16[1,2,3,1024,128]{4,3,2,1,0:T(8,128)(2,1)} %get-tuple-element.129), channel_id=1, source_target_pairs={{0,16},{4,20},{8,24},{12,28},{16,0},{20,4},{24,8},{28,12},{1,17},{... | collective-permute-start | bytes 4718600 | tf_op jit(solution)/shard_map/ppermute | solution.py:1047
  398.9 59.3 %reduce-scatter.4.cloned.1.call-start = ((), (), s32[]{:S(2)}) async-start(), calls=%async_computation.5 | async-start | bytes 1253376 | tf_op jit(solution)/shard_map/reduce_scatter | solution.py:1164
  416.2 15.8 %collective-permute-start.25 = (bf16[256,1024]{1,0:T(8,128)(2,1)}, bf16[256,1024]{1,0:T(8,128)(2,1)S(1)}, u32[]{:S(2)}, u32[]{:S(2)}) collective-permute-start(bf16[256,1024]{1,0:T(8,128)(2,1)} %get-tuple-element.127), channel_id=1, source_target_pairs={{0,1},{1,2},{2,3},{3,0},{4,5},{5,6},{6,7},{7,4},{8,9},{9,10},{10,1... | collective-permute-start | bytes 1572872 | tf_op jit(solution)/shard_map/ppermute | solution.py:1151
  436.5 41.1 %collective-permute-start.34 = (bf16[1,2,3,1024,128]{4,3,2,1,0:T(8,128)(2,1)}, bf16[1,2,3,1024,128]{4,3,2,1,0:T(8,128)(2,1)}, u32[]{:S(2)}, u32[]{:S(2)}) collective-permute-start(bf16[1,2,3,1024,128]{4,3,2,1,0:T(8,128)(2,1)} %get-tuple-element.126.refs_12_), channel_id=1, source_target_pairs={{0,8},{4,12},{8,0},{12,4},{16,24},{20,28},{24,16},{28,20},{1,9},{5... | collective-permute-start | bytes 4718600 | tf_op jit(solution)/shard_map/ppermute | solution.py:1047
  437.2 40.5 %collective-permute-start.35 = (bf16[1,2,3,1024,128]{4,3,2,1,0:T(8,128)(2,1)}, bf16[1,2,3,1024,128]{4,3,2,1,0:T(8,128)(2,1)}, u32[]{:S(2)}, u32[]{:S(2)}) collective-permute-start(bf16[1,2,3,1024,128]{4,3,2,1,0:T(8,128)(2,1)} %get-tuple-element.142), channel_id=1, source_target_pairs={{0,16},{4,20},{8,24},{12,28},{16,0},{20,4},{24,8},{28,12},{1,17},{... | collective-permute-start | bytes 4718600 | tf_op jit(solution)/shard_map/ppermute | solution.py:1047
  (36 other events, 352.0 us)
Sparse Core Ops, SparseCore 0:
  10.5 29.4 all-gather.5
  41.8 37.7 all-gather.7
  329.7 47.1 reduce-scatter.5
  399.0 16.3 reduce-scatter.7
  419.0 39.0 reduce-scatter.3
